TPU v7x, 32 devices: a whole 2x2x4 slice. The times are simulated.
32 devices in a mesh: row: 8 (over z, core), col: 4 (over y, x).
Axes of the slice: x: 2, y: 2, z: 4, core: 2. Of those that a mesh axis runs over, the one named last changes fastest.
Arguments:
- momentum_shards: bfloat16 [7168, 18432], P(('row', 'col')), may hold values from -0.078125 to 0.078125
- shard_starts: int32 [32], replicated, may hold values from 0 to 3528, as said below
Outputs:
- update_shards: bfloat16 [7168, 18432], P(('row', 'col'))
Inputs may be any that keep to these rules, and one draw needn't show every extreme that they name: `shard_starts`: starts never fall and the first is 0; shard d starts within 56 rows of d * 112, and the last one exactly 56 rows after it. Every shard has at most 224 rows and some shard has exactly 224; the 4 shards of one index of row hold at most 560 rows together, and on some index exactly 560.
All inputs are finite; a program needn't handle non-finite values.
Results may differ from a plain program's by a relative error of at most 0.02.
Values may be sent and summed in bfloat16 or wider, within the bound.
No kernel may reach another device: no remote copies, remote signals or barrier semaphores. Data moves between devices by JAX's collectives and lax.ppermute only.
A program may use at most 128 MiB of HBM per device.

v0:
```python
import math

import jax
import jax.numpy as jnp
from jax import lax
from jax.sharding import PartitionSpec as P

M = 3584
N = 18432


coef_one = 3.4445
coef_two = -4.775
coef_three = 2.0315


def packing(shard_starts, row_block, col_count, shard_rows, window):
    shard_ends = jnp.concatenate([shard_starts[1:], jnp.full((1,), M, jnp.int32)])
    first_starts = lax.dynamic_slice_in_dim(shard_starts, row_block * col_count, col_count)
    last_ends = lax.dynamic_slice_in_dim(shard_ends, row_block * col_count, col_count)
    slot_index = jnp.arange(col_count * shard_rows, dtype=jnp.int32)
    member = slot_index // shard_rows
    offset = slot_index % shard_rows
    pick = member[:, None] == jnp.arange(col_count, dtype=jnp.int32)[None, :]
    shard_begin = jnp.sum(jnp.where(pick, first_starts[None, :], 0), axis=1)
    length = jnp.sum(jnp.where(pick, (last_ends - first_starts)[None, :], 0), axis=1)
    target = shard_begin - first_starts[0] + offset
    is_valid = offset < length
    window_rows = jnp.arange(window, dtype=jnp.int32)
    return ((window_rows[:, None] == target[None, :]) & is_valid[None, :]).astype(jnp.bfloat16)


def body(momentum_shards, shard_starts):
    col_count = lax.axis_size("col")
    row_count = lax.axis_size("row")
    shard_rows = momentum_shards.shape[0]
    mean_rows = M // (row_count * col_count)
    jitter = 4 * (mean_rows // 8)
    window = col_count * mean_rows + 2 * jitter
    packer = packing(shard_starts, lax.axis_index("row"), col_count, shard_rows, window)
    columns = lax.all_to_all(momentum_shards, "col", split_axis=1, concat_axis=0, tiled=True)
    local_tile = jnp.dot(packer, columns, preferred_element_type=jnp.float32).astype(jnp.bfloat16)
    col_panel = lax.all_gather(local_tile, "row", axis=0, tiled=True)
    own_block = lax.psum_scatter(
        lax.dot_general(
            col_panel, local_tile, (((1,), (1,)), ((), ())), preferred_element_type=jnp.float32
        ).astype(jnp.bfloat16),
        "col",
        scatter_dimension=0,
        tiled=True,
    )
    across = lax.all_gather(own_block, "row", axis=1, tiled=True)
    square_own = lax.psum_scatter(
        lax.dot_general(
            across, own_block, (((0,), (0,)), ((), ())), preferred_element_type=jnp.float32
        ).astype(jnp.bfloat16),
        "col",
        scatter_dimension=0,
        tiled=True,
    ).astype(jnp.float32)
    poly_own = (coef_two * own_block.astype(jnp.float32) + coef_three * square_own).astype(
        jnp.bfloat16
    )
    poly_block = lax.all_gather(poly_own, "col", axis=0, tiled=True)
    mixed_part = lax.dot_general(
        poly_block, col_panel, (((0,), (0,)), ((), ())), preferred_element_type=jnp.float32
    )
    update = (math.sqrt(N) * (coef_one * local_tile.astype(jnp.float32) + mixed_part)).astype(
        jnp.bfloat16
    )
    back_rows = lax.dot_general(
        packer, update, (((0,), (0,)), ((), ())), preferred_element_type=jnp.float32
    ).astype(jnp.bfloat16)
    return lax.all_to_all(back_rows, "col", split_axis=0, concat_axis=1, tiled=True)


def solution(mesh):
    in_specs = (P(("row", "col"), None), P())
    out_specs = P(("row", "col"), None)
    return jax.shard_map(body, mesh=mesh, in_specs=in_specs, out_specs=out_specs, check_vma=False)
```

profile of v0, /device:TPU:0, one launch (start us, length us, event | category | flops | bytes accessed | tf_op | source)
XLA Modules:
  0.0 995.4 jit_solution(9713402960707273552)
XLA Ops:
  6.5 7.5 copy.22
  14.0 5.8 all-to-all-start
  20.1 0.1 select_reduce_fusion
  20.2 92.0 %all-to-all-done = bf16[224,4,4608]{2,0,1:T(8,128)(2,1)} async-done(((bf16[224,4,4608]{2,0,1:T(8,128)(2,1)}), bf16[224,4,4608]{2,0,1:T(8,128)(2,1)}, u32[]{:S(2)}, u32[]{:S(2)}) %all-to-all-start) | async-done | bytes 8257568 | tf_op jit(solution)/shard_map/all_to_all | solution.py:41
  112.2 10.5 %convolution_convert_fusion.3 = bf16[560,4608]{1,0:T(8,128)(2,1)} fusion(bf16[896,4608]{1,0:T(8,128)(2,1)} %bitcast.2, s32[896]{0:T(1024)S(1)} %fusion.15, pred[896]{0:T(1024)(128)(4,1)S(1)} %fusion.14), kind=kOutput, calls=%fused_computation.5 | convolution fusion | flops 4627804160 | bytes 13422976 | tf_op jit(solution)/shard_map/dot_general | solution.py:42
  122.8 354.1 %all-gather.5.cloned.1.call-done = bf16[4480,4608]{1,0:T(8,128)(2,1)} async-done(((bf16[560,4608]{1,0:T(8,128)(2,1)}), bf16[4480,4608]{1,0:T(8,128)(2,1)}) %all-gather.5.cloned.1.call-update) | async-done | bytes 41287696 | tf_op jit(solution)/shard_map/all_gather | solution.py:43
  476.9 32.3 %convolution_convert_fusion.2 = bf16[4480,560]{0,1:T(8,128)(2,1)} fusion(bf16[4480,4608]{1,0:T(8,128)(2,1)} %all-gather.5.cloned.1.call-done, bf16[560,4608]{1,0:T(8,128)(2,1)} %convolution_convert_fusion.3), kind=kOutput, calls=%fused_computation.4 | convolution fusion | flops 23123609600 | bytes 51466240 | tf_op jit(solution)/shard_map/dot_general | solution.py:45
  509.2 8.1 copy.15
  517.4 64.3 %reduce-scatter.7.cloned.1.call-done = bf16[1120,560]{1,0:T(8,128)(2,1)} async-done(((bf16[4480,560]{1,0:T(8,128)(2,1)}), bf16[1120,560]{1,0:T(8,128)(2,1)}) %reduce-scatter.7.cloned.1.call-update) | async-done | bytes 1254416
  581.7 2.6 copy.16
  584.3 0.2 reduce-scatter.9.cloned.1.call-start
  584.5 98.0 %all-gather.7.cloned.1.call-done = bf16[1120,4480]{0,1:T(8,128)(2,1)} async-done(((bf16[1120,560]{0,1:T(8,128)(2,1)}), bf16[1120,4480]{0,1:T(8,128)(2,1)}) %all-gather.7.cloned.1.call-update) | async-done | bytes 10035216 | tf_op jit(solution)/shard_map/all_gather | solution.py:52
  682.5 11.6 %convolution_convert_fusion.1 = bf16[4480,560]{0,1:T(8,128)(2,1)} fusion(bf16[1120,4480]{0,1:T(8,128)(2,1)} %all-gather.7.cloned.1.call-done, bf16[1120,560]{1,0:T(8,128)(2,1)} %reduce-scatter.7.cloned.1.call-done), kind=kOutput, calls=%fused_computation.3 | convolution fusion | flops 5622220800 | bytes 16307200 | tf_op jit(solution)/shard_map/dot_general | solution.py:54
  694.0 8.1 copy.17
  702.3 64.1 %reduce-scatter.9.cloned.1.call-done = bf16[1120,560]{1,0:T(8,128)(2,1)} async-done(((bf16[4480,560]{1,0:T(8,128)(2,1)}), bf16[1120,560]{1,0:T(8,128)(2,1)}) %reduce-scatter.9.cloned.1.call-update) | async-done | bytes 1254416
  766.3 1.9 copy.18
  768.2 1.5 fusion.3
  769.8 60.9 %all-gather.9.cloned.1.call-done = bf16[4,1120,560]{1,2,0:T(8,128)(2,1)} async-done(((bf16[1,1120,560]{1,2,0:T(8,128)(2,1)}), bf16[4,1120,560]{1,2,0:T(8,128)(2,1)}) %all-gather.9.cloned.1.call-update) | async-done | bytes 5017616 | tf_op jit(solution)/shard_map/all_gather | solution.py:64
  830.7 6.8 copy.13
  837.5 9.6 reshape.40
  847.0 31.4 %multiply_convert_fusion = bf16[560,4608]{1,0:T(8,128)(2,1)S(1)} fusion(bf16[560,4608]{1,0:T(8,128)(2,1)} %convolution_convert_fusion.3, bf16[4480,560]{0,1:T(8,128)(2,1)} %reshape.40, bf16[4480,4608]{1,0:T(8,128)(2,1)} %all-gather.5.cloned.1.call-done), kind=kOutput, calls=%fused_computation | convolution fusion | flops 23134003200 | bytes 56627200 | tf_op jit(solution)/shard_map/dot_general | solution.py:65
  878.5 7.2 convolution_convert_fusion
  885.6 95.4 %all_to_all.38 = bf16[4,224,4608]{2,1,0:T(8,128)(2,1)} all-to-all(bf16[4,224,4608]{2,1,0:T(8,128)(2,1)S(1)} %bitcast.30), channel_id=1, replica_groups=mesh['row'=8,'col'=4] {'col'}, dimensions={0} | all-to-all | bytes 16515072 | tf_op jit(solution)/shard_map/all_to_all | solution.py:74
  981.1 7.8 copy.20
  (19 shorter events, 0.6 us)
Async XLA Ops:
  14.0 5.8 copy-start.1
  14.0 98.2 %all-to-all-start = ((bf16[224,4,4608]{2,0,1:T(8,128)(2,1)}), bf16[224,4,4608]{2,0,1:T(8,128)(2,1)}, u32[]{:S(2)}, u32[]{:S(2)}) async-start(bf16[224,4,4608]{2,0,1:T(8,128)(2,1)} %bitcast.27), calls=%async_computation | async-start | bytes 16515072 | tf_op jit(solution)/shard_map/all_to_all | solution.py:41
  19.8 457.1 %all-gather.5.cloned.1.call-start = ((), (), s32[]{:S(2)}) async-start(), calls=%async_computation.4 | async-start | bytes 46448640 | tf_op jit(solution)/shard_map/all_gather | solution.py:43
  122.7 458.9 %reduce-scatter.7.cloned.1.call-start = ((), (), s32[]{:S(2)}) async-start(), calls=%async_computation.7 | async-start | bytes 7168000
  517.3 165.1 %all-gather.7.cloned.1.call-start = ((), (), s32[]{:S(2)}) async-start(), calls=%async_computation.5 | async-start | bytes 11612160 | tf_op jit(solution)/shard_map/all_gather | solution.py:52
  584.3 182.1 %reduce-scatter.9.cloned.1.call-start = ((), (), s32[]{:S(2)}) async-start(), calls=%async_computation.8 | async-start | bytes 7168000
  702.2 66.0 %copy-start = (bf16[1120,560]{0,1:T(8,128)(2,1)S(1)}, bf16[1120,560]{0,1:T(8,128)(2,1)}, u32[]{:S(2)}) copy-start(bf16[1120,560]{0,1:T(8,128)(2,1)} %copy.16) | copy-start | bytes 3763204
  702.2 128.5 %all-gather.9.cloned.1.call-start = ((), (), s32[]{:S(2)}) async-start(), calls=%async_computation.6 | async-start | bytes 6451200 | tf_op jit(solution)/shard_map/all_gather | solution.py:64
Sparse Core Ops, SparseCore 0:
  122.9 353.9 all-gather.4
  517.5 64.1 reduce-scatter.6
  584.4 98.0 all-gather.6
  702.3 63.9 reduce-scatter.8
  769.9 60.7 all-gather.8
where the time goes:
time: 996 us; the launch traced here: 995 us
  waiting for transfers between devices  733 us (74%)
  blocking collectives  95.4 us (10%)
  matrix products  93 us (9%)
  local copies, waits for them, and re-layouts  52.4 us (5%)
  between operations  13.2 us (1%)
    all_gather x1, waiting for transfers between devices, body(): col_panel = lax.all_gather(local_tile, 'row', axis=0, tiled=True)  354 us
    unnamed x7, waiting for transfers between devices  128 us
    all_gather x1, waiting for transfers between devices, body(): across = lax.all_gather(own_block, 'row', axis=1, tiled=True)  98 us
    all_to_all x1, blocking collectives, body(): lax.all_to_all(back_rows, 'col', split_axis=0, concat_axis=1, tiled=True)  95.4 us
    all_to_all x1, waiting for transfers between devices, body(): lax.all_to_all(momentum_shards, 'col', split_axis=1, concat_axis=0, tiled...  92 us
    all_gather x1, waiting for transfers between devices, body(): poly_block = lax.all_gather(poly_own, 'col', axis=0, tiled=True)  60.9 us
    dot_general x1, matrix products, body(): lax.dot_general(col_panel, local_tile, (((1,), (1,)), ((), ())), preferre...  32.3 us
    dot_general x1, matrix products, body(): lax.dot_general(poly_block, col_panel, (((0,), (0,)), ((), ())), preferre...  31.4 us
  transfers between devices with their start and end apart: 6, of which 6 were waited for; matrix products, arithmetic and copies ran while one was open for 0% of the time, Pallas kernels for 0%

commit v1 on v0

v1 whole, which is shorter than its diff:
```python
import math

import jax
import jax.numpy as jnp
import numpy as np
from jax import lax
from jax.experimental import pallas as pl
from jax.experimental.pallas import tpu as pltpu
from jax.sharding import PartitionSpec as P

M = 3584
N = 18432
TILE = 512
BLOCKS = M // TILE

coef_one = 3.4445
coef_two = -4.775
coef_three = 2.0315

PAIRS = [(i, j) for i in range(BLOCKS) for j in range(i, BLOCKS)]
PAIR_ROWS = np.array([i for i, _ in PAIRS], np.int32)
PAIR_COLS = np.array([j for _, j in PAIRS], np.int32)


def packing(shard_starts, row_block, col_count, shard_rows, window, first_row):
    shard_ends = jnp.concatenate([shard_starts[1:], jnp.full((1,), M, jnp.int32)])
    first_starts = lax.dynamic_slice_in_dim(shard_starts, row_block * col_count, col_count)
    last_ends = lax.dynamic_slice_in_dim(shard_ends, row_block * col_count, col_count)
    slot_index = jnp.arange(col_count * shard_rows, dtype=jnp.int32)
    member = slot_index // shard_rows
    offset = slot_index % shard_rows
    pick = member[:, None] == jnp.arange(col_count, dtype=jnp.int32)[None, :]
    shard_begin = jnp.sum(jnp.where(pick, first_starts[None, :], 0), axis=1)
    length = jnp.sum(jnp.where(pick, (last_ends - first_starts)[None, :], 0), axis=1)
    target = shard_begin - first_row + offset
    is_valid = offset < length
    window_rows = jnp.arange(window, dtype=jnp.int32)
    return ((window_rows[:, None] == target[None, :]) & is_valid[None, :]).astype(jnp.bfloat16)


def gram_kernel(rows_ref, cols_ref, left_ref, right_ref, out_ref):
    out_ref[...] = lax.dot_general(
        left_ref[...], right_ref[...], (((1,), (1,)), ((), ())), preferred_element_type=jnp.float32
    ).astype(jnp.bfloat16)


def gram_tiles(matrix):
    width = matrix.shape[1]
    count = len(PAIRS)
    return pl.pallas_call(
        gram_kernel,
        out_shape=jax.ShapeDtypeStruct((count * TILE, TILE), jnp.bfloat16),
        grid_spec=pltpu.PrefetchScalarGridSpec(
            num_scalar_prefetch=2,
            grid=(count,),
            in_specs=[
                pl.BlockSpec((TILE, width), lambda p, rows, cols: (rows[p], 0)),
                pl.BlockSpec((TILE, width), lambda p, rows, cols: (cols[p], 0)),
            ],
            out_specs=pl.BlockSpec((TILE, TILE), lambda p, rows, cols: (p, 0)),
        ),
        compiler_params=pltpu.CompilerParams(vmem_limit_bytes=32 * 1024 * 1024),
        cost_estimate=pl.CostEstimate(
            flops=2 * count * TILE * TILE * width,
            bytes_accessed=2 * count * TILE * (TILE + width),
            transcendentals=0,
        ),
    )(jnp.asarray(PAIR_ROWS), jnp.asarray(PAIR_COLS), matrix, matrix)


def apply_kernel(rows_ref, cols_ref, tile_ref, matrix_ref, out_ref, total, factor):
    turn = pl.program_id(0)
    pair = pl.program_id(1)
    i = rows_ref[pair]
    j = cols_ref[pair]
    here = pl.ds(pl.multiple_of(i * TILE, TILE), TILE)
    there = pl.ds(pl.multiple_of(j * TILE, TILE), TILE)

    @pl.when((turn == 0) & (pair == 0))
    def _():
        total[...] = jnp.zeros_like(total)
        factor[...] = matrix_ref[...]

    @pl.when((turn == 1) & (pair == 0))
    def _():
        @pl.loop(0, BLOCKS)
        def _(b):
            part = pl.ds(pl.multiple_of(b * TILE, TILE), TILE)
            product = total[part, :]
            factor[part, :] = (coef_three * product).astype(jnp.bfloat16)
            total[part, :] = coef_one * matrix_ref[part, :].astype(jnp.float32) + coef_two * product

    total[here, :] += jnp.dot(tile_ref[...], factor[there, :], preferred_element_type=jnp.float32)

    @pl.when(i != j)
    def _():
        total[there, :] += lax.dot_general(
            tile_ref[...], factor[here, :], (((0,), (0,)), ((), ())), preferred_element_type=jnp.float32
        )

    @pl.when((turn == 1) & (pair == pl.num_programs(1) - 1))
    def _():
        @pl.loop(0, BLOCKS)
        def _(b):
            part = pl.ds(pl.multiple_of(b * TILE, TILE), TILE)
            out_ref[part, :] = (math.sqrt(N) * total[part, :]).astype(jnp.bfloat16)


def apply_polynomial(tiles, matrix):
    rows, width = matrix.shape
    count = len(PAIRS)
    return pl.pallas_call(
        apply_kernel,
        out_shape=jax.ShapeDtypeStruct((rows, width), jnp.bfloat16),
        grid_spec=pltpu.PrefetchScalarGridSpec(
            num_scalar_prefetch=2,
            grid=(2, count),
            in_specs=[
                pl.BlockSpec((TILE, TILE), lambda t, p, rows, cols: (p, 0)),
                pl.BlockSpec((rows, width), lambda t, p, rows, cols: (0, 0)),
            ],
            out_specs=pl.BlockSpec((rows, width), lambda t, p, rows, cols: (0, 0)),
            scratch_shapes=[
                pltpu.VMEM((rows, width), jnp.float32),
                pltpu.VMEM((rows, width), jnp.bfloat16),
            ],
        ),
        compiler_params=pltpu.CompilerParams(vmem_limit_bytes=48 * 1024 * 1024),
        cost_estimate=pl.CostEstimate(
            flops=4 * rows * rows * width,
            bytes_accessed=4 * rows * width + 4 * count * TILE * TILE,
            transcendentals=0,
        ),
    )(jnp.asarray(PAIR_ROWS), jnp.asarray(PAIR_COLS), tiles, matrix)


def body(momentum_shards, shard_starts):
    col_count = lax.axis_size("col")
    row_count = lax.axis_size("row")
    shard_rows = momentum_shards.shape[0]
    mean_rows = M // (row_count * col_count)
    jitter = 4 * (mean_rows // 8)
    even = col_count * mean_rows
    window = even + 2 * jitter
    row_block = lax.axis_index("row")
    packer = packing(
        shard_starts, row_block, col_count, shard_rows, window, row_block * even - jitter
    )
    columns = lax.all_to_all(momentum_shards, "col", split_axis=1, concat_axis=0, tiled=True)
    local_tile = jnp.dot(packer, columns, preferred_element_type=jnp.float32).astype(jnp.bfloat16)
    windows = lax.all_to_all(local_tile, "row", split_axis=1, concat_axis=0, tiled=True)
    width = windows.shape[1]
    windows = windows.reshape(row_count, window, width)
    nothing = jnp.zeros((1, jitter, width), jnp.bfloat16)
    head = jnp.concatenate([nothing, windows[:-1, jitter + even :]], axis=0)
    tail = jnp.concatenate([windows[1:, :jitter], nothing], axis=0)
    middle = windows[:, jitter : jitter + even]
    matrix = jnp.concatenate(
        [
            middle[:, :jitter] + head,
            middle[:, jitter : even - jitter],
            middle[:, even - jitter :] + tail,
        ],
        axis=1,
    ).reshape(M, width)

    tiles = lax.psum(gram_tiles(matrix), ("row", "col"))
    update = apply_polynomial(tiles, matrix).reshape(row_count, even, width)

    before = jnp.concatenate([nothing, update[:-1, even - jitter :]], axis=0)
    after = jnp.concatenate([update[1:, :jitter], nothing], axis=0)
    spread = jnp.concatenate([before, update, after], axis=1).reshape(row_count * window, width)
    own_rows = lax.all_to_all(spread, "row", split_axis=0, concat_axis=1, tiled=True)
    back_rows = lax.dot_general(
        packer, own_rows, (((0,), (0,)), ((), ())), preferred_element_type=jnp.float32
    ).astype(jnp.bfloat16)
    return lax.all_to_all(back_rows, "col", split_axis=0, concat_axis=1, tiled=True)


def solution(mesh):
    in_specs = (P(("row", "col"), None), P())
    out_specs = P(("row", "col"), None)
    return jax.shard_map(body, mesh=mesh, in_specs=in_specs, out_specs=out_specs, check_vma=False)
```

time: 996 us -> 883 us (0.89)
  waiting for transfers between devices: 733 us -> 343 us
  blocking collectives: 95.4 us -> 358 us
  Pallas kernels: 0 us -> 88.7 us
  matrix products: 93 us -> 19.2 us
    all_gather x3 -> x0, waiting for transfers between devices: 513 us -> none  [the longest x1 354 us: body(): col_panel = lax.all_gather(local_tile, 'row', axis=0, tiled=True)]
    all_to_all x0 -> x2, blocking collectives: none -> 263 us  [the longest x1 132 us: body(): lax.all_to_all(local_tile, 'row', split_axis=1, concat_axis=0, tiled=True)]
    psum x0 -> x1, waiting for transfers between devices: none -> 251 us  [body(): tiles = lax.psum(gram_tiles(matrix), ('row', 'col'))]
    unnamed x7 -> x1, waiting for transfers between devices: 128 us -> 0.02 us
    pallas_call x0 -> x2, Pallas kernels: none -> 88.7 us  [the longest x1 71 us: apply_polynomial(): pl.pallas_call(apply_kernel, out_shape=jax.ShapeDtypeStruct((rows, width)...]
    dot_general x4 -> x1, matrix products: 82.5 us -> 8.61 us  [body(): lax.dot_general(packer, own_rows, (((0,), (0,)), ((), ())), preferred_ele...]
    all_to_all x0 -> x4, local copies, waits for them, and re-layouts: none -> 26.7 us  [the longest x2 13.4 us: body(): lax.all_to_all(spread, 'row', split_axis=0, concat_axis=1, tiled=True)]
    unnamed x9 -> x10, local copies, waits for them, and re-layouts: 30.3 us -> 7.31 us
  transfers between devices with their start and end apart: 6 -> 2, of which waited for: 6 -> 2; matrix products, arithmetic and copies ran while one was open for 0% -> 0% of each run, Pallas kernels for 0% -> 0%
where the time goes in v1:
time: 883 us; the launch traced here: 882 us
  blocking collectives  358 us (41%)
  waiting for transfers between devices  343 us (39%)
  Pallas kernels  88.7 us (10%)
  local copies, waits for them, and re-layouts  49.8 us (6%)
  matrix products  19.2 us (2%)
  between operations  13.6 us (2%)
    psum x1, waiting for transfers between devices, body(): tiles = lax.psum(gram_tiles(matrix), ('row', 'col'))  251 us
    all_to_all x1, blocking collectives, body(): lax.all_to_all(local_tile, 'row', split_axis=1, concat_axis=0, tiled=True)  132 us
    all_to_all x1, blocking collectives, body(): lax.all_to_all(spread, 'row', split_axis=0, concat_axis=1, tiled=True)  131 us
    all_to_all x1, blocking collectives, body(): lax.all_to_all(back_rows, 'col', split_axis=0, concat_axis=1, tiled=True)  95.1 us
    all_to_all x1, waiting for transfers between devices, body(): lax.all_to_all(momentum_shards, 'col', split_axis=1, concat_axis=0, tiled...  92 us
    pallas_call x1, Pallas kernels, apply_polynomial(): pl.pallas_call(apply_kernel, out_shape=jax.ShapeDtypeStruct((rows, width)...  71 us
    pallas_call x1, Pallas kernels, gram_tiles(): pl.pallas_call(gram_kernel, out_shape=jax.ShapeDtypeStruct((count * TILE,...  17.8 us
  transfers between devices with their start and end apart: 2, of which 2 were waited for; matrix products, arithmetic and copies ran while one was open for 0% of the time, Pallas kernels for 0%

profile of v1, /device:TPU:0, one launch (start us, length us, event | category | flops | bytes accessed | tf_op | source)
XLA Modules:
  0.0 882.0 jit_solution(17346491066482884925)
XLA Ops:
  6.5 7.5 copy.29
  14.0 5.7 all-to-all-start
  20.0 0.1 select_reduce_fusion
  20.2 92.0 %all-to-all-done = bf16[224,4,4608]{2,0,1:T(8,128)(2,1)} async-done(((bf16[224,4,4608]{2,0,1:T(8,128)(2,1)}), bf16[224,4,4608]{2,0,1:T(8,128)(2,1)}, u32[]{:S(2)}, u32[]{:S(2)}) %all-to-all-start) | async-done | bytes 8257568 | tf_op jit(solution)/shard_map/all_to_all | solution.py:149
  112.2 10.6 %convolution_convert_fusion.1 = bf16[560,4608]{1,0:T(8,128)(2,1)} fusion(bf16[896,4608]{1,0:T(8,128)(2,1)} %bitcast.1, s32[896]{0:T(1024)S(1)} %fusion.18, pred[896]{0:T(1024)(128)(4,1)S(1)} %fusion.17), kind=kOutput, calls=%fused_computation.6 | convolution fusion | flops 4627804160 | bytes 13422976 | tf_op jit(solution)/shard_map/dot_general | solution.py:150
  122.7 10.0 %all_to_all.56 = bf16[560,8,576]{2,1,0:T(8,128)(2,1)} reshape(bf16[560,4608]{1,0:T(8,128)(2,1)} %convolution_convert_fusion.1) | data formatting | bytes 10321920 | tf_op jit(solution)/shard_map/all_to_all | solution.py:151
  132.7 3.4 copy.23
  136.0 132.0 %all_to_all.70 = bf16[560,8,576]{2,0,1:T(8,128)(2,1)S(1)} all-to-all(bf16[560,8,576]{2,0,1:T(8,128)(2,1)S(1)} %copy.23), channel_id=1, replica_groups=mesh['row'=8,'col'=4] {'row'}, dimensions={1} | all-to-all | bytes 10321920 | tf_op jit(solution)/shard_map/all_to_all | solution.py:151
  268.2 0.3 slice.38
  268.5 0.2 slice_add_fusion.1
  268.7 0.5 pad_maximum_fusion
  269.2 17.8 %shard_map.46 = bf16[14336,512]{1,0:T(8,128)(2,1)S(1)} custom-call(s32[28]{0:T(128)S(1)} %copy-done.3, s32[28]{0:T(128)S(1)} %copy-done.2, bf16[3584,576]{1,0:T(8,128)(2,1)S(1)} %bitcast.19, bf16[3584,576]{1,0:T(8,128)(2,1)S(1)} %bitcast.20), custom_call_target="tpu_custom_call" | custom-call | flops 8455716864 | bytes 31195136 | tf_op jit(solution)/shard_map/pallas_call | solution.py:50
  287.0 5.2 copy-done
  292.1 2.1 copy-done.1
  294.3 250.6 %all-reduce.6.cloned.1.call-done.tile_ref = bf16[14336,512]{1,0:T(8,128)(2,1)} async-done(((bf16[14336,512]{1,0:T(8,128)(2,1)}), bf16[14336,512]{1,0:T(8,128)(2,1)}) %all-reduce.6.cloned.1.call-update) | async-done | bytes 14680080 | tf_op jit(solution)/shard_map/psum | solution.py:167
  544.9 71.0 %shard_map.47 = bf16[3584,576]{1,0:T(8,128)(2,1)S(1)} custom-call(s32[28]{0:T(128)S(1)} %copy-done.3, s32[28]{0:T(128)S(1)} %copy-done.2, bf16[14336,512]{1,0:T(8,128)(2,1)} %all-reduce.6.cloned.1.call-done.tile_ref, bf16[3584,576]{1,0:T(8,128)(2,1)} %bitcast.21), custom_call_target="tpu_custom_call" | custom-call | flops 29595009024 | bytes 37617664 | tf_op jit(solution)/shard_map/pallas_call | solution.py:112
  615.8 0.1 fusion.21
  615.9 3.6 fusion.2
  619.6 130.6 %all_to_all.71 = bf16[8,560,576]{2,1,0:T(8,128)(2,1)S(1)} all-to-all(bf16[8,560,576]{2,1,0:T(8,128)(2,1)S(1)} %fusion.2), channel_id=1, replica_groups=mesh['row'=8,'col'=4] {'row'}, dimensions={0} | all-to-all | bytes 10321920 | tf_op jit(solution)/shard_map/all_to_all | solution.py:173
  750.2 3.7 copy.24
  753.9 9.7 %all_to_all.61 = bf16[560,4608]{1,0:T(8,128)(2,1)} reshape(bf16[560,8,576]{2,1,0:T(8,128)(2,1)} %copy.24) | data formatting | bytes 10321920 | tf_op jit(solution)/shard_map/all_to_all | solution.py:173
  763.6 8.6 convolution_convert_fusion
  772.3 95.1 %all_to_all.72 = bf16[4,224,4608]{2,1,0:T(8,128)(2,1)} all-to-all(bf16[4,224,4608]{2,1,0:T(8,128)(2,1)S(1)} %bitcast.29), channel_id=1, replica_groups=mesh['row'=8,'col'=4] {'col'}, dimensions={0} | all-to-all | bytes 16515072 | tf_op jit(solution)/shard_map/all_to_all | solution.py:177
  867.4 7.8 copy.27
  (17 shorter events, 0.4 us)
Async XLA Ops:
  14.0 5.8 copy-start.4
  14.0 98.2 %all-to-all-start = ((bf16[224,4,4608]{2,0,1:T(8,128)(2,1)}), bf16[224,4,4608]{2,0,1:T(8,128)(2,1)}, u32[]{:S(2)}, u32[]{:S(2)}) async-start(bf16[224,4,4608]{2,0,1:T(8,128)(2,1)} %bitcast.22), calls=%async_computation | async-start | bytes 16515072 | tf_op jit(solution)/shard_map/all_to_all | solution.py:149
  19.7 525.1 %all-reduce.6.cloned.1.call-start = ((), (), s32[]{:S(2)}) async-start(), calls=%async_computation.4 | async-start | bytes 29360128 | tf_op jit(solution)/shard_map/psum | solution.py:167
  268.5 0.7 copy-start.2
  268.5 0.7 copy-start.3
  287.0 5.2 copy-start
  292.1 2.1 copy-start.1
Sparse Core Ops, SparseCore 0:
  294.4 250.3 all-reduce.5

commit v2 on v1

--- a/solution.py
+++ b/solution.py
@@ -134,7 +134,7 @@
     )(jnp.asarray(PAIR_ROWS), jnp.asarray(PAIR_COLS), tiles, matrix)
 
 
-def body(momentum_shards, shard_starts):
+def plain_body(momentum_shards, shard_starts):
     col_count = lax.axis_size("col")
     row_count = lax.axis_size("row")
     shard_rows = momentum_shards.shape[0]
@@ -177,6 +177,377 @@
     return lax.all_to_all(back_rows, "col", split_axis=0, concat_axis=1, tiled=True)
 
 
+CHUNK = 256
+LAST = 128
+VMEM_LIMIT = 56 * 1024 * 1024
+
+
+def swap(value, axis, size, distance):
+    return lax.ppermute(value, axis, perm=[(i, i ^ distance) for i in range(size)])
+
+
+def pack_kernel(step, col_count, meta_ref, *refs):
+    pieces, outs, choose = refs[:col_count], refs[col_count:-1], refs[-1]
+    turn = pl.program_id(0)
+    _, window, slots = choose.shape
+
+    @pl.when(turn == 0)
+    def _():
+        rows = lax.broadcasted_iota(jnp.int32, (window, slots), 0)
+        columns = lax.broadcasted_iota(jnp.int32, (window, slots), 1)
+        for k in range(col_count):
+            hit = (rows == columns + meta_ref[2 + k]) & (columns < meta_ref[2 + col_count + k])
+            choose[k] = jnp.where(hit, 1.0, 0.0).astype(jnp.bfloat16)
+
+    total = jnp.dot(choose[0], pieces[0][...], preferred_element_type=jnp.float32)
+    for k in range(1, col_count):
+        total += jnp.dot(choose[k], pieces[k][...], preferred_element_type=jnp.float32)
+    for q, out in enumerate(outs):
+
+        @pl.when(turn == q)
+        def _():
+            out[...] = total.astype(jnp.bfloat16)
+
+
+def pack(meta, momentum, received, base, width, step, count, window):
+    slots = momentum.shape[0]
+    col_count = len(received) + 1
+    first = base // width
+    return pl.pallas_call(
+        lambda *refs: pack_kernel(step, col_count, *refs),
+        out_shape=[jax.ShapeDtypeStruct((window, width), jnp.bfloat16)] * count,
+        grid_spec=pltpu.PrefetchScalarGridSpec(
+            num_scalar_prefetch=1,
+            grid=(count,),
+            in_specs=[
+                pl.BlockSpec(
+                    (slots, width),
+                    lambda q, meta: (0, first + meta[1] * count + ((meta[0] // step) ^ q)),
+                )
+            ]
+            + [pl.BlockSpec((slots, width), lambda q, meta: (0, (meta[0] // step) ^ q))]
+            * (col_count - 1),
+            out_specs=[pl.BlockSpec((window, width), lambda q, meta: (0, 0))] * count,
+            scratch_shapes=[pltpu.VMEM((col_count, window, slots), jnp.bfloat16)],
+        ),
+        compiler_params=pltpu.CompilerParams(vmem_limit_bytes=VMEM_LIMIT),
+        cost_estimate=pl.CostEstimate(
+            flops=2 * window * slots * col_count * width * count,
+            bytes_accessed=2 * count * width * (slots * col_count + window),
+            transcendentals=0,
+        ),
+    )(meta, momentum, *received)
+
+
+def unpack_kernel(col_count, meta_ref, *refs):
+    pieces, outs, choose = refs[: -1 - col_count], refs[-1 - col_count : -1], refs[-1]
+    turn = pl.program_id(0)
+    _, slots, window = choose.shape
+
+    @pl.when(turn == 0)
+    def _():
+        rows = lax.broadcasted_iota(jnp.int32, (slots, window), 1)
+        columns = lax.broadcasted_iota(jnp.int32, (slots, window), 0)
+        for k in range(col_count):
+            hit = (rows == columns + meta_ref[2 + k]) & (columns < meta_ref[2 + col_count + k])
+            choose[k] = jnp.where(hit, 1.0, 0.0).astype(jnp.bfloat16)
+
+    for q, piece in enumerate(pieces):
+
+        @pl.when(turn == q)
+        def _():
+            for k in range(col_count):
+                outs[k][...] = jnp.dot(
+                    choose[k], piece[...], preferred_element_type=jnp.float32
+                ).astype(jnp.bfloat16)
+
+
+def unpack(meta, pieces, col_count, slots, step):
+    window, width = pieces[0].shape
+    count = len(pieces)
+    return pl.pallas_call(
+        lambda *refs: unpack_kernel(col_count, *refs),
+        out_shape=[jax.ShapeDtypeStruct((slots, count * width), jnp.bfloat16)] * col_count,
+        grid_spec=pltpu.PrefetchScalarGridSpec(
+            num_scalar_prefetch=1,
+            grid=(count,),
+            in_specs=[pl.BlockSpec((window, width), lambda q, meta: (0, 0))] * count,
+            out_specs=[pl.BlockSpec((slots, width), lambda q, meta: (0, (meta[0] // step) ^ q))]
+            * col_count,
+            scratch_shapes=[pltpu.VMEM((col_count, slots, window), jnp.bfloat16)],
+        ),
+        compiler_params=pltpu.CompilerParams(vmem_limit_bytes=VMEM_LIMIT),
+        cost_estimate=pl.CostEstimate(
+            flops=2 * window * slots * col_count * width * count,
+            bytes_accessed=2 * count * width * (slots * col_count + window),
+            transcendentals=0,
+        ),
+    )(meta, *pieces)
+
+
+def merge_kernel(even, jitter, distances, meta_ref, *refs):
+    pieces, out_ref, total = refs[:-2], refs[-2], refs[-1]
+    window = pieces[0].shape[0]
+    total[...] = jnp.zeros_like(total)
+    for distance, piece in zip(distances, pieces):
+        place = pl.ds(pl.multiple_of((meta_ref[0] ^ distance) * even, 8), window)
+        total[place, :] += piece[...].astype(jnp.float32)
+
+    @pl.loop(0, BLOCKS)
+    def _(b):
+        source = pl.ds(pl.multiple_of(b * TILE + jitter, 8), TILE)
+        out_ref[pl.ds(pl.multiple_of(b * TILE, TILE), TILE), :] = total[source, :].astype(
+            jnp.bfloat16
+        )
+
+
+def merge(meta, pieces, distances, even, jitter):
+    width = pieces[0].shape[1]
+    whole = pl.BlockSpec(memory_space=pltpu.VMEM)
+    return pl.pallas_call(
+        lambda *refs: merge_kernel(even, jitter, distances, *refs),
+        out_shape=jax.ShapeDtypeStruct((M, width), jnp.bfloat16),
+        in_specs=[pl.BlockSpec(memory_space=pltpu.SMEM)] + [whole] * len(pieces),
+        out_specs=whole,
+        scratch_shapes=[pltpu.VMEM((M + 2 * jitter, width), jnp.float32)],
+        compiler_params=pltpu.CompilerParams(vmem_limit_bytes=VMEM_LIMIT),
+        cost_estimate=pl.CostEstimate(
+            flops=2 * M * width, bytes_accessed=5 * M * width, transcendentals=0
+        ),
+    )(meta, *pieces)
+
+
+def chunk_gram_kernel(rows_ref, cols_ref, meta_ref, *refs):
+    out_ref = refs[-1]
+    lefts, rights = refs[:-1:2], refs[1:-1:2]
+    dims = (((1,), (1,)), ((), ()))
+    mine = (pl.program_id(0) + meta_ref[0]) % 2 == 0
+
+    def product(count):
+        total = lax.dot_general(
+            lefts[0][...], rights[0][...], dims, preferred_element_type=jnp.float32
+        )
+        for c in range(1, count):
+            total += lax.dot_general(
+                lefts[c][...], rights[c][...], dims, preferred_element_type=jnp.float32
+            )
+        out_ref[...] = total.astype(jnp.bfloat16)
+
+    @pl.when(mine)
+    def _():
+        product(len(lefts))
+
+    @pl.when(jnp.logical_not(mine))
+    def _():
+        product(len(lefts) - 1)
+
+
+def chunk_gram(meta, chunks):
+    count = len(PAIRS)
+    in_specs = []
+    operands = []
+    width = sum(x.shape[1] for x in chunks)
+    for x in chunks:
+        in_specs.append(pl.BlockSpec((TILE, x.shape[1]), lambda p, rows, cols, meta: (rows[p], 0)))
+        in_specs.append(pl.BlockSpec((TILE, x.shape[1]), lambda p, rows, cols, meta: (cols[p], 0)))
+        operands += [x, x]
+    return pl.pallas_call(
+        chunk_gram_kernel,
+        out_shape=jax.ShapeDtypeStruct((count * TILE, TILE), jnp.bfloat16),
+        grid_spec=pltpu.PrefetchScalarGridSpec(
+            num_scalar_prefetch=3,
+            grid=(count,),
+            in_specs=in_specs,
+            out_specs=pl.BlockSpec((TILE, TILE), lambda p, rows, cols, meta: (p, 0)),
+        ),
+        compiler_params=pltpu.CompilerParams(vmem_limit_bytes=VMEM_LIMIT),
+        cost_estimate=pl.CostEstimate(
+            flops=2 * count * TILE * TILE * width,
+            bytes_accessed=2 * count * TILE * (TILE + width),
+            transcendentals=0,
+        ),
+    )(jnp.asarray(PAIR_ROWS), jnp.asarray(PAIR_COLS), meta, *operands)
+
+
+def windows_kernel(even, jitter, sends, rows_ref, cols_ref, meta_ref, tile_ref, *refs):
+    chunks = len(sends)
+    outs_count = sum(len(s) for s in sends)
+    matrices = refs[:chunks]
+    outs = refs[chunks : chunks + outs_count]
+    gram = refs[chunks + outs_count]
+    totals = refs[chunks + outs_count + 1 : 2 * chunks + outs_count + 1]
+    factors = refs[2 * chunks + outs_count + 1 :]
+    turn = pl.program_id(0)
+    count = len(PAIRS)
+
+    @pl.when(turn == 0)
+    def _():
+        for total in totals:
+            edge = jnp.zeros((jitter, total.shape[1]), jnp.float32)
+            total[pl.ds(0, jitter), :] = edge
+            total[pl.ds(M + jitter, jitter), :] = edge
+
+    @pl.when(turn < count)
+    def _():
+        i = rows_ref[jnp.minimum(turn, count - 1)]
+        j = cols_ref[jnp.minimum(turn, count - 1)]
+        gram[i, :, pl.ds(pl.multiple_of(j * TILE, TILE), TILE)] = tile_ref[...]
+
+        @pl.when(i != j)
+        def _():
+            gram[j, :, pl.ds(pl.multiple_of(i * TILE, TILE), TILE)] = tile_ref[...].T
+
+    @pl.when((turn >= count) & (turn < count + BLOCKS))
+    def _():
+        b = turn - count
+        part = pl.ds(pl.multiple_of(b * TILE, TILE), TILE)
+        place = pl.ds(pl.multiple_of(b * TILE + jitter, 8), TILE)
+        for matrix, total, factor in zip(matrices, totals, factors):
+            product = jnp.dot(gram[b], matrix[...], preferred_element_type=jnp.float32)
+            factor[part, :] = (coef_three * product).astype(jnp.bfloat16)
+            total[place, :] = (
+                coef_one * matrix[part, :].astype(jnp.float32) + coef_two * product
+            )
+
+    @pl.when(turn >= count + BLOCKS)
+    def _():
+        b = turn - count - BLOCKS
+        place = pl.ds(pl.multiple_of(b * TILE + jitter, 8), TILE)
+        for total, factor in zip(totals, factors):
+            total[place, :] = math.sqrt(N) * (
+                total[place, :] + jnp.dot(gram[b], factor[...], preferred_element_type=jnp.float32)
+            )
+
+    @pl.when(turn == count + 2 * BLOCKS - 1)
+    def _():
+        number = 0
+        for total, send in zip(totals, sends):
+            for distance in send:
+                window = outs[number].shape[0]
+                place = pl.ds(pl.multiple_of((meta_ref[0] ^ distance) * even, 8), window)
+                outs[number][...] = total[place, :].astype(jnp.bfloat16)
+                number += 1
+
+
+def apply_windows(meta, tiles, matrices, sends, even, jitter):
+    count = len(PAIRS)
+    widths = [x.shape[1] for x in matrices]
+    shapes = [
+        (even + 2 * jitter, width) for width, send in zip(widths, sends) for _ in send
+    ]
+    whole = lambda t, rows, cols, meta: (0, 0)
+    outs = pl.pallas_call(
+        lambda *refs: windows_kernel(even, jitter, sends, *refs),
+        out_shape=[jax.ShapeDtypeStruct(shape, jnp.bfloat16) for shape in shapes],
+        grid_spec=pltpu.PrefetchScalarGridSpec(
+            num_scalar_prefetch=3,
+            grid=(count + 2 * BLOCKS,),
+            in_specs=[
+                pl.BlockSpec(
+                    (TILE, TILE), lambda t, rows, cols, meta: (jnp.minimum(t, count - 1), 0)
+                )
+            ]
+            + [pl.BlockSpec((M, width), whole) for width in widths],
+            out_specs=[pl.BlockSpec(shape, whole) for shape in shapes],
+            scratch_shapes=[pltpu.VMEM((BLOCKS, TILE, M), jnp.bfloat16)]
+            + [pltpu.VMEM((M + 2 * jitter, width), jnp.float32) for width in widths]
+            + [pltpu.VMEM((M, width), jnp.bfloat16) for width in widths],
+        ),
+        compiler_params=pltpu.CompilerParams(vmem_limit_bytes=VMEM_LIMIT),
+        cost_estimate=pl.CostEstimate(
+            flops=4 * M * M * sum(widths),
+            bytes_accessed=4 * M * sum(widths) + 2 * count * TILE * TILE,
+            transcendentals=0,
+        ),
+    )(jnp.asarray(PAIR_ROWS), jnp.asarray(PAIR_COLS), meta, tiles, *matrices)
+    result = []
+    for send in sends:
+        result.append(outs[: len(send)])
+        outs = outs[len(send) :]
+    return result
+
+
+def reduce_tiles(tiles):
+    return lax.psum(tiles, ("row", "col"))
+
+
+def chunk_body(momentum_shards, shard_starts):
+    col_count = lax.axis_size("col")
+    row_count = lax.axis_size("row")
+    pair_count = row_count // 2
+    slots = momentum_shards.shape[0]
+    mean_rows = M // (row_count * col_count)
+    jitter = 4 * (mean_rows // 8)
+    even = col_count * mean_rows
+    window = even + 2 * jitter
+    row = lax.axis_index("row").astype(jnp.int32)
+    col = lax.axis_index("col").astype(jnp.int32)
+    shard_ends = jnp.concatenate([shard_starts[1:], jnp.full((1,), M, jnp.int32)])
+    members = row * col_count + (col ^ jnp.arange(col_count, dtype=jnp.int32))
+    begins = shard_starts[members]
+    meta = jnp.concatenate(
+        [row[None], col[None], begins - (row * even - jitter), shard_ends[members] - begins]
+    )
+
+    wide = row_count * col_count * CHUNK
+    number = (N // (row_count * col_count)) // CHUNK
+    plan = [(c * wide, CHUNK, 1, row_count) for c in range(number)]
+    plan.append((number * wide, LAST, 2, pair_count))
+
+    matrices = []
+    for base, width, step, count in plan:
+        span = count * width
+        received = [
+            swap(
+                lax.dynamic_slice_in_dim(momentum_shards, base + (col ^ k) * span, span, axis=1),
+                "col",
+                col_count,
+                k,
+            )
+            for k in range(1, col_count)
+        ]
+        pieces = pack(meta, momentum_shards, received, base, width, step, count, window)
+        landed = [pieces[0]] + [
+            swap(pieces[q], "row", row_count, q * step) for q in range(1, count)
+        ]
+        distances = [q * step for q in range(count)]
+        if step == 2:
+            landed += [swap(piece, "row", row_count, 1) for piece in landed]
+            distances += [d ^ 1 for d in distances]
+        matrices.append(merge(meta, landed, distances, even, jitter))
+
+    tiles = reduce_tiles(chunk_gram(meta, matrices))
+
+    sends = [[q * step for q in range(count)] for _, _, step, count in plan]
+    results = []
+    for group in [[c] for c in range(number - 1)] + [[number - 1, number]]:
+        results += apply_windows(
+            meta, tiles, [matrices[c] for c in group], [sends[c] for c in group], even, jitter
+        )
+
+    out = jnp.zeros(momentum_shards.shape, jnp.bfloat16)
+    for (base, width, step, count), pieces in zip(plan, results):
+        span = count * width
+        landed = [pieces[0]] + [
+            swap(pieces[q], "row", row_count, q * step) for q in range(1, count)
+        ]
+        backs = unpack(meta, landed, col_count, slots, step)
+        for k in range(col_count):
+            back = backs[0] if k == 0 else swap(backs[k], "col", col_count, k)
+            out = lax.dynamic_update_slice_in_dim(out, back, base + (col ^ k) * span, axis=1)
+    return out
+
+
+def body(momentum_shards, shard_starts):
+    devices = lax.axis_size("col") * lax.axis_size("row")
+    chunks = (N // devices) % CHUNK == LAST // 2 and N // devices > CHUNK
+    powers = all(lax.axis_size(a) & (lax.axis_size(a) - 1) == 0 for a in ("row", "col"))
+    jitter = 4 * (M // devices // 8)
+    if chunks and powers and jitter % 8 == 0:
+        return chunk_body(momentum_shards, shard_starts)
+    return plain_body(momentum_shards, shard_starts)
+
+
 def solution(mesh):
     in_specs = (P(("row", "col"), None), P())
     out_specs = P(("row", "col"), None)

time: 883 us -> 814 us (0.922)
  blocking collectives: 358 us -> 0 us
  waiting for transfers between devices: 343 us -> 507 us
  starting transfers between devices: 5.78 us -> 96.7 us
  Pallas kernels: 88.7 us -> 175 us
  local copies, waits for them, and re-layouts: 49.8 us -> 18.8 us
  matrix products: 19.2 us -> 0 us
    all_to_all x3 -> x0, blocking collectives: 358 us -> none  [the longest x1 132 us: body(): lax.all_to_all(local_tile, 'row', split_axis=1, concat_axis=0, tiled=True)]
    ppermute x0 -> x56, waiting for transfers between devices: none -> 244 us  [swap(): lax.ppermute(value, axis, perm=[(i, i ^ distance) for i in range(size)])]
    ppermute x0 -> x56, starting transfers between devices: none -> 96.7 us  [swap(): lax.ppermute(value, axis, perm=[(i, i ^ distance) for i in range(size)])]
    all_to_all x1 -> x0, waiting for transfers between devices: 92 us -> none  [body(): lax.all_to_all(momentum_shards, 'col', split_axis=1, concat_axis=0, tiled...]
    pallas_call x2 -> x12, Pallas kernels: 88.7 us -> 175 us  [the longest x2 89.7 us: apply_windows(): pl.pallas_call(lambda *refs: windows_kernel(even, jitter, sends, *refs),...]
    all_to_all x6 -> x0, local copies, waits for them, and re-layouts: 41.9 us -> none  [the longest x2 13.4 us: body(): lax.all_to_all(spread, 'row', split_axis=0, concat_axis=1, tiled=True)]
    dot_general x2 -> x0, matrix products: 19.2 us -> none  [the longest x1 10.6 us: body(): jnp.dot(packer, columns, preferred_element_type=jnp.float32)]
    psum x1, waiting for transfers between devices: 251 us -> 264 us  [reduce_tiles(): return lax.psum(tiles, ('row', 'col'))]
  transfers between devices with their start and end apart: 2 -> 57, of which waited for: 2 -> 21; matrix products, arithmetic and copies ran while one was open for 0% -> 1% of each run, Pallas kernels for 0% -> 13%
where the time goes in v2:
time: 814 us; the launch traced here: 812 us
  waiting for transfers between devices  507 us (62%)
  Pallas kernels  175 us (21%)
  starting transfers between devices  96.7 us (12%)
  local copies, waits for them, and re-layouts  18.8 us (2%)
  between operations  14 us (2%)
    psum x1, waiting for transfers between devices, reduce_tiles(): return lax.psum(tiles, ('row', 'col'))  264 us
    ppermute x56, waiting for transfers between devices, swap(): lax.ppermute(value, axis, perm=[(i, i ^ distance) for i in range(size)])  244 us
    ppermute x56, starting transfers between devices, swap(): lax.ppermute(value, axis, perm=[(i, i ^ distance) for i in range(size)])  96.7 us
    pallas_call x2, Pallas kernels, apply_windows(): pl.pallas_call(lambda *refs: windows_kernel(even, jitter, sends, *refs),...  89.7 us
    pallas_call x1, Pallas kernels, chunk_gram(): pl.pallas_call(chunk_gram_kernel, out_shape=jax.ShapeDtypeStruct((count *...  29.3 us
    pallas_call x3, Pallas kernels, pack(): pl.pallas_call(lambda *refs: pack_kernel(step, col_count, *refs), out_sha...  23.8 us
    pallas_call x3, Pallas kernels, unpack(): pl.pallas_call(lambda *refs: unpack_kernel(col_count, *refs), out_shape=[...  21.9 us
  transfers between devices with their start and end apart: 57, of which 21 were waited for; matrix products, arithmetic and copies ran while one was open for 1% of the time, Pallas kernels for 13%

profile of v2, /device:TPU:0, one launch (start us, length us, event | category | flops | bytes accessed | tf_op | source)
XLA Modules:
  0.0 812.3 jit_solution(5957449258443692025)
XLA Ops:
  21.5 18.7 %collective-permute-done.20.refs_2_ = bf16[224,512]{1,0:T(8,128)(2,1)S(1)} collective-permute-done((bf16[224,512]{1,0:T(8,128)(2,1)}, bf16[224,512]{1,0:T(8,128)(2,1)S(1)}, u32[]{:S(2)}, u32[]{:S(2)}) %collective-permute-start.20) | collective-permute-done | bytes 229408 | tf_op jit(solution)/shard_map/ppermute | solution.py:186
  40.2 5.4 collective-permute-done.22.refs_4_
  68.8 47.3 %collective-permute-done.11.refs_3_ = bf16[224,2048]{1,0:T(8,128)(2,1)S(1)} collective-permute-done((bf16[224,2048]{1,0:T(8,128)(2,1)S(1)}, bf16[224,2048]{1,0:T(8,128)(2,1)S(1)}, u32[]{:S(2)}, u32[]{:S(2)}) %collective-permute-start.11) | collective-permute-done | bytes 917536 | tf_op jit(solution)/shard_map/ppermute | solution.py:186
  118.0 9.3 %shard_map.48 = (bf16[560,256]{1,0:T(8,128)(2,1)}, bf16[560,256]{1,0:T(8,128)(2,1)}, bf16[560,256]{1,0:T(8,128)(2,1)}, bf16[560,256]{1,0:T(8,128)(2,1)}, bf16[56...) custom-call(s32[10]{0:T(128)} %pad_add_fusion.1.refs_0_.meta_ref.refs_2_, ...), custom_call_target="tpu_custom_call" | custom-call | flops 2055208960 | bytes 5963776 | tf_op jit(solution)/shard_map/pallas_call | solution.py:216
  135.8 9.3 %shard_map.46 = (bf16[560,256]{1,0:T(8,128)(2,1)}, bf16[560,256]{1,0:T(8,128)(2,1)}, bf16[560,256]{1,0:T(8,128)(2,1)}, bf16[560,256]{1,0:T(8,128)(2,1)}, bf16[56...) custom-call(s32[10]{0:T(128)} %pad_add_fusion.1.refs_0_.meta_ref.refs_2_, ...), custom_call_target="tpu_custom_call" | custom-call | flops 2055208960 | bytes 5963776 | tf_op jit(solution)/shard_map/pallas_call | solution.py:216
  151.1 16.9 %collective-permute-done.16.refs_5_ = bf16[560,256]{1,0:T(8,128)(2,1)S(1)} collective-permute-done((bf16[560,256]{1,0:T(8,128)(2,1)}, bf16[560,256]{1,0:T(8,128)(2,1)S(1)}, u32[]{:S(2)}, u32[]{:S(2)}) %collective-permute-start.16) | collective-permute-done | bytes 286752 | tf_op jit(solution)/shard_map/ppermute | solution.py:186
  168.0 5.9 collective-permute-done.17.refs_6_
  174.0 7.3 collective-permute-start.6
  181.2 12.0 %collective-permute-start.7 = (bf16[560,256]{1,0:T(8,128)(2,1)}, bf16[560,256]{1,0:T(8,128)(2,1)S(1)}, u32[]{:S(2)}, u32[]{:S(2)}) collective-permute-start(bf16[560,256]{1,0:T(8,128)(2,1)} %get-tuple-element.62), channel_id=1, source_target_pairs={{0,20},{4,16},{8,28},{12,24},{16,4},{20,0},{24,12},{28,8},{1,21},{... | collective-permute-start | bytes 860168 | tf_op jit(solution)/shard_map/ppermute | solution.py:186
  203.8 13.3 %collective-permute-done.6.refs_5_ = bf16[560,256]{1,0:T(8,128)(2,1)S(1)} collective-permute-done((bf16[560,256]{1,0:T(8,128)(2,1)}, bf16[560,256]{1,0:T(8,128)(2,1)S(1)}, u32[]{:S(2)}, u32[]{:S(2)}) %collective-permute-start.6) | collective-permute-done | bytes 286752 | tf_op jit(solution)/shard_map/ppermute | solution.py:186
  217.1 5.9 collective-permute-done.7.refs_6_
  227.7 29.3 %shard_map.52 = bf16[14336,512]{1,0:T(8,128)(2,1)} custom-call(s32[28]{0:T(128)} %constant.55.clone.rows_ref.refs_0_, s32[28]{0:T(128)} %constant.56.clone.cols_ref.refs_1_, s32[10]{0:T(128)} %pad_add_fusion.1.refs_0_.meta_ref.refs_2_, bf16[3584,256]{1,0:T(8,128)(2,1)} %shard_map.47.refs_0_.refs_1_.refs_4_, ...), custom_call_target="tpu_custom_call" | custom-call | flops 9395240960 | bytes 33030144 | tf_op jit(solution)/shard_map/pallas_call | solution.py:354
  257.0 263.7 %all-reduce.2.cloned.1.call-done.refs_3_ = bf16[14336,512]{1,0:T(8,128)(2,1)} async-done(((bf16[14336,512]{1,0:T(8,128)(2,1)}), bf16[14336,512]{1,0:T(8,128)(2,1)}) %all-reduce.2.cloned.1.call-update) | async-done | bytes 14680080 | tf_op jit(solution)/shard_map/psum | solution.py:471
  520.8 37.6 %shard_map.53 = (bf16[560,256]{1,0:T(8,128)(2,1)}, bf16[560,256]{1,0:T(8,128)(2,1)}, bf16[560,256]{1,0:T(8,128)(2,1)}, bf16[560,256]{1,0:T(8,128)(2,1)}, bf16[56...) custom-call(s32[28]{0:T(128)} %constant.55.clone.rows_ref.refs_0_, ...), custom_call_target="tpu_custom_call" | custom-call | flops 13153337344 | bytes 18350080 | tf_op jit(solution)/shard_map/pallas_call | solution.py:439
  559.9 52.1 %shard_map.55 = (bf16[560,256]{1,0:T(8,128)(2,1)}, bf16[560,256]{1,0:T(8,128)(2,1)}, bf16[560,256]{1,0:T(8,128)(2,1)}, bf16[560,256]{1,0:T(8,128)(2,1)}, bf16[56...) custom-call(s32[28]{0:T(128)} %constant.55.clone.rows_ref.refs_0_, ...), custom_call_target="tpu_custom_call" | custom-call | flops 19730006016 | bytes 20185088 | tf_op jit(solution)/shard_map/pallas_call | solution.py:439
  614.8 6.8 collective-permute-done.50.refs_2_
  633.5 26.4 %collective-permute-done.33.refs_5_ = bf16[560,256]{1,0:T(8,128)(2,1)S(1)} collective-permute-done((bf16[560,256]{1,0:T(8,128)(2,1)S(1)}, bf16[560,256]{1,0:T(8,128)(2,1)S(1)}, u32[]{:S(2)}, u32[]{:S(2)}) %collective-permute-start.33) | collective-permute-done | bytes 286752 | tf_op jit(solution)/shard_map/ppermute | solution.py:186
  667.7 9.3 %collective-permute-start.43 = (bf16[560,256]{1,0:T(8,128)(2,1)}, bf16[560,256]{1,0:T(8,128)(2,1)S(1)}, u32[]{:S(2)}, u32[]{:S(2)}) collective-permute-start(bf16[560,256]{1,0:T(8,128)(2,1)} %get-tuple-element.93), channel_id=1, source_target_pairs={{0,16},{4,20},{8,24},{12,28},{16,0},{20,4},{24,8},{28,12},{1,17},{... | collective-permute-start | bytes 860168 | tf_op jit(solution)/shard_map/ppermute | solution.py:186
  677.1 8.4 %shard_map.54 = (bf16[224,2048]{1,0:T(8,128)(2,1)}, bf16[224,2048]{1,0:T(8,128)(2,1)}, bf16[224,2048]{1,0:T(8,128)(2,1)}, bf16[224,2048]{1,0:T(8,128)(2,1)}) custom-call(s32[10]{0:T(128)} %pad_add_fusion.1.refs_0_.meta_ref.refs_2_, bf16[560,256]{1,0:T(8,128)(2,1)} %get-tuple-element.77.refs_1_, bf16[560,256]{1,0:T(8,128)(2,1)} %copy-done.42, ...), custom_call_target="tpu_custom_call" | custom-call | flops 2055208960 | bytes 5963776 | tf_op jit(solution)/shard_map/pallas_call | solution.py:268
  691.0 18.9 %collective-permute-done.43.refs_5_ = bf16[560,256]{1,0:T(8,128)(2,1)S(1)} collective-permute-done((bf16[560,256]{1,0:T(8,128)(2,1)}, bf16[560,256]{1,0:T(8,128)(2,1)S(1)}, u32[]{:S(2)}, u32[]{:S(2)}) %collective-permute-start.43) | collective-permute-done | bytes 286752 | tf_op jit(solution)/shard_map/ppermute | solution.py:186
  720.5 8.6 %shard_map.56 = (bf16[224,2048]{1,0:T(8,128)(2,1)}, bf16[224,2048]{1,0:T(8,128)(2,1)}, bf16[224,2048]{1,0:T(8,128)(2,1)}, bf16[224,2048]{1,0:T(8,128)(2,1)}) custom-call(s32[10]{0:T(128)} %pad_add_fusion.1.refs_0_.meta_ref.refs_2_, bf16[560,256]{1,0:T(8,128)(2,1)} %get-tuple-element.89.refs_1_, bf16[560,256]{1,0:T(8,128)(2,1)} %copy-done.38, ...), custom_call_target="tpu_custom_call" | custom-call | flops 2055208960 | bytes 5963776 | tf_op jit(solution)/shard_map/pallas_call | solution.py:268
  731.8 21.1 %collective-permute-done.38 = bf16[224,2048]{1,0:T(8,128)(2,1)S(1)} collective-permute-done((bf16[224,2048]{1,0:T(8,128)(2,1)}, bf16[224,2048]{1,0:T(8,128)(2,1)S(1)}, u32[]{:S(2)}, u32[]{:S(2)}) %collective-permute-start.38) | collective-permute-done | bytes 917536 | tf_op jit(solution)/shard_map/ppermute | solution.py:186
  756.3 8.8 %collective-permute-done.47 = bf16[224,2048]{1,0:T(8,128)(2,1)S(1)} collective-permute-done((bf16[224,2048]{1,0:T(8,128)(2,1)S(1)}, bf16[224,2048]{1,0:T(8,128)(2,1)S(1)}, u32[]{:S(2)}, u32[]{:S(2)}) %collective-permute-start.47) | collective-permute-done | bytes 917536 | tf_op jit(solution)/shard_map/ppermute | solution.py:186
  767.0 34.0 %collective-permute-done.48 = bf16[224,2048]{1,0:T(8,128)(2,1)S(1)} collective-permute-done((bf16[224,2048]{1,0:T(8,128)(2,1)S(1)}, bf16[224,2048]{1,0:T(8,128)(2,1)S(1)}, u32[]{:S(2)}, u32[]{:S(2)}) %collective-permute-start.48) | collective-permute-done | bytes 917536 | tf_op jit(solution)/shard_map/ppermute | solution.py:186
  (244 shorter events, 121.8 us)
Async XLA Ops:
  6.5 514.2 %all-reduce.2.cloned.1.call-start = ((), (), s32[]{:S(2)}) async-start(), calls=%async_computation | async-start | bytes 29360128 | tf_op jit(solution)/shard_map/psum | solution.py:471
  10.9 56.4 %collective-permute-start.10 = (bf16[224,2048]{1,0:T(8,128)(2,1)}, bf16[224,2048]{1,0:T(8,128)(2,1)}, u32[]{:S(2)}, u32[]{:S(2)}) collective-permute-start(bf16[224,2048]{1,0:T(8,128)(2,1)} %get-tuple-element.114), channel_id=1, source_target_pairs={{0,1},{1,0},{2,3},{3,2},{4,5},{5,4},{6,7},{7,6},{8,9},{9,8},{10,11... | collective-permute-start | bytes 2752520 | tf_op jit(solution)/shard_map/ppermute | solution.py:186
  54.9 61.3 %collective-permute-start.11 = (bf16[224,2048]{1,0:T(8,128)(2,1)S(1)}, bf16[224,2048]{1,0:T(8,128)(2,1)S(1)}, u32[]{:S(2)}, u32[]{:S(2)}) collective-permute-start(bf16[224,2048]{1,0:T(8,128)(2,1)S(1)} %copy-done.3), channel_id=1, source_target_pairs={{0,2},{1,3},{2,0},{3,1},{4,6},{5,7},{6,4},{7,5},{8,10},{9,11},{10,... | collective-permute-start | bytes 2752520 | tf_op jit(solution)/shard_map/ppermute | solution.py:186
  55.4 60.8 %collective-permute-start.12 = (bf16[224,2048]{1,0:T(8,128)(2,1)S(1)}, bf16[224,2048]{1,0:T(8,128)(2,1)S(1)}, u32[]{:S(2)}, u32[]{:S(2)}) collective-permute-start(bf16[224,2048]{1,0:T(8,128)(2,1)S(1)} %copy-done.2), channel_id=1, source_target_pairs={{0,3},{1,2},{2,1},{3,0},{4,7},{5,6},{6,5},{7,4},{8,11},{9,10},{10,... | collective-permute-start | bytes 2752520 | tf_op jit(solution)/shard_map/ppermute | solution.py:186
  65.3 63.1 %collective-permute-start = (bf16[224,2048]{1,0:T(8,128)(2,1)S(1)}, bf16[224,2048]{1,0:T(8,128)(2,1)S(1)}, u32[]{:S(2)}, u32[]{:S(2)}) collective-permute-start(bf16[224,2048]{1,0:T(8,128)(2,1)S(1)} %get-tuple-element.117), channel_id=1, source_target_pairs={{0,1},{1,0},{2,3},{3,2},{4,5},{5,4},{6,7},{7,6},{8,9},{9,8},{10,11... | collective-permute-start | bytes 2752520 | tf_op jit(solution)/shard_map/ppermute | solution.py:186
  66.8 67.7 %collective-permute-start.1 = (bf16[224,2048]{1,0:T(8,128)(2,1)S(1)}, bf16[224,2048]{1,0:T(8,128)(2,1)S(1)}, u32[]{:S(2)}, u32[]{:S(2)}) collective-permute-start(bf16[224,2048]{1,0:T(8,128)(2,1)S(1)} %get-tuple-element.116), channel_id=1, source_target_pairs={{0,2},{1,3},{2,0},{3,1},{4,6},{5,7},{6,4},{7,5},{8,10},{9,11},{10,... | collective-permute-start | bytes 2752520 | tf_op jit(solution)/shard_map/ppermute | solution.py:186
  67.3 67.5 %collective-permute-start.2 = (bf16[224,2048]{1,0:T(8,128)(2,1)S(1)}, bf16[224,2048]{1,0:T(8,128)(2,1)S(1)}, u32[]{:S(2)}, u32[]{:S(2)}) collective-permute-start(bf16[224,2048]{1,0:T(8,128)(2,1)S(1)} %get-tuple-element.115), channel_id=1, source_target_pairs={{0,3},{1,2},{2,1},{3,0},{4,7},{5,6},{6,5},{7,4},{8,11},{9,10},{10,... | collective-permute-start | bytes 2752520 | tf_op jit(solution)/shard_map/ppermute | solution.py:186
  151.1 42.1 %collective-permute-start.3 = (bf16[560,256]{1,0:T(8,128)(2,1)}, bf16[560,256]{1,0:T(8,128)(2,1)S(1)}, u32[]{:S(2)}, u32[]{:S(2)}) collective-permute-start(bf16[560,256]{1,0:T(8,128)(2,1)} %get-tuple-element.58), channel_id=1, source_target_pairs={{0,4},{4,0},{8,12},{12,8},{16,20},{20,16},{24,28},{28,24},{1,5},{5... | collective-permute-start | bytes 860168 | tf_op jit(solution)/shard_map/ppermute | solution.py:186
  174.0 43.1 %collective-permute-start.6 = (bf16[560,256]{1,0:T(8,128)(2,1)}, bf16[560,256]{1,0:T(8,128)(2,1)S(1)}, u32[]{:S(2)}, u32[]{:S(2)}) collective-permute-start(bf16[560,256]{1,0:T(8,128)(2,1)} %get-tuple-element.61), channel_id=1, source_target_pairs={{0,16},{4,20},{8,24},{12,28},{16,0},{20,4},{24,8},{28,12},{1,17},{... | collective-permute-start | bytes 860168 | tf_op jit(solution)/shard_map/ppermute | solution.py:186
  181.2 41.8 %collective-permute-start.7 = (bf16[560,256]{1,0:T(8,128)(2,1)}, bf16[560,256]{1,0:T(8,128)(2,1)S(1)}, u32[]{:S(2)}, u32[]{:S(2)}) collective-permute-start(bf16[560,256]{1,0:T(8,128)(2,1)} %get-tuple-element.62), channel_id=1, source_target_pairs={{0,20},{4,16},{8,28},{12,24},{16,4},{20,0},{24,12},{28,8},{1,21},{... | collective-permute-start | bytes 860168 | tf_op jit(solution)/shard_map/ppermute | solution.py:186
  558.3 64.8 %collective-permute-start.30 = (bf16[560,256]{1,0:T(8,128)(2,1)}, bf16[560,256]{1,0:T(8,128)(2,1)S(1)}, u32[]{:S(2)}, u32[]{:S(2)}) collective-permute-start(bf16[560,256]{1,0:T(8,128)(2,1)} %get-tuple-element.78), channel_id=1, source_target_pairs={{0,4},{4,0},{8,12},{12,8},{16,20},{20,16},{24,28},{28,24},{1,5},{5... | collective-permute-start | bytes 860168 | tf_op jit(solution)/shard_map/ppermute | solution.py:186
  558.4 67.4 %collective-permute-start.31 = (bf16[560,256]{1,0:T(8,128)(2,1)}, bf16[560,256]{1,0:T(8,128)(2,1)S(1)}, u32[]{:S(2)}, u32[]{:S(2)}) collective-permute-start(bf16[560,256]{1,0:T(8,128)(2,1)} %get-tuple-element.79), channel_id=1, source_target_pairs={{0,8},{4,12},{8,0},{12,4},{16,24},{20,28},{24,16},{28,20},{1,9},{5... | collective-permute-start | bytes 860168 | tf_op jit(solution)/shard_map/ppermute | solution.py:186
  621.6 38.3 %collective-permute-start.33 = (bf16[560,256]{1,0:T(8,128)(2,1)S(1)}, bf16[560,256]{1,0:T(8,128)(2,1)S(1)}, u32[]{:S(2)}, u32[]{:S(2)}) collective-permute-start(bf16[560,256]{1,0:T(8,128)(2,1)S(1)} %copy-done.48), channel_id=1, source_target_pairs={{0,16},{4,20},{8,24},{12,28},{16,0},{20,4},{24,8},{28,12},{1,17},{... | collective-permute-start | bytes 860168 | tf_op jit(solution)/shard_map/ppermute | solution.py:186
  622.8 38.5 %collective-permute-start.34 = (bf16[560,256]{1,0:T(8,128)(2,1)S(1)}, bf16[560,256]{1,0:T(8,128)(2,1)S(1)}, u32[]{:S(2)}, u32[]{:S(2)}) collective-permute-start(bf16[560,256]{1,0:T(8,128)(2,1)S(1)} %copy-done.47), channel_id=1, source_target_pairs={{0,20},{4,16},{8,28},{12,24},{16,4},{20,0},{24,12},{28,8},{1,21},{... | collective-permute-start | bytes 860168 | tf_op jit(solution)/shard_map/ppermute | solution.py:186
  623.1 40.4 %collective-permute-start.35 = (bf16[560,256]{1,0:T(8,128)(2,1)S(1)}, bf16[560,256]{1,0:T(8,128)(2,1)S(1)}, u32[]{:S(2)}, u32[]{:S(2)}) collective-permute-start(bf16[560,256]{1,0:T(8,128)(2,1)S(1)} %copy-done.46), channel_id=1, source_target_pairs={{0,24},{4,28},{8,16},{12,20},{16,8},{20,12},{24,0},{28,4},{1,25},{... | collective-permute-start | bytes 860168 | tf_op jit(solution)/shard_map/ppermute | solution.py:186
  625.8 42.0 %collective-permute-start.36 = (bf16[560,256]{1,0:T(8,128)(2,1)S(1)}, bf16[560,256]{1,0:T(8,128)(2,1)S(1)}, u32[]{:S(2)}, u32[]{:S(2)}) collective-permute-start(bf16[560,256]{1,0:T(8,128)(2,1)S(1)} %copy-done.44), channel_id=1, source_target_pairs={{0,28},{4,24},{8,20},{12,16},{16,12},{20,8},{24,4},{28,0},{1,29},{... | collective-permute-start | bytes 860168 | tf_op jit(solution)/shard_map/ppermute | solution.py:186
  631.2 54.3 %collective-permute-start.52 = (bf16[560,128]{1,0:T(8,128)(2,1)}, bf16[560,128]{1,0:T(8,128)(2,1)S(1)}, u32[]{:S(2)}, u32[]{:S(2)}) collective-permute-start(bf16[560,128]{1,0:T(8,128)(2,1)} %get-tuple-element.104), channel_id=1, source_target_pairs={{0,24},{4,28},{8,16},{12,20},{16,8},{20,12},{24,0},{28,4},{1,25},{... | collective-permute-start | bytes 430088 | tf_op jit(solution)/shard_map/ppermute | solution.py:186
  667.7 42.1 %collective-permute-start.43 = (bf16[560,256]{1,0:T(8,128)(2,1)}, bf16[560,256]{1,0:T(8,128)(2,1)S(1)}, u32[]{:S(2)}, u32[]{:S(2)}) collective-permute-start(bf16[560,256]{1,0:T(8,128)(2,1)} %get-tuple-element.93), channel_id=1, source_target_pairs={{0,16},{4,20},{8,24},{12,28},{16,0},{20,4},{24,8},{28,12},{1,17},{... | collective-permute-start | bytes 860168 | tf_op jit(solution)/shard_map/ppermute | solution.py:186
  685.5 44.6 %collective-permute-start.37 = (bf16[224,2048]{1,0:T(8,128)(2,1)}, bf16[224,2048]{1,0:T(8,128)(2,1)S(1)}, u32[]{:S(2)}, u32[]{:S(2)}) collective-permute-start(bf16[224,2048]{1,0:T(8,128)(2,1)} %get-tuple-element.86), channel_id=1, source_target_pairs={{0,1},{1,0},{2,3},{3,2},{4,5},{5,4},{6,7},{7,6},{8,9},{9,8},{10,11... | collective-permute-start | bytes 2752520 | tf_op jit(solution)/shard_map/ppermute | solution.py:186
  709.9 43.1 %collective-permute-start.38 = (bf16[224,2048]{1,0:T(8,128)(2,1)}, bf16[224,2048]{1,0:T(8,128)(2,1)S(1)}, u32[]{:S(2)}, u32[]{:S(2)}) collective-permute-start(bf16[224,2048]{1,0:T(8,128)(2,1)} %get-tuple-element.87), channel_id=1, source_target_pairs={{0,2},{1,3},{2,0},{3,1},{4,6},{5,7},{6,4},{7,5},{8,10},{9,11},{10,... | collective-permute-start | bytes 2752520 | tf_op jit(solution)/shard_map/ppermute | solution.py:186
  717.0 84.3 %collective-permute-start.53 = (bf16[224,512]{1,0:T(8,128)(2,1)}, bf16[224,512]{1,0:T(8,128)(2,1)S(1)}, u32[]{:S(2)}, u32[]{:S(2)}) collective-permute-start(bf16[224,512]{1,0:T(8,128)(2,1)} %get-tuple-element.106), channel_id=1, source_target_pairs={{0,1},{1,0},{2,3},{3,2},{4,5},{5,4},{6,7},{7,6},{8,9},{9,8},{10,11... | collective-permute-start | bytes 688136 | tf_op jit(solution)/shard_map/ppermute | solution.py:186
  718.5 82.9 %collective-permute-start.54 = (bf16[224,512]{1,0:T(8,128)(2,1)}, bf16[224,512]{1,0:T(8,128)(2,1)S(1)}, u32[]{:S(2)}, u32[]{:S(2)}) collective-permute-start(bf16[224,512]{1,0:T(8,128)(2,1)} %get-tuple-element.107), channel_id=1, source_target_pairs={{0,2},{1,3},{2,0},{3,1},{4,6},{5,7},{6,4},{7,5},{8,10},{9,11},{10,... | collective-permute-start | bytes 688136 | tf_op jit(solution)/shard_map/ppermute | solution.py:186
  753.0 48.1 %collective-permute-start.48 = (bf16[224,2048]{1,0:T(8,128)(2,1)S(1)}, bf16[224,2048]{1,0:T(8,128)(2,1)S(1)}, u32[]{:S(2)}, u32[]{:S(2)}) collective-permute-start(bf16[224,2048]{1,0:T(8,128)(2,1)S(1)} %copy-done.36), channel_id=1, source_target_pairs={{0,2},{1,3},{2,0},{3,1},{4,6},{5,7},{6,4},{7,5},{8,10},{9,11},{10,... | collective-permute-start | bytes 2752520 | tf_op jit(solution)/shard_map/ppermute | solution.py:186
  754.6 46.6 %collective-permute-start.49 = (bf16[224,2048]{1,0:T(8,128)(2,1)S(1)}, bf16[224,2048]{1,0:T(8,128)(2,1)S(1)}, u32[]{:S(2)}, u32[]{:S(2)}) collective-permute-start(bf16[224,2048]{1,0:T(8,128)(2,1)S(1)} %copy-done.35), channel_id=1, source_target_pairs={{0,3},{1,2},{2,1},{3,0},{4,7},{5,6},{6,5},{7,4},{8,11},{9,10},{10,... | collective-permute-start | bytes 2752520 | tf_op jit(solution)/shard_map/ppermute | solution.py:186
  (92 other events, 2867.7 us)
Sparse Core Ops, SparseCore 0:
  257.1 263.5 all-reduce.1

commit v3 on v2

--- a/solution.py
+++ b/solution.py
@@ -239,6 +239,189 @@
     )(meta, momentum, *received)
 
 
+def pack_pair_kernel(col_count, meta_ref, *refs):
+    pieces, keep, give, choose = refs[:col_count], refs[col_count], refs[col_count + 1], refs[-1]
+    other = pl.program_id(0) == 0
+    _, window, slots = choose.shape
+
+    @pl.when(other & (pl.program_id(1) == 0))
+    def _():
+        fill_choose(meta_ref, choose, 0)
+
+    total = jnp.dot(choose[0], pieces[0][...], preferred_element_type=jnp.float32)
+    for k in range(1, col_count):
+        total += jnp.dot(choose[k], pieces[k][...], preferred_element_type=jnp.float32)
+
+    @pl.when(other)
+    def _():
+        give[...] = total.astype(jnp.bfloat16)
+
+    @pl.when(jnp.logical_not(other))
+    def _():
+        keep[...] = total.astype(jnp.bfloat16)
+
+
+def fill_choose(meta_ref, choose, slot_axis):
+    col_count = choose.shape[0]
+    shape = choose.shape[1:]
+    rows = lax.broadcasted_iota(jnp.int32, shape, slot_axis)
+    slots = lax.broadcasted_iota(jnp.int32, shape, 1 - slot_axis)
+    for k in range(col_count):
+        hit = (rows == slots + meta_ref[2 + k]) & (slots < meta_ref[2 + col_count + k])
+        choose[k] = jnp.where(hit, 1.0, 0.0).astype(jnp.bfloat16)
+
+
+def pack_pair(meta, momentum, received, base, width, row_count, window):
+    slots = momentum.shape[0]
+    col_count = len(received) + 1
+    pairs = row_count // 2
+    first = base // width
+    block = lambda e, q, meta: meta[0] ^ (2 * q + 1 - e)
+    shape = jax.ShapeDtypeStruct((pairs * window, width), jnp.bfloat16)
+    return pl.pallas_call(
+        lambda *refs: pack_pair_kernel(col_count, *refs),
+        out_shape=[shape, shape],
+        grid_spec=pltpu.PrefetchScalarGridSpec(
+            num_scalar_prefetch=1,
+            grid=(2, pairs),
+            in_specs=[
+                pl.BlockSpec(
+                    (slots, width),
+                    lambda e, q, meta: (0, first + meta[1] * row_count + block(e, q, meta)),
+                )
+            ]
+            + [pl.BlockSpec((slots, width), lambda e, q, meta: (0, block(e, q, meta)))]
+            * (col_count - 1),
+            out_specs=[
+                pl.BlockSpec((window, width), lambda e, q, meta: (jnp.where(e == 0, 0, q), 0)),
+                pl.BlockSpec(
+                    (window, width), lambda e, q, meta: (jnp.where(e == 0, q, pairs - 1), 0)
+                ),
+            ],
+            scratch_shapes=[pltpu.VMEM((col_count, window, slots), jnp.bfloat16)],
+        ),
+        compiler_params=pltpu.CompilerParams(vmem_limit_bytes=VMEM_LIMIT),
+        cost_estimate=pl.CostEstimate(
+            flops=2 * window * slots * col_count * width * row_count,
+            bytes_accessed=2 * row_count * width * (slots * col_count + window),
+            transcendentals=0,
+        ),
+    )(meta, momentum, *received)
+
+
+def join_kernel(even, window, meta_ref, keep, got, *outs):
+    def write(low, high):
+        for q, out in enumerate(outs):
+            base = q * window
+            lap = window - even
+            out[:even, :] = low[base : base + even, :]
+            out[even:window, :] = (
+                low[base + even : base + window, :].astype(jnp.float32)
+                + high[base : base + lap, :].astype(jnp.float32)
+            ).astype(jnp.bfloat16)
+            out[window:, :] = high[base + lap : base + window, :]
+
+    @pl.when(meta_ref[0] % 2 == 0)
+    def _():
+        write(keep, got)
+
+    @pl.when(meta_ref[0] % 2 == 1)
+    def _():
+        write(got, keep)
+
+
+def local_call(kernel, out_shape, operands, moved, scratch=()):
+    whole = pl.BlockSpec(memory_space=pltpu.VMEM)
+    return pl.pallas_call(
+        kernel,
+        out_shape=out_shape,
+        in_specs=[pl.BlockSpec(memory_space=pltpu.SMEM)] + [whole] * (len(operands) - 1),
+        out_specs=jax.tree.map(lambda _: whole, out_shape),
+        scratch_shapes=list(scratch),
+        compiler_params=pltpu.CompilerParams(vmem_limit_bytes=VMEM_LIMIT),
+        cost_estimate=pl.CostEstimate(flops=moved, bytes_accessed=moved, transcendentals=0),
+    )(*operands)
+
+
+def join(meta, keep, got, even, window, pairs):
+    width = keep.shape[1]
+    shape = jax.ShapeDtypeStruct((even + window, width), jnp.bfloat16)
+    return local_call(
+        lambda *refs: join_kernel(even, window, *refs),
+        [shape] * pairs,
+        (meta, keep, got),
+        8 * pairs * window * width,
+    )
+
+
+def cut_kernel(even, window, meta_ref, *refs):
+    pieces, out = refs[:-1], refs[-1]
+    place = pl.ds(pl.multiple_of((1 - meta_ref[0] % 2) * even, 16), window)
+    for q, piece in enumerate(pieces):
+        out[q * window : (q + 1) * window, :] = piece[place, :]
+
+
+def cut(meta, pieces, even, window):
+    width = pieces[0].shape[1]
+    return local_call(
+        lambda *refs: cut_kernel(even, window, *refs),
+        jax.ShapeDtypeStruct((len(pieces) * window, width), jnp.bfloat16),
+        (meta, *pieces),
+        4 * len(pieces) * window * width,
+    )
+
+
+def unpack_pair_kernel(col_count, even, window, meta_ref, *refs):
+    got, outs, choose = refs[-2 - col_count], refs[-1 - col_count : -1], refs[-1]
+    pieces = refs[: -2 - col_count]
+    turn = pl.program_id(0)
+
+    @pl.when(turn == 0)
+    def _():
+        fill_choose(meta_ref, choose, 1)
+
+    def place(block):
+        for k in range(col_count):
+            outs[k][...] = jnp.dot(
+                choose[k], block, preferred_element_type=jnp.float32
+            ).astype(jnp.bfloat16)
+
+    for q, piece in enumerate(pieces):
+
+        @pl.when(turn == 2 * q)
+        def _():
+            own = pl.ds(pl.multiple_of(meta_ref[0] % 2 * even, 16), window)
+            place(piece[own, :])
+
+    @pl.when(turn % 2 == 1)
+    def _():
+        part = pl.ds(pl.multiple_of(turn // 2 * window, 16), window)
+        place(got[part, :])
+
+
+def unpack_pair(meta, pieces, got, col_count, slots, even, window):
+    width = got.shape[1]
+    count = 2 * len(pieces)
+    return pl.pallas_call(
+        lambda *refs: unpack_pair_kernel(col_count, even, window, *refs),
+        out_shape=[jax.ShapeDtypeStruct((slots, count * width), jnp.bfloat16)] * col_count,
+        grid_spec=pltpu.PrefetchScalarGridSpec(
+            num_scalar_prefetch=1,
+            grid=(count,),
+            in_specs=[pl.BlockSpec(x.shape, lambda q, meta: (0, 0)) for x in (*pieces, got)],
+            out_specs=[pl.BlockSpec((slots, width), lambda q, meta: (0, meta[0] ^ q))]
+            * col_count,
+            scratch_shapes=[pltpu.VMEM((col_count, slots, window), jnp.bfloat16)],
+        ),
+        compiler_params=pltpu.CompilerParams(vmem_limit_bytes=VMEM_LIMIT),
+        cost_estimate=pl.CostEstimate(
+            flops=2 * window * slots * col_count * width * count,
+            bytes_accessed=2 * count * width * (slots * col_count + window),
+            transcendentals=0,
+        ),
+    )(meta, *pieces, got)
+
+
 def unpack_kernel(col_count, meta_ref, *refs):
     pieces, outs, choose = refs[: -1 - col_count], refs[-1 - col_count : -1], refs[-1]
     turn = pl.program_id(0)
@@ -285,185 +468,234 @@
     )(meta, *pieces)
 
 
-def merge_kernel(even, jitter, distances, meta_ref, *refs):
+def merge_kernel(unit, share, distances, meta_ref, *refs):
     pieces, out_ref, total = refs[:-2], refs[-2], refs[-1]
-    window = pieces[0].shape[0]
+    jitter = (total.shape[0] - M) // 2
     total[...] = jnp.zeros_like(total)
-    for distance, piece in zip(distances, pieces):
-        place = pl.ds(pl.multiple_of((meta_ref[0] ^ distance) * even, 8), window)
-        total[place, :] += piece[...].astype(jnp.float32)
+    for places, piece in zip(distances, pieces):
+        rows = piece.shape[0] // len(places)
+        for n, distance in enumerate(places):
+            place = pl.ds(pl.multiple_of(((meta_ref[0] // share) ^ distance) * unit, 8), rows)
+            total[place, :] += piece[n * rows : (n + 1) * rows, :].astype(jnp.float32)
 
     @pl.loop(0, BLOCKS)
     def _(b):
         source = pl.ds(pl.multiple_of(b * TILE + jitter, 8), TILE)
-        out_ref[pl.ds(pl.multiple_of(b * TILE, TILE), TILE), :] = total[source, :].astype(
-            jnp.bfloat16
-        )
-
-
-def merge(meta, pieces, distances, even, jitter):
+        out_ref[tile_rows(b), :] = total[source, :].astype(jnp.bfloat16)
+
+
+def merge(meta, pieces, distances, unit, share, jitter):
     width = pieces[0].shape[1]
-    whole = pl.BlockSpec(memory_space=pltpu.VMEM)
-    return pl.pallas_call(
-        lambda *refs: merge_kernel(even, jitter, distances, *refs),
-        out_shape=jax.ShapeDtypeStruct((M, width), jnp.bfloat16),
-        in_specs=[pl.BlockSpec(memory_space=pltpu.SMEM)] + [whole] * len(pieces),
-        out_specs=whole,
-        scratch_shapes=[pltpu.VMEM((M + 2 * jitter, width), jnp.float32)],
-        compiler_params=pltpu.CompilerParams(vmem_limit_bytes=VMEM_LIMIT),
-        cost_estimate=pl.CostEstimate(
-            flops=2 * M * width, bytes_accessed=5 * M * width, transcendentals=0
-        ),
-    )(meta, *pieces)
+    return local_call(
+        lambda *refs: merge_kernel(unit, share, distances, *refs),
+        jax.ShapeDtypeStruct((M, width), jnp.bfloat16),
+        (meta, *pieces),
+        5 * M * width,
+        [pltpu.VMEM((M + 2 * jitter, width), jnp.float32)],
+    )
 
 
 def chunk_gram_kernel(rows_ref, cols_ref, meta_ref, *refs):
-    out_ref = refs[-1]
-    lefts, rights = refs[:-1:2], refs[1:-1:2]
-    dims = (((1,), (1,)), ((), ()))
-    mine = (pl.program_id(0) + meta_ref[0]) % 2 == 0
-
-    def product(count):
-        total = lax.dot_general(
-            lefts[0][...], rights[0][...], dims, preferred_element_type=jnp.float32
-        )
-        for c in range(1, count):
-            total += lax.dot_general(
-                lefts[c][...], rights[c][...], dims, preferred_element_type=jnp.float32
-            )
-        out_ref[...] = total.astype(jnp.bfloat16)
-
-    @pl.when(mine)
-    def _():
-        product(len(lefts))
-
-    @pl.when(jnp.logical_not(mine))
-    def _():
-        product(len(lefts) - 1)
+    matrices, out_ref, joined = refs[:-2], refs[-2], refs[-1]
+    turn = pl.program_id(0)
+
+    @pl.when(turn == 0)
+    def _():
+        place = 0
+        for matrix in matrices[:-1]:
+            joined[:, place : place + matrix.shape[1]] = matrix[...]
+            place += matrix.shape[1]
+        lane = lax.broadcasted_iota(jnp.int32, (TILE, LAST), 1)
+        own = lane // (LAST // 2) == meta_ref[0] % 2
+
+        @pl.loop(0, BLOCKS)
+        def _(b):
+            part = pl.ds(pl.multiple_of(b * TILE, TILE), TILE)
+            block = matrices[-1][part, :].astype(jnp.float32)
+            joined[part, place:] = jnp.where(own, block, 0.0).astype(jnp.bfloat16)
+
+    here = pl.ds(pl.multiple_of(rows_ref[turn] * TILE, TILE), TILE)
+    there = pl.ds(pl.multiple_of(cols_ref[turn] * TILE, TILE), TILE)
+    out_ref[...] = lax.dot_general(
+        joined[here, :],
+        joined[there, :],
+        (((1,), (1,)), ((), ())),
+        preferred_element_type=jnp.float32,
+    ).astype(jnp.bfloat16)
 
 
 def chunk_gram(meta, chunks):
     count = len(PAIRS)
-    in_specs = []
-    operands = []
     width = sum(x.shape[1] for x in chunks)
-    for x in chunks:
-        in_specs.append(pl.BlockSpec((TILE, x.shape[1]), lambda p, rows, cols, meta: (rows[p], 0)))
-        in_specs.append(pl.BlockSpec((TILE, x.shape[1]), lambda p, rows, cols, meta: (cols[p], 0)))
-        operands += [x, x]
     return pl.pallas_call(
         chunk_gram_kernel,
         out_shape=jax.ShapeDtypeStruct((count * TILE, TILE), jnp.bfloat16),
         grid_spec=pltpu.PrefetchScalarGridSpec(
             num_scalar_prefetch=3,
             grid=(count,),
-            in_specs=in_specs,
+            in_specs=[
+                pl.BlockSpec((M, x.shape[1]), lambda p, rows, cols, meta: (0, 0)) for x in chunks
+            ],
             out_specs=pl.BlockSpec((TILE, TILE), lambda p, rows, cols, meta: (p, 0)),
+            scratch_shapes=[pltpu.VMEM((M, width), jnp.bfloat16)],
         ),
         compiler_params=pltpu.CompilerParams(vmem_limit_bytes=VMEM_LIMIT),
         cost_estimate=pl.CostEstimate(
             flops=2 * count * TILE * TILE * width,
-            bytes_accessed=2 * count * TILE * (TILE + width),
+            bytes_accessed=2 * count * TILE * TILE + 2 * M * width,
             transcendentals=0,
         ),
-    )(jnp.asarray(PAIR_ROWS), jnp.asarray(PAIR_COLS), meta, *operands)
-
-
-def windows_kernel(even, jitter, sends, rows_ref, cols_ref, meta_ref, tile_ref, *refs):
+    )(jnp.asarray(PAIR_ROWS), jnp.asarray(PAIR_COLS), meta, *chunks)
+
+
+def tile_rows(b):
+    return pl.ds(pl.multiple_of(b * TILE, TILE), TILE)
+
+
+def first_product(panel, b, jitter, matrix, total, factor):
+    product = jnp.dot(panel, matrix[...], preferred_element_type=jnp.float32)
+    factor[tile_rows(b), :] = (coef_three * product).astype(jnp.bfloat16)
+    total[pl.ds(pl.multiple_of(b * TILE + jitter, 8), TILE), :] = (
+        coef_one * matrix[tile_rows(b), :].astype(jnp.float32) + coef_two * product
+    )
+
+
+def second_product(panel, b, jitter, total, factor):
+    place = pl.ds(pl.multiple_of(b * TILE + jitter, 8), TILE)
+    total[place, :] = math.sqrt(N) * (
+        total[place, :] + jnp.dot(panel, factor[...], preferred_element_type=jnp.float32)
+    )
+
+
+def clear_edges(total, jitter):
+    edge = jnp.zeros((jitter, total.shape[1]), jnp.float32)
+    total[pl.ds(0, jitter), :] = edge
+    total[pl.ds(M + jitter, jitter), :] = edge
+
+
+def store_windows(row, send, total, outs):
+    unit, share, rows, distances = send
+    for distance, out in zip(distances, outs):
+        place = pl.ds(pl.multiple_of(((row // share) ^ distance) * unit, 8), rows)
+        out[...] = total[place, :].astype(jnp.bfloat16)
+
+
+def first_apply_kernel(jitter, send, meta_ref, tiles_ref, matrix, *refs):
+    outs, gram_out = refs[:-6], refs[-6]
+    gram, total, factor, tile_sems, out_sem = refs[-5:]
+    copies = []
+    for p, (i, j) in enumerate(PAIRS):
+        copies.append(
+            pltpu.make_async_copy(
+                tiles_ref.at[pl.ds(p * TILE, TILE), :],
+                gram.at[i, :, pl.ds(j * TILE, TILE)],
+                tile_sems.at[p],
+            )
+        )
+        copies[-1].start()
+    clear_edges(total, jitter)
+    for p, (i, j) in enumerate(PAIRS):
+        copies[p].wait()
+        if i != j:
+            gram[j, :, pl.ds(i * TILE, TILE)] = gram[i, :, pl.ds(j * TILE, TILE)].T
+    back = pltpu.make_async_copy(gram, gram_out, out_sem)
+    back.start()
+
+    @pl.loop(0, BLOCKS)
+    def _(b):
+        first_product(gram[b], b, jitter, matrix, total, factor)
+
+    @pl.loop(0, BLOCKS)
+    def _(b):
+        second_product(gram[b], b, jitter, total, factor)
+
+    store_windows(meta_ref[0], send, total, outs)
+    back.wait()
+
+
+def first_apply(meta, tiles, matrix, send, jitter):
+    width = matrix.shape[1]
+    whole = pl.BlockSpec(memory_space=pltpu.VMEM)
+    outs = pl.pallas_call(
+        lambda *refs: first_apply_kernel(jitter, send, *refs),
+        out_shape=[jax.ShapeDtypeStruct((send[2], width), jnp.bfloat16)] * len(send[3])
+        + [jax.ShapeDtypeStruct((BLOCKS, TILE, M), jnp.bfloat16)],
+        in_specs=[
+            pl.BlockSpec(memory_space=pltpu.SMEM),
+            pl.BlockSpec(memory_space=pl.ANY),
+            whole,
+        ],
+        out_specs=[whole] * len(send[3]) + [pl.BlockSpec(memory_space=pl.ANY)],
+        scratch_shapes=[
+            pltpu.VMEM((BLOCKS, TILE, M), jnp.bfloat16),
+            pltpu.VMEM((M + 2 * jitter, width), jnp.float32),
+            pltpu.VMEM((M, width), jnp.bfloat16),
+            pltpu.SemaphoreType.DMA((len(PAIRS),)),
+            pltpu.SemaphoreType.DMA,
+        ],
+        compiler_params=pltpu.CompilerParams(vmem_limit_bytes=VMEM_LIMIT),
+        cost_estimate=pl.CostEstimate(
+            flops=4 * M * M * width, bytes_accessed=4 * M * width + 4 * M * M, transcendentals=0
+        ),
+    )(meta, tiles, matrix)
+    return outs[:-1], outs[-1]
+
+
+def next_apply_kernel(jitter, sends, meta_ref, panel_ref, *refs):
     chunks = len(sends)
-    outs_count = sum(len(s) for s in sends)
+    outs_count = sum(len(s[3]) for s in sends)
     matrices = refs[:chunks]
     outs = refs[chunks : chunks + outs_count]
-    gram = refs[chunks + outs_count]
-    totals = refs[chunks + outs_count + 1 : 2 * chunks + outs_count + 1]
-    factors = refs[2 * chunks + outs_count + 1 :]
+    totals = refs[chunks + outs_count : 2 * chunks + outs_count]
+    factors = refs[2 * chunks + outs_count :]
     turn = pl.program_id(0)
-    count = len(PAIRS)
-
-    @pl.when(turn == 0)
-    def _():
-        for total in totals:
-            edge = jnp.zeros((jitter, total.shape[1]), jnp.float32)
-            total[pl.ds(0, jitter), :] = edge
-            total[pl.ds(M + jitter, jitter), :] = edge
-
-    @pl.when(turn < count)
-    def _():
-        i = rows_ref[jnp.minimum(turn, count - 1)]
-        j = cols_ref[jnp.minimum(turn, count - 1)]
-        gram[i, :, pl.ds(pl.multiple_of(j * TILE, TILE), TILE)] = tile_ref[...]
-
-        @pl.when(i != j)
-        def _():
-            gram[j, :, pl.ds(pl.multiple_of(i * TILE, TILE), TILE)] = tile_ref[...].T
-
-    @pl.when((turn >= count) & (turn < count + BLOCKS))
-    def _():
-        b = turn - count
-        part = pl.ds(pl.multiple_of(b * TILE, TILE), TILE)
-        place = pl.ds(pl.multiple_of(b * TILE + jitter, 8), TILE)
+
+    @pl.when(turn < BLOCKS)
+    def _():
         for matrix, total, factor in zip(matrices, totals, factors):
-            product = jnp.dot(gram[b], matrix[...], preferred_element_type=jnp.float32)
-            factor[part, :] = (coef_three * product).astype(jnp.bfloat16)
-            total[place, :] = (
-                coef_one * matrix[part, :].astype(jnp.float32) + coef_two * product
-            )
-
-    @pl.when(turn >= count + BLOCKS)
-    def _():
-        b = turn - count - BLOCKS
-        place = pl.ds(pl.multiple_of(b * TILE + jitter, 8), TILE)
+            first_product(panel_ref[0], turn, jitter, matrix, total, factor)
+
+    @pl.when(turn >= BLOCKS)
+    def _():
         for total, factor in zip(totals, factors):
-            total[place, :] = math.sqrt(N) * (
-                total[place, :] + jnp.dot(gram[b], factor[...], preferred_element_type=jnp.float32)
-            )
-
-    @pl.when(turn == count + 2 * BLOCKS - 1)
-    def _():
-        number = 0
+            second_product(panel_ref[0], turn - BLOCKS, jitter, total, factor)
+
+    @pl.when(turn == 2 * BLOCKS - 1)
+    def _():
+        place = 0
         for total, send in zip(totals, sends):
-            for distance in send:
-                window = outs[number].shape[0]
-                place = pl.ds(pl.multiple_of((meta_ref[0] ^ distance) * even, 8), window)
-                outs[number][...] = total[place, :].astype(jnp.bfloat16)
-                number += 1
-
-
-def apply_windows(meta, tiles, matrices, sends, even, jitter):
-    count = len(PAIRS)
+            clear_edges(total, jitter)
+            store_windows(meta_ref[0], send, total, outs[place : place + len(send[3])])
+            place += len(send[3])
+
+
+def next_apply(meta, gram, matrices, sends, jitter):
     widths = [x.shape[1] for x in matrices]
-    shapes = [
-        (even + 2 * jitter, width) for width, send in zip(widths, sends) for _ in send
-    ]
-    whole = lambda t, rows, cols, meta: (0, 0)
+    shapes = [(send[2], width) for width, send in zip(widths, sends) for _ in send[3]]
+    whole = lambda t, meta: (0, 0)
     outs = pl.pallas_call(
-        lambda *refs: windows_kernel(even, jitter, sends, *refs),
+        lambda *refs: next_apply_kernel(jitter, sends, *refs),
         out_shape=[jax.ShapeDtypeStruct(shape, jnp.bfloat16) for shape in shapes],
         grid_spec=pltpu.PrefetchScalarGridSpec(
-            num_scalar_prefetch=3,
-            grid=(count + 2 * BLOCKS,),
-            in_specs=[
-                pl.BlockSpec(
-                    (TILE, TILE), lambda t, rows, cols, meta: (jnp.minimum(t, count - 1), 0)
-                )
-            ]
+            num_scalar_prefetch=1,
+            grid=(2 * BLOCKS,),
+            in_specs=[pl.BlockSpec((1, TILE, M), lambda t, meta: (t % BLOCKS, 0, 0))]
             + [pl.BlockSpec((M, width), whole) for width in widths],
             out_specs=[pl.BlockSpec(shape, whole) for shape in shapes],
-            scratch_shapes=[pltpu.VMEM((BLOCKS, TILE, M), jnp.bfloat16)]
-            + [pltpu.VMEM((M + 2 * jitter, width), jnp.float32) for width in widths]
+            scratch_shapes=[pltpu.VMEM((M + 2 * jitter, width), jnp.float32) for width in widths]
             + [pltpu.VMEM((M, width), jnp.bfloat16) for width in widths],
         ),
         compiler_params=pltpu.CompilerParams(vmem_limit_bytes=VMEM_LIMIT),
         cost_estimate=pl.CostEstimate(
             flops=4 * M * M * sum(widths),
-            bytes_accessed=4 * M * sum(widths) + 2 * count * TILE * TILE,
+            bytes_accessed=4 * M * sum(widths) + 4 * M * M,
             transcendentals=0,
         ),
-    )(jnp.asarray(PAIR_ROWS), jnp.asarray(PAIR_COLS), meta, tiles, *matrices)
+    )(meta, gram, *matrices)
     result = []
     for send in sends:
-        result.append(outs[: len(send)])
-        outs = outs[len(send) :]
+        result.append(outs[: len(send[3])])
+        outs = outs[len(send[3]) :]
     return result
 
 
@@ -491,50 +723,89 @@
 
     wide = row_count * col_count * CHUNK
     number = (N // (row_count * col_count)) // CHUNK
-    plan = [(c * wide, CHUNK, 1, row_count) for c in range(number)]
-    plan.append((number * wide, LAST, 2, pair_count))
-
-    matrices = []
-    for base, width, step, count in plan:
-        span = count * width
+    distances = list(range(pair_count))
+
+    def fetch(base, span, after):
+        place, after = lax.optimization_barrier((col, after))
         received = [
             swap(
-                lax.dynamic_slice_in_dim(momentum_shards, base + (col ^ k) * span, span, axis=1),
+                lax.dynamic_slice_in_dim(
+                    momentum_shards, base + (place ^ k) * span, span, axis=1
+                ),
                 "col",
                 col_count,
                 k,
             )
             for k in range(1, col_count)
         ]
-        pieces = pack(meta, momentum_shards, received, base, width, step, count, window)
-        landed = [pieces[0]] + [
-            swap(pieces[q], "row", row_count, q * step) for q in range(1, count)
-        ]
-        distances = [q * step for q in range(count)]
-        if step == 2:
-            landed += [swap(piece, "row", row_count, 1) for piece in landed]
-            distances += [d ^ 1 for d in distances]
-        matrices.append(merge(meta, landed, distances, even, jitter))
+        return received, after
+
+    def across(pieces):
+        return [pieces[0]] + [swap(pieces[q], "row", row_count, 2 * q) for q in distances[1:]]
+
+    def gather_chunk(c, received):
+        keep, give = pack_pair(
+            meta, momentum_shards, received, c * wide, CHUNK, row_count, window
+        )
+        return join(meta, keep, swap(give, "row", row_count, 1), even, window, pair_count)
+
+    received, _ = fetch(0, row_count * CHUNK, shard_starts)
+    last, received = fetch(number * wide, pair_count * LAST, received)
+    joined = gather_chunk(0, received)
+    landed = []
+    for c in range(1, number):
+        received, (last, joined) = fetch(c * wide, row_count * CHUNK, (last, joined))
+        crossed, received = lax.optimization_barrier((across(joined), received))
+        landed.append(crossed)
+        joined = gather_chunk(c, received)
+    landed.append(across(joined))
+    matrices = [
+        merge(meta, pieces, [[q] for q in distances], 2 * even, 2, jitter) for pieces in landed
+    ]
+    pieces = pack(
+        meta, momentum_shards, last, number * wide, LAST, 2, pair_count, window
+    )
+    stack = jnp.concatenate(across(pieces), axis=0)
+    twin = swap(stack, "row", row_count, 1)
+    matrices.append(
+        merge(
+            meta,
+            [stack, twin],
+            [[2 * q for q in distances], [2 * q + 1 for q in distances]],
+            even,
+            1,
+            jitter,
+        )
+    )
 
     tiles = reduce_tiles(chunk_gram(meta, matrices))
 
-    sends = [[q * step for q in range(count)] for _, _, step, count in plan]
-    results = []
-    for group in [[c] for c in range(number - 1)] + [[number - 1, number]]:
-        results += apply_windows(
-            meta, tiles, [matrices[c] for c in group], [sends[c] for c in group], even, jitter
-        )
-
+    sends = [(2 * even, 2, even + window, distances)] * number
+    sends.append((even, 1, window, [2 * q for q in distances]))
+    first, gram = first_apply(meta, tiles, matrices[0], sends[0], jitter)
+    results = [first] + next_apply(meta, gram, matrices[1:], sends[1:], jitter)
+
+    crossed = [across(results[0])]
+    crossed[0], results[1:] = lax.optimization_barrier((crossed[0], results[1:]))
+    crossed += [across(pieces) for pieces in results[1:]]
+    backs = []
+    for c in range(number + 1):
+        if c < number:
+            got = swap(cut(meta, crossed[c], even, window), "row", row_count, 1)
+            parts = unpack_pair(meta, crossed[c], got, col_count, slots, even, window)
+        else:
+            parts = unpack(meta, crossed[c], col_count, slots, 2)
+        back = [parts[0]] + [swap(parts[k], "col", col_count, k) for k in range(1, col_count)]
+        if c + 1 < number:
+            back, crossed[c + 1 :] = lax.optimization_barrier((back, crossed[c + 1 :]))
+        backs.append(back)
     out = jnp.zeros(momentum_shards.shape, jnp.bfloat16)
-    for (base, width, step, count), pieces in zip(plan, results):
-        span = count * width
-        landed = [pieces[0]] + [
-            swap(pieces[q], "row", row_count, q * step) for q in range(1, count)
-        ]
-        backs = unpack(meta, landed, col_count, slots, step)
+    for c, back in enumerate(backs):
+        span = row_count * CHUNK if c < number else pair_count * LAST
         for k in range(col_count):
-            back = backs[0] if k == 0 else swap(backs[k], "col", col_count, k)
-            out = lax.dynamic_update_slice_in_dim(out, back, base + (col ^ k) * span, axis=1)
+            out = lax.dynamic_update_slice_in_dim(
+                out, back[k], c * wide + (col ^ k) * span, axis=1
+            )
     return out
 
 

time: 814 us -> 732 us (0.90); the launches traced: 812 us -> 722 us
  waiting for transfers between devices: 507 us -> 462 us
  starting transfers between devices: 96.7 us -> 65.1 us
  Pallas kernels: 175 us -> 150 us
  local copies, waits for them, and re-layouts: 18.8 us -> 30.3 us
    ppermute x56 -> x41, waiting for transfers between devices: 244 us -> 201 us  [swap(): lax.ppermute(value, axis, perm=[(i, i ^ distance) for i in range(size)])]
    ppermute x56 -> x41, starting transfers between devices: 96.7 us -> 65.1 us  [swap(): lax.ppermute(value, axis, perm=[(i, i ^ distance) for i in range(size)])]
    pallas_call x3 -> x1, Pallas kernels: 23.8 us -> 5.11 us  [pack(): pl.pallas_call(lambda *refs: pack_kernel(step, col_count, *refs), out_sha...]
    pallas_call x3 -> x1, Pallas kernels: 21.9 us -> 4.93 us  [unpack(): pl.pallas_call(lambda *refs: unpack_kernel(col_count, *refs), out_shape=[...]
    pallas_call x5 -> x13, Pallas kernels: 99.8 us -> 116 us  [the longest x1 35.1 us: next_apply(): pl.pallas_call(lambda *refs: next_apply_kernel(jitter, sends, *refs), out...]
  transfers between devices with their start and end apart: 57 -> 42, of which waited for: 21 -> 19; matrix products, arithmetic and copies ran while one was open for 1% -> 2% of each run, Pallas kernels for 13% -> 10%
where the time goes in v3:
time: 732 us; the launch traced here: 722 us
  waiting for transfers between devices  462 us (63%)
  Pallas kernels  150 us (20%)
  starting transfers between devices  65.1 us (9%)
  local copies, waits for them, and re-layouts  30.3 us (4%)
  between operations  13.8 us (2%)
    psum x1, waiting for transfers between devices, reduce_tiles(): return lax.psum(tiles, ('row', 'col'))  261 us
    ppermute x41, waiting for transfers between devices, swap(): lax.ppermute(value, axis, perm=[(i, i ^ distance) for i in range(size)])  201 us
    ppermute x41, starting transfers between devices, swap(): lax.ppermute(value, axis, perm=[(i, i ^ distance) for i in range(size)])  65.1 us
    pallas_call x1, Pallas kernels, next_apply(): pl.pallas_call(lambda *refs: next_apply_kernel(jitter, sends, *refs), out...  35.1 us
    pallas_call x1, Pallas kernels, first_apply(): pl.pallas_call(lambda *refs: first_apply_kernel(jitter, send, *refs), out...  24.1 us
    pallas_call x1, Pallas kernels, chunk_gram(): pl.pallas_call(chunk_gram_kernel, out_shape=jax.ShapeDtypeStruct((count *...  23.8 us
    pallas_call x7, Pallas kernels, local_call(): pl.pallas_call(kernel, out_shape=out_shape, in_specs=[pl.BlockSpec(memory...  21.5 us
    pallas_call x2, Pallas kernels, pack_pair(): pl.pallas_call(lambda *refs: pack_pair_kernel(col_count, *refs), out_shap...  17.9 us
  transfers between devices with their start and end apart: 42, of which 19 were waited for; matrix products, arithmetic and copies ran while one was open for 2% of the time, Pallas kernels for 10%

profile of v3, /device:TPU:0, one launch (start us, length us, event | category | flops | bytes accessed | tf_op | source)
XLA Modules:
  0.0 721.9 jit_solution(4582643324741225459)
XLA Ops:
  16.4 16.3 %collective-permute-done.refs_2_ = bf16[224,2048]{1,0:T(8,128)(2,1)} collective-permute-done((bf16[224,2048]{1,0:T(8,128)(2,1)S(1)}, bf16[224,2048]{1,0:T(8,128)(2,1)}, u32[]{:S(2)}, u32[]{:S(2)}) %collective-permute-start) | collective-permute-done | bytes 917536 | tf_op jit(solution)/shard_map/ppermute | solution.py:186
  32.8 20.3 %collective-permute-done.1.refs_3_ = bf16[224,2048]{1,0:T(8,128)(2,1)} collective-permute-done((bf16[224,2048]{1,0:T(8,128)(2,1)S(1)}, bf16[224,2048]{1,0:T(8,128)(2,1)}, u32[]{:S(2)}, u32[]{:S(2)}) %collective-permute-start.1) | collective-permute-done | bytes 917536 | tf_op jit(solution)/shard_map/ppermute | solution.py:186
  53.0 8.9 %shard_map.46 = (bf16[2240,256]{1,0:T(8,128)(2,1)}, bf16[2240,256]{1,0:T(8,128)(2,1)}) custom-call(s32[10]{0:T(128)} %pad_add_fusion.1.refs_0_.meta_ref, bf16[224,18432]{1,0:T(8,128)(2,1)} %refs_1_.5, bf16[224,2048]{1,0:T(8,128)(2,1)} %collective-permute-done.refs_2_, bf16[224,2048]{1,0:T(8,128)(2,1)} %collective-permute-done.1.refs_3_, ...), custom_call_target="tpu_custom_call" | custom-call | flops 2055208960 | bytes 5963776 | tf_op jit(solution)/shard_map/pallas_call | solution.py:281
  86.8 10.2 %collective-permute-done.7.refs_2_ = bf16[1008,256]{1,0:T(8,128)(2,1)S(1)} collective-permute-done((bf16[1008,256]{1,0:T(8,128)(2,1)}, bf16[1008,256]{1,0:T(8,128)(2,1)S(1)}, u32[]{:S(2)}, u32[]{:S(2)}) %collective-permute-start.7) | collective-permute-done | bytes 516128 | tf_op jit(solution)/shard_map/ppermute | solution.py:186
  99.5 22.6 %collective-permute-done.8.refs_3_ = bf16[1008,256]{1,0:T(8,128)(2,1)S(1)} collective-permute-done((bf16[1008,256]{1,0:T(8,128)(2,1)}, bf16[1008,256]{1,0:T(8,128)(2,1)S(1)}, u32[]{:S(2)}, u32[]{:S(2)}) %collective-permute-start.8) | collective-permute-done | bytes 516128 | tf_op jit(solution)/shard_map/ppermute | solution.py:186
  124.4 8.9 %shard_map.49 = (bf16[2240,256]{1,0:T(8,128)(2,1)}, bf16[2240,256]{1,0:T(8,128)(2,1)}) custom-call(s32[10]{0:T(128)} %pad_add_fusion.1.refs_0_.meta_ref, bf16[224,18432]{1,0:T(8,128)(2,1)} %refs_1_.5, bf16[224,2048]{1,0:T(8,128)(2,1)} %copy-done.4, bf16[224,2048]{1,0:T(8,128)(2,1)} %copy-done.5, bf16[224,2048]{1,0:T(8,128)(2,1)} %copy-done.6), custom_call_target="tpu_custom_call" | custom-call | flops 2055208960 | bytes 5963776 | tf_op jit(solution)/shard_map/pallas_call | solution.py:281
  133.5 5.1 shard_map.52
  138.6 9.1 %collective-permute-start.17 = (bf16[560,128]{1,0:T(8,128)(2,1)}, bf16[560,128]{1,0:T(8,128)(2,1)S(1)}, u32[]{:S(2)}, u32[]{:S(2)}) collective-permute-start(bf16[560,128]{1,0:T(8,128)(2,1)} %get-tuple-element.123), channel_id=1, source_target_pairs={{0,8},{4,12},{8,0},{12,4},{16,24},{20,28},{24,16},{28,20},{1,9},{5... | collective-permute-start | bytes 430088 | tf_op jit(solution)/shard_map/ppermute | solution.py:186
  155.0 6.7 collective-permute-done.18
  178.6 13.4 %collective-permute-done.14.refs_2_ = bf16[1008,256]{1,0:T(8,128)(2,1)S(1)} collective-permute-done((bf16[1008,256]{1,0:T(8,128)(2,1)}, bf16[1008,256]{1,0:T(8,128)(2,1)S(1)}, u32[]{:S(2)}, u32[]{:S(2)}) %collective-permute-start.14) | collective-permute-done | bytes 516128 | tf_op jit(solution)/shard_map/ppermute | solution.py:186
  192.0 14.7 %collective-permute-done.15.refs_3_ = bf16[1008,256]{1,0:T(8,128)(2,1)S(1)} collective-permute-done((bf16[1008,256]{1,0:T(8,128)(2,1)}, bf16[1008,256]{1,0:T(8,128)(2,1)S(1)}, u32[]{:S(2)}, u32[]{:S(2)}) %collective-permute-start.15) | collective-permute-done | bytes 516128 | tf_op jit(solution)/shard_map/ppermute | solution.py:186
  211.3 23.8 %shard_map.54 = bf16[14336,512]{1,0:T(8,128)(2,1)} custom-call(s32[28]{0:T(128)} %constant.61.clone.rows_ref, s32[28]{0:T(128)} %constant.62.clone.cols_ref, s32[10]{0:T(128)} %pad_add_fusion.1.refs_0_.meta_ref, bf16[3584,256]{1,0:T(8,128)(2,1)} %shard_map.48.refs_0_.refs_2_, bf16[3584,256]{1,0:T(8,128)(2,1)} %shard_map.51.refs_1_.refs_2_, ...), custom_call_target="tpu_custom_call" | custom-call | flops 9395240960 | bytes 19267584 | tf_op jit(solution)/shard_map/pallas_call | solution.py:530
  235.2 260.8 %all-reduce.2.cloned.1.call-done.refs_1_ = bf16[14336,512]{1,0:T(8,128)(2,1)} async-done(((bf16[14336,512]{1,0:T(8,128)(2,1)}), bf16[14336,512]{1,0:T(8,128)(2,1)}) %all-reduce.2.cloned.1.call-update) | async-done | bytes 14680080 | tf_op jit(solution)/shard_map/psum | solution.py:703
  496.0 24.1 %shard_map.55 = (bf16[1008,256]{1,0:T(8,128)(2,1)}, bf16[1008,256]{1,0:T(8,128)(2,1)}, bf16[1008,256]{1,0:T(8,128)(2,1)}, bf16[1008,256]{1,0:T(8,128)(2,1)}, bf16[7,512,3584]{2,1,0:T(8,128)(2,1)}) custom-call(s32[10]{0:T(128)} %pad_add_fusion.1.refs_0_.meta_ref, bf16[14336,512]{1,0:T(8,128)(2,1)} %all-reduce.2.cloned.1.call-done.refs_1_, ...), custom_call_target="tpu_custom_call" | custom-call | flops 13153337344 | bytes 55050240 | tf_op jit(solution)/shard_map/pallas_call | solution.py:619
  524.5 35.1 %shard_map.56 = (bf16[1008,256]{1,0:T(8,128)(2,1)}, bf16[1008,256]{1,0:T(8,128)(2,1)}, bf16[1008,256]{1,0:T(8,128)(2,1)}, bf16[1008,256]{1,0:T(8,128)(2,1)}, bf1...) custom-call(s32[10]{0:T(128)} %pad_add_fusion.1.refs_0_.meta_ref, ...), custom_call_target="tpu_custom_call" | custom-call | flops 19730006016 | bytes 56885248 | tf_op jit(solution)/shard_map/pallas_call | solution.py:676
  563.4 9.3 %collective-permute-start.28 = (bf16[1008,256]{1,0:T(8,128)(2,1)}, bf16[1008,256]{1,0:T(8,128)(2,1)S(1)}, u32[]{:S(2)}, u32[]{:S(2)}) collective-permute-start(bf16[1008,256]{1,0:T(8,128)(2,1)} %get-tuple-element.148), channel_id=1, source_target_pairs={{0,8},{4,12},{8,0},{12,4},{16,24},{20,28},{24,16},{28,20},{1,9},{5... | collective-permute-start | bytes 1548296 | tf_op jit(solution)/shard_map/ppermute | solution.py:186
  573.8 9.0 %shard_map.58 = (bf16[224,2048]{1,0:T(8,128)(2,1)}, bf16[224,2048]{1,0:T(8,128)(2,1)}, bf16[224,2048]{1,0:T(8,128)(2,1)}, bf16[224,2048]{1,0:T(8,128)(2,1)}) custom-call(s32[10]{0:T(128)} %pad_add_fusion.1.refs_0_.meta_ref, bf16[1008,256]{1,0:T(8,128)(2,1)} %get-tuple-element.139.refs_1_, bf16[1008,256]{1,0:T(8,128)(2,1)} %copy-done.18, ...), custom_call_target="tpu_custom_call" | custom-call | flops 2055208960 | bytes 5963776 | tf_op jit(solution)/shard_map/pallas_call | solution.py:405
  590.3 7.8 %collective-permute-done.32.refs_3_ = bf16[560,128]{1,0:T(8,128)(2,1)S(1)} collective-permute-done((bf16[560,128]{1,0:T(8,128)(2,1)S(1)}, bf16[560,128]{1,0:T(8,128)(2,1)S(1)}, u32[]{:S(2)}, u32[]{:S(2)}) %collective-permute-start.32) | collective-permute-done | bytes 143392 | tf_op jit(solution)/shard_map/ppermute | solution.py:186
  599.7 5.3 collective-permute-done.33.refs_4_
  606.7 32.1 %collective-permute-done.29.refs_3_ = bf16[1008,256]{1,0:T(8,128)(2,1)S(1)} collective-permute-done((bf16[1008,256]{1,0:T(8,128)(2,1)S(1)}, bf16[1008,256]{1,0:T(8,128)(2,1)S(1)}, u32[]{:S(2)}, u32[]{:S(2)}) %collective-permute-start.29) | collective-permute-done | bytes 516128 | tf_op jit(solution)/shard_map/ppermute | solution.py:186
  642.5 4.9 shard_map.61
  651.5 8.7 %shard_map.60 = (bf16[224,2048]{1,0:T(8,128)(2,1)}, bf16[224,2048]{1,0:T(8,128)(2,1)}, bf16[224,2048]{1,0:T(8,128)(2,1)}, bf16[224,2048]{1,0:T(8,128)(2,1)}) custom-call(s32[10]{0:T(128)} %pad_add_fusion.1.refs_0_.meta_ref, bf16[1008,256]{1,0:T(8,128)(2,1)} %get-tuple-element.159.refs_1_, bf16[1008,256]{1,0:T(8,128)(2,1)} %copy-done.15, ...), custom_call_target="tpu_custom_call" | custom-call | flops 2055208960 | bytes 5963776 | tf_op jit(solution)/shard_map/pallas_call | solution.py:405
  669.0 14.6 %collective-permute-done.35 = bf16[224,2048]{1,0:T(8,128)(2,1)S(1)} collective-permute-done((bf16[224,2048]{1,0:T(8,128)(2,1)}, bf16[224,2048]{1,0:T(8,128)(2,1)S(1)}, u32[]{:S(2)}, u32[]{:S(2)}) %collective-permute-start.35) | collective-permute-done | bytes 917536 | tf_op jit(solution)/shard_map/ppermute | solution.py:186
  684.3 24.5 %collective-permute-done.36 = bf16[224,2048]{1,0:T(8,128)(2,1)S(1)} collective-permute-done((bf16[224,2048]{1,0:T(8,128)(2,1)}, bf16[224,2048]{1,0:T(8,128)(2,1)S(1)}, u32[]{:S(2)}, u32[]{:S(2)}) %collective-permute-start.36) | collective-permute-done | bytes 917536 | tf_op jit(solution)/shard_map/ppermute | solution.py:186
  (171 shorter events, 111.6 us)
Async XLA Ops:
  6.5 489.5 %all-reduce.2.cloned.1.call-start = ((), (), s32[]{:S(2)}) async-start(), calls=%async_computation | async-start | bytes 29360128 | tf_op jit(solution)/shard_map/psum | solution.py:703
  11.5 41.6 %collective-permute-start.1 = (bf16[224,2048]{1,0:T(8,128)(2,1)S(1)}, bf16[224,2048]{1,0:T(8,128)(2,1)}, u32[]{:S(2)}, u32[]{:S(2)}) collective-permute-start(bf16[224,2048]{1,0:T(8,128)(2,1)S(1)} %get-tuple-element.182), channel_id=1, source_target_pairs={{0,2},{1,3},{2,0},{3,1},{4,6},{5,7},{6,4},{7,5},{8,10},{9,11},{10,... | collective-permute-start | bytes 2752520 | tf_op jit(solution)/shard_map/ppermute | solution.py:186
  13.0 40.1 %collective-permute-start.2 = (bf16[224,2048]{1,0:T(8,128)(2,1)S(1)}, bf16[224,2048]{1,0:T(8,128)(2,1)}, u32[]{:S(2)}, u32[]{:S(2)}) collective-permute-start(bf16[224,2048]{1,0:T(8,128)(2,1)S(1)} %get-tuple-element.181), channel_id=1, source_target_pairs={{0,3},{1,2},{2,1},{3,0},{4,7},{5,6},{6,5},{7,4},{8,11},{9,10},{10,... | collective-permute-start | bytes 2752520 | tf_op jit(solution)/shard_map/ppermute | solution.py:186
  80.7 41.5 %collective-permute-start.10 = (bf16[224,2048]{1,0:T(8,128)(2,1)S(1)}, bf16[224,2048]{1,0:T(8,128)(2,1)S(1)}, u32[]{:S(2)}, u32[]{:S(2)}) collective-permute-start(bf16[224,2048]{1,0:T(8,128)(2,1)S(1)} %get-tuple-element.177), channel_id=1, source_target_pairs={{0,1},{1,0},{2,3},{3,2},{4,5},{5,4},{6,7},{7,6},{8,9},{9,8},{10,11... | collective-permute-start | bytes 2752520 | tf_op jit(solution)/shard_map/ppermute | solution.py:186
  81.6 40.8 %collective-permute-start.11 = (bf16[224,2048]{1,0:T(8,128)(2,1)S(1)}, bf16[224,2048]{1,0:T(8,128)(2,1)S(1)}, u32[]{:S(2)}, u32[]{:S(2)}) collective-permute-start(bf16[224,2048]{1,0:T(8,128)(2,1)S(1)} %get-tuple-element.176), channel_id=1, source_target_pairs={{0,2},{1,3},{2,0},{3,1},{4,6},{5,7},{6,4},{7,5},{8,10},{9,11},{10,... | collective-permute-start | bytes 2752520 | tf_op jit(solution)/shard_map/ppermute | solution.py:186
  83.1 39.3 %collective-permute-start.12 = (bf16[224,2048]{1,0:T(8,128)(2,1)S(1)}, bf16[224,2048]{1,0:T(8,128)(2,1)S(1)}, u32[]{:S(2)}, u32[]{:S(2)}) collective-permute-start(bf16[224,2048]{1,0:T(8,128)(2,1)S(1)} %get-tuple-element.175), channel_id=1, source_target_pairs={{0,3},{1,2},{2,1},{3,0},{4,7},{5,6},{6,5},{7,4},{8,11},{9,10},{10,... | collective-permute-start | bytes 2752520 | tf_op jit(solution)/shard_map/ppermute | solution.py:186
  84.2 37.9 %collective-permute-start.8 = (bf16[1008,256]{1,0:T(8,128)(2,1)}, bf16[1008,256]{1,0:T(8,128)(2,1)S(1)}, u32[]{:S(2)}, u32[]{:S(2)}) collective-permute-start(bf16[1008,256]{1,0:T(8,128)(2,1)} %get-tuple-element.103), channel_id=1, source_target_pairs={{0,16},{4,20},{8,24},{12,28},{16,0},{20,4},{24,8},{28,12},{1,17},{... | collective-permute-start | bytes 1548296 | tf_op jit(solution)/shard_map/ppermute | solution.py:186
  133.4 28.4 %collective-permute-start.13 = (bf16[2240,256]{1,0:T(8,128)(2,1)}, bf16[2240,256]{1,0:T(8,128)(2,1)S(1)}, u32[]{:S(2)}, u32[]{:S(2)}) collective-permute-start(bf16[2240,256]{1,0:T(8,128)(2,1)} %get-tuple-element.114), channel_id=1, source_target_pairs={{0,4},{4,0},{8,12},{12,8},{16,20},{20,16},{24,28},{28,24},{1,5},{5... | collective-permute-start | bytes 3440648 | tf_op jit(solution)/shard_map/ppermute | solution.py:186
  168.9 37.9 %collective-permute-start.15 = (bf16[1008,256]{1,0:T(8,128)(2,1)}, bf16[1008,256]{1,0:T(8,128)(2,1)S(1)}, u32[]{:S(2)}, u32[]{:S(2)}) collective-permute-start(bf16[1008,256]{1,0:T(8,128)(2,1)} %get-tuple-element.117), channel_id=1, source_target_pairs={{0,16},{4,20},{8,24},{12,28},{16,0},{20,4},{24,8},{28,12},{1,17},{... | collective-permute-start | bytes 1548296 | tf_op jit(solution)/shard_map/ppermute | solution.py:186
  169.9 36.8 %collective-permute-start.16 = (bf16[1008,256]{1,0:T(8,128)(2,1)}, bf16[1008,256]{1,0:T(8,128)(2,1)S(1)}, u32[]{:S(2)}, u32[]{:S(2)}) collective-permute-start(bf16[1008,256]{1,0:T(8,128)(2,1)} %get-tuple-element.118), channel_id=1, source_target_pairs={{0,24},{4,28},{8,16},{12,20},{16,8},{20,12},{24,0},{28,4},{1,25},{... | collective-permute-start | bytes 1548296 | tf_op jit(solution)/shard_map/ppermute | solution.py:186
  520.1 39.5 %collective-permute-start.21 = (bf16[1008,256]{1,0:T(8,128)(2,1)}, bf16[1008,256]{1,0:T(8,128)(2,1)S(1)}, u32[]{:S(2)}, u32[]{:S(2)}) collective-permute-start(bf16[1008,256]{1,0:T(8,128)(2,1)} %get-tuple-element.127), channel_id=1, source_target_pairs={{0,8},{4,12},{8,0},{12,4},{16,24},{20,28},{24,16},{28,20},{1,9},{5... | collective-permute-start | bytes 1548296 | tf_op jit(solution)/shard_map/ppermute | solution.py:186
  521.6 38.1 %collective-permute-start.22 = (bf16[1008,256]{1,0:T(8,128)(2,1)}, bf16[1008,256]{1,0:T(8,128)(2,1)S(1)}, u32[]{:S(2)}, u32[]{:S(2)}) collective-permute-start(bf16[1008,256]{1,0:T(8,128)(2,1)} %get-tuple-element.128), channel_id=1, source_target_pairs={{0,16},{4,20},{8,24},{12,28},{16,0},{20,4},{24,8},{28,12},{1,17},{... | collective-permute-start | bytes 1548296 | tf_op jit(solution)/shard_map/ppermute | solution.py:186
  523.1 36.5 %collective-permute-start.23 = (bf16[1008,256]{1,0:T(8,128)(2,1)}, bf16[1008,256]{1,0:T(8,128)(2,1)S(1)}, u32[]{:S(2)}, u32[]{:S(2)}) collective-permute-start(bf16[1008,256]{1,0:T(8,128)(2,1)} %get-tuple-element.129), channel_id=1, source_target_pairs={{0,24},{4,28},{8,16},{12,20},{16,8},{20,12},{24,0},{28,4},{1,25},{... | collective-permute-start | bytes 1548296 | tf_op jit(solution)/shard_map/ppermute | solution.py:186
  563.4 42.4 %collective-permute-start.28 = (bf16[1008,256]{1,0:T(8,128)(2,1)}, bf16[1008,256]{1,0:T(8,128)(2,1)S(1)}, u32[]{:S(2)}, u32[]{:S(2)}) collective-permute-start(bf16[1008,256]{1,0:T(8,128)(2,1)} %get-tuple-element.148), channel_id=1, source_target_pairs={{0,8},{4,12},{8,0},{12,4},{16,24},{20,28},{24,16},{28,20},{1,9},{5... | collective-permute-start | bytes 1548296 | tf_op jit(solution)/shard_map/ppermute | solution.py:186
  582.8 56.0 %collective-permute-start.25 = (bf16[224,2048]{1,0:T(8,128)(2,1)}, bf16[224,2048]{1,0:T(8,128)(2,1)}, u32[]{:S(2)}, u32[]{:S(2)}) collective-permute-start(bf16[224,2048]{1,0:T(8,128)(2,1)} %get-tuple-element.144), channel_id=1, source_target_pairs={{0,1},{1,0},{2,3},{3,2},{4,5},{5,4},{6,7},{7,6},{8,9},{9,8},{10,11... | collective-permute-start | bytes 2752520 | tf_op jit(solution)/shard_map/ppermute | solution.py:186
  584.3 54.6 %collective-permute-start.26 = (bf16[224,2048]{1,0:T(8,128)(2,1)}, bf16[224,2048]{1,0:T(8,128)(2,1)}, u32[]{:S(2)}, u32[]{:S(2)}) collective-permute-start(bf16[224,2048]{1,0:T(8,128)(2,1)} %get-tuple-element.145), channel_id=1, source_target_pairs={{0,2},{1,3},{2,0},{3,1},{4,6},{5,7},{6,4},{7,5},{8,10},{9,11},{10,... | collective-permute-start | bytes 2752520 | tf_op jit(solution)/shard_map/ppermute | solution.py:186
  585.8 53.1 %collective-permute-start.27 = (bf16[224,2048]{1,0:T(8,128)(2,1)}, bf16[224,2048]{1,0:T(8,128)(2,1)}, u32[]{:S(2)}, u32[]{:S(2)}) collective-permute-start(bf16[224,2048]{1,0:T(8,128)(2,1)} %get-tuple-element.146), channel_id=1, source_target_pairs={{0,3},{1,2},{2,1},{3,0},{4,7},{5,6},{6,5},{7,4},{8,11},{9,10},{10,... | collective-permute-start | bytes 2752520 | tf_op jit(solution)/shard_map/ppermute | solution.py:186
  605.0 33.9 %collective-permute-start.29 = (bf16[1008,256]{1,0:T(8,128)(2,1)S(1)}, bf16[1008,256]{1,0:T(8,128)(2,1)S(1)}, u32[]{:S(2)}, u32[]{:S(2)}) collective-permute-start(bf16[1008,256]{1,0:T(8,128)(2,1)S(1)} %copy-done.27), channel_id=1, source_target_pairs={{0,16},{4,20},{8,24},{12,28},{16,0},{20,4},{24,8},{28,12},{1,17},{... | collective-permute-start | bytes 1548296 | tf_op jit(solution)/shard_map/ppermute | solution.py:186
  605.8 33.0 %collective-permute-start.30 = (bf16[1008,256]{1,0:T(8,128)(2,1)S(1)}, bf16[1008,256]{1,0:T(8,128)(2,1)S(1)}, u32[]{:S(2)}, u32[]{:S(2)}) collective-permute-start(bf16[1008,256]{1,0:T(8,128)(2,1)S(1)} %copy-done.26), channel_id=1, source_target_pairs={{0,24},{4,28},{8,16},{12,20},{16,8},{20,12},{24,0},{28,4},{1,25},{... | collective-permute-start | bytes 1548296 | tf_op jit(solution)/shard_map/ppermute | solution.py:186
  647.5 61.6 %collective-permute-start.38 = (bf16[224,512]{1,0:T(8,128)(2,1)}, bf16[224,512]{1,0:T(8,128)(2,1)}, u32[]{:S(2)}, u32[]{:S(2)}) collective-permute-start(bf16[224,512]{1,0:T(8,128)(2,1)} %get-tuple-element.172), channel_id=1, source_target_pairs={{0,1},{1,0},{2,3},{3,2},{4,5},{5,4},{6,7},{7,6},{8,9},{9,8},{10,11... | collective-permute-start | bytes 688136 | tf_op jit(solution)/shard_map/ppermute | solution.py:186
  649.0 61.1 %collective-permute-start.39 = (bf16[224,512]{1,0:T(8,128)(2,1)}, bf16[224,512]{1,0:T(8,128)(2,1)}, u32[]{:S(2)}, u32[]{:S(2)}) collective-permute-start(bf16[224,512]{1,0:T(8,128)(2,1)} %get-tuple-element.173), channel_id=1, source_target_pairs={{0,2},{1,3},{2,0},{3,1},{4,6},{5,7},{6,4},{7,5},{8,10},{9,11},{10,... | collective-permute-start | bytes 688136 | tf_op jit(solution)/shard_map/ppermute | solution.py:186
  662.1 46.7 %collective-permute-start.36 = (bf16[224,2048]{1,0:T(8,128)(2,1)}, bf16[224,2048]{1,0:T(8,128)(2,1)S(1)}, u32[]{:S(2)}, u32[]{:S(2)}) collective-permute-start(bf16[224,2048]{1,0:T(8,128)(2,1)} %get-tuple-element.165), channel_id=1, source_target_pairs={{0,2},{1,3},{2,0},{3,1},{4,6},{5,7},{6,4},{7,5},{8,10},{9,11},{10,... | collective-permute-start | bytes 2752520 | tf_op jit(solution)/shard_map/ppermute | solution.py:186
  664.0 44.9 %collective-permute-start.37 = (bf16[224,2048]{1,0:T(8,128)(2,1)}, bf16[224,2048]{1,0:T(8,128)(2,1)S(1)}, u32[]{:S(2)}, u32[]{:S(2)}) collective-permute-start(bf16[224,2048]{1,0:T(8,128)(2,1)} %get-tuple-element.166), channel_id=1, source_target_pairs={{0,3},{1,2},{2,1},{3,0},{4,7},{5,6},{6,5},{7,4},{8,11},{9,10},{10,... | collective-permute-start | bytes 2752520 | tf_op jit(solution)/shard_map/ppermute | solution.py:186
  683.7 27.4 %collective-permute-start.40 = (bf16[224,512]{1,0:T(8,128)(2,1)}, bf16[224,512]{1,0:T(8,128)(2,1)S(1)}, u32[]{:S(2)}, u32[]{:S(2)}) collective-permute-start(bf16[224,512]{1,0:T(8,128)(2,1)} %get-tuple-element.174), channel_id=1, source_target_pairs={{0,3},{1,2},{2,1},{3,0},{4,7},{5,6},{6,5},{7,4},{8,11},{9,10},{10,... | collective-permute-start | bytes 688136 | tf_op jit(solution)/shard_map/ppermute | solution.py:186
  (51 other events, 1038.6 us)
Sparse Core Ops, SparseCore 0:
  235.3 260.6 all-reduce.1

commit v4 on v3

--- a/solution.py
+++ b/solution.py
@@ -495,57 +495,178 @@
     )
 
 
-def chunk_gram_kernel(rows_ref, cols_ref, meta_ref, *refs):
-    matrices, out_ref, joined = refs[:-2], refs[-2], refs[-1]
+def collect_kernel(meta_ref, *refs):
+    matrices, joined = refs[:-1], refs[-1]
+    place = 0
+    for matrix in matrices[:-1]:
+        joined[:, place : place + matrix.shape[1]] = matrix[...]
+        place += matrix.shape[1]
+    lane = lax.broadcasted_iota(jnp.int32, (TILE, LAST), 1)
+    own = lane // (LAST // 2) == meta_ref[0] % 2
+
+    @pl.loop(0, BLOCKS)
+    def _(b):
+        block = matrices[-1][tile_rows(b), :].astype(jnp.float32)
+        joined[tile_rows(b), place:] = jnp.where(own, block, 0.0).astype(jnp.bfloat16)
+
+
+def collect(meta, chunks):
+    width = sum(x.shape[1] for x in chunks)
+    return local_call(
+        collect_kernel,
+        jax.ShapeDtypeStruct((M, width), jnp.bfloat16),
+        (meta, *chunks),
+        4 * M * width,
+    )
+
+
+PIECES = 2
+HALF = len(PAIRS) // 2
+PART = HALF // PIECES
+
+
+def half_gram_kernel(flip, rows_ref, cols_ref, meta_ref, joined, *outs):
     turn = pl.program_id(0)
-
-    @pl.when(turn == 0)
-    def _():
-        place = 0
-        for matrix in matrices[:-1]:
-            joined[:, place : place + matrix.shape[1]] = matrix[...]
-            place += matrix.shape[1]
-        lane = lax.broadcasted_iota(jnp.int32, (TILE, LAST), 1)
-        own = lane // (LAST // 2) == meta_ref[0] % 2
-
-        @pl.loop(0, BLOCKS)
-        def _(b):
-            part = pl.ds(pl.multiple_of(b * TILE, TILE), TILE)
-            block = matrices[-1][part, :].astype(jnp.float32)
-            joined[part, place:] = jnp.where(own, block, 0.0).astype(jnp.bfloat16)
-
-    here = pl.ds(pl.multiple_of(rows_ref[turn] * TILE, TILE), TILE)
-    there = pl.ds(pl.multiple_of(cols_ref[turn] * TILE, TILE), TILE)
-    out_ref[...] = lax.dot_general(
+    pair = (meta_ref[0] % 2 ^ flip) * HALF + turn
+    here = pl.ds(pl.multiple_of(rows_ref[pair] * TILE, TILE), TILE)
+    there = pl.ds(pl.multiple_of(cols_ref[pair] * TILE, TILE), TILE)
+    tile = lax.dot_general(
         joined[here, :],
         joined[there, :],
         (((1,), (1,)), ((), ())),
         preferred_element_type=jnp.float32,
     ).astype(jnp.bfloat16)
-
-
-def chunk_gram(meta, chunks):
-    count = len(PAIRS)
-    width = sum(x.shape[1] for x in chunks)
+    for n, out in enumerate(outs):
+
+        @pl.when(turn // PART == n)
+        def _():
+            out[...] = tile
+
+
+def half_gram(meta, joined, flip):
+    width = joined.shape[1]
+    place = lambda n: lambda p, rows, cols, meta: (jnp.clip(p - n * PART, 0, PART - 1), 0)
     return pl.pallas_call(
-        chunk_gram_kernel,
-        out_shape=jax.ShapeDtypeStruct((count * TILE, TILE), jnp.bfloat16),
+        lambda *refs: half_gram_kernel(flip, *refs),
+        out_shape=[jax.ShapeDtypeStruct((PART * TILE, TILE), jnp.bfloat16)] * PIECES,
         grid_spec=pltpu.PrefetchScalarGridSpec(
             num_scalar_prefetch=3,
-            grid=(count,),
-            in_specs=[
-                pl.BlockSpec((M, x.shape[1]), lambda p, rows, cols, meta: (0, 0)) for x in chunks
-            ],
-            out_specs=pl.BlockSpec((TILE, TILE), lambda p, rows, cols, meta: (p, 0)),
-            scratch_shapes=[pltpu.VMEM((M, width), jnp.bfloat16)],
+            grid=(HALF,),
+            in_specs=[pl.BlockSpec((M, width), lambda p, rows, cols, meta: (0, 0))],
+            out_specs=[pl.BlockSpec((TILE, TILE), place(n)) for n in range(PIECES)],
         ),
         compiler_params=pltpu.CompilerParams(vmem_limit_bytes=VMEM_LIMIT),
         cost_estimate=pl.CostEstimate(
-            flops=2 * count * TILE * TILE * width,
-            bytes_accessed=2 * count * TILE * TILE + 2 * M * width,
+            flops=2 * HALF * TILE * TILE * width,
+            bytes_accessed=2 * HALF * TILE * TILE + 2 * M * width,
             transcendentals=0,
         ),
-    )(jnp.asarray(PAIR_ROWS), jnp.asarray(PAIR_COLS), meta, *chunks)
+    )(jnp.asarray(PAIR_ROWS), jnp.asarray(PAIR_COLS), meta, joined)
+
+
+def lane_block(block, lanes):
+    return pl.ds(pl.multiple_of(block * lanes, lanes), lanes)
+
+
+def add_halves_kernel(meta_ref, keep, got, *outs):
+    lanes = outs[0].shape[1]
+    for k, out in enumerate(outs):
+        part = lane_block(meta_ref[1] ^ k, lanes)
+        out[...] = (keep[:, part].astype(jnp.float32) + got[:, part].astype(jnp.float32)).astype(
+            jnp.bfloat16
+        )
+
+
+def gridded(kernel, meta, operands, outs, moved):
+    rows = operands[0].shape[0]
+    block = lambda x: pl.BlockSpec((TILE, x.shape[1]), lambda t, meta: (t, 0))
+    return pl.pallas_call(
+        kernel,
+        out_shape=outs,
+        grid_spec=pltpu.PrefetchScalarGridSpec(
+            num_scalar_prefetch=1,
+            grid=(rows // TILE,),
+            in_specs=[block(x) for x in operands],
+            out_specs=jax.tree.map(block, outs),
+        ),
+        compiler_params=pltpu.CompilerParams(vmem_limit_bytes=VMEM_LIMIT),
+        cost_estimate=pl.CostEstimate(flops=moved, bytes_accessed=moved, transcendentals=0),
+    )(meta, *operands)
+
+
+def add_halves(meta, keep, got, col_count):
+    rows, lanes = keep.shape
+    shape = jax.ShapeDtypeStruct((rows, lanes // col_count), jnp.bfloat16)
+    return gridded(add_halves_kernel, meta, (keep, got), [shape] * col_count, 6 * rows * lanes)
+
+
+def total_of(refs, part):
+    total = refs[0][part, :].astype(jnp.float32)
+    for ref in refs[1:]:
+        total += ref[part, :].astype(jnp.float32)
+    return total.astype(jnp.bfloat16)
+
+
+def add_quarters_kernel(col_count, meta_ref, *refs):
+    blocks, outs = refs[:col_count], refs[col_count:]
+    rows = outs[0].shape[0]
+    for q, out in enumerate(outs):
+        place = (meta_ref[0] // 2 ^ q) * rows
+        out[...] = total_of(blocks, pl.ds(pl.multiple_of(place, rows), rows))
+
+
+def add_quarters(meta, blocks, pair_count):
+    rows, lanes = blocks[0].shape
+    shape = jax.ShapeDtypeStruct((rows // pair_count, lanes), jnp.bfloat16)
+    return local_call(
+        lambda *refs: add_quarters_kernel(len(blocks), *refs),
+        [shape] * pair_count,
+        (meta, *blocks),
+        10 * rows * lanes,
+    )
+
+
+def add_parts_kernel(meta_ref, *refs):
+    rows = refs[-1].shape[0]
+    refs[-1][...] = total_of(refs[:-1], pl.ds(0, rows))
+
+
+def add_parts(meta, parts):
+    return local_call(
+        add_parts_kernel,
+        jax.ShapeDtypeStruct(parts[0].shape, jnp.bfloat16),
+        (meta, *parts),
+        10 * parts[0].size,
+    )
+
+
+def stack_kernel(meta_ref, *refs):
+    parts, out = refs[:-1], refs[-1]
+    rows = parts[0].shape[0]
+    for q, part in enumerate(parts):
+        out[pl.ds(pl.multiple_of((meta_ref[0] // 2 ^ q) * rows, rows), rows), :] = part[...]
+
+
+def stack(meta, parts):
+    rows, lanes = parts[0].shape
+    return local_call(
+        stack_kernel,
+        jax.ShapeDtypeStruct((rows * len(parts), lanes), jnp.bfloat16),
+        (meta, *parts),
+        4 * rows * lanes * len(parts),
+    )
+
+
+def widen_kernel(meta_ref, *refs):
+    blocks, out = refs[:-1], refs[-1]
+    for k, block in enumerate(blocks):
+        out[:, lane_block(meta_ref[1] ^ k, block.shape[1])] = block[...]
+
+
+def widen(meta, blocks):
+    rows, lanes = blocks[0].shape
+    shape = jax.ShapeDtypeStruct((rows, lanes * len(blocks)), jnp.bfloat16)
+    return gridded(widen_kernel, meta, blocks, shape, 4 * rows * lanes * len(blocks))
 
 
 def tile_rows(b):
@@ -580,24 +701,30 @@
         out[...] = total[place, :].astype(jnp.bfloat16)
 
 
-def first_apply_kernel(jitter, send, meta_ref, tiles_ref, matrix, *refs):
-    outs, gram_out = refs[:-6], refs[-6]
+def first_apply_kernel(jitter, send, rows_ref, cols_ref, meta_ref, *refs):
+    pieces, matrix = refs[: 2 * PIECES], refs[2 * PIECES]
+    outs, gram_out = refs[2 * PIECES + 1 : -6], refs[-6]
     gram, total, factor, tile_sems, out_sem = refs[-5:]
     copies = []
-    for p, (i, j) in enumerate(PAIRS):
-        copies.append(
-            pltpu.make_async_copy(
-                tiles_ref.at[pl.ds(p * TILE, TILE), :],
-                gram.at[i, :, pl.ds(j * TILE, TILE)],
-                tile_sems.at[p],
-            )
+    for n in range(2 * HALF):
+        half, part = divmod(n, HALF)
+        pair = (meta_ref[0] % 2 ^ half) * HALF + part
+        i, j = rows_ref[pair], cols_ref[pair]
+        copy = pltpu.make_async_copy(
+            pieces[half * PIECES + part // PART].at[pl.ds(part % PART * TILE, TILE), :],
+            gram.at[i, :, lane_block(j, TILE)],
+            tile_sems.at[n],
         )
-        copies[-1].start()
+        copy.start()
+        copies.append((copy, i, j))
     clear_edges(total, jitter)
-    for p, (i, j) in enumerate(PAIRS):
-        copies[p].wait()
-        if i != j:
-            gram[j, :, pl.ds(i * TILE, TILE)] = gram[i, :, pl.ds(j * TILE, TILE)].T
+    for copy, i, j in copies:
+        copy.wait()
+
+        @pl.when(i != j)
+        def _():
+            gram[j, :, lane_block(i, TILE)] = gram[i, :, lane_block(j, TILE)].T
+
     back = pltpu.make_async_copy(gram, gram_out, out_sem)
     back.start()
 
@@ -613,18 +740,16 @@
     back.wait()
 
 
-def first_apply(meta, tiles, matrix, send, jitter):
+def first_apply(meta, pieces, matrix, send, jitter):
     width = matrix.shape[1]
     whole = pl.BlockSpec(memory_space=pltpu.VMEM)
     outs = pl.pallas_call(
         lambda *refs: first_apply_kernel(jitter, send, *refs),
         out_shape=[jax.ShapeDtypeStruct((send[2], width), jnp.bfloat16)] * len(send[3])
         + [jax.ShapeDtypeStruct((BLOCKS, TILE, M), jnp.bfloat16)],
-        in_specs=[
-            pl.BlockSpec(memory_space=pltpu.SMEM),
-            pl.BlockSpec(memory_space=pl.ANY),
-            whole,
-        ],
+        in_specs=[pl.BlockSpec(memory_space=pltpu.SMEM)] * 3
+        + [pl.BlockSpec(memory_space=pl.ANY)] * len(pieces)
+        + [whole],
         out_specs=[whole] * len(send[3]) + [pl.BlockSpec(memory_space=pl.ANY)],
         scratch_shapes=[
             pltpu.VMEM((BLOCKS, TILE, M), jnp.bfloat16),
@@ -637,7 +762,7 @@
         cost_estimate=pl.CostEstimate(
             flops=4 * M * M * width, bytes_accessed=4 * M * width + 4 * M * M, transcendentals=0
         ),
-    )(meta, tiles, matrix)
+    )(jnp.asarray(PAIR_ROWS), jnp.asarray(PAIR_COLS), meta, *pieces, matrix)
     return outs[:-1], outs[-1]
 
 
@@ -699,8 +824,45 @@
     return result
 
 
-def reduce_tiles(tiles):
-    return lax.psum(tiles, ("row", "col"))
+def sum_tiles(meta, joined, row_count, col_count):
+    pair_count = row_count // 2
+    tie = lax.optimization_barrier
+
+    def over_cols(blocks):
+        return [swap(blocks[k], "col", col_count, k) for k in range(1, col_count)]
+
+    def over_pairs(blocks):
+        return [swap(blocks[q], "row", row_count, 2 * q) for q in range(1, pair_count)]
+
+    give = half_gram(meta, joined, 1)
+    got = [swap(piece, "row", row_count, 1) for piece in give]
+    keep = half_gram(meta, joined, 0)
+
+    early = add_halves(meta, keep[0], got[0], col_count)
+    early_in = over_cols(early)
+    late = add_halves(meta, keep[1], got[1], col_count)
+    late, early_in = tie((late, early_in))
+    late_in = over_cols(late)
+    early_parts = add_quarters(meta, [early[0]] + early_in, pair_count)
+    early_in = over_pairs(early_parts)
+    late_in, early_in = tie((late_in, early_in))
+    early_part = add_parts(meta, [early_parts[0]] + early_in)
+    early_in = over_pairs([early_part] * pair_count)
+    late_parts = add_quarters(meta, [late[0]] + late_in, pair_count)
+    late_parts, early_in = tie((late_parts, early_in))
+    early_block = stack(meta, [early_part] + early_in)
+    early_in = over_cols([early_block] * col_count)
+    late_in = over_pairs(late_parts)
+    late_part = add_parts(meta, [late_parts[0]] + late_in)
+    late_in = over_pairs([late_part] * pair_count)
+    late_in, early_in = tie((late_in, early_in))
+    late_block = stack(meta, [late_part] + late_in)
+    late_in = over_cols([late_block] * col_count)
+    early = widen(meta, [early_block] + early_in)
+    early_twin = swap(early, "row", row_count, 1)
+    late = widen(meta, [late_block] + late_in)
+    late_twin = swap(late, "row", row_count, 1)
+    return [early, late, early_twin, late_twin]
 
 
 def chunk_body(momentum_shards, shard_starts):
@@ -778,7 +940,7 @@
         )
     )
 
-    tiles = reduce_tiles(chunk_gram(meta, matrices))
+    tiles = sum_tiles(meta, collect(meta, matrices), row_count, col_count)
 
     sends = [(2 * even, 2, even + window, distances)] * number
     sends.append((even, 1, window, [2 * q for q in distances]))

time: 732 us -> 711 us (0.971)
  waiting for transfers between devices: 462 us -> 330 us
  starting transfers between devices: 65.1 us -> 125 us
  Pallas kernels: 150 us -> 205 us
  between operations: 13.8 us -> 0.54 us
  local copies, waits for them, and re-layouts: 30.3 us -> 39.5 us
    psum x1 -> x0, waiting for transfers between devices: 261 us -> none  [reduce_tiles(): return lax.psum(tiles, ('row', 'col'))]
    ppermute x41 -> x69, waiting for transfers between devices: 201 us -> 330 us  [swap(): lax.ppermute(value, axis, perm=[(i, i ^ distance) for i in range(size)])]
    ppermute x41 -> x69, starting transfers between devices: 65.1 us -> 125 us  [swap(): lax.ppermute(value, axis, perm=[(i, i ^ distance) for i in range(size)])]
    pallas_call x1 -> x6, Pallas kernels: 23.8 us -> 57.4 us  [the longest x4 29 us: gridded(): pl.pallas_call(kernel, out_shape=outs, grid_spec=pltpu.PrefetchScalarGrid...]
    pallas_call x7 -> x14, Pallas kernels: 21.5 us -> 42.5 us  [local_call(): pl.pallas_call(kernel, out_shape=out_shape, in_specs=[pl.BlockSpec(memory...]
    unnamed x69 -> x123, local copies, waits for them, and re-layouts: 13.4 us -> 22.6 us
  transfers between devices with their start and end apart: 42 -> 69, of which waited for: 19 -> 33; matrix products, arithmetic and copies ran while one was open for 2% -> 2% of each run, Pallas kernels for 10% -> 19%
where the time goes in v4:
time: 711 us; the launch traced here: 701 us
  waiting for transfers between devices  330 us (46%)
  Pallas kernels  205 us (29%)
  starting transfers between devices  125 us (18%)
  local copies, waits for them, and re-layouts  39.5 us (6%)
    ppermute x69, waiting for transfers between devices, swap(): lax.ppermute(value, axis, perm=[(i, i ^ distance) for i in range(size)])  330 us
    ppermute x69, starting transfers between devices, swap(): lax.ppermute(value, axis, perm=[(i, i ^ distance) for i in range(size)])  125 us
    pallas_call x14, Pallas kernels, local_call(): pl.pallas_call(kernel, out_shape=out_shape, in_specs=[pl.BlockSpec(memory...  42.5 us
    pallas_call x1, Pallas kernels, next_apply(): pl.pallas_call(lambda *refs: next_apply_kernel(jitter, sends, *refs), out...  35.1 us
    pallas_call x4, Pallas kernels, gridded(): pl.pallas_call(kernel, out_shape=outs, grid_spec=pltpu.PrefetchScalarGrid...  29 us
    pallas_call x2, Pallas kernels, half_gram(): pl.pallas_call(lambda *refs: half_gram_kernel(flip, *refs), out_shape=[ja...  28.3 us
    pallas_call x1, Pallas kernels, first_apply(): pl.pallas_call(lambda *refs: first_apply_kernel(jitter, send, *refs), out...  24.4 us
    unnamed x123, local copies, waits for them, and re-layouts  22.6 us
  transfers between devices with their start and end apart: 69, of which 33 were waited for; matrix products, arithmetic and copies ran while one was open for 2% of the time, Pallas kernels for 19%

profile of v4, /device:TPU:0, one launch (start us, length us, event | category | flops | bytes accessed | tf_op | source)
XLA Modules:
  0.0 700.6 jit_solution(9193633342616669908)
XLA Ops:
  9.9 16.4 %collective-permute-done.refs_2_ = bf16[224,2048]{1,0:T(8,128)(2,1)} collective-permute-done((bf16[224,2048]{1,0:T(8,128)(2,1)S(1)}, bf16[224,2048]{1,0:T(8,128)(2,1)}, u32[]{:S(2)}, u32[]{:S(2)}) %collective-permute-start) | collective-permute-done | bytes 917536 | tf_op jit(solution)/shard_map/ppermute | solution.py:186
  26.2 20.3 %collective-permute-done.1.refs_3_ = bf16[224,2048]{1,0:T(8,128)(2,1)} collective-permute-done((bf16[224,2048]{1,0:T(8,128)(2,1)S(1)}, bf16[224,2048]{1,0:T(8,128)(2,1)}, u32[]{:S(2)}, u32[]{:S(2)}) %collective-permute-start.1) | collective-permute-done | bytes 917536 | tf_op jit(solution)/shard_map/ppermute | solution.py:186
  80.3 10.2 %collective-permute-done.7.refs_2_ = bf16[1008,256]{1,0:T(8,128)(2,1)S(1)} collective-permute-done((bf16[1008,256]{1,0:T(8,128)(2,1)}, bf16[1008,256]{1,0:T(8,128)(2,1)S(1)}, u32[]{:S(2)}, u32[]{:S(2)}) %collective-permute-start.7) | collective-permute-done | bytes 516128 | tf_op jit(solution)/shard_map/ppermute | solution.py:186
  93.0 22.6 %collective-permute-done.8.refs_3_ = bf16[1008,256]{1,0:T(8,128)(2,1)S(1)} collective-permute-done((bf16[1008,256]{1,0:T(8,128)(2,1)}, bf16[1008,256]{1,0:T(8,128)(2,1)S(1)}, u32[]{:S(2)}, u32[]{:S(2)}) %collective-permute-start.8) | collective-permute-done | bytes 516128 | tf_op jit(solution)/shard_map/ppermute | solution.py:186
  132.0 9.1 %collective-permute-start.17 = (bf16[560,128]{1,0:T(8,128)(2,1)}, bf16[560,128]{1,0:T(8,128)(2,1)S(1)}, u32[]{:S(2)}, u32[]{:S(2)}) collective-permute-start(bf16[560,128]{1,0:T(8,128)(2,1)} %get-tuple-element.169), channel_id=1, source_target_pairs={{0,8},{4,12},{8,0},{12,4},{16,24},{20,28},{24,16},{28,20},{1,9},{5... | collective-permute-start | bytes 430088 | tf_op jit(solution)/shard_map/ppermute | solution.py:186
  172.1 13.5 %collective-permute-done.14.refs_2_ = bf16[1008,256]{1,0:T(8,128)(2,1)S(1)} collective-permute-done((bf16[1008,256]{1,0:T(8,128)(2,1)}, bf16[1008,256]{1,0:T(8,128)(2,1)S(1)}, u32[]{:S(2)}, u32[]{:S(2)}) %collective-permute-start.14) | collective-permute-done | bytes 516128 | tf_op jit(solution)/shard_map/ppermute | solution.py:186
  185.6 14.7 %collective-permute-done.15.refs_3_ = bf16[1008,256]{1,0:T(8,128)(2,1)S(1)} collective-permute-done((bf16[1008,256]{1,0:T(8,128)(2,1)}, bf16[1008,256]{1,0:T(8,128)(2,1)S(1)}, u32[]{:S(2)}, u32[]{:S(2)}) %collective-permute-start.15) | collective-permute-done | bytes 516128 | tf_op jit(solution)/shard_map/ppermute | solution.py:186
  209.8 14.2 %shard_map.56 = (bf16[3584,512]{1,0:T(8,128)(2,1)}, bf16[3584,512]{1,0:T(8,128)(2,1)}) custom-call(s32[28]{0:T(128)} %constant.61.clone.refs_0_, s32[28]{0:T(128)} %constant.62.clone.refs_1_, s32[10]{0:T(128)} %pad_add_fusion.1.refs_0_.meta_ref.refs_2_, bf16[3584,640]{1,0:T(8,128)(2,1)} %shard_map.54.refs_3_), custom_call_target="tpu_custom_call" | custom-call | flops 4697620480 | bytes 11927552 | tf_op jit(solution)/shard_map/pallas_call | solution.py:549
  224.5 14.1 %shard_map.55 = (bf16[3584,512]{1,0:T(8,128)(2,1)}, bf16[3584,512]{1,0:T(8,128)(2,1)}) custom-call(s32[28]{0:T(128)} %constant.61.clone.refs_0_, s32[28]{0:T(128)} %constant.62.clone.refs_1_, s32[10]{0:T(128)} %pad_add_fusion.1.refs_0_.meta_ref.refs_2_, bf16[3584,640]{1,0:T(8,128)(2,1)} %shard_map.54.refs_3_), custom_call_target="tpu_custom_call" | custom-call | flops 4697620480 | bytes 11927552 | tf_op jit(solution)/shard_map/pallas_call | solution.py:549
  261.0 10.5 %collective-permute-done.23.refs_2_ = bf16[3584,128]{1,0:T(8,128)(2,1)S(1)} collective-permute-done((bf16[3584,128]{1,0:T(8,128)(2,1)}, bf16[3584,128]{1,0:T(8,128)(2,1)S(1)}, u32[]{:S(2)}, u32[]{:S(2)}) %collective-permute-start.23) | collective-permute-done | bytes 917536 | tf_op jit(solution)/shard_map/ppermute | solution.py:186
  271.5 19.0 %collective-permute-done.24.refs_3_ = bf16[3584,128]{1,0:T(8,128)(2,1)S(1)} collective-permute-done((bf16[3584,128]{1,0:T(8,128)(2,1)}, bf16[3584,128]{1,0:T(8,128)(2,1)S(1)}, u32[]{:S(2)}, u32[]{:S(2)}) %collective-permute-start.24) | collective-permute-done | bytes 917536 | tf_op jit(solution)/shard_map/ppermute | solution.py:186
  297.4 10.7 %collective-permute-start.29 = (bf16[896,128]{1,0:T(8,128)(2,1)}, bf16[896,128]{1,0:T(8,128)(2,1)S(1)}, u32[]{:S(2)}, u32[]{:S(2)}) collective-permute-start(bf16[896,128]{1,0:T(8,128)(2,1)} %get-tuple-element.191), channel_id=1, source_target_pairs={{0,8},{4,12},{8,0},{12,4},{16,24},{20,28},{24,16},{28,20},{1,9},{5... | collective-permute-start | bytes 688136 | tf_op jit(solution)/shard_map/ppermute | solution.py:186
  334.9 10.7 %collective-permute-start.32 = (bf16[896,128]{1,0:T(8,128)(2,1)}, bf16[896,128]{1,0:T(8,128)(2,1)S(1)}, u32[]{:S(2)}, u32[]{:S(2)}) collective-permute-start(bf16[896,128]{1,0:T(8,128)(2,1)} %shard_map.60.refs_0_), channel_id=1, source_target_pairs={{0,8},{4,12},{8,0},{12,4},{16,24},{20,28},{24,16},{28,20},{1,9},{5... | collective-permute-start | bytes 688136 | tf_op jit(solution)/shard_map/ppermute | solution.py:186
  352.7 11.7 %collective-permute-done.33.refs_2_ = bf16[896,128]{1,0:T(8,128)(2,1)S(1)} collective-permute-done((bf16[896,128]{1,0:T(8,128)(2,1)}, bf16[896,128]{1,0:T(8,128)(2,1)S(1)}, u32[]{:S(2)}, u32[]{:S(2)}) %collective-permute-start.33) | collective-permute-done | bytes 229408 | tf_op jit(solution)/shard_map/ppermute | solution.py:186
  376.2 12.7 %collective-permute-done.36.refs_2_ = bf16[896,128]{1,0:T(8,128)(2,1)S(1)} collective-permute-done((bf16[896,128]{1,0:T(8,128)(2,1)}, bf16[896,128]{1,0:T(8,128)(2,1)S(1)}, u32[]{:S(2)}, u32[]{:S(2)}) %collective-permute-start.36) | collective-permute-done | bytes 229408 | tf_op jit(solution)/shard_map/ppermute | solution.py:186
  428.7 13.1 %collective-permute-done.44.refs_1_ = bf16[3584,128]{1,0:T(8,128)(2,1)S(1)} collective-permute-done((bf16[3584,128]{1,0:T(8,128)(2,1)}, bf16[3584,128]{1,0:T(8,128)(2,1)S(1)}, u32[]{:S(2)}, u32[]{:S(2)}) %collective-permute-start.44) | collective-permute-done | bytes 917536 | tf_op jit(solution)/shard_map/ppermute | solution.py:186
  441.8 16.5 %collective-permute-done.45.refs_2_ = bf16[3584,128]{1,0:T(8,128)(2,1)S(1)} collective-permute-done((bf16[3584,128]{1,0:T(8,128)(2,1)}, bf16[3584,128]{1,0:T(8,128)(2,1)S(1)}, u32[]{:S(2)}, u32[]{:S(2)}) %collective-permute-start.45) | collective-permute-done | bytes 917536 | tf_op jit(solution)/shard_map/ppermute | solution.py:186
  475.6 24.4 %shard_map.67 = (bf16[1008,256]{1,0:T(8,128)(2,1)}, bf16[1008,256]{1,0:T(8,128)(2,1)}, bf16[1008,256]{1,0:T(8,128)(2,1)}, bf16[1008,256]{1,0:T(8,128)(2,1)}, bf16[7,512,3584]{2,1,0:T(8,128)(2,1)}) custom-call(s32[28]{0:T(128)} %constant.61.clone.refs_0_, s32[28]{0:T(128)} %constant.62.clone.refs_1_, s32[10]{0:T(128)} %pad_add_fusion.1.refs_0_.meta_ref.refs_2_, ...), custom_call_target="tpu_custom_call" | custom-call | flops 13153337344 | bytes 55050240 | tf_op jit(solution)/shard_map/pallas_call | solution.py:746
  509.7 35.1 %shard_map.68 = (bf16[1008,256]{1,0:T(8,128)(2,1)}, bf16[1008,256]{1,0:T(8,128)(2,1)}, bf16[1008,256]{1,0:T(8,128)(2,1)}, bf16[1008,256]{1,0:T(8,128)(2,1)}, bf1...) custom-call(s32[10]{0:T(128)} %pad_add_fusion.1.refs_0_.meta_ref.refs_2_,, ...), custom_call_target="tpu_custom_call" | custom-call | flops 19730006016 | bytes 56885248 | tf_op jit(solution)/shard_map/pallas_call | solution.py:801
  548.7 10.6 %collective-permute-start.56 = (bf16[1008,256]{1,0:T(8,128)(2,1)}, bf16[1008,256]{1,0:T(8,128)(2,1)S(1)}, u32[]{:S(2)}, u32[]{:S(2)}) collective-permute-start(bf16[1008,256]{1,0:T(8,128)(2,1)} %get-tuple-element.240), channel_id=1, source_target_pairs={{0,8},{4,12},{8,0},{12,4},{16,24},{20,28},{24,16},{28,20},{1,9},{5... | collective-permute-start | bytes 1548296 | tf_op jit(solution)/shard_map/ppermute | solution.py:186
  593.2 32.0 %collective-permute-done.57.refs_3_ = bf16[1008,256]{1,0:T(8,128)(2,1)S(1)} collective-permute-done((bf16[1008,256]{1,0:T(8,128)(2,1)S(1)}, bf16[1008,256]{1,0:T(8,128)(2,1)S(1)}, u32[]{:S(2)}, u32[]{:S(2)}) %collective-permute-start.57) | collective-permute-done | bytes 516128 | tf_op jit(solution)/shard_map/ppermute | solution.py:186
  636.8 9.0 %shard_map.72 = (bf16[224,2048]{1,0:T(8,128)(2,1)}, bf16[224,2048]{1,0:T(8,128)(2,1)}, bf16[224,2048]{1,0:T(8,128)(2,1)}, bf16[224,2048]{1,0:T(8,128)(2,1)}) custom-call(s32[10]{0:T(128)} %pad_add_fusion.1.refs_0_.meta_ref.refs_2_, bf16[1008,256]{1,0:T(8,128)(2,1)} %get-tuple-element.251.refs_1_, bf16[1008,256]{1,0:T(8,128)(2,1)} %copy-done.29, ...), custom_call_target="tpu_custom_call" | custom-call | flops 2055208960 | bytes 5963776 | tf_op jit(solution)/shard_map/pallas_call | solution.py:405
  654.6 14.6 %collective-permute-done.63 = bf16[224,2048]{1,0:T(8,128)(2,1)S(1)} collective-permute-done((bf16[224,2048]{1,0:T(8,128)(2,1)}, bf16[224,2048]{1,0:T(8,128)(2,1)S(1)}, u32[]{:S(2)}, u32[]{:S(2)}) %collective-permute-start.63) | collective-permute-done | bytes 917536 | tf_op jit(solution)/shard_map/ppermute | solution.py:186
  670.8 23.5 %collective-permute-done.64 = bf16[224,2048]{1,0:T(8,128)(2,1)S(1)} collective-permute-done((bf16[224,2048]{1,0:T(8,128)(2,1)}, bf16[224,2048]{1,0:T(8,128)(2,1)S(1)}, u32[]{:S(2)}, u32[]{:S(2)}) %collective-permute-start.64) | collective-permute-done | bytes 917536 | tf_op jit(solution)/shard_map/ppermute | solution.py:186
  (290 shorter events, 310.9 us)
Async XLA Ops:
  4.9 41.6 %collective-permute-start.1 = (bf16[224,2048]{1,0:T(8,128)(2,1)S(1)}, bf16[224,2048]{1,0:T(8,128)(2,1)}, u32[]{:S(2)}, u32[]{:S(2)}) collective-permute-start(bf16[224,2048]{1,0:T(8,128)(2,1)S(1)} %get-tuple-element.274), channel_id=1, source_target_pairs={{0,2},{1,3},{2,0},{3,1},{4,6},{5,7},{6,4},{7,5},{8,10},{9,11},{10,... | collective-permute-start | bytes 2752520 | tf_op jit(solution)/shard_map/ppermute | solution.py:186
  6.5 40.1 %collective-permute-start.2 = (bf16[224,2048]{1,0:T(8,128)(2,1)S(1)}, bf16[224,2048]{1,0:T(8,128)(2,1)}, u32[]{:S(2)}, u32[]{:S(2)}) collective-permute-start(bf16[224,2048]{1,0:T(8,128)(2,1)S(1)} %get-tuple-element.273), channel_id=1, source_target_pairs={{0,3},{1,2},{2,1},{3,0},{4,7},{5,6},{6,5},{7,4},{8,11},{9,10},{10,... | collective-permute-start | bytes 2752520 | tf_op jit(solution)/shard_map/ppermute | solution.py:186
  74.1 41.5 %collective-permute-start.10 = (bf16[224,2048]{1,0:T(8,128)(2,1)S(1)}, bf16[224,2048]{1,0:T(8,128)(2,1)S(1)}, u32[]{:S(2)}, u32[]{:S(2)}) collective-permute-start(bf16[224,2048]{1,0:T(8,128)(2,1)S(1)} %get-tuple-element.269), channel_id=1, source_target_pairs={{0,1},{1,0},{2,3},{3,2},{4,5},{5,4},{6,7},{7,6},{8,9},{9,8},{10,11... | collective-permute-start | bytes 2752520 | tf_op jit(solution)/shard_map/ppermute | solution.py:186
  75.0 40.8 %collective-permute-start.11 = (bf16[224,2048]{1,0:T(8,128)(2,1)S(1)}, bf16[224,2048]{1,0:T(8,128)(2,1)S(1)}, u32[]{:S(2)}, u32[]{:S(2)}) collective-permute-start(bf16[224,2048]{1,0:T(8,128)(2,1)S(1)} %get-tuple-element.268), channel_id=1, source_target_pairs={{0,2},{1,3},{2,0},{3,1},{4,6},{5,7},{6,4},{7,5},{8,10},{9,11},{10,... | collective-permute-start | bytes 2752520 | tf_op jit(solution)/shard_map/ppermute | solution.py:186
  76.6 39.3 %collective-permute-start.12 = (bf16[224,2048]{1,0:T(8,128)(2,1)S(1)}, bf16[224,2048]{1,0:T(8,128)(2,1)S(1)}, u32[]{:S(2)}, u32[]{:S(2)}) collective-permute-start(bf16[224,2048]{1,0:T(8,128)(2,1)S(1)} %get-tuple-element.267), channel_id=1, source_target_pairs={{0,3},{1,2},{2,1},{3,0},{4,7},{5,6},{6,5},{7,4},{8,11},{9,10},{10,... | collective-permute-start | bytes 2752520 | tf_op jit(solution)/shard_map/ppermute | solution.py:186
  248.7 41.8 %collective-permute-start.24 = (bf16[3584,128]{1,0:T(8,128)(2,1)}, bf16[3584,128]{1,0:T(8,128)(2,1)S(1)}, u32[]{:S(2)}, u32[]{:S(2)}) collective-permute-start(bf16[3584,128]{1,0:T(8,128)(2,1)} %get-tuple-element.182), channel_id=1, source_target_pairs={{0,2},{1,3},{2,0},{3,1},{4,6},{5,7},{6,4},{7,5},{8,10},{9,11},{10,... | collective-permute-start | bytes 2752520 | tf_op jit(solution)/shard_map/ppermute | solution.py:186
  249.9 40.6 %collective-permute-start.25 = (bf16[3584,128]{1,0:T(8,128)(2,1)}, bf16[3584,128]{1,0:T(8,128)(2,1)S(1)}, u32[]{:S(2)}, u32[]{:S(2)}) collective-permute-start(bf16[3584,128]{1,0:T(8,128)(2,1)} %get-tuple-element.183), channel_id=1, source_target_pairs={{0,3},{1,2},{2,1},{3,0},{4,7},{5,6},{6,5},{7,4},{8,11},{9,10},{10,... | collective-permute-start | bytes 2752520 | tf_op jit(solution)/shard_map/ppermute | solution.py:186
  292.0 38.9 %collective-permute-start.27 = (bf16[3584,128]{1,0:T(8,128)(2,1)}, bf16[3584,128]{1,0:T(8,128)(2,1)S(1)}, u32[]{:S(2)}, u32[]{:S(2)}) collective-permute-start(bf16[3584,128]{1,0:T(8,128)(2,1)} %get-tuple-element.189), channel_id=1, source_target_pairs={{0,2},{1,3},{2,0},{3,1},{4,6},{5,7},{6,4},{7,5},{8,10},{9,11},{10,... | collective-permute-start | bytes 2752520 | tf_op jit(solution)/shard_map/ppermute | solution.py:186
  292.6 39.9 %collective-permute-start.28 = (bf16[3584,128]{1,0:T(8,128)(2,1)}, bf16[3584,128]{1,0:T(8,128)(2,1)S(1)}, u32[]{:S(2)}, u32[]{:S(2)}) collective-permute-start(bf16[3584,128]{1,0:T(8,128)(2,1)} %get-tuple-element.190), channel_id=1, source_target_pairs={{0,3},{1,2},{2,1},{3,0},{4,7},{5,6},{6,5},{7,4},{8,11},{9,10},{10,... | collective-permute-start | bytes 2752520 | tf_op jit(solution)/shard_map/ppermute | solution.py:186
  369.7 45.3 %collective-permute-start.41 = (bf16[3584,128]{1,0:T(8,128)(2,1)}, bf16[3584,128]{1,0:T(8,128)(2,1)S(1)}, u32[]{:S(2)}, u32[]{:S(2)}) collective-permute-start(bf16[3584,128]{1,0:T(8,128)(2,1)} %shard_map.62.refs_0_), channel_id=1, source_target_pairs={{0,1},{1,0},{2,3},{3,2},{4,5},{5,4},{6,7},{7,6},{8,9},{9,8},{10,11... | collective-permute-start | bytes 2752520 | tf_op jit(solution)/shard_map/ppermute | solution.py:186
  370.1 44.9 %collective-permute-start.42 = (bf16[3584,128]{1,0:T(8,128)(2,1)}, bf16[3584,128]{1,0:T(8,128)(2,1)S(1)}, u32[]{:S(2)}, u32[]{:S(2)}) collective-permute-start(bf16[3584,128]{1,0:T(8,128)(2,1)} %shard_map.62.refs_0_), channel_id=1, source_target_pairs={{0,2},{1,3},{2,0},{3,1},{4,6},{5,7},{6,4},{7,5},{8,10},{9,11},{10,... | collective-permute-start | bytes 2752520 | tf_op jit(solution)/shard_map/ppermute | solution.py:186
  371.0 44.0 %collective-permute-start.43 = (bf16[3584,128]{1,0:T(8,128)(2,1)}, bf16[3584,128]{1,0:T(8,128)(2,1)S(1)}, u32[]{:S(2)}, u32[]{:S(2)}) collective-permute-start(bf16[3584,128]{1,0:T(8,128)(2,1)} %shard_map.62.refs_0_), channel_id=1, source_target_pairs={{0,3},{1,2},{2,1},{3,0},{4,7},{5,6},{6,5},{7,4},{8,11},{9,10},{10,... | collective-permute-start | bytes 2752520 | tf_op jit(solution)/shard_map/ppermute | solution.py:186
  418.6 39.7 %collective-permute-start.45 = (bf16[3584,128]{1,0:T(8,128)(2,1)}, bf16[3584,128]{1,0:T(8,128)(2,1)S(1)}, u32[]{:S(2)}, u32[]{:S(2)}) collective-permute-start(bf16[3584,128]{1,0:T(8,128)(2,1)} %shard_map.65.refs_0_), channel_id=1, source_target_pairs={{0,2},{1,3},{2,0},{3,1},{4,6},{5,7},{6,4},{7,5},{8,10},{9,11},{10,... | collective-permute-start | bytes 2752520 | tf_op jit(solution)/shard_map/ppermute | solution.py:186
  419.7 38.7 %collective-permute-start.46 = (bf16[3584,128]{1,0:T(8,128)(2,1)}, bf16[3584,128]{1,0:T(8,128)(2,1)S(1)}, u32[]{:S(2)}, u32[]{:S(2)}) collective-permute-start(bf16[3584,128]{1,0:T(8,128)(2,1)} %shard_map.65.refs_0_), channel_id=1, source_target_pairs={{0,3},{1,2},{2,1},{3,0},{4,7},{5,6},{6,5},{7,4},{8,11},{9,10},{10,... | collective-permute-start | bytes 2752520 | tf_op jit(solution)/shard_map/ppermute | solution.py:186
  428.7 38.4 %collective-permute-start.47 = (bf16[3584,512]{1,0:T(8,128)(2,1)}, bf16[3584,512]{1,0:T(8,128)(2,1)}, u32[]{:S(2)}, u32[]{:S(2)}) collective-permute-start(bf16[3584,512]{1,0:T(8,128)(2,1)} %shard_map.64.refs_3_), channel_id=1, source_target_pairs={{0,4},{4,0},{8,12},{12,8},{16,20},{20,16},{24,28},{28,24},{1,5},{5... | collective-permute-start | bytes 11010056 | tf_op jit(solution)/shard_map/ppermute | solution.py:186
  500.0 44.8 %collective-permute-start.49 = (bf16[1008,256]{1,0:T(8,128)(2,1)}, bf16[1008,256]{1,0:T(8,128)(2,1)S(1)}, u32[]{:S(2)}, u32[]{:S(2)}) collective-permute-start(bf16[1008,256]{1,0:T(8,128)(2,1)} %get-tuple-element.219), channel_id=1, source_target_pairs={{0,8},{4,12},{8,0},{12,4},{16,24},{20,28},{24,16},{28,20},{1,9},{5... | collective-permute-start | bytes 1548296 | tf_op jit(solution)/shard_map/ppermute | solution.py:186
  548.7 43.9 %collective-permute-start.56 = (bf16[1008,256]{1,0:T(8,128)(2,1)}, bf16[1008,256]{1,0:T(8,128)(2,1)S(1)}, u32[]{:S(2)}, u32[]{:S(2)}) collective-permute-start(bf16[1008,256]{1,0:T(8,128)(2,1)} %get-tuple-element.240), channel_id=1, source_target_pairs={{0,8},{4,12},{8,0},{12,4},{16,24},{20,28},{24,16},{28,20},{1,9},{5... | collective-permute-start | bytes 1548296 | tf_op jit(solution)/shard_map/ppermute | solution.py:186
  569.3 55.9 %collective-permute-start.53 = (bf16[224,2048]{1,0:T(8,128)(2,1)}, bf16[224,2048]{1,0:T(8,128)(2,1)}, u32[]{:S(2)}, u32[]{:S(2)}) collective-permute-start(bf16[224,2048]{1,0:T(8,128)(2,1)} %get-tuple-element.236), channel_id=1, source_target_pairs={{0,1},{1,0},{2,3},{3,2},{4,5},{5,4},{6,7},{7,6},{8,9},{9,8},{10,11... | collective-permute-start | bytes 2752520 | tf_op jit(solution)/shard_map/ppermute | solution.py:186
  571.0 54.2 %collective-permute-start.54 = (bf16[224,2048]{1,0:T(8,128)(2,1)}, bf16[224,2048]{1,0:T(8,128)(2,1)}, u32[]{:S(2)}, u32[]{:S(2)}) collective-permute-start(bf16[224,2048]{1,0:T(8,128)(2,1)} %get-tuple-element.237), channel_id=1, source_target_pairs={{0,2},{1,3},{2,0},{3,1},{4,6},{5,7},{6,4},{7,5},{8,10},{9,11},{10,... | collective-permute-start | bytes 2752520 | tf_op jit(solution)/shard_map/ppermute | solution.py:186
  571.3 53.9 %collective-permute-start.55 = (bf16[224,2048]{1,0:T(8,128)(2,1)}, bf16[224,2048]{1,0:T(8,128)(2,1)}, u32[]{:S(2)}, u32[]{:S(2)}) collective-permute-start(bf16[224,2048]{1,0:T(8,128)(2,1)} %get-tuple-element.238), channel_id=1, source_target_pairs={{0,3},{1,2},{2,1},{3,0},{4,7},{5,6},{6,5},{7,4},{8,11},{9,10},{10,... | collective-permute-start | bytes 2752520 | tf_op jit(solution)/shard_map/ppermute | solution.py:186
  633.7 60.9 %collective-permute-start.66 = (bf16[224,512]{1,0:T(8,128)(2,1)}, bf16[224,512]{1,0:T(8,128)(2,1)}, u32[]{:S(2)}, u32[]{:S(2)}) collective-permute-start(bf16[224,512]{1,0:T(8,128)(2,1)} %get-tuple-element.264), channel_id=1, source_target_pairs={{0,1},{1,0},{2,3},{3,2},{4,5},{5,4},{6,7},{7,6},{8,9},{9,8},{10,11... | collective-permute-start | bytes 688136 | tf_op jit(solution)/shard_map/ppermute | solution.py:186
  635.4 60.2 %collective-permute-start.67 = (bf16[224,512]{1,0:T(8,128)(2,1)}, bf16[224,512]{1,0:T(8,128)(2,1)}, u32[]{:S(2)}, u32[]{:S(2)}) collective-permute-start(bf16[224,512]{1,0:T(8,128)(2,1)} %get-tuple-element.265), channel_id=1, source_target_pairs={{0,2},{1,3},{2,0},{3,1},{4,6},{5,7},{6,4},{7,5},{8,10},{9,11},{10,... | collective-permute-start | bytes 688136 | tf_op jit(solution)/shard_map/ppermute | solution.py:186
  647.6 46.8 %collective-permute-start.64 = (bf16[224,2048]{1,0:T(8,128)(2,1)}, bf16[224,2048]{1,0:T(8,128)(2,1)S(1)}, u32[]{:S(2)}, u32[]{:S(2)}) collective-permute-start(bf16[224,2048]{1,0:T(8,128)(2,1)} %get-tuple-element.257), channel_id=1, source_target_pairs={{0,2},{1,3},{2,0},{3,1},{4,6},{5,7},{6,4},{7,5},{8,10},{9,11},{10,... | collective-permute-start | bytes 2752520 | tf_op jit(solution)/shard_map/ppermute | solution.py:186
  650.5 43.9 %collective-permute-start.65 = (bf16[224,2048]{1,0:T(8,128)(2,1)}, bf16[224,2048]{1,0:T(8,128)(2,1)S(1)}, u32[]{:S(2)}, u32[]{:S(2)}) collective-permute-start(bf16[224,2048]{1,0:T(8,128)(2,1)} %get-tuple-element.258), channel_id=1, source_target_pairs={{0,3},{1,2},{2,1},{3,0},{4,7},{5,6},{6,5},{7,4},{8,11},{9,10},{10,... | collective-permute-start | bytes 2752520 | tf_op jit(solution)/shard_map/ppermute | solution.py:186
  (105 other events, 1869.8 us)

commit v5 on v4

--- a/solution.py
+++ b/solution.py
@@ -239,26 +239,44 @@
     )(meta, momentum, *received)
 
 
-def pack_pair_kernel(col_count, meta_ref, *refs):
-    pieces, keep, give, choose = refs[:col_count], refs[col_count], refs[col_count + 1], refs[-1]
+def pack_pair_kernel(meta_ref, *refs):
+    pieces, (keep, give, choose, joined) = refs[:-4], refs[-4:]
     other = pl.program_id(0) == 0
-    _, window, slots = choose.shape
 
     @pl.when(other & (pl.program_id(1) == 0))
     def _():
-        fill_choose(meta_ref, choose, 0)
-
-    total = jnp.dot(choose[0], pieces[0][...], preferred_element_type=jnp.float32)
-    for k in range(1, col_count):
-        total += jnp.dot(choose[k], pieces[k][...], preferred_element_type=jnp.float32)
+        fill_wide(meta_ref, choose, 1, len(pieces))
+
+    slots = pieces[0].shape[0]
+    for k, piece in enumerate(pieces):
+        joined[k * slots : (k + 1) * slots, :] = piece[...]
+    block = jnp.dot(choose[...], joined[...], preferred_element_type=jnp.float32).astype(
+        jnp.bfloat16
+    )
 
     @pl.when(other)
     def _():
-        give[...] = total.astype(jnp.bfloat16)
+        give[...] = block
 
     @pl.when(jnp.logical_not(other))
     def _():
-        keep[...] = total.astype(jnp.bfloat16)
+        keep[...] = block
+
+
+def fill_wide(meta_ref, choose, slot_axis, col_count):
+    shape = choose.shape
+    slots = shape[slot_axis] // col_count
+    rows = lax.broadcasted_iota(jnp.int32, shape, 1 - slot_axis)
+    slot = lax.broadcasted_iota(jnp.int32, shape, slot_axis)
+    hit = jnp.zeros(shape, jnp.bool_)
+    for k in range(col_count):
+        first = k * slots
+        hit |= (
+            (rows == slot + (meta_ref[2 + k] - first))
+            & (slot >= first)
+            & (slot < first + meta_ref[2 + col_count + k])
+        )
+    choose[...] = jnp.where(hit, 1.0, 0.0).astype(jnp.bfloat16)
 
 
 def fill_choose(meta_ref, choose, slot_axis):
@@ -279,7 +297,7 @@
     block = lambda e, q, meta: meta[0] ^ (2 * q + 1 - e)
     shape = jax.ShapeDtypeStruct((pairs * window, width), jnp.bfloat16)
     return pl.pallas_call(
-        lambda *refs: pack_pair_kernel(col_count, *refs),
+        pack_pair_kernel,
         out_shape=[shape, shape],
         grid_spec=pltpu.PrefetchScalarGridSpec(
             num_scalar_prefetch=1,
@@ -298,7 +316,10 @@
                     (window, width), lambda e, q, meta: (jnp.where(e == 0, q, pairs - 1), 0)
                 ),
             ],
-            scratch_shapes=[pltpu.VMEM((col_count, window, slots), jnp.bfloat16)],
+            scratch_shapes=[
+                pltpu.VMEM((window, col_count * slots), jnp.bfloat16),
+                pltpu.VMEM((col_count * slots, width), jnp.bfloat16),
+            ],
         ),
         compiler_params=pltpu.CompilerParams(vmem_limit_bytes=VMEM_LIMIT),
         cost_estimate=pl.CostEstimate(
@@ -378,13 +399,13 @@
 
     @pl.when(turn == 0)
     def _():
-        fill_choose(meta_ref, choose, 1)
+        fill_wide(meta_ref, choose, 0, col_count)
 
     def place(block):
+        rows = jnp.dot(choose[...], block, preferred_element_type=jnp.float32)
+        slots = outs[0].shape[0]
         for k in range(col_count):
-            outs[k][...] = jnp.dot(
-                choose[k], block, preferred_element_type=jnp.float32
-            ).astype(jnp.bfloat16)
+            outs[k][...] = rows[k * slots : (k + 1) * slots, :].astype(jnp.bfloat16)
 
     for q, piece in enumerate(pieces):
 
@@ -411,7 +432,7 @@
             in_specs=[pl.BlockSpec(x.shape, lambda q, meta: (0, 0)) for x in (*pieces, got)],
             out_specs=[pl.BlockSpec((slots, width), lambda q, meta: (0, meta[0] ^ q))]
             * col_count,
-            scratch_shapes=[pltpu.VMEM((col_count, slots, window), jnp.bfloat16)],
+            scratch_shapes=[pltpu.VMEM((col_count * slots, window), jnp.bfloat16)],
         ),
         compiler_params=pltpu.CompilerParams(vmem_limit_bytes=VMEM_LIMIT),
         cost_estimate=pl.CostEstimate(
@@ -496,7 +517,7 @@
 
 
 def collect_kernel(meta_ref, *refs):
-    matrices, joined = refs[:-1], refs[-1]
+    matrices, joined, turned = refs[:-2], refs[-2], refs[-1]
     place = 0
     for matrix in matrices[:-1]:
         joined[:, place : place + matrix.shape[1]] = matrix[...]
@@ -508,13 +529,14 @@
     def _(b):
         block = matrices[-1][tile_rows(b), :].astype(jnp.float32)
         joined[tile_rows(b), place:] = jnp.where(own, block, 0.0).astype(jnp.bfloat16)
+        turned[:, lane_block(b, TILE)] = joined[tile_rows(b), :].T
 
 
 def collect(meta, chunks):
     width = sum(x.shape[1] for x in chunks)
     return local_call(
         collect_kernel,
-        jax.ShapeDtypeStruct((M, width), jnp.bfloat16),
+        [jax.ShapeDtypeStruct(shape, jnp.bfloat16) for shape in ((M, width), (width, M))],
         (meta, *chunks),
         4 * M * width,
     )
@@ -525,43 +547,37 @@
 PART = HALF // PIECES
 
 
-def half_gram_kernel(flip, rows_ref, cols_ref, meta_ref, joined, *outs):
-    turn = pl.program_id(0)
-    pair = (meta_ref[0] % 2 ^ flip) * HALF + turn
+def some_gram_kernel(flip, piece, rows_ref, cols_ref, meta_ref, joined, turned, out):
+    pair = (meta_ref[0] % 2 ^ flip) * HALF + piece * PART + pl.program_id(0)
     here = pl.ds(pl.multiple_of(rows_ref[pair] * TILE, TILE), TILE)
-    there = pl.ds(pl.multiple_of(cols_ref[pair] * TILE, TILE), TILE)
-    tile = lax.dot_general(
+    out[...] = jnp.dot(
         joined[here, :],
-        joined[there, :],
-        (((1,), (1,)), ((), ())),
+        turned[:, lane_block(cols_ref[pair], TILE)],
         preferred_element_type=jnp.float32,
     ).astype(jnp.bfloat16)
-    for n, out in enumerate(outs):
-
-        @pl.when(turn // PART == n)
-        def _():
-            out[...] = tile
-
-
-def half_gram(meta, joined, flip):
+
+
+def some_gram(meta, joined, turned, flip, piece):
+    count = PART
     width = joined.shape[1]
-    place = lambda n: lambda p, rows, cols, meta: (jnp.clip(p - n * PART, 0, PART - 1), 0)
     return pl.pallas_call(
-        lambda *refs: half_gram_kernel(flip, *refs),
-        out_shape=[jax.ShapeDtypeStruct((PART * TILE, TILE), jnp.bfloat16)] * PIECES,
+        lambda *refs: some_gram_kernel(flip, piece, *refs),
+        out_shape=jax.ShapeDtypeStruct((count * TILE, TILE), jnp.bfloat16),
         grid_spec=pltpu.PrefetchScalarGridSpec(
             num_scalar_prefetch=3,
-            grid=(HALF,),
-            in_specs=[pl.BlockSpec((M, width), lambda p, rows, cols, meta: (0, 0))],
-            out_specs=[pl.BlockSpec((TILE, TILE), place(n)) for n in range(PIECES)],
+            grid=(count,),
+            in_specs=[
+                pl.BlockSpec(x.shape, lambda p, rows, cols, meta: (0, 0)) for x in (joined, turned)
+            ],
+            out_specs=pl.BlockSpec((TILE, TILE), lambda p, rows, cols, meta: (p, 0)),
         ),
         compiler_params=pltpu.CompilerParams(vmem_limit_bytes=VMEM_LIMIT),
         cost_estimate=pl.CostEstimate(
-            flops=2 * HALF * TILE * TILE * width,
-            bytes_accessed=2 * HALF * TILE * TILE + 2 * M * width,
+            flops=2 * count * TILE * TILE * width,
+            bytes_accessed=2 * count * TILE * TILE + 4 * M * width,
             transcendentals=0,
         ),
-    )(jnp.asarray(PAIR_ROWS), jnp.asarray(PAIR_COLS), meta, joined)
+    )(jnp.asarray(PAIR_ROWS), jnp.asarray(PAIR_COLS), meta, joined, turned)
 
 
 def lane_block(block, lanes):
@@ -824,7 +840,7 @@
     return result
 
 
-def sum_tiles(meta, joined, row_count, col_count):
+def sum_tiles(meta, joined, turned, row_count, col_count):
     pair_count = row_count // 2
     tie = lax.optimization_barrier
 
@@ -834,13 +850,15 @@
     def over_pairs(blocks):
         return [swap(blocks[q], "row", row_count, 2 * q) for q in range(1, pair_count)]
 
-    give = half_gram(meta, joined, 1)
-    got = [swap(piece, "row", row_count, 1) for piece in give]
-    keep = half_gram(meta, joined, 0)
-
-    early = add_halves(meta, keep[0], got[0], col_count)
+    def halves(piece):
+        got = swap(some_gram(meta, joined, turned, 1, piece), "row", row_count, 1)
+        keep = some_gram(meta, joined, turned, 0, piece)
+        return add_halves(meta, keep, got, col_count)
+
+    early = halves(0)
+    early, (joined, turned) = tie((early, (joined, turned)))
     early_in = over_cols(early)
-    late = add_halves(meta, keep[1], got[1], col_count)
+    late = halves(1)
     late, early_in = tie((late, early_in))
     late_in = over_cols(late)
     early_parts = add_quarters(meta, [early[0]] + early_in, pair_count)
@@ -887,7 +905,7 @@
     number = (N // (row_count * col_count)) // CHUNK
     distances = list(range(pair_count))
 
-    def fetch(base, span, after):
+    def fetch(base, span, steps, after):
         place, after = lax.optimization_barrier((col, after))
         received = [
             swap(
@@ -898,7 +916,7 @@
                 col_count,
                 k,
             )
-            for k in range(1, col_count)
+            for k in steps
         ]
         return received, after
 
@@ -911,15 +929,24 @@
         )
         return join(meta, keep, swap(give, "row", row_count, 1), even, window, pair_count)
 
-    received, _ = fetch(0, row_count * CHUNK, shard_starts)
-    last, received = fetch(number * wide, pair_count * LAST, received)
-    joined = gather_chunk(0, received)
+    half, span = col_count // 2, row_count * CHUNK
+    received, _ = fetch(0, span, range(1, col_count), shard_starts)
     landed = []
     for c in range(1, number):
-        received, (last, joined) = fetch(c * wide, row_count * CHUNK, (last, joined))
-        crossed, received = lax.optimization_barrier((across(joined), received))
+        some, received = fetch(c * wide, span, range(1, half + 1), received)
+        joined = gather_chunk(c - 1, received)
+        rest, (some, joined) = fetch(
+            c * wide, span, range(half + 1, col_count), (some, joined)
+        )
+        crossed = across(joined)
+        received = some + rest
+        crossed[pair_count // 2], received = lax.optimization_barrier(
+            (crossed[pair_count // 2], received)
+        )
         landed.append(crossed)
-        joined = gather_chunk(c, received)
+    last, received = fetch(number * wide, pair_count * LAST, range(1, col_count), received)
+    joined = gather_chunk(number - 1, received)
+    joined, last, landed = lax.optimization_barrier((joined, last, landed))
     landed.append(across(joined))
     matrices = [
         merge(meta, pieces, [[q] for q in distances], 2 * even, 2, jitter) for pieces in landed
@@ -940,7 +967,7 @@
         )
     )
 
-    tiles = sum_tiles(meta, collect(meta, matrices), row_count, col_count)
+    tiles = sum_tiles(meta, *collect(meta, matrices), row_count, col_count)
 
     sends = [(2 * even, 2, even + window, distances)] * number
     sends.append((even, 1, window, [2 * q for q in distances]))

time: 711 us -> 739 us (1.039)
  Pallas kernels: 205 us -> 232 us
  starting transfers between devices: 125 us -> 116 us
    pallas_call x4 -> x6, Pallas kernels: 46.2 us -> 59.9 us  [the longest x4 40 us: some_gram(): pl.pallas_call(lambda *refs: some_gram_kernel(flip, piece, *refs), out_sh...]
    pallas_call x1, Pallas kernels: 24.4 us -> 33.3 us  [first_apply(): pl.pallas_call(lambda *refs: first_apply_kernel(jitter, send, *refs), out...]
    ppermute x69, starting transfers between devices: 125 us -> 116 us  [swap(): lax.ppermute(value, axis, perm=[(i, i ^ distance) for i in range(size)])]
    unnamed x123 -> x133, local copies, waits for them, and re-layouts: 22.6 us -> 22.1 us
  transfers between devices with their start and end apart: 69 -> 69, of which waited for: 33 -> 32; matrix products, arithmetic and copies ran while one was open for 2% -> 2% of each run, Pallas kernels for 19% -> 17%
where the time goes in v5:
time: 739 us; the launch traced here: 727 us
  waiting for transfers between devices  337 us (46%)
  Pallas kernels  232 us (31%)
  starting transfers between devices  116 us (16%)
  local copies, waits for them, and re-layouts  40.3 us (5%)
    ppermute x69, waiting for transfers between devices, swap(): lax.ppermute(value, axis, perm=[(i, i ^ distance) for i in range(size)])  337 us
    ppermute x69, starting transfers between devices, swap(): lax.ppermute(value, axis, perm=[(i, i ^ distance) for i in range(size)])  116 us
    pallas_call x14, Pallas kernels, local_call(): pl.pallas_call(kernel, out_shape=out_shape, in_specs=[pl.BlockSpec(memory...  45.6 us
    pallas_call x4, Pallas kernels, some_gram(): pl.pallas_call(lambda *refs: some_gram_kernel(flip, piece, *refs), out_sh...  40 us
    pallas_call x1, Pallas kernels, next_apply(): pl.pallas_call(lambda *refs: next_apply_kernel(jitter, sends, *refs), out...  35.1 us
    pallas_call x1, Pallas kernels, first_apply(): pl.pallas_call(lambda *refs: first_apply_kernel(jitter, send, *refs), out...  33.3 us
    pallas_call x4, Pallas kernels, gridded(): pl.pallas_call(kernel, out_shape=outs, grid_spec=pltpu.PrefetchScalarGrid...  29.1 us
    unnamed x133, local copies, waits for them, and re-layouts  22.1 us
  transfers between devices with their start and end apart: 69, of which 32 were waited for; matrix products, arithmetic and copies ran while one was open for 2% of the time, Pallas kernels for 17%

profile of v5, /device:TPU:0, one launch (start us, length us, event | category | flops | bytes accessed | tf_op | source)
XLA Modules:
  0.0 727.3 jit_solution(3816236852413364474)
XLA Ops:
  9.8 16.4 %collective-permute-done.refs_1_ = bf16[224,2048]{1,0:T(8,128)(2,1)} collective-permute-done((bf16[224,2048]{1,0:T(8,128)(2,1)S(1)}, bf16[224,2048]{1,0:T(8,128)(2,1)}, u32[]{:S(2)}, u32[]{:S(2)}) %collective-permute-start) | collective-permute-done | bytes 917536 | tf_op jit(solution)/shard_map/ppermute | solution.py:186
  26.2 20.3 %collective-permute-done.1.refs_2_ = bf16[224,2048]{1,0:T(8,128)(2,1)} collective-permute-done((bf16[224,2048]{1,0:T(8,128)(2,1)S(1)}, bf16[224,2048]{1,0:T(8,128)(2,1)}, u32[]{:S(2)}, u32[]{:S(2)}) %collective-permute-start.1) | collective-permute-done | bytes 917536 | tf_op jit(solution)/shard_map/ppermute | solution.py:186
  46.5 10.0 %shard_map.46 = (bf16[2240,256]{1,0:T(8,128)(2,1)}, bf16[2240,256]{1,0:T(8,128)(2,1)}) custom-call(s32[10]{0:T(128)} %pad_add_fusion.1.meta_ref.refs_0_.refs_2_, bf16[224,18432]{1,0:T(8,128)(2,1)} %refs_1_.6, bf16[224,2048]{1,0:T(8,128)(2,1)} %collective-permute-done.refs_1_, bf16[224,2048]{1,0:T(8,128)(2,1)} %collective-permute-done.1.refs_2_, ...), custom_call_target="tpu_custom_call" | custom-call | flops 2055208960 | bytes 5963776 | tf_op jit(solution)/shard_map/pallas_call | solution.py:299
  64.4 16.6 %collective-permute-done.3.refs_1_ = bf16[224,2048]{1,0:T(8,128)(2,1)S(1)} collective-permute-done((bf16[224,2048]{1,0:T(8,128)(2,1)S(1)}, bf16[224,2048]{1,0:T(8,128)(2,1)S(1)}, u32[]{:S(2)}, u32[]{:S(2)}) %collective-permute-start.3) | collective-permute-done | bytes 917536 | tf_op jit(solution)/shard_map/ppermute | solution.py:186
  87.9 22.4 %collective-permute-done.6.refs_3_ = bf16[1008,256]{1,0:T(8,128)(2,1)S(1)} collective-permute-done((bf16[1008,256]{1,0:T(8,128)(2,1)}, bf16[1008,256]{1,0:T(8,128)(2,1)S(1)}, u32[]{:S(2)}, u32[]{:S(2)}) %collective-permute-start.6) | collective-permute-done | bytes 516128 | tf_op jit(solution)/shard_map/ppermute | solution.py:186
  135.6 12.9 %collective-permute-done.13.refs_4_ = bf16[1008,256]{1,0:T(8,128)(2,1)S(1)} collective-permute-done((bf16[1008,256]{1,0:T(8,128)(2,1)}, bf16[1008,256]{1,0:T(8,128)(2,1)S(1)}, u32[]{:S(2)}, u32[]{:S(2)}) %collective-permute-start.13) | collective-permute-done | bytes 516128 | tf_op jit(solution)/shard_map/ppermute | solution.py:186
  177.5 16.7 %collective-permute-done.14.refs_2_ = bf16[1008,256]{1,0:T(8,128)(2,1)S(1)} collective-permute-done((bf16[1008,256]{1,0:T(8,128)(2,1)S(1)}, bf16[1008,256]{1,0:T(8,128)(2,1)S(1)}, u32[]{:S(2)}, u32[]{:S(2)}) %collective-permute-start.14) | collective-permute-done | bytes 516128 | tf_op jit(solution)/shard_map/ppermute | solution.py:186
  194.1 14.7 %collective-permute-done.15.refs_3_ = bf16[1008,256]{1,0:T(8,128)(2,1)S(1)} collective-permute-done((bf16[1008,256]{1,0:T(8,128)(2,1)S(1)}, bf16[1008,256]{1,0:T(8,128)(2,1)S(1)}, u32[]{:S(2)}, u32[]{:S(2)}) %collective-permute-start.15) | collective-permute-done | bytes 516128 | tf_op jit(solution)/shard_map/ppermute | solution.py:186
  235.1 10.0 %shard_map.55.keep = bf16[3584,512]{1,0:T(8,128)(2,1)} custom-call(s32[28]{0:T(128)} %constant.61.clone.refs_0_, s32[28]{0:T(128)} %constant.62.clone.refs_1_, s32[10]{0:T(128)} %pad_add_fusion.1.meta_ref.refs_0_.refs_2_, bf16[3584,640]{1,0:T(8,128)(2,1)} %get-tuple-element.205.refs_3_, bf16[640,3584]{1,0:T(8,128)(2,1)} %get-tuple-element.206.refs_4_), custom_call_target="tpu_custom_call" | custom-call | flops 2348810240 | bytes 12845056 | tf_op jit(solution)/shard_map/pallas_call | solution.py:563
  254.6 10.1 %shard_map.59 = bf16[3584,512]{1,0:T(8,128)(2,1)} custom-call(s32[28]{0:T(128)} %constant.61.clone.refs_0_, s32[28]{0:T(128)} %constant.62.clone.refs_1_, s32[10]{0:T(128)} %pad_add_fusion.1.meta_ref.refs_0_.refs_2_, bf16[3584,640]{1,0:T(8,128)(2,1)} %get-tuple-element.205.refs_3_, bf16[640,3584]{1,0:T(8,128)(2,1)} %get-tuple-element.206.refs_4_), custom_call_target="tpu_custom_call" | custom-call | flops 2348810240 | bytes 12845056 | tf_op jit(solution)/shard_map/pallas_call | solution.py:563
  268.7 10.0 %shard_map.58.keep = bf16[3584,512]{1,0:T(8,128)(2,1)} custom-call(s32[28]{0:T(128)} %constant.61.clone.refs_0_, s32[28]{0:T(128)} %constant.62.clone.refs_1_, s32[10]{0:T(128)} %pad_add_fusion.1.meta_ref.refs_0_.refs_2_, bf16[3584,640]{1,0:T(8,128)(2,1)} %get-tuple-element.205.refs_3_, bf16[640,3584]{1,0:T(8,128)(2,1)} %get-tuple-element.206.refs_4_), custom_call_target="tpu_custom_call" | custom-call | flops 2348810240 | bytes 12845056 | tf_op jit(solution)/shard_map/pallas_call | solution.py:563
  288.6 19.2 %collective-permute-done.24.refs_3_ = bf16[3584,128]{1,0:T(8,128)(2,1)S(1)} collective-permute-done((bf16[3584,128]{1,0:T(8,128)(2,1)S(1)}, bf16[3584,128]{1,0:T(8,128)(2,1)S(1)}, u32[]{:S(2)}, u32[]{:S(2)}) %collective-permute-start.24) | collective-permute-done | bytes 917536 | tf_op jit(solution)/shard_map/ppermute | solution.py:186
  314.8 10.1 %collective-permute-start.29 = (bf16[896,128]{1,0:T(8,128)(2,1)}, bf16[896,128]{1,0:T(8,128)(2,1)S(1)}, u32[]{:S(2)}, u32[]{:S(2)}) collective-permute-start(bf16[896,128]{1,0:T(8,128)(2,1)} %get-tuple-element.221), channel_id=1, source_target_pairs={{0,8},{4,12},{8,0},{12,4},{16,24},{20,28},{24,16},{28,20},{1,9},{5... | collective-permute-start | bytes 688136 | tf_op jit(solution)/shard_map/ppermute | solution.py:186
  352.0 10.1 %collective-permute-start.32 = (bf16[896,128]{1,0:T(8,128)(2,1)}, bf16[896,128]{1,0:T(8,128)(2,1)S(1)}, u32[]{:S(2)}, u32[]{:S(2)}) collective-permute-start(bf16[896,128]{1,0:T(8,128)(2,1)} %shard_map.62.refs_0_), channel_id=1, source_target_pairs={{0,8},{4,12},{8,0},{12,4},{16,24},{20,28},{24,16},{28,20},{1,9},{5... | collective-permute-start | bytes 688136 | tf_op jit(solution)/shard_map/ppermute | solution.py:186
  369.3 11.6 %collective-permute-done.33.refs_2_ = bf16[896,128]{1,0:T(8,128)(2,1)S(1)} collective-permute-done((bf16[896,128]{1,0:T(8,128)(2,1)}, bf16[896,128]{1,0:T(8,128)(2,1)S(1)}, u32[]{:S(2)}, u32[]{:S(2)}) %collective-permute-start.33) | collective-permute-done | bytes 229408 | tf_op jit(solution)/shard_map/ppermute | solution.py:186
  392.8 12.8 %collective-permute-done.36.refs_2_ = bf16[896,128]{1,0:T(8,128)(2,1)S(1)} collective-permute-done((bf16[896,128]{1,0:T(8,128)(2,1)}, bf16[896,128]{1,0:T(8,128)(2,1)S(1)}, u32[]{:S(2)}, u32[]{:S(2)}) %collective-permute-start.36) | collective-permute-done | bytes 229408 | tf_op jit(solution)/shard_map/ppermute | solution.py:186
  445.3 13.1 %collective-permute-done.44.refs_1_ = bf16[3584,128]{1,0:T(8,128)(2,1)S(1)} collective-permute-done((bf16[3584,128]{1,0:T(8,128)(2,1)}, bf16[3584,128]{1,0:T(8,128)(2,1)S(1)}, u32[]{:S(2)}, u32[]{:S(2)}) %collective-permute-start.44) | collective-permute-done | bytes 917536 | tf_op jit(solution)/shard_map/ppermute | solution.py:186
  458.4 17.0 %collective-permute-done.45.refs_2_ = bf16[3584,128]{1,0:T(8,128)(2,1)S(1)} collective-permute-done((bf16[3584,128]{1,0:T(8,128)(2,1)}, bf16[3584,128]{1,0:T(8,128)(2,1)S(1)}, u32[]{:S(2)}, u32[]{:S(2)}) %collective-permute-start.45) | collective-permute-done | bytes 917536 | tf_op jit(solution)/shard_map/ppermute | solution.py:186
  492.8 33.3 %shard_map.69 = (bf16[1008,256]{1,0:T(8,128)(2,1)}, bf16[1008,256]{1,0:T(8,128)(2,1)}, bf16[1008,256]{1,0:T(8,128)(2,1)}, bf16[1008,256]{1,0:T(8,128)(2,1)}, bf16[7,512,3584]{2,1,0:T(8,128)(2,1)}) custom-call(s32[28]{0:T(128)} %constant.61.clone.refs_0_, s32[28]{0:T(128)} %constant.62.clone.refs_1_, s32[10]{0:T(128)} %pad_add_fusion.1.meta_ref.refs_0_.refs_2_, ...), custom_call_target="tpu_custom_call" | custom-call | flops 13153337344 | bytes 55050240 | tf_op jit(solution)/shard_map/pallas_call | solution.py:762
  535.8 35.1 %shard_map.70 = (bf16[1008,256]{1,0:T(8,128)(2,1)}, bf16[1008,256]{1,0:T(8,128)(2,1)}, bf16[1008,256]{1,0:T(8,128)(2,1)}, bf16[1008,256]{1,0:T(8,128)(2,1)}, bf1...) custom-call(s32[10]{0:T(128)} %pad_add_fusion.1.meta_ref.refs_0_.refs_2_,, ...), custom_call_target="tpu_custom_call" | custom-call | flops 19730006016 | bytes 56885248 | tf_op jit(solution)/shard_map/pallas_call | solution.py:817
  574.8 10.6 %collective-permute-start.56 = (bf16[1008,256]{1,0:T(8,128)(2,1)}, bf16[1008,256]{1,0:T(8,128)(2,1)S(1)}, u32[]{:S(2)}, u32[]{:S(2)}) collective-permute-start(bf16[1008,256]{1,0:T(8,128)(2,1)} %get-tuple-element.270), channel_id=1, source_target_pairs={{0,8},{4,12},{8,0},{12,4},{16,24},{20,28},{24,16},{28,20},{1,9},{5... | collective-permute-start | bytes 1548296 | tf_op jit(solution)/shard_map/ppermute | solution.py:186
  619.2 32.0 %collective-permute-done.57.refs_3_ = bf16[1008,256]{1,0:T(8,128)(2,1)S(1)} collective-permute-done((bf16[1008,256]{1,0:T(8,128)(2,1)S(1)}, bf16[1008,256]{1,0:T(8,128)(2,1)S(1)}, u32[]{:S(2)}, u32[]{:S(2)}) %collective-permute-start.57) | collective-permute-done | bytes 516128 | tf_op jit(solution)/shard_map/ppermute | solution.py:186
  680.4 14.6 %collective-permute-done.63 = bf16[224,2048]{1,0:T(8,128)(2,1)S(1)} collective-permute-done((bf16[224,2048]{1,0:T(8,128)(2,1)}, bf16[224,2048]{1,0:T(8,128)(2,1)S(1)}, u32[]{:S(2)}, u32[]{:S(2)}) %collective-permute-start.63) | collective-permute-done | bytes 917536 | tf_op jit(solution)/shard_map/ppermute | solution.py:186
  697.5 23.3 %collective-permute-done.64 = bf16[224,2048]{1,0:T(8,128)(2,1)S(1)} collective-permute-done((bf16[224,2048]{1,0:T(8,128)(2,1)}, bf16[224,2048]{1,0:T(8,128)(2,1)S(1)}, u32[]{:S(2)}, u32[]{:S(2)}) %collective-permute-start.64) | collective-permute-done | bytes 917536 | tf_op jit(solution)/shard_map/ppermute | solution.py:186
  (303 shorter events, 324.0 us)
Async XLA Ops:
  4.9 41.6 %collective-permute-start.1 = (bf16[224,2048]{1,0:T(8,128)(2,1)S(1)}, bf16[224,2048]{1,0:T(8,128)(2,1)}, u32[]{:S(2)}, u32[]{:S(2)}) collective-permute-start(bf16[224,2048]{1,0:T(8,128)(2,1)S(1)} %get-tuple-element.303), channel_id=1, source_target_pairs={{0,2},{1,3},{2,0},{3,1},{4,6},{5,7},{6,4},{7,5},{8,10},{9,11},{10,... | collective-permute-start | bytes 2752520 | tf_op jit(solution)/shard_map/ppermute | solution.py:186
  6.5 40.1 %collective-permute-start.2 = (bf16[224,2048]{1,0:T(8,128)(2,1)S(1)}, bf16[224,2048]{1,0:T(8,128)(2,1)}, u32[]{:S(2)}, u32[]{:S(2)}) collective-permute-start(bf16[224,2048]{1,0:T(8,128)(2,1)S(1)} %get-tuple-element.302), channel_id=1, source_target_pairs={{0,3},{1,2},{2,1},{3,0},{4,7},{5,6},{6,5},{7,4},{8,11},{9,10},{10,... | collective-permute-start | bytes 2752520 | tf_op jit(solution)/shard_map/ppermute | solution.py:186
  168.7 45.4 %collective-permute-start.20 = (bf16[2240,128]{1,0:T(8,128)(2,1)S(1)}, bf16[2240,128]{1,0:T(8,128)(2,1)S(1)}, u32[]{:S(2)}, u32[]{:S(2)}) collective-permute-start(bf16[2240,128]{1,0:T(8,128)(2,1)S(1)} %constant_dynamic-update-slice_fusion.refs_1_), channel_id=1, source_target_pairs={{0,4},{4,0},{8,12},{12,8},{16,20},{20,16},{24,28},{28,24},{1,5},{5... | collective-permute-start | bytes 1720328 | tf_op jit(solution)/shard_map/ppermute | solution.py:186
  266.1 41.6 %collective-permute-start.24 = (bf16[3584,128]{1,0:T(8,128)(2,1)S(1)}, bf16[3584,128]{1,0:T(8,128)(2,1)S(1)}, u32[]{:S(2)}, u32[]{:S(2)}) collective-permute-start(bf16[3584,128]{1,0:T(8,128)(2,1)S(1)} %copy-done.54), channel_id=1, source_target_pairs={{0,2},{1,3},{2,0},{3,1},{4,6},{5,7},{6,4},{7,5},{8,10},{9,11},{10,... | collective-permute-start | bytes 2752520 | tf_op jit(solution)/shard_map/ppermute | solution.py:186
  267.0 40.8 %collective-permute-start.25 = (bf16[3584,128]{1,0:T(8,128)(2,1)S(1)}, bf16[3584,128]{1,0:T(8,128)(2,1)S(1)}, u32[]{:S(2)}, u32[]{:S(2)}) collective-permute-start(bf16[3584,128]{1,0:T(8,128)(2,1)S(1)} %copy-done.53), channel_id=1, source_target_pairs={{0,3},{1,2},{2,1},{3,0},{4,7},{5,6},{6,5},{7,4},{8,11},{9,10},{10,... | collective-permute-start | bytes 2752520 | tf_op jit(solution)/shard_map/ppermute | solution.py:186
  308.9 39.4 %collective-permute-start.27 = (bf16[3584,128]{1,0:T(8,128)(2,1)}, bf16[3584,128]{1,0:T(8,128)(2,1)S(1)}, u32[]{:S(2)}, u32[]{:S(2)}) collective-permute-start(bf16[3584,128]{1,0:T(8,128)(2,1)} %get-tuple-element.219), channel_id=1, source_target_pairs={{0,2},{1,3},{2,0},{3,1},{4,6},{5,7},{6,4},{7,5},{8,10},{9,11},{10,... | collective-permute-start | bytes 2752520 | tf_op jit(solution)/shard_map/ppermute | solution.py:186
  309.7 39.8 %collective-permute-start.28 = (bf16[3584,128]{1,0:T(8,128)(2,1)}, bf16[3584,128]{1,0:T(8,128)(2,1)S(1)}, u32[]{:S(2)}, u32[]{:S(2)}) collective-permute-start(bf16[3584,128]{1,0:T(8,128)(2,1)} %get-tuple-element.220), channel_id=1, source_target_pairs={{0,3},{1,2},{2,1},{3,0},{4,7},{5,6},{6,5},{7,4},{8,11},{9,10},{10,... | collective-permute-start | bytes 2752520 | tf_op jit(solution)/shard_map/ppermute | solution.py:186
  386.2 45.4 %collective-permute-start.41 = (bf16[3584,128]{1,0:T(8,128)(2,1)}, bf16[3584,128]{1,0:T(8,128)(2,1)S(1)}, u32[]{:S(2)}, u32[]{:S(2)}) collective-permute-start(bf16[3584,128]{1,0:T(8,128)(2,1)} %shard_map.64.refs_0_), channel_id=1, source_target_pairs={{0,1},{1,0},{2,3},{3,2},{4,5},{5,4},{6,7},{7,6},{8,9},{9,8},{10,11... | collective-permute-start | bytes 2752520 | tf_op jit(solution)/shard_map/ppermute | solution.py:186
  387.2 44.4 %collective-permute-start.42 = (bf16[3584,128]{1,0:T(8,128)(2,1)}, bf16[3584,128]{1,0:T(8,128)(2,1)S(1)}, u32[]{:S(2)}, u32[]{:S(2)}) collective-permute-start(bf16[3584,128]{1,0:T(8,128)(2,1)} %shard_map.64.refs_0_), channel_id=1, source_target_pairs={{0,2},{1,3},{2,0},{3,1},{4,6},{5,7},{6,4},{7,5},{8,10},{9,11},{10,... | collective-permute-start | bytes 2752520 | tf_op jit(solution)/shard_map/ppermute | solution.py:186
  387.7 43.9 %collective-permute-start.43 = (bf16[3584,128]{1,0:T(8,128)(2,1)}, bf16[3584,128]{1,0:T(8,128)(2,1)S(1)}, u32[]{:S(2)}, u32[]{:S(2)}) collective-permute-start(bf16[3584,128]{1,0:T(8,128)(2,1)} %shard_map.64.refs_0_), channel_id=1, source_target_pairs={{0,3},{1,2},{2,1},{3,0},{4,7},{5,6},{6,5},{7,4},{8,11},{9,10},{10,... | collective-permute-start | bytes 2752520 | tf_op jit(solution)/shard_map/ppermute | solution.py:186
  435.8 39.7 %collective-permute-start.45 = (bf16[3584,128]{1,0:T(8,128)(2,1)}, bf16[3584,128]{1,0:T(8,128)(2,1)S(1)}, u32[]{:S(2)}, u32[]{:S(2)}) collective-permute-start(bf16[3584,128]{1,0:T(8,128)(2,1)} %shard_map.67.refs_0_), channel_id=1, source_target_pairs={{0,2},{1,3},{2,0},{3,1},{4,6},{5,7},{6,4},{7,5},{8,10},{9,11},{10,... | collective-permute-start | bytes 2752520 | tf_op jit(solution)/shard_map/ppermute | solution.py:186
  436.3 39.2 %collective-permute-start.46 = (bf16[3584,128]{1,0:T(8,128)(2,1)}, bf16[3584,128]{1,0:T(8,128)(2,1)S(1)}, u32[]{:S(2)}, u32[]{:S(2)}) collective-permute-start(bf16[3584,128]{1,0:T(8,128)(2,1)} %shard_map.67.refs_0_), channel_id=1, source_target_pairs={{0,3},{1,2},{2,1},{3,0},{4,7},{5,6},{6,5},{7,4},{8,11},{9,10},{10,... | collective-permute-start | bytes 2752520 | tf_op jit(solution)/shard_map/ppermute | solution.py:186
  445.3 39.0 %collective-permute-start.47 = (bf16[3584,512]{1,0:T(8,128)(2,1)}, bf16[3584,512]{1,0:T(8,128)(2,1)}, u32[]{:S(2)}, u32[]{:S(2)}) collective-permute-start(bf16[3584,512]{1,0:T(8,128)(2,1)} %shard_map.66.refs_3_), channel_id=1, source_target_pairs={{0,4},{4,0},{8,12},{12,8},{16,20},{20,16},{24,28},{28,24},{1,5},{5... | collective-permute-start | bytes 11010056 | tf_op jit(solution)/shard_map/ppermute | solution.py:186
  526.0 44.9 %collective-permute-start.49 = (bf16[1008,256]{1,0:T(8,128)(2,1)}, bf16[1008,256]{1,0:T(8,128)(2,1)S(1)}, u32[]{:S(2)}, u32[]{:S(2)}) collective-permute-start(bf16[1008,256]{1,0:T(8,128)(2,1)} %get-tuple-element.249), channel_id=1, source_target_pairs={{0,8},{4,12},{8,0},{12,4},{16,24},{20,28},{24,16},{28,20},{1,9},{5... | collective-permute-start | bytes 1548296 | tf_op jit(solution)/shard_map/ppermute | solution.py:186
  533.3 37.9 %collective-permute-start.50 = (bf16[1008,256]{1,0:T(8,128)(2,1)}, bf16[1008,256]{1,0:T(8,128)(2,1)S(1)}, u32[]{:S(2)}, u32[]{:S(2)}) collective-permute-start(bf16[1008,256]{1,0:T(8,128)(2,1)} %get-tuple-element.250), channel_id=1, source_target_pairs={{0,16},{4,20},{8,24},{12,28},{16,0},{20,4},{24,8},{28,12},{1,17},{... | collective-permute-start | bytes 1548296 | tf_op jit(solution)/shard_map/ppermute | solution.py:186
  533.3 37.9 %collective-permute-start.51 = (bf16[1008,256]{1,0:T(8,128)(2,1)}, bf16[1008,256]{1,0:T(8,128)(2,1)S(1)}, u32[]{:S(2)}, u32[]{:S(2)}) collective-permute-start(bf16[1008,256]{1,0:T(8,128)(2,1)} %get-tuple-element.251), channel_id=1, source_target_pairs={{0,24},{4,28},{8,16},{12,20},{16,8},{20,12},{24,0},{28,4},{1,25},{... | collective-permute-start | bytes 1548296 | tf_op jit(solution)/shard_map/ppermute | solution.py:186
  574.8 43.9 %collective-permute-start.56 = (bf16[1008,256]{1,0:T(8,128)(2,1)}, bf16[1008,256]{1,0:T(8,128)(2,1)S(1)}, u32[]{:S(2)}, u32[]{:S(2)}) collective-permute-start(bf16[1008,256]{1,0:T(8,128)(2,1)} %get-tuple-element.270), channel_id=1, source_target_pairs={{0,8},{4,12},{8,0},{12,4},{16,24},{20,28},{24,16},{28,20},{1,9},{5... | collective-permute-start | bytes 1548296 | tf_op jit(solution)/shard_map/ppermute | solution.py:186
  596.2 55.1 %collective-permute-start.53 = (bf16[224,2048]{1,0:T(8,128)(2,1)}, bf16[224,2048]{1,0:T(8,128)(2,1)}, u32[]{:S(2)}, u32[]{:S(2)}) collective-permute-start(bf16[224,2048]{1,0:T(8,128)(2,1)} %get-tuple-element.266), channel_id=1, source_target_pairs={{0,1},{1,0},{2,3},{3,2},{4,5},{5,4},{6,7},{7,6},{8,9},{9,8},{10,11... | collective-permute-start | bytes 2752520 | tf_op jit(solution)/shard_map/ppermute | solution.py:186
  597.3 53.9 %collective-permute-start.54 = (bf16[224,2048]{1,0:T(8,128)(2,1)}, bf16[224,2048]{1,0:T(8,128)(2,1)}, u32[]{:S(2)}, u32[]{:S(2)}) collective-permute-start(bf16[224,2048]{1,0:T(8,128)(2,1)} %get-tuple-element.267), channel_id=1, source_target_pairs={{0,2},{1,3},{2,0},{3,1},{4,6},{5,7},{6,4},{7,5},{8,10},{9,11},{10,... | collective-permute-start | bytes 2752520 | tf_op jit(solution)/shard_map/ppermute | solution.py:186
  597.3 54.0 %collective-permute-start.55 = (bf16[224,2048]{1,0:T(8,128)(2,1)}, bf16[224,2048]{1,0:T(8,128)(2,1)}, u32[]{:S(2)}, u32[]{:S(2)}) collective-permute-start(bf16[224,2048]{1,0:T(8,128)(2,1)} %get-tuple-element.268), channel_id=1, source_target_pairs={{0,3},{1,2},{2,1},{3,0},{4,7},{5,6},{6,5},{7,4},{8,11},{9,10},{10,... | collective-permute-start | bytes 2752520 | tf_op jit(solution)/shard_map/ppermute | solution.py:186
  659.7 61.3 %collective-permute-start.66 = (bf16[224,512]{1,0:T(8,128)(2,1)}, bf16[224,512]{1,0:T(8,128)(2,1)}, u32[]{:S(2)}, u32[]{:S(2)}) collective-permute-start(bf16[224,512]{1,0:T(8,128)(2,1)} %get-tuple-element.294), channel_id=1, source_target_pairs={{0,1},{1,0},{2,3},{3,2},{4,5},{5,4},{6,7},{7,6},{8,9},{9,8},{10,11... | collective-permute-start | bytes 688136 | tf_op jit(solution)/shard_map/ppermute | solution.py:186
  661.0 61.1 %collective-permute-start.67 = (bf16[224,512]{1,0:T(8,128)(2,1)}, bf16[224,512]{1,0:T(8,128)(2,1)}, u32[]{:S(2)}, u32[]{:S(2)}) collective-permute-start(bf16[224,512]{1,0:T(8,128)(2,1)} %get-tuple-element.295), channel_id=1, source_target_pairs={{0,2},{1,3},{2,0},{3,1},{4,6},{5,7},{6,4},{7,5},{8,10},{9,11},{10,... | collective-permute-start | bytes 688136 | tf_op jit(solution)/shard_map/ppermute | solution.py:186
  673.8 47.0 %collective-permute-start.64 = (bf16[224,2048]{1,0:T(8,128)(2,1)}, bf16[224,2048]{1,0:T(8,128)(2,1)S(1)}, u32[]{:S(2)}, u32[]{:S(2)}) collective-permute-start(bf16[224,2048]{1,0:T(8,128)(2,1)} %get-tuple-element.287), channel_id=1, source_target_pairs={{0,2},{1,3},{2,0},{3,1},{4,6},{5,7},{6,4},{7,5},{8,10},{9,11},{10,... | collective-permute-start | bytes 2752520 | tf_op jit(solution)/shard_map/ppermute | solution.py:186
  677.2 43.7 %collective-permute-start.65 = (bf16[224,2048]{1,0:T(8,128)(2,1)}, bf16[224,2048]{1,0:T(8,128)(2,1)S(1)}, u32[]{:S(2)}, u32[]{:S(2)}) collective-permute-start(bf16[224,2048]{1,0:T(8,128)(2,1)} %get-tuple-element.288), channel_id=1, source_target_pairs={{0,3},{1,2},{2,1},{3,0},{4,7},{5,6},{6,5},{7,4},{8,11},{9,10},{10,... | collective-permute-start | bytes 2752520 | tf_op jit(solution)/shard_map/ppermute | solution.py:186
  (110 other events, 1816.6 us)

commit v6 on v4

--- a/solution.py
+++ b/solution.py
@@ -905,35 +905,41 @@
     def across(pieces):
         return [pieces[0]] + [swap(pieces[q], "row", row_count, 2 * q) for q in distances[1:]]
 
+    far_first = distances[pair_count // 2 :] + distances[: pair_count // 2]
+
+    def tie(crossed, other):
+        ordered, other = lax.optimization_barrier(([crossed[q] for q in far_first], other))
+        return [ordered[far_first.index(q)] for q in distances], other
+
     def gather_chunk(c, received):
         keep, give = pack_pair(
             meta, momentum_shards, received, c * wide, CHUNK, row_count, window
         )
         return join(meta, keep, swap(give, "row", row_count, 1), even, window, pair_count)
 
-    received, _ = fetch(0, row_count * CHUNK, shard_starts)
-    last, received = fetch(number * wide, pair_count * LAST, received)
+    last, _ = fetch(number * wide, pair_count * LAST, shard_starts)
+    received, last = fetch(0, row_count * CHUNK, last)
+    pieces = pack(
+        meta, momentum_shards, last, number * wide, LAST, 2, pair_count, window
+    )
+    crossed_last, received = tie(across(pieces), received)
     joined = gather_chunk(0, received)
     landed = []
     for c in range(1, number):
-        received, (last, joined) = fetch(c * wide, row_count * CHUNK, (last, joined))
-        crossed, received = lax.optimization_barrier((across(joined), received))
+        received, joined = fetch(c * wide, row_count * CHUNK, joined)
+        crossed, received = tie(across(joined), received)
         landed.append(crossed)
         joined = gather_chunk(c, received)
     landed.append(across(joined))
     matrices = [
         merge(meta, pieces, [[q] for q in distances], 2 * even, 2, jitter) for pieces in landed
     ]
-    pieces = pack(
-        meta, momentum_shards, last, number * wide, LAST, 2, pair_count, window
-    )
-    stack = jnp.concatenate(across(pieces), axis=0)
-    twin = swap(stack, "row", row_count, 1)
+    twin = [swap(piece, "row", row_count, 1) for piece in crossed_last]
     matrices.append(
         merge(
             meta,
-            [stack, twin],
-            [[2 * q for q in distances], [2 * q + 1 for q in distances]],
+            crossed_last + twin,
+            [[2 * q] for q in distances] + [[2 * q + 1] for q in distances],
             even,
             1,
             jitter,
@@ -948,18 +954,24 @@
     results = [first] + next_apply(meta, gram, matrices[1:], sends[1:], jitter)
 
     crossed = [across(results[0])]
-    crossed[0], results[1:] = lax.optimization_barrier((crossed[0], results[1:]))
-    crossed += [across(pieces) for pieces in results[1:]]
+    crossed[0], results[1:] = tie(crossed[0], results[1:])
+    for pieces in results[1:]:
+        crossed[-1], pieces = tie(crossed[-1], pieces)
+        crossed.append(across(pieces))
     backs = []
     for c in range(number + 1):
         if c < number:
             got = swap(cut(meta, crossed[c], even, window), "row", row_count, 1)
-            parts = unpack_pair(meta, crossed[c], got, col_count, slots, even, window)
+            parts = list(
+                unpack_pair(meta, crossed[c], got, col_count, slots, even, window)
+            )
         else:
             parts = unpack(meta, crossed[c], col_count, slots, 2)
+        if c + 1 == number:
+            crossed[c + 1], parts[0] = tie(crossed[c + 1], parts[0])
         back = [parts[0]] + [swap(parts[k], "col", col_count, k) for k in range(1, col_count)]
         if c + 1 < number:
-            back, crossed[c + 1 :] = lax.optimization_barrier((back, crossed[c + 1 :]))
+            crossed[c + 1], back = tie(crossed[c + 1], back)
         backs.append(back)
     out = jnp.zeros(momentum_shards.shape, jnp.bfloat16)
     for c, back in enumerate(backs):

time: 711 us -> 673 us (0.947); the launches traced: 701 us -> 670 us
  waiting for transfers between devices: 330 us -> 309 us
  starting transfers between devices: 125 us -> 114 us
    ppermute x69 -> x72, waiting for transfers between devices: 330 us -> 309 us  [swap(): lax.ppermute(value, axis, perm=[(i, i ^ distance) for i in range(size)])]
    ppermute x69 -> x72, starting transfers between devices: 125 us -> 114 us  [swap(): lax.ppermute(value, axis, perm=[(i, i ^ distance) for i in range(size)])]
    unnamed x123 -> x120, local copies, waits for them, and re-layouts: 22.6 us -> 21.3 us
  transfers between devices with their start and end apart: 69 -> 72, of which waited for: 33 -> 35; matrix products, arithmetic and copies ran while one was open for 2% -> 2% of each run, Pallas kernels for 19% -> 18%
where the time goes in v6:
time: 673 us; the launch traced here: 670 us
  waiting for transfers between devices  309 us (46%)
  Pallas kernels  205 us (30%)
  starting transfers between devices  114 us (17%)
  local copies, waits for them, and re-layouts  41 us (6%)
    ppermute x72, waiting for transfers between devices, swap(): lax.ppermute(value, axis, perm=[(i, i ^ distance) for i in range(size)])  309 us
    ppermute x72, starting transfers between devices, swap(): lax.ppermute(value, axis, perm=[(i, i ^ distance) for i in range(size)])  114 us
    pallas_call x14, Pallas kernels, local_call(): pl.pallas_call(kernel, out_shape=out_shape, in_specs=[pl.BlockSpec(memory...  42.6 us
    pallas_call x1, Pallas kernels, next_apply(): pl.pallas_call(lambda *refs: next_apply_kernel(jitter, sends, *refs), out...  35.1 us
    pallas_call x4, Pallas kernels, gridded(): pl.pallas_call(kernel, out_shape=outs, grid_spec=pltpu.PrefetchScalarGrid...  29.2 us
    pallas_call x2, Pallas kernels, half_gram(): pl.pallas_call(lambda *refs: half_gram_kernel(flip, *refs), out_shape=[ja...  28.2 us
    pallas_call x1, Pallas kernels, first_apply(): pl.pallas_call(lambda *refs: first_apply_kernel(jitter, send, *refs), out...  24.4 us
    unnamed x120, local copies, waits for them, and re-layouts  21.3 us
  transfers between devices with their start and end apart: 72, of which 35 were waited for; matrix products, arithmetic and copies ran while one was open for 2% of the time, Pallas kernels for 18%

profile of v6, /device:TPU:0, one launch (start us, length us, event | category | flops | bytes accessed | tf_op | source)
XLA Modules:
  0.0 670.3 jit_solution(4697718184251880276)
XLA Ops:
  48.0 12.3 %collective-permute-done.7.refs_3_ = bf16[224,2048]{1,0:T(8,128)(2,1)} collective-permute-done((bf16[224,2048]{1,0:T(8,128)(2,1)S(1)}, bf16[224,2048]{1,0:T(8,128)(2,1)}, u32[]{:S(2)}, u32[]{:S(2)}) %collective-permute-start.7) | collective-permute-done | bytes 917536 | tf_op jit(solution)/shard_map/ppermute | solution.py:186
  85.7 28.4 %collective-permute-done.10.refs_3_ = bf16[1008,256]{1,0:T(8,128)(2,1)S(1)} collective-permute-done((bf16[1008,256]{1,0:T(8,128)(2,1)}, bf16[1008,256]{1,0:T(8,128)(2,1)S(1)}, u32[]{:S(2)}, u32[]{:S(2)}) %collective-permute-start.10) | collective-permute-done | bytes 516128 | tf_op jit(solution)/shard_map/ppermute | solution.py:186
  114.1 12.3 %collective-permute-done.12.refs_2_ = bf16[1008,256]{1,0:T(8,128)(2,1)S(1)} collective-permute-done((bf16[1008,256]{1,0:T(8,128)(2,1)}, bf16[1008,256]{1,0:T(8,128)(2,1)S(1)}, u32[]{:S(2)}, u32[]{:S(2)}) %collective-permute-start.12) | collective-permute-done | bytes 516128 | tf_op jit(solution)/shard_map/ppermute | solution.py:186
  128.7 8.9 %shard_map.50 = (bf16[2240,256]{1,0:T(8,128)(2,1)}, bf16[2240,256]{1,0:T(8,128)(2,1)}) custom-call(s32[10]{0:T(128)} %pad_add_fusion.1.refs_0_.meta_ref.refs_2_, bf16[224,18432]{1,0:T(8,128)(2,1)} %refs_1_.8, bf16[224,2048]{1,0:T(8,128)(2,1)} %copy-done.12, bf16[224,2048]{1,0:T(8,128)(2,1)} %copy-done.13, bf16[224,2048]{1,0:T(8,128)(2,1)} %copy-done.14), custom_call_target="tpu_custom_call" | custom-call | flops 2055208960 | bytes 5963776 | tf_op jit(solution)/shard_map/pallas_call | solution.py:281
  160.2 9.3 %collective-permute-done.17.refs_2_ = bf16[1008,256]{1,0:T(8,128)(2,1)S(1)} collective-permute-done((bf16[1008,256]{1,0:T(8,128)(2,1)}, bf16[1008,256]{1,0:T(8,128)(2,1)S(1)}, u32[]{:S(2)}, u32[]{:S(2)}) %collective-permute-start.17) | collective-permute-done | bytes 516128 | tf_op jit(solution)/shard_map/ppermute | solution.py:186
  169.5 15.2 %collective-permute-done.18.refs_3_ = bf16[1008,256]{1,0:T(8,128)(2,1)S(1)} collective-permute-done((bf16[1008,256]{1,0:T(8,128)(2,1)}, bf16[1008,256]{1,0:T(8,128)(2,1)S(1)}, u32[]{:S(2)}, u32[]{:S(2)}) %collective-permute-start.18) | collective-permute-done | bytes 516128 | tf_op jit(solution)/shard_map/ppermute | solution.py:186
  194.1 14.1 %shard_map.56 = (bf16[3584,512]{1,0:T(8,128)(2,1)}, bf16[3584,512]{1,0:T(8,128)(2,1)}) custom-call(s32[28]{0:T(128)} %constant.61.clone.refs_0_, s32[28]{0:T(128)} %constant.62.clone.refs_1_, s32[10]{0:T(128)} %pad_add_fusion.1.refs_0_.meta_ref.refs_2_, bf16[3584,640]{1,0:T(8,128)(2,1)} %shard_map.54.refs_3_), custom_call_target="tpu_custom_call" | custom-call | flops 4697620480 | bytes 11927552 | tf_op jit(solution)/shard_map/pallas_call | solution.py:549
  208.8 14.1 %shard_map.55 = (bf16[3584,512]{1,0:T(8,128)(2,1)}, bf16[3584,512]{1,0:T(8,128)(2,1)}) custom-call(s32[28]{0:T(128)} %constant.61.clone.refs_0_, s32[28]{0:T(128)} %constant.62.clone.refs_1_, s32[10]{0:T(128)} %pad_add_fusion.1.refs_0_.meta_ref.refs_2_, bf16[3584,640]{1,0:T(8,128)(2,1)} %shard_map.54.refs_3_), custom_call_target="tpu_custom_call" | custom-call | flops 4697620480 | bytes 11927552 | tf_op jit(solution)/shard_map/pallas_call | solution.py:549
  245.4 10.5 %collective-permute-done.26.refs_2_ = bf16[3584,128]{1,0:T(8,128)(2,1)S(1)} collective-permute-done((bf16[3584,128]{1,0:T(8,128)(2,1)}, bf16[3584,128]{1,0:T(8,128)(2,1)S(1)}, u32[]{:S(2)}, u32[]{:S(2)}) %collective-permute-start.26) | collective-permute-done | bytes 917536 | tf_op jit(solution)/shard_map/ppermute | solution.py:186
  255.9 19.0 %collective-permute-done.27.refs_3_ = bf16[3584,128]{1,0:T(8,128)(2,1)S(1)} collective-permute-done((bf16[3584,128]{1,0:T(8,128)(2,1)}, bf16[3584,128]{1,0:T(8,128)(2,1)S(1)}, u32[]{:S(2)}, u32[]{:S(2)}) %collective-permute-start.27) | collective-permute-done | bytes 917536 | tf_op jit(solution)/shard_map/ppermute | solution.py:186
  281.8 10.6 %collective-permute-start.32 = (bf16[896,128]{1,0:T(8,128)(2,1)}, bf16[896,128]{1,0:T(8,128)(2,1)S(1)}, u32[]{:S(2)}, u32[]{:S(2)}) collective-permute-start(bf16[896,128]{1,0:T(8,128)(2,1)} %get-tuple-element.216), channel_id=1, source_target_pairs={{0,8},{4,12},{8,0},{12,4},{16,24},{20,28},{24,16},{28,20},{1,9},{5... | collective-permute-start | bytes 688136 | tf_op jit(solution)/shard_map/ppermute | solution.py:186
  301.8 8.9 %collective-permute-done.33.refs_2_ = bf16[896,128]{1,0:T(8,128)(2,1)S(1)} collective-permute-done((bf16[896,128]{1,0:T(8,128)(2,1)}, bf16[896,128]{1,0:T(8,128)(2,1)S(1)}, u32[]{:S(2)}, u32[]{:S(2)}) %collective-permute-start.33) | collective-permute-done | bytes 229408 | tf_op jit(solution)/shard_map/ppermute | solution.py:186
  319.3 10.6 %collective-permute-start.35 = (bf16[896,128]{1,0:T(8,128)(2,1)}, bf16[896,128]{1,0:T(8,128)(2,1)S(1)}, u32[]{:S(2)}, u32[]{:S(2)}) collective-permute-start(bf16[896,128]{1,0:T(8,128)(2,1)} %shard_map.60.refs_0_), channel_id=1, source_target_pairs={{0,8},{4,12},{8,0},{12,4},{16,24},{20,28},{24,16},{28,20},{1,9},{5... | collective-permute-start | bytes 688136 | tf_op jit(solution)/shard_map/ppermute | solution.py:186
  337.1 11.6 %collective-permute-done.36.refs_2_ = bf16[896,128]{1,0:T(8,128)(2,1)S(1)} collective-permute-done((bf16[896,128]{1,0:T(8,128)(2,1)}, bf16[896,128]{1,0:T(8,128)(2,1)S(1)}, u32[]{:S(2)}, u32[]{:S(2)}) %collective-permute-start.36) | collective-permute-done | bytes 229408 | tf_op jit(solution)/shard_map/ppermute | solution.py:186
  360.7 12.7 %collective-permute-done.39.refs_2_ = bf16[896,128]{1,0:T(8,128)(2,1)S(1)} collective-permute-done((bf16[896,128]{1,0:T(8,128)(2,1)}, bf16[896,128]{1,0:T(8,128)(2,1)S(1)}, u32[]{:S(2)}, u32[]{:S(2)}) %collective-permute-start.39) | collective-permute-done | bytes 229408 | tf_op jit(solution)/shard_map/ppermute | solution.py:186
  413.0 13.1 %collective-permute-done.47.refs_1_ = bf16[3584,128]{1,0:T(8,128)(2,1)S(1)} collective-permute-done((bf16[3584,128]{1,0:T(8,128)(2,1)}, bf16[3584,128]{1,0:T(8,128)(2,1)S(1)}, u32[]{:S(2)}, u32[]{:S(2)}) %collective-permute-start.47) | collective-permute-done | bytes 917536 | tf_op jit(solution)/shard_map/ppermute | solution.py:186
  426.1 16.5 %collective-permute-done.48.refs_2_ = bf16[3584,128]{1,0:T(8,128)(2,1)S(1)} collective-permute-done((bf16[3584,128]{1,0:T(8,128)(2,1)}, bf16[3584,128]{1,0:T(8,128)(2,1)S(1)}, u32[]{:S(2)}, u32[]{:S(2)}) %collective-permute-start.48) | collective-permute-done | bytes 917536 | tf_op jit(solution)/shard_map/ppermute | solution.py:186
  459.9 24.4 %shard_map.67 = (bf16[1008,256]{1,0:T(8,128)(2,1)}, bf16[1008,256]{1,0:T(8,128)(2,1)}, bf16[1008,256]{1,0:T(8,128)(2,1)}, bf16[1008,256]{1,0:T(8,128)(2,1)}, bf16[7,512,3584]{2,1,0:T(8,128)(2,1)}) custom-call(s32[28]{0:T(128)} %constant.61.clone.refs_0_, s32[28]{0:T(128)} %constant.62.clone.refs_1_, s32[10]{0:T(128)} %pad_add_fusion.1.refs_0_.meta_ref.refs_2_, ...), custom_call_target="tpu_custom_call" | custom-call | flops 13153337344 | bytes 55050240 | tf_op jit(solution)/shard_map/pallas_call | solution.py:746
  493.9 35.1 %shard_map.68 = (bf16[1008,256]{1,0:T(8,128)(2,1)}, bf16[1008,256]{1,0:T(8,128)(2,1)}, bf16[1008,256]{1,0:T(8,128)(2,1)}, bf16[1008,256]{1,0:T(8,128)(2,1)}, bf1...) custom-call(s32[10]{0:T(128)} %pad_add_fusion.1.refs_0_.meta_ref.refs_2_,, ...), custom_call_target="tpu_custom_call" | custom-call | flops 19730006016 | bytes 56885248 | tf_op jit(solution)/shard_map/pallas_call | solution.py:801
  532.8 9.6 %collective-permute-start.55 = (bf16[1008,256]{1,0:T(8,128)(2,1)}, bf16[1008,256]{1,0:T(8,128)(2,1)S(1)}, u32[]{:S(2)}, u32[]{:S(2)}) collective-permute-start(bf16[1008,256]{1,0:T(8,128)(2,1)} %get-tuple-element.264), channel_id=1, source_target_pairs={{0,16},{4,20},{8,24},{12,28},{16,0},{20,4},{24,8},{28,12},{1,17},{... | collective-permute-start | bytes 1548296 | tf_op jit(solution)/shard_map/ppermute | solution.py:186
  543.3 9.0 %shard_map.70 = (bf16[224,2048]{1,0:T(8,128)(2,1)}, bf16[224,2048]{1,0:T(8,128)(2,1)}, bf16[224,2048]{1,0:T(8,128)(2,1)}, bf16[224,2048]{1,0:T(8,128)(2,1)}) custom-call(s32[10]{0:T(128)} %pad_add_fusion.1.refs_0_.meta_ref.refs_2_, bf16[1008,256]{1,0:T(8,128)(2,1)} %get-tuple-element.276.refs_1_, bf16[1008,256]{1,0:T(8,128)(2,1)} %copy-done.32, ...), custom_call_target="tpu_custom_call" | custom-call | flops 2055208960 | bytes 5963776 | tf_op jit(solution)/shard_map/pallas_call | solution.py:405
  557.1 20.1 %collective-permute-done.55.refs_3_ = bf16[1008,256]{1,0:T(8,128)(2,1)S(1)} collective-permute-done((bf16[1008,256]{1,0:T(8,128)(2,1)}, bf16[1008,256]{1,0:T(8,128)(2,1)S(1)}, u32[]{:S(2)}, u32[]{:S(2)}) %collective-permute-start.55) | collective-permute-done | bytes 516128 | tf_op jit(solution)/shard_map/ppermute | solution.py:186
  577.3 13.5 %collective-permute-done.57.refs_2_ = bf16[1008,256]{1,0:T(8,128)(2,1)S(1)} collective-permute-done((bf16[1008,256]{1,0:T(8,128)(2,1)S(1)}, bf16[1008,256]{1,0:T(8,128)(2,1)S(1)}, u32[]{:S(2)}, u32[]{:S(2)}) %collective-permute-start.57) | collective-permute-done | bytes 516128 | tf_op jit(solution)/shard_map/ppermute | solution.py:186
  638.9 18.9 %collective-permute-done.67 = bf16[224,2048]{1,0:T(8,128)(2,1)} collective-permute-done((bf16[224,2048]{1,0:T(8,128)(2,1)}, bf16[224,2048]{1,0:T(8,128)(2,1)}, u32[]{:S(2)}, u32[]{:S(2)}) %collective-permute-start.67) | collective-permute-done | bytes 917536 | tf_op jit(solution)/shard_map/ppermute | solution.py:186
  (292 shorter events, 311.2 us)
Async XLA Ops:
  19.5 40.7 %collective-permute-start.7 = (bf16[224,2048]{1,0:T(8,128)(2,1)S(1)}, bf16[224,2048]{1,0:T(8,128)(2,1)}, u32[]{:S(2)}, u32[]{:S(2)}) collective-permute-start(bf16[224,2048]{1,0:T(8,128)(2,1)S(1)} %get-tuple-element.313), channel_id=1, source_target_pairs={{0,2},{1,3},{2,0},{3,1},{4,6},{5,7},{6,4},{7,5},{8,10},{9,11},{10,... | collective-permute-start | bytes 2752520 | tf_op jit(solution)/shard_map/ppermute | solution.py:186
  20.4 39.8 %collective-permute-start.8 = (bf16[224,2048]{1,0:T(8,128)(2,1)S(1)}, bf16[224,2048]{1,0:T(8,128)(2,1)}, u32[]{:S(2)}, u32[]{:S(2)}) collective-permute-start(bf16[224,2048]{1,0:T(8,128)(2,1)S(1)} %get-tuple-element.312), channel_id=1, source_target_pairs={{0,3},{1,2},{2,1},{3,0},{4,7},{5,6},{6,5},{7,4},{8,11},{9,10},{10,... | collective-permute-start | bytes 2752520 | tf_op jit(solution)/shard_map/ppermute | solution.py:186
  80.8 45.6 %collective-permute-start.13 = (bf16[224,2048]{1,0:T(8,128)(2,1)S(1)}, bf16[224,2048]{1,0:T(8,128)(2,1)S(1)}, u32[]{:S(2)}, u32[]{:S(2)}) collective-permute-start(bf16[224,2048]{1,0:T(8,128)(2,1)S(1)} %get-tuple-element.311), channel_id=1, source_target_pairs={{0,1},{1,0},{2,3},{3,2},{4,5},{5,4},{6,7},{7,6},{8,9},{9,8},{10,11... | collective-permute-start | bytes 2752520 | tf_op jit(solution)/shard_map/ppermute | solution.py:186
  81.4 45.0 %collective-permute-start.14 = (bf16[224,2048]{1,0:T(8,128)(2,1)S(1)}, bf16[224,2048]{1,0:T(8,128)(2,1)S(1)}, u32[]{:S(2)}, u32[]{:S(2)}) collective-permute-start(bf16[224,2048]{1,0:T(8,128)(2,1)S(1)} %get-tuple-element.310), channel_id=1, source_target_pairs={{0,2},{1,3},{2,0},{3,1},{4,6},{5,7},{6,4},{7,5},{8,10},{9,11},{10,... | collective-permute-start | bytes 2752520 | tf_op jit(solution)/shard_map/ppermute | solution.py:186
  82.6 43.9 %collective-permute-start.15 = (bf16[224,2048]{1,0:T(8,128)(2,1)S(1)}, bf16[224,2048]{1,0:T(8,128)(2,1)S(1)}, u32[]{:S(2)}, u32[]{:S(2)}) collective-permute-start(bf16[224,2048]{1,0:T(8,128)(2,1)S(1)} %get-tuple-element.309), channel_id=1, source_target_pairs={{0,3},{1,2},{2,1},{3,0},{4,7},{5,6},{6,5},{7,4},{8,11},{9,10},{10,... | collective-permute-start | bytes 2752520 | tf_op jit(solution)/shard_map/ppermute | solution.py:186
  146.4 38.2 %collective-permute-start.18 = (bf16[1008,256]{1,0:T(8,128)(2,1)}, bf16[1008,256]{1,0:T(8,128)(2,1)S(1)}, u32[]{:S(2)}, u32[]{:S(2)}) collective-permute-start(bf16[1008,256]{1,0:T(8,128)(2,1)} %get-tuple-element.191), channel_id=1, source_target_pairs={{0,16},{4,20},{8,24},{12,28},{16,0},{20,4},{24,8},{28,12},{1,17},{... | collective-permute-start | bytes 1548296 | tf_op jit(solution)/shard_map/ppermute | solution.py:186
  233.1 41.9 %collective-permute-start.27 = (bf16[3584,128]{1,0:T(8,128)(2,1)}, bf16[3584,128]{1,0:T(8,128)(2,1)S(1)}, u32[]{:S(2)}, u32[]{:S(2)}) collective-permute-start(bf16[3584,128]{1,0:T(8,128)(2,1)} %get-tuple-element.207), channel_id=1, source_target_pairs={{0,2},{1,3},{2,0},{3,1},{4,6},{5,7},{6,4},{7,5},{8,10},{9,11},{10,... | collective-permute-start | bytes 2752520 | tf_op jit(solution)/shard_map/ppermute | solution.py:186
  234.2 40.7 %collective-permute-start.28 = (bf16[3584,128]{1,0:T(8,128)(2,1)}, bf16[3584,128]{1,0:T(8,128)(2,1)S(1)}, u32[]{:S(2)}, u32[]{:S(2)}) collective-permute-start(bf16[3584,128]{1,0:T(8,128)(2,1)} %get-tuple-element.208), channel_id=1, source_target_pairs={{0,3},{1,2},{2,1},{3,0},{4,7},{5,6},{6,5},{7,4},{8,11},{9,10},{10,... | collective-permute-start | bytes 2752520 | tf_op jit(solution)/shard_map/ppermute | solution.py:186
  276.5 38.9 %collective-permute-start.30 = (bf16[3584,128]{1,0:T(8,128)(2,1)}, bf16[3584,128]{1,0:T(8,128)(2,1)S(1)}, u32[]{:S(2)}, u32[]{:S(2)}) collective-permute-start(bf16[3584,128]{1,0:T(8,128)(2,1)} %get-tuple-element.214), channel_id=1, source_target_pairs={{0,2},{1,3},{2,0},{3,1},{4,6},{5,7},{6,4},{7,5},{8,10},{9,11},{10,... | collective-permute-start | bytes 2752520 | tf_op jit(solution)/shard_map/ppermute | solution.py:186
  277.0 39.9 %collective-permute-start.31 = (bf16[3584,128]{1,0:T(8,128)(2,1)}, bf16[3584,128]{1,0:T(8,128)(2,1)S(1)}, u32[]{:S(2)}, u32[]{:S(2)}) collective-permute-start(bf16[3584,128]{1,0:T(8,128)(2,1)} %get-tuple-element.215), channel_id=1, source_target_pairs={{0,3},{1,2},{2,1},{3,0},{4,7},{5,6},{6,5},{7,4},{8,11},{9,10},{10,... | collective-permute-start | bytes 2752520 | tf_op jit(solution)/shard_map/ppermute | solution.py:186
  354.1 45.2 %collective-permute-start.44 = (bf16[3584,128]{1,0:T(8,128)(2,1)}, bf16[3584,128]{1,0:T(8,128)(2,1)S(1)}, u32[]{:S(2)}, u32[]{:S(2)}) collective-permute-start(bf16[3584,128]{1,0:T(8,128)(2,1)} %shard_map.62.refs_0_), channel_id=1, source_target_pairs={{0,1},{1,0},{2,3},{3,2},{4,5},{5,4},{6,7},{7,6},{8,9},{9,8},{10,11... | collective-permute-start | bytes 2752520 | tf_op jit(solution)/shard_map/ppermute | solution.py:186
  354.5 44.8 %collective-permute-start.45 = (bf16[3584,128]{1,0:T(8,128)(2,1)}, bf16[3584,128]{1,0:T(8,128)(2,1)S(1)}, u32[]{:S(2)}, u32[]{:S(2)}) collective-permute-start(bf16[3584,128]{1,0:T(8,128)(2,1)} %shard_map.62.refs_0_), channel_id=1, source_target_pairs={{0,2},{1,3},{2,0},{3,1},{4,6},{5,7},{6,4},{7,5},{8,10},{9,11},{10,... | collective-permute-start | bytes 2752520 | tf_op jit(solution)/shard_map/ppermute | solution.py:186
  355.3 44.0 %collective-permute-start.46 = (bf16[3584,128]{1,0:T(8,128)(2,1)}, bf16[3584,128]{1,0:T(8,128)(2,1)S(1)}, u32[]{:S(2)}, u32[]{:S(2)}) collective-permute-start(bf16[3584,128]{1,0:T(8,128)(2,1)} %shard_map.62.refs_0_), channel_id=1, source_target_pairs={{0,3},{1,2},{2,1},{3,0},{4,7},{5,6},{6,5},{7,4},{8,11},{9,10},{10,... | collective-permute-start | bytes 2752520 | tf_op jit(solution)/shard_map/ppermute | solution.py:186
  402.9 39.6 %collective-permute-start.48 = (bf16[3584,128]{1,0:T(8,128)(2,1)}, bf16[3584,128]{1,0:T(8,128)(2,1)S(1)}, u32[]{:S(2)}, u32[]{:S(2)}) collective-permute-start(bf16[3584,128]{1,0:T(8,128)(2,1)} %shard_map.65.refs_0_), channel_id=1, source_target_pairs={{0,2},{1,3},{2,0},{3,1},{4,6},{5,7},{6,4},{7,5},{8,10},{9,11},{10,... | collective-permute-start | bytes 2752520 | tf_op jit(solution)/shard_map/ppermute | solution.py:186
  403.8 38.8 %collective-permute-start.49 = (bf16[3584,128]{1,0:T(8,128)(2,1)}, bf16[3584,128]{1,0:T(8,128)(2,1)S(1)}, u32[]{:S(2)}, u32[]{:S(2)}) collective-permute-start(bf16[3584,128]{1,0:T(8,128)(2,1)} %shard_map.65.refs_0_), channel_id=1, source_target_pairs={{0,3},{1,2},{2,1},{3,0},{4,7},{5,6},{6,5},{7,4},{8,11},{9,10},{10,... | collective-permute-start | bytes 2752520 | tf_op jit(solution)/shard_map/ppermute | solution.py:186
  413.0 38.4 %collective-permute-start.50 = (bf16[3584,512]{1,0:T(8,128)(2,1)}, bf16[3584,512]{1,0:T(8,128)(2,1)}, u32[]{:S(2)}, u32[]{:S(2)}) collective-permute-start(bf16[3584,512]{1,0:T(8,128)(2,1)} %shard_map.64.refs_3_), channel_id=1, source_target_pairs={{0,4},{4,0},{8,12},{12,8},{16,20},{20,16},{24,28},{28,24},{1,5},{5... | collective-permute-start | bytes 11010056 | tf_op jit(solution)/shard_map/ppermute | solution.py:186
  484.3 44.8 %collective-permute-start.52 = (bf16[1008,256]{1,0:T(8,128)(2,1)}, bf16[1008,256]{1,0:T(8,128)(2,1)S(1)}, u32[]{:S(2)}, u32[]{:S(2)}) collective-permute-start(bf16[1008,256]{1,0:T(8,128)(2,1)} %get-tuple-element.243), channel_id=1, source_target_pairs={{0,16},{4,20},{8,24},{12,28},{16,0},{20,4},{24,8},{28,12},{1,17},{... | collective-permute-start | bytes 1548296 | tf_op jit(solution)/shard_map/ppermute | solution.py:186
  532.8 44.5 %collective-permute-start.55 = (bf16[1008,256]{1,0:T(8,128)(2,1)}, bf16[1008,256]{1,0:T(8,128)(2,1)S(1)}, u32[]{:S(2)}, u32[]{:S(2)}) collective-permute-start(bf16[1008,256]{1,0:T(8,128)(2,1)} %get-tuple-element.264), channel_id=1, source_target_pairs={{0,16},{4,20},{8,24},{12,28},{16,0},{20,4},{24,8},{28,12},{1,17},{... | collective-permute-start | bytes 1548296 | tf_op jit(solution)/shard_map/ppermute | solution.py:186
  552.3 38.5 %collective-permute-start.59 = (bf16[224,2048]{1,0:T(8,128)(2,1)}, bf16[224,2048]{1,0:T(8,128)(2,1)}, u32[]{:S(2)}, u32[]{:S(2)}) collective-permute-start(bf16[224,2048]{1,0:T(8,128)(2,1)} %get-tuple-element.281), channel_id=1, source_target_pairs={{0,1},{1,0},{2,3},{3,2},{4,5},{5,4},{6,7},{7,6},{8,9},{9,8},{10,11... | collective-permute-start | bytes 2752520 | tf_op jit(solution)/shard_map/ppermute | solution.py:186
  554.0 42.2 %collective-permute-start.60 = (bf16[224,2048]{1,0:T(8,128)(2,1)}, bf16[224,2048]{1,0:T(8,128)(2,1)}, u32[]{:S(2)}, u32[]{:S(2)}) collective-permute-start(bf16[224,2048]{1,0:T(8,128)(2,1)} %get-tuple-element.282), channel_id=1, source_target_pairs={{0,2},{1,3},{2,0},{3,1},{4,6},{5,7},{6,4},{7,5},{8,10},{9,11},{10,... | collective-permute-start | bytes 2752520 | tf_op jit(solution)/shard_map/ppermute | solution.py:186
  554.3 41.9 %collective-permute-start.61 = (bf16[224,2048]{1,0:T(8,128)(2,1)}, bf16[224,2048]{1,0:T(8,128)(2,1)}, u32[]{:S(2)}, u32[]{:S(2)}) collective-permute-start(bf16[224,2048]{1,0:T(8,128)(2,1)} %get-tuple-element.283), channel_id=1, source_target_pairs={{0,3},{1,2},{2,1},{3,0},{4,7},{5,6},{6,5},{7,4},{8,11},{9,10},{10,... | collective-permute-start | bytes 2752520 | tf_op jit(solution)/shard_map/ppermute | solution.py:186
  614.5 43.3 %collective-permute-start.67 = (bf16[224,2048]{1,0:T(8,128)(2,1)}, bf16[224,2048]{1,0:T(8,128)(2,1)}, u32[]{:S(2)}, u32[]{:S(2)}) collective-permute-start(bf16[224,2048]{1,0:T(8,128)(2,1)} %get-tuple-element.299), channel_id=1, source_target_pairs={{0,2},{1,3},{2,0},{3,1},{4,6},{5,7},{6,4},{7,5},{8,10},{9,11},{10,... | collective-permute-start | bytes 2752520 | tf_op jit(solution)/shard_map/ppermute | solution.py:186
  617.3 41.8 %collective-permute-start.68 = (bf16[224,2048]{1,0:T(8,128)(2,1)}, bf16[224,2048]{1,0:T(8,128)(2,1)}, u32[]{:S(2)}, u32[]{:S(2)}) collective-permute-start(bf16[224,2048]{1,0:T(8,128)(2,1)} %get-tuple-element.300), channel_id=1, source_target_pairs={{0,3},{1,2},{2,1},{3,0},{4,7},{5,6},{6,5},{7,4},{8,11},{9,10},{10,... | collective-permute-start | bytes 2752520 | tf_op jit(solution)/shard_map/ppermute | solution.py:186
  625.9 40.3 %collective-permute-start.70 = (bf16[224,512]{1,0:T(8,128)(2,1)}, bf16[224,512]{1,0:T(8,128)(2,1)S(1)}, u32[]{:S(2)}, u32[]{:S(2)}) collective-permute-start(bf16[224,512]{1,0:T(8,128)(2,1)} %get-tuple-element.307), channel_id=1, source_target_pairs={{0,2},{1,3},{2,0},{3,1},{4,6},{5,7},{6,4},{7,5},{8,10},{9,11},{10,... | collective-permute-start | bytes 688136 | tf_op jit(solution)/shard_map/ppermute | solution.py:186
  (108 other events, 1717.8 us)

commit v7 on v6

--- a/solution.py
+++ b/solution.py
@@ -568,36 +568,31 @@
     return pl.ds(pl.multiple_of(block * lanes, lanes), lanes)
 
 
-def add_halves_kernel(meta_ref, keep, got, *outs):
-    lanes = outs[0].shape[1]
-    for k, out in enumerate(outs):
-        part = lane_block(meta_ref[1] ^ k, lanes)
-        out[...] = (keep[:, part].astype(jnp.float32) + got[:, part].astype(jnp.float32)).astype(
-            jnp.bfloat16
-        )
-
-
-def gridded(kernel, meta, operands, outs, moved):
-    rows = operands[0].shape[0]
-    block = lambda x: pl.BlockSpec((TILE, x.shape[1]), lambda t, meta: (t, 0))
+def add_halves_kernel(meta_ref, *refs):
+    count = len(refs) // 3
+    for keep, got, out in zip(refs[:count], refs[count : 2 * count], refs[2 * count :]):
+        out[...] = keep[...] + got[...]
+
+
+def add_halves(meta, keep, got, col_count):
+    rows, lanes = keep.shape
+    lanes //= col_count
+    tall = rows // 4
+    place = lambda k: lambda t, meta: (t, meta[1] ^ k)
     return pl.pallas_call(
-        kernel,
-        out_shape=outs,
+        add_halves_kernel,
+        out_shape=[jax.ShapeDtypeStruct((rows, lanes), jnp.bfloat16)] * col_count,
         grid_spec=pltpu.PrefetchScalarGridSpec(
             num_scalar_prefetch=1,
-            grid=(rows // TILE,),
-            in_specs=[block(x) for x in operands],
-            out_specs=jax.tree.map(block, outs),
+            grid=(rows // tall,),
+            in_specs=[pl.BlockSpec((tall, lanes), place(k)) for k in range(col_count)] * 2,
+            out_specs=[pl.BlockSpec((tall, lanes), lambda t, meta: (t, 0))] * col_count,
         ),
         compiler_params=pltpu.CompilerParams(vmem_limit_bytes=VMEM_LIMIT),
-        cost_estimate=pl.CostEstimate(flops=moved, bytes_accessed=moved, transcendentals=0),
-    )(meta, *operands)
-
-
-def add_halves(meta, keep, got, col_count):
-    rows, lanes = keep.shape
-    shape = jax.ShapeDtypeStruct((rows, lanes // col_count), jnp.bfloat16)
-    return gridded(add_halves_kernel, meta, (keep, got), [shape] * col_count, 6 * rows * lanes)
+        cost_estimate=pl.CostEstimate(
+            flops=keep.size, bytes_accessed=6 * keep.size, transcendentals=0
+        ),
+    )(meta, *[keep] * col_count, *[got] * col_count)
 
 
 def total_of(refs, part):
@@ -657,18 +652,6 @@
     )
 
 
-def widen_kernel(meta_ref, *refs):
-    blocks, out = refs[:-1], refs[-1]
-    for k, block in enumerate(blocks):
-        out[:, lane_block(meta_ref[1] ^ k, block.shape[1])] = block[...]
-
-
-def widen(meta, blocks):
-    rows, lanes = blocks[0].shape
-    shape = jax.ShapeDtypeStruct((rows, lanes * len(blocks)), jnp.bfloat16)
-    return gridded(widen_kernel, meta, blocks, shape, 4 * rows * lanes * len(blocks))
-
-
 def tile_rows(b):
     return pl.ds(pl.multiple_of(b * TILE, TILE), TILE)
 
@@ -701,25 +684,36 @@
         out[...] = total[place, :].astype(jnp.bfloat16)
 
 
-def first_apply_kernel(jitter, send, rows_ref, cols_ref, meta_ref, *refs):
-    pieces, matrix = refs[: 2 * PIECES], refs[2 * PIECES]
-    outs, gram_out = refs[2 * PIECES + 1 : -6], refs[-6]
+def first_apply_kernel(jitter, send, col_count, rows_ref, cols_ref, meta_ref, *refs):
+    count = 2 * PIECES * col_count
+    blocks, matrix, outs, gram_out = refs[:count], refs[count], refs[count + 1 : -6], refs[-6]
     gram, total, factor, tile_sems, out_sem = refs[-5:]
-    copies = []
+    lanes = TILE // col_count
+    tiles = []
     for n in range(2 * HALF):
         half, part = divmod(n, HALF)
         pair = (meta_ref[0] % 2 ^ half) * HALF + part
         i, j = rows_ref[pair], cols_ref[pair]
-        copy = pltpu.make_async_copy(
-            pieces[half * PIECES + part // PART].at[pl.ds(part % PART * TILE, TILE), :],
-            gram.at[i, :, lane_block(j, TILE)],
-            tile_sems.at[n],
-        )
-        copy.start()
-        copies.append((copy, i, j))
+        rows = pl.ds(part % PART * TILE, TILE)
+        first = (half * PIECES + part // PART) * col_count
+        moves = [
+            (
+                blocks[first + k].at[rows, :],
+                gram.at[i, :, lane_block(j * col_count + (meta_ref[1] ^ k), lanes)],
+            )
+            for k in range(col_count)
+        ]
+        copies = [
+            pltpu.make_async_copy(source, target, tile_sems.at[n, k])
+            for k, (source, target) in enumerate(moves)
+        ]
+        for copy in copies:
+            copy.start()
+        tiles.append((copies, i, j))
     clear_edges(total, jitter)
-    for copy, i, j in copies:
-        copy.wait()
+    for copies, i, j in tiles:
+        for copy in copies:
+            copy.wait()
 
         @pl.when(i != j)
         def _():
@@ -740,11 +734,13 @@
     back.wait()
 
 
-def first_apply(meta, pieces, matrix, send, jitter):
+def first_apply(meta, own, twin, matrix, send, jitter):
+    pieces = [*own, *twin]
+    col_count = len(own) // PIECES
     width = matrix.shape[1]
     whole = pl.BlockSpec(memory_space=pltpu.VMEM)
     outs = pl.pallas_call(
-        lambda *refs: first_apply_kernel(jitter, send, *refs),
+        lambda *refs: first_apply_kernel(jitter, send, col_count, *refs),
         out_shape=[jax.ShapeDtypeStruct((send[2], width), jnp.bfloat16)] * len(send[3])
         + [jax.ShapeDtypeStruct((BLOCKS, TILE, M), jnp.bfloat16)],
         in_specs=[pl.BlockSpec(memory_space=pltpu.SMEM)] * 3
@@ -755,7 +751,7 @@
             pltpu.VMEM((BLOCKS, TILE, M), jnp.bfloat16),
             pltpu.VMEM((M + 2 * jitter, width), jnp.float32),
             pltpu.VMEM((M, width), jnp.bfloat16),
-            pltpu.SemaphoreType.DMA((len(PAIRS),)),
+            pltpu.SemaphoreType.DMA((len(PAIRS), col_count)),
             pltpu.SemaphoreType.DMA,
         ],
         compiler_params=pltpu.CompilerParams(vmem_limit_bytes=VMEM_LIMIT),
@@ -845,11 +841,10 @@
     late_in = over_cols(late)
     early_parts = add_quarters(meta, [early[0]] + early_in, pair_count)
     early_in = over_pairs(early_parts)
-    late_in, early_in = tie((late_in, early_in))
     early_part = add_parts(meta, [early_parts[0]] + early_in)
     early_in = over_pairs([early_part] * pair_count)
+    late_in, early_in = tie((late_in, early_in))
     late_parts = add_quarters(meta, [late[0]] + late_in, pair_count)
-    late_parts, early_in = tie((late_parts, early_in))
     early_block = stack(meta, [early_part] + early_in)
     early_in = over_cols([early_block] * col_count)
     late_in = over_pairs(late_parts)
@@ -858,11 +853,11 @@
     late_in, early_in = tie((late_in, early_in))
     late_block = stack(meta, [late_part] + late_in)
     late_in = over_cols([late_block] * col_count)
-    early = widen(meta, [early_block] + early_in)
-    early_twin = swap(early, "row", row_count, 1)
-    late = widen(meta, [late_block] + late_in)
-    late_twin = swap(late, "row", row_count, 1)
-    return [early, late, early_twin, late_twin]
+    early = [early_block] + early_in
+    early_twin = [swap(block, "row", row_count, 1) for block in early]
+    late = [late_block] + late_in
+    late_twin = [swap(block, "row", row_count, 1) for block in late]
+    return early + late, early_twin + late_twin
 
 
 def chunk_body(momentum_shards, shard_starts):
@@ -950,7 +945,7 @@
 
     sends = [(2 * even, 2, even + window, distances)] * number
     sends.append((even, 1, window, [2 * q for q in distances]))
-    first, gram = first_apply(meta, tiles, matrices[0], sends[0], jitter)
+    first, gram = first_apply(meta, *tiles, matrices[0], sends[0], jitter)
     results = [first] + next_apply(meta, gram, matrices[1:], sends[1:], jitter)
 
     crossed = [across(results[0])]

time: 673 us -> 656 us (0.975)
  Pallas kernels: 205 us -> 190 us
  starting transfers between devices: 114 us -> 107 us
    pallas_call x5 -> x3, Pallas kernels: 53.6 us -> 38.4 us  [the longest x1 25.4 us: first_apply(): pl.pallas_call(lambda *refs: first_apply_kernel(jitter, send, col_count,...]
    ppermute x72 -> x78, starting transfers between devices: 114 us -> 107 us  [swap(): lax.ppermute(value, axis, perm=[(i, i ^ distance) for i in range(size)])]
    ppermute x72 -> x78, waiting for transfers between devices: 309 us -> 314 us  [swap(): lax.ppermute(value, axis, perm=[(i, i ^ distance) for i in range(size)])]
    unnamed x120 -> x132, local copies, waits for them, and re-layouts: 21.3 us -> 22.1 us
  transfers between devices with their start and end apart: 72 -> 78, of which waited for: 35 -> 38; matrix products, arithmetic and copies ran while one was open for 2% -> 3% of each run, Pallas kernels for 18% -> 16%
where the time goes in v7:
time: 656 us; the launch traced here: 654 us
  waiting for transfers between devices  314 us (48%)
  Pallas kernels  190 us (29%)
  starting transfers between devices  107 us (16%)
  local copies, waits for them, and re-layouts  41.8 us (6%)
    ppermute x78, waiting for transfers between devices, swap(): lax.ppermute(value, axis, perm=[(i, i ^ distance) for i in range(size)])  314 us
    ppermute x78, starting transfers between devices, swap(): lax.ppermute(value, axis, perm=[(i, i ^ distance) for i in range(size)])  107 us
    pallas_call x14, Pallas kernels, local_call(): pl.pallas_call(kernel, out_shape=out_shape, in_specs=[pl.BlockSpec(memory...  42.3 us
    pallas_call x1, Pallas kernels, next_apply(): pl.pallas_call(lambda *refs: next_apply_kernel(jitter, sends, *refs), out...  35.1 us
    pallas_call x2, Pallas kernels, half_gram(): pl.pallas_call(lambda *refs: half_gram_kernel(flip, *refs), out_shape=[ja...  28.2 us
    pallas_call x1, Pallas kernels, first_apply(): pl.pallas_call(lambda *refs: first_apply_kernel(jitter, send, col_count,...  25.4 us
    unnamed x132, local copies, waits for them, and re-layouts  22.1 us
    pallas_call x2, Pallas kernels, pack_pair(): pl.pallas_call(lambda *refs: pack_pair_kernel(col_count, *refs), out_shap...  17.8 us
  transfers between devices with their start and end apart: 78, of which 38 were waited for; matrix products, arithmetic and copies ran while one was open for 3% of the time, Pallas kernels for 16%

profile of v7, /device:TPU:0, one launch (start us, length us, event | category | flops | bytes accessed | tf_op | source)
XLA Modules:
  0.0 653.7 jit_solution(6171638814705520588)
XLA Ops:
  47.9 12.3 %collective-permute-done.7.refs_3_ = bf16[224,2048]{1,0:T(8,128)(2,1)} collective-permute-done((bf16[224,2048]{1,0:T(8,128)(2,1)S(1)}, bf16[224,2048]{1,0:T(8,128)(2,1)}, u32[]{:S(2)}, u32[]{:S(2)}) %collective-permute-start.7) | collective-permute-done | bytes 917536 | tf_op jit(solution)/shard_map/ppermute | solution.py:186
  60.2 8.9 %shard_map.47 = (bf16[2240,256]{1,0:T(8,128)(2,1)}, bf16[2240,256]{1,0:T(8,128)(2,1)}) custom-call(s32[10]{0:T(128)} %pad_add_fusion.1.refs_0_.meta_ref.refs_2_, bf16[224,18432]{1,0:T(8,128)(2,1)} %refs_1_.8, bf16[224,2048]{1,0:T(8,128)(2,1)} %collective-permute-done.6.refs_2_, bf16[224,2048]{1,0:T(8,128)(2,1)} %collective-permute-done.7.refs_3_, ...), custom_call_target="tpu_custom_call" | custom-call | flops 2055208960 | bytes 5963776 | tf_op jit(solution)/shard_map/pallas_call | solution.py:281
  85.7 28.4 %collective-permute-done.10.refs_3_ = bf16[1008,256]{1,0:T(8,128)(2,1)S(1)} collective-permute-done((bf16[1008,256]{1,0:T(8,128)(2,1)}, bf16[1008,256]{1,0:T(8,128)(2,1)S(1)}, u32[]{:S(2)}, u32[]{:S(2)}) %collective-permute-start.10) | collective-permute-done | bytes 516128 | tf_op jit(solution)/shard_map/ppermute | solution.py:186
  114.1 12.3 %collective-permute-done.12.refs_2_ = bf16[1008,256]{1,0:T(8,128)(2,1)S(1)} collective-permute-done((bf16[1008,256]{1,0:T(8,128)(2,1)}, bf16[1008,256]{1,0:T(8,128)(2,1)S(1)}, u32[]{:S(2)}, u32[]{:S(2)}) %collective-permute-start.12) | collective-permute-done | bytes 516128 | tf_op jit(solution)/shard_map/ppermute | solution.py:186
  128.7 8.9 %shard_map.50 = (bf16[2240,256]{1,0:T(8,128)(2,1)}, bf16[2240,256]{1,0:T(8,128)(2,1)}) custom-call(s32[10]{0:T(128)} %pad_add_fusion.1.refs_0_.meta_ref.refs_2_, bf16[224,18432]{1,0:T(8,128)(2,1)} %refs_1_.8, bf16[224,2048]{1,0:T(8,128)(2,1)} %copy-done.9, bf16[224,2048]{1,0:T(8,128)(2,1)} %copy-done.10, bf16[224,2048]{1,0:T(8,128)(2,1)} %copy-done.12), custom_call_target="tpu_custom_call" | custom-call | flops 2055208960 | bytes 5963776 | tf_op jit(solution)/shard_map/pallas_call | solution.py:281
  160.2 9.3 %collective-permute-done.17.refs_2_ = bf16[1008,256]{1,0:T(8,128)(2,1)S(1)} collective-permute-done((bf16[1008,256]{1,0:T(8,128)(2,1)}, bf16[1008,256]{1,0:T(8,128)(2,1)S(1)}, u32[]{:S(2)}, u32[]{:S(2)}) %collective-permute-start.17) | collective-permute-done | bytes 516128 | tf_op jit(solution)/shard_map/ppermute | solution.py:186
  169.5 15.2 %collective-permute-done.18.refs_3_ = bf16[1008,256]{1,0:T(8,128)(2,1)S(1)} collective-permute-done((bf16[1008,256]{1,0:T(8,128)(2,1)}, bf16[1008,256]{1,0:T(8,128)(2,1)S(1)}, u32[]{:S(2)}, u32[]{:S(2)}) %collective-permute-start.18) | collective-permute-done | bytes 516128 | tf_op jit(solution)/shard_map/ppermute | solution.py:186
  194.2 14.1 %shard_map.56 = (bf16[3584,512]{1,0:T(8,128)(2,1)}, bf16[3584,512]{1,0:T(8,128)(2,1)}) custom-call(s32[28]{0:T(128)} %constant.61.clone.refs_0_, s32[28]{0:T(128)} %constant.62.clone.refs_1_, s32[10]{0:T(128)} %pad_add_fusion.1.refs_0_.meta_ref.refs_2_, bf16[3584,640]{1,0:T(8,128)(2,1)} %shard_map.54.refs_3_), custom_call_target="tpu_custom_call" | custom-call | flops 4697620480 | bytes 11927552 | tf_op jit(solution)/shard_map/pallas_call | solution.py:549
  208.8 14.1 %shard_map.55 = (bf16[3584,512]{1,0:T(8,128)(2,1)}, bf16[3584,512]{1,0:T(8,128)(2,1)}) custom-call(s32[28]{0:T(128)} %constant.61.clone.refs_0_, s32[28]{0:T(128)} %constant.62.clone.refs_1_, s32[10]{0:T(128)} %pad_add_fusion.1.refs_0_.meta_ref.refs_2_, bf16[3584,640]{1,0:T(8,128)(2,1)} %shard_map.54.refs_3_), custom_call_target="tpu_custom_call" | custom-call | flops 4697620480 | bytes 11927552 | tf_op jit(solution)/shard_map/pallas_call | solution.py:549
  243.1 11.6 %collective-permute-done.26.refs_2_ = bf16[3584,128]{1,0:T(8,128)(2,1)S(1)} collective-permute-done((bf16[3584,128]{1,0:T(8,128)(2,1)}, bf16[3584,128]{1,0:T(8,128)(2,1)S(1)}, u32[]{:S(2)}, u32[]{:S(2)}) %collective-permute-start.26) | collective-permute-done | bytes 917536 | tf_op jit(solution)/shard_map/ppermute | solution.py:186
  254.7 19.0 %collective-permute-done.27.refs_3_ = bf16[3584,128]{1,0:T(8,128)(2,1)S(1)} collective-permute-done((bf16[3584,128]{1,0:T(8,128)(2,1)}, bf16[3584,128]{1,0:T(8,128)(2,1)S(1)}, u32[]{:S(2)}, u32[]{:S(2)}) %collective-permute-start.27) | collective-permute-done | bytes 917536 | tf_op jit(solution)/shard_map/ppermute | solution.py:186
  278.3 10.6 %collective-permute-start.29 = (bf16[896,128]{1,0:T(8,128)(2,1)}, bf16[896,128]{1,0:T(8,128)(2,1)S(1)}, u32[]{:S(2)}, u32[]{:S(2)}) collective-permute-start(bf16[896,128]{1,0:T(8,128)(2,1)} %get-tuple-element.206), channel_id=1, source_target_pairs={{0,8},{4,12},{8,0},{12,4},{16,24},{20,28},{24,16},{28,20},{1,9},{5... | collective-permute-start | bytes 688136 | tf_op jit(solution)/shard_map/ppermute | solution.py:186
  297.5 12.5 %collective-permute-done.30.refs_2_ = bf16[896,128]{1,0:T(8,128)(2,1)S(1)} collective-permute-done((bf16[896,128]{1,0:T(8,128)(2,1)}, bf16[896,128]{1,0:T(8,128)(2,1)S(1)}, u32[]{:S(2)}, u32[]{:S(2)}) %collective-permute-start.30) | collective-permute-done | bytes 229408 | tf_op jit(solution)/shard_map/ppermute | solution.py:186
  353.6 10.0 %collective-permute-done.39.refs_2_ = bf16[896,128]{1,0:T(8,128)(2,1)S(1)} collective-permute-done((bf16[896,128]{1,0:T(8,128)(2,1)}, bf16[896,128]{1,0:T(8,128)(2,1)S(1)}, u32[]{:S(2)}, u32[]{:S(2)}) %collective-permute-start.39) | collective-permute-done | bytes 229408 | tf_op jit(solution)/shard_map/ppermute | solution.py:186
  376.6 9.3 %collective-permute-done.42.refs_2_ = bf16[896,128]{1,0:T(8,128)(2,1)S(1)} collective-permute-done((bf16[896,128]{1,0:T(8,128)(2,1)}, bf16[896,128]{1,0:T(8,128)(2,1)S(1)}, u32[]{:S(2)}, u32[]{:S(2)}) %collective-permute-start.42) | collective-permute-done | bytes 229408 | tf_op jit(solution)/shard_map/ppermute | solution.py:186
  402.1 19.5 %collective-permute-done.47.refs_8_ = bf16[3584,128]{1,0:T(8,128)(2,1)S(1)} collective-permute-done((bf16[3584,128]{1,0:T(8,128)(2,1)}, bf16[3584,128]{1,0:T(8,128)(2,1)S(1)}, u32[]{:S(2)}, u32[]{:S(2)}) %collective-permute-start.47) | collective-permute-done | bytes 917536 | tf_op jit(solution)/shard_map/ppermute | solution.py:186
  421.6 16.3 %collective-permute-done.48.refs_9_ = bf16[3584,128]{1,0:T(8,128)(2,1)S(1)} collective-permute-done((bf16[3584,128]{1,0:T(8,128)(2,1)}, bf16[3584,128]{1,0:T(8,128)(2,1)S(1)}, u32[]{:S(2)}, u32[]{:S(2)}) %collective-permute-start.48) | collective-permute-done | bytes 917536 | tf_op jit(solution)/shard_map/ppermute | solution.py:186
  445.5 25.4 %shard_map.65 = (bf16[1008,256]{1,0:T(8,128)(2,1)}, bf16[1008,256]{1,0:T(8,128)(2,1)}, bf16[1008,256]{1,0:T(8,128)(2,1)}, bf16[1008,256]{1,0:T(8,128)(2,1)}, bf16[7,512,3584]{2,1,0:T(8,128)(2,1)}) custom-call(s32[28]{0:T(128)} %constant.61.clone.refs_0_, s32[28]{0:T(128)} %constant.62.clone.refs_1_, s32[10]{0:T(128)} %pad_add_fusion.1.refs_0_.meta_ref.refs_2_, ...), custom_call_target="tpu_custom_call" | custom-call | flops 13153337344 | bytes 55050240 | tf_op jit(solution)/shard_map/pallas_call | solution.py:742
  476.8 35.1 %shard_map.66 = (bf16[1008,256]{1,0:T(8,128)(2,1)}, bf16[1008,256]{1,0:T(8,128)(2,1)}, bf16[1008,256]{1,0:T(8,128)(2,1)}, bf16[1008,256]{1,0:T(8,128)(2,1)}, bf1...) custom-call(s32[10]{0:T(128)} %pad_add_fusion.1.refs_0_.meta_ref.refs_2_,, ...), custom_call_target="tpu_custom_call" | custom-call | flops 19730006016 | bytes 56885248 | tf_op jit(solution)/shard_map/pallas_call | solution.py:797
  515.6 9.5 %collective-permute-start.61 = (bf16[1008,256]{1,0:T(8,128)(2,1)}, bf16[1008,256]{1,0:T(8,128)(2,1)S(1)}, u32[]{:S(2)}, u32[]{:S(2)}) collective-permute-start(bf16[1008,256]{1,0:T(8,128)(2,1)} %get-tuple-element.250), channel_id=1, source_target_pairs={{0,16},{4,20},{8,24},{12,28},{16,0},{20,4},{24,8},{28,12},{1,17},{... | collective-permute-start | bytes 1548296 | tf_op jit(solution)/shard_map/ppermute | solution.py:186
  526.1 9.0 %shard_map.68 = (bf16[224,2048]{1,0:T(8,128)(2,1)}, bf16[224,2048]{1,0:T(8,128)(2,1)}, bf16[224,2048]{1,0:T(8,128)(2,1)}, bf16[224,2048]{1,0:T(8,128)(2,1)}) custom-call(s32[10]{0:T(128)} %pad_add_fusion.1.refs_0_.meta_ref.refs_2_, bf16[1008,256]{1,0:T(8,128)(2,1)} %get-tuple-element.262.refs_1_, bf16[1008,256]{1,0:T(8,128)(2,1)} %copy-done.26, ...), custom_call_target="tpu_custom_call" | custom-call | flops 2055208960 | bytes 5963776 | tf_op jit(solution)/shard_map/pallas_call | solution.py:405
  539.4 20.6 %collective-permute-done.61.refs_3_ = bf16[1008,256]{1,0:T(8,128)(2,1)S(1)} collective-permute-done((bf16[1008,256]{1,0:T(8,128)(2,1)}, bf16[1008,256]{1,0:T(8,128)(2,1)S(1)}, u32[]{:S(2)}, u32[]{:S(2)}) %collective-permute-start.61) | collective-permute-done | bytes 516128 | tf_op jit(solution)/shard_map/ppermute | solution.py:186
  560.1 13.4 %collective-permute-done.63.refs_2_ = bf16[1008,256]{1,0:T(8,128)(2,1)S(1)} collective-permute-done((bf16[1008,256]{1,0:T(8,128)(2,1)S(1)}, bf16[1008,256]{1,0:T(8,128)(2,1)S(1)}, u32[]{:S(2)}, u32[]{:S(2)}) %collective-permute-start.63) | collective-permute-done | bytes 516128 | tf_op jit(solution)/shard_map/ppermute | solution.py:186
  621.9 19.3 %collective-permute-done.73 = bf16[224,2048]{1,0:T(8,128)(2,1)} collective-permute-done((bf16[224,2048]{1,0:T(8,128)(2,1)}, bf16[224,2048]{1,0:T(8,128)(2,1)}, u32[]{:S(2)}, u32[]{:S(2)}) %collective-permute-start.73) | collective-permute-done | bytes 917536 | tf_op jit(solution)/shard_map/ppermute | solution.py:186
  (314 shorter events, 288.5 us)
Async XLA Ops:
  19.5 40.7 %collective-permute-start.7 = (bf16[224,2048]{1,0:T(8,128)(2,1)S(1)}, bf16[224,2048]{1,0:T(8,128)(2,1)}, u32[]{:S(2)}, u32[]{:S(2)}) collective-permute-start(bf16[224,2048]{1,0:T(8,128)(2,1)S(1)} %get-tuple-element.299), channel_id=1, source_target_pairs={{0,2},{1,3},{2,0},{3,1},{4,6},{5,7},{6,4},{7,5},{8,10},{9,11},{10,... | collective-permute-start | bytes 2752520 | tf_op jit(solution)/shard_map/ppermute | solution.py:186
  20.4 39.8 %collective-permute-start.8 = (bf16[224,2048]{1,0:T(8,128)(2,1)S(1)}, bf16[224,2048]{1,0:T(8,128)(2,1)}, u32[]{:S(2)}, u32[]{:S(2)}) collective-permute-start(bf16[224,2048]{1,0:T(8,128)(2,1)S(1)} %get-tuple-element.298), channel_id=1, source_target_pairs={{0,3},{1,2},{2,1},{3,0},{4,7},{5,6},{6,5},{7,4},{8,11},{9,10},{10,... | collective-permute-start | bytes 2752520 | tf_op jit(solution)/shard_map/ppermute | solution.py:186
  80.8 45.6 %collective-permute-start.13 = (bf16[224,2048]{1,0:T(8,128)(2,1)S(1)}, bf16[224,2048]{1,0:T(8,128)(2,1)S(1)}, u32[]{:S(2)}, u32[]{:S(2)}) collective-permute-start(bf16[224,2048]{1,0:T(8,128)(2,1)S(1)} %get-tuple-element.297), channel_id=1, source_target_pairs={{0,1},{1,0},{2,3},{3,2},{4,5},{5,4},{6,7},{7,6},{8,9},{9,8},{10,11... | collective-permute-start | bytes 2752520 | tf_op jit(solution)/shard_map/ppermute | solution.py:186
  81.5 45.0 %collective-permute-start.14 = (bf16[224,2048]{1,0:T(8,128)(2,1)S(1)}, bf16[224,2048]{1,0:T(8,128)(2,1)S(1)}, u32[]{:S(2)}, u32[]{:S(2)}) collective-permute-start(bf16[224,2048]{1,0:T(8,128)(2,1)S(1)} %get-tuple-element.296), channel_id=1, source_target_pairs={{0,2},{1,3},{2,0},{3,1},{4,6},{5,7},{6,4},{7,5},{8,10},{9,11},{10,... | collective-permute-start | bytes 2752520 | tf_op jit(solution)/shard_map/ppermute | solution.py:186
  82.6 43.9 %collective-permute-start.15 = (bf16[224,2048]{1,0:T(8,128)(2,1)S(1)}, bf16[224,2048]{1,0:T(8,128)(2,1)S(1)}, u32[]{:S(2)}, u32[]{:S(2)}) collective-permute-start(bf16[224,2048]{1,0:T(8,128)(2,1)S(1)} %get-tuple-element.295), channel_id=1, source_target_pairs={{0,3},{1,2},{2,1},{3,0},{4,7},{5,6},{6,5},{7,4},{8,11},{9,10},{10,... | collective-permute-start | bytes 2752520 | tf_op jit(solution)/shard_map/ppermute | solution.py:186
  231.9 41.9 %collective-permute-start.27 = (bf16[3584,128]{1,0:T(8,128)(2,1)}, bf16[3584,128]{1,0:T(8,128)(2,1)S(1)}, u32[]{:S(2)}, u32[]{:S(2)}) collective-permute-start(bf16[3584,128]{1,0:T(8,128)(2,1)} %get-tuple-element.200), channel_id=1, source_target_pairs={{0,2},{1,3},{2,0},{3,1},{4,6},{5,7},{6,4},{7,5},{8,10},{9,11},{10,... | collective-permute-start | bytes 2752520 | tf_op jit(solution)/shard_map/ppermute | solution.py:186
  233.1 40.7 %collective-permute-start.28 = (bf16[3584,128]{1,0:T(8,128)(2,1)}, bf16[3584,128]{1,0:T(8,128)(2,1)S(1)}, u32[]{:S(2)}, u32[]{:S(2)}) collective-permute-start(bf16[3584,128]{1,0:T(8,128)(2,1)} %get-tuple-element.201), channel_id=1, source_target_pairs={{0,3},{1,2},{2,1},{3,0},{4,7},{5,6},{6,5},{7,4},{8,11},{9,10},{10,... | collective-permute-start | bytes 2752520 | tf_op jit(solution)/shard_map/ppermute | solution.py:186
  288.9 46.0 %collective-permute-start.32 = (bf16[3584,128]{1,0:T(8,128)(2,1)}, bf16[3584,128]{1,0:T(8,128)(2,1)S(1)}, u32[]{:S(2)}, u32[]{:S(2)}) collective-permute-start(bf16[3584,128]{1,0:T(8,128)(2,1)} %get-tuple-element.209), channel_id=1, source_target_pairs={{0,1},{1,0},{2,3},{3,2},{4,5},{5,4},{6,7},{7,6},{8,9},{9,8},{10,11... | collective-permute-start | bytes 2752520 | tf_op jit(solution)/shard_map/ppermute | solution.py:186
  290.4 44.6 %collective-permute-start.33 = (bf16[3584,128]{1,0:T(8,128)(2,1)}, bf16[3584,128]{1,0:T(8,128)(2,1)S(1)}, u32[]{:S(2)}, u32[]{:S(2)}) collective-permute-start(bf16[3584,128]{1,0:T(8,128)(2,1)} %get-tuple-element.210), channel_id=1, source_target_pairs={{0,2},{1,3},{2,0},{3,1},{4,6},{5,7},{6,4},{7,5},{8,10},{9,11},{10,... | collective-permute-start | bytes 2752520 | tf_op jit(solution)/shard_map/ppermute | solution.py:186
  291.0 44.1 %collective-permute-start.34 = (bf16[3584,128]{1,0:T(8,128)(2,1)}, bf16[3584,128]{1,0:T(8,128)(2,1)S(1)}, u32[]{:S(2)}, u32[]{:S(2)}) collective-permute-start(bf16[3584,128]{1,0:T(8,128)(2,1)} %get-tuple-element.211), channel_id=1, source_target_pairs={{0,3},{1,2},{2,1},{3,0},{4,7},{5,6},{6,5},{7,4},{8,11},{9,10},{10,... | collective-permute-start | bytes 2752520 | tf_op jit(solution)/shard_map/ppermute | solution.py:186
  349.1 45.6 %collective-permute-start.44 = (bf16[3584,128]{1,0:T(8,128)(2,1)}, bf16[3584,128]{1,0:T(8,128)(2,1)S(1)}, u32[]{:S(2)}, u32[]{:S(2)}) collective-permute-start(bf16[3584,128]{1,0:T(8,128)(2,1)} %shard_map.61.refs_3_), channel_id=1, source_target_pairs={{0,1},{1,0},{2,3},{3,2},{4,5},{5,4},{6,7},{7,6},{8,9},{9,8},{10,11... | collective-permute-start | bytes 2752520 | tf_op jit(solution)/shard_map/ppermute | solution.py:186
  350.1 44.6 %collective-permute-start.45 = (bf16[3584,128]{1,0:T(8,128)(2,1)}, bf16[3584,128]{1,0:T(8,128)(2,1)S(1)}, u32[]{:S(2)}, u32[]{:S(2)}) collective-permute-start(bf16[3584,128]{1,0:T(8,128)(2,1)} %shard_map.61.refs_3_), channel_id=1, source_target_pairs={{0,2},{1,3},{2,0},{3,1},{4,6},{5,7},{6,4},{7,5},{8,10},{9,11},{10,... | collective-permute-start | bytes 2752520 | tf_op jit(solution)/shard_map/ppermute | solution.py:186
  352.1 42.7 %collective-permute-start.46 = (bf16[3584,128]{1,0:T(8,128)(2,1)}, bf16[3584,128]{1,0:T(8,128)(2,1)S(1)}, u32[]{:S(2)}, u32[]{:S(2)}) collective-permute-start(bf16[3584,128]{1,0:T(8,128)(2,1)} %shard_map.61.refs_3_), channel_id=1, source_target_pairs={{0,3},{1,2},{2,1},{3,0},{4,7},{5,6},{6,5},{7,4},{8,11},{9,10},{10,... | collective-permute-start | bytes 2752520 | tf_op jit(solution)/shard_map/ppermute | solution.py:186
  399.1 38.8 %collective-permute-start.48 = (bf16[3584,128]{1,0:T(8,128)(2,1)}, bf16[3584,128]{1,0:T(8,128)(2,1)S(1)}, u32[]{:S(2)}, u32[]{:S(2)}) collective-permute-start(bf16[3584,128]{1,0:T(8,128)(2,1)} %shard_map.64.refs_7_), channel_id=1, source_target_pairs={{0,2},{1,3},{2,0},{3,1},{4,6},{5,7},{6,4},{7,5},{8,10},{9,11},{10,... | collective-permute-start | bytes 2752520 | tf_op jit(solution)/shard_map/ppermute | solution.py:186
  400.1 39.3 %collective-permute-start.49 = (bf16[3584,128]{1,0:T(8,128)(2,1)}, bf16[3584,128]{1,0:T(8,128)(2,1)S(1)}, u32[]{:S(2)}, u32[]{:S(2)}) collective-permute-start(bf16[3584,128]{1,0:T(8,128)(2,1)} %shard_map.64.refs_7_), channel_id=1, source_target_pairs={{0,3},{1,2},{2,1},{3,0},{4,7},{5,6},{6,5},{7,4},{8,11},{9,10},{10,... | collective-permute-start | bytes 2752520 | tf_op jit(solution)/shard_map/ppermute | solution.py:186
  470.9 40.9 %collective-permute-start.58 = (bf16[1008,256]{1,0:T(8,128)(2,1)}, bf16[1008,256]{1,0:T(8,128)(2,1)S(1)}, u32[]{:S(2)}, u32[]{:S(2)}) collective-permute-start(bf16[1008,256]{1,0:T(8,128)(2,1)} %get-tuple-element.229), channel_id=1, source_target_pairs={{0,16},{4,20},{8,24},{12,28},{16,0},{20,4},{24,8},{28,12},{1,17},{... | collective-permute-start | bytes 1548296 | tf_op jit(solution)/shard_map/ppermute | solution.py:186
  473.5 38.4 %collective-permute-start.59 = (bf16[1008,256]{1,0:T(8,128)(2,1)}, bf16[1008,256]{1,0:T(8,128)(2,1)S(1)}, u32[]{:S(2)}, u32[]{:S(2)}) collective-permute-start(bf16[1008,256]{1,0:T(8,128)(2,1)} %get-tuple-element.230), channel_id=1, source_target_pairs={{0,24},{4,28},{8,16},{12,20},{16,8},{20,12},{24,0},{28,4},{1,25},{... | collective-permute-start | bytes 1548296 | tf_op jit(solution)/shard_map/ppermute | solution.py:186
  515.6 44.4 %collective-permute-start.61 = (bf16[1008,256]{1,0:T(8,128)(2,1)}, bf16[1008,256]{1,0:T(8,128)(2,1)S(1)}, u32[]{:S(2)}, u32[]{:S(2)}) collective-permute-start(bf16[1008,256]{1,0:T(8,128)(2,1)} %get-tuple-element.250), channel_id=1, source_target_pairs={{0,16},{4,20},{8,24},{12,28},{16,0},{20,4},{24,8},{28,12},{1,17},{... | collective-permute-start | bytes 1548296 | tf_op jit(solution)/shard_map/ppermute | solution.py:186
  535.1 38.4 %collective-permute-start.65 = (bf16[224,2048]{1,0:T(8,128)(2,1)}, bf16[224,2048]{1,0:T(8,128)(2,1)}, u32[]{:S(2)}, u32[]{:S(2)}) collective-permute-start(bf16[224,2048]{1,0:T(8,128)(2,1)} %get-tuple-element.267), channel_id=1, source_target_pairs={{0,1},{1,0},{2,3},{3,2},{4,5},{5,4},{6,7},{7,6},{8,9},{9,8},{10,11... | collective-permute-start | bytes 2752520 | tf_op jit(solution)/shard_map/ppermute | solution.py:186
  537.3 42.2 %collective-permute-start.66 = (bf16[224,2048]{1,0:T(8,128)(2,1)}, bf16[224,2048]{1,0:T(8,128)(2,1)}, u32[]{:S(2)}, u32[]{:S(2)}) collective-permute-start(bf16[224,2048]{1,0:T(8,128)(2,1)} %get-tuple-element.268), channel_id=1, source_target_pairs={{0,2},{1,3},{2,0},{3,1},{4,6},{5,7},{6,4},{7,5},{8,10},{9,11},{10,... | collective-permute-start | bytes 2752520 | tf_op jit(solution)/shard_map/ppermute | solution.py:186
  538.1 41.4 %collective-permute-start.67 = (bf16[224,2048]{1,0:T(8,128)(2,1)}, bf16[224,2048]{1,0:T(8,128)(2,1)}, u32[]{:S(2)}, u32[]{:S(2)}) collective-permute-start(bf16[224,2048]{1,0:T(8,128)(2,1)} %get-tuple-element.269), channel_id=1, source_target_pairs={{0,3},{1,2},{2,1},{3,0},{4,7},{5,6},{6,5},{7,4},{8,11},{9,10},{10,... | collective-permute-start | bytes 2752520 | tf_op jit(solution)/shard_map/ppermute | solution.py:186
  597.9 43.3 %collective-permute-start.73 = (bf16[224,2048]{1,0:T(8,128)(2,1)}, bf16[224,2048]{1,0:T(8,128)(2,1)}, u32[]{:S(2)}, u32[]{:S(2)}) collective-permute-start(bf16[224,2048]{1,0:T(8,128)(2,1)} %get-tuple-element.285), channel_id=1, source_target_pairs={{0,2},{1,3},{2,0},{3,1},{4,6},{5,7},{6,4},{7,5},{8,10},{9,11},{10,... | collective-permute-start | bytes 2752520 | tf_op jit(solution)/shard_map/ppermute | solution.py:186
  600.3 42.3 %collective-permute-start.74 = (bf16[224,2048]{1,0:T(8,128)(2,1)}, bf16[224,2048]{1,0:T(8,128)(2,1)}, u32[]{:S(2)}, u32[]{:S(2)}) collective-permute-start(bf16[224,2048]{1,0:T(8,128)(2,1)} %get-tuple-element.286), channel_id=1, source_target_pairs={{0,3},{1,2},{2,1},{3,0},{4,7},{5,6},{6,5},{7,4},{8,11},{9,10},{10,... | collective-permute-start | bytes 2752520 | tf_op jit(solution)/shard_map/ppermute | solution.py:186
  609.4 40.3 %collective-permute-start.76 = (bf16[224,512]{1,0:T(8,128)(2,1)}, bf16[224,512]{1,0:T(8,128)(2,1)S(1)}, u32[]{:S(2)}, u32[]{:S(2)}) collective-permute-start(bf16[224,512]{1,0:T(8,128)(2,1)} %get-tuple-element.293), channel_id=1, source_target_pairs={{0,2},{1,3},{2,0},{3,1},{4,6},{5,7},{6,4},{7,5},{8,10},{9,11},{10,... | collective-permute-start | bytes 688136 | tf_op jit(solution)/shard_map/ppermute | solution.py:186
  (120 other events, 1995.2 us)

commit v8 on v7

--- a/solution.py
+++ b/solution.py
@@ -303,7 +303,7 @@
         compiler_params=pltpu.CompilerParams(vmem_limit_bytes=VMEM_LIMIT),
         cost_estimate=pl.CostEstimate(
             flops=2 * window * slots * col_count * width * row_count,
-            bytes_accessed=2 * row_count * width * (slots * col_count + window),
+            bytes_accessed=10 * row_count * width * (slots * col_count + window),
             transcendentals=0,
         ),
     )(meta, momentum, *received)
@@ -416,7 +416,7 @@
         compiler_params=pltpu.CompilerParams(vmem_limit_bytes=VMEM_LIMIT),
         cost_estimate=pl.CostEstimate(
             flops=2 * window * slots * col_count * width * count,
-            bytes_accessed=2 * count * width * (slots * col_count + window),
+            bytes_accessed=10 * count * width * (slots * col_count + window),
             transcendentals=0,
         ),
     )(meta, *pieces, got)
@@ -462,7 +462,7 @@
         compiler_params=pltpu.CompilerParams(vmem_limit_bytes=VMEM_LIMIT),
         cost_estimate=pl.CostEstimate(
             flops=2 * window * slots * col_count * width * count,
-            bytes_accessed=2 * count * width * (slots * col_count + window),
+            bytes_accessed=10 * count * width * (slots * col_count + window),
             transcendentals=0,
         ),
     )(meta, *pieces)
@@ -635,17 +635,17 @@
     )
 
 
-def stack_kernel(meta_ref, *refs):
+def stack_kernel(order, meta_ref, *refs):
     parts, out = refs[:-1], refs[-1]
     rows = parts[0].shape[0]
-    for q, part in enumerate(parts):
+    for q, part in zip(order, parts):
         out[pl.ds(pl.multiple_of((meta_ref[0] // 2 ^ q) * rows, rows), rows), :] = part[...]
 
 
-def stack(meta, parts):
+def stack(meta, parts, order):
     rows, lanes = parts[0].shape
     return local_call(
-        stack_kernel,
+        lambda *refs: stack_kernel(order, *refs),
         jax.ShapeDtypeStruct((rows * len(parts), lanes), jnp.bfloat16),
         (meta, *parts),
         4 * rows * lanes * len(parts),
@@ -808,7 +808,7 @@
         ),
         compiler_params=pltpu.CompilerParams(vmem_limit_bytes=VMEM_LIMIT),
         cost_estimate=pl.CostEstimate(
-            flops=4 * M * M * sum(widths),
+            flops=8 * M * M * sum(widths),
             bytes_accessed=4 * M * sum(widths) + 4 * M * M,
             transcendentals=0,
         ),
@@ -827,8 +827,10 @@
     def over_cols(blocks):
         return [swap(blocks[k], "col", col_count, k) for k in range(1, col_count)]
 
+    order = list(range(pair_count // 2, pair_count)) + list(range(1, pair_count // 2))
+
     def over_pairs(blocks):
-        return [swap(blocks[q], "row", row_count, 2 * q) for q in range(1, pair_count)]
+        return [swap(blocks[q], "row", row_count, 2 * q) for q in order]
 
     give = half_gram(meta, joined, 1)
     got = [swap(piece, "row", row_count, 1) for piece in give]
@@ -845,13 +847,13 @@
     early_in = over_pairs([early_part] * pair_count)
     late_in, early_in = tie((late_in, early_in))
     late_parts = add_quarters(meta, [late[0]] + late_in, pair_count)
-    early_block = stack(meta, [early_part] + early_in)
+    early_block = stack(meta, [early_part] + early_in, [0] + order)
     early_in = over_cols([early_block] * col_count)
     late_in = over_pairs(late_parts)
     late_part = add_parts(meta, [late_parts[0]] + late_in)
     late_in = over_pairs([late_part] * pair_count)
     late_in, early_in = tie((late_in, early_in))
-    late_block = stack(meta, [late_part] + late_in)
+    late_block = stack(meta, [late_part] + late_in, [0] + order)
     late_in = over_cols([late_block] * col_count)
     early = [early_block] + early_in
     early_twin = [swap(block, "row", row_count, 1) for block in early]

time: 656 us -> 658 us (level)
  waiting for transfers between devices: 314 us -> 322 us
    ppermute x78, waiting for transfers between devices: 314 us -> 322 us  [swap(): lax.ppermute(value, axis, perm=[(i, i ^ distance) for i in range(size)])]
  transfers between devices with their start and end apart: 78 -> 78, of which waited for: 38 -> 37; matrix products, arithmetic and copies ran while one was open for 3% -> 2% of each run, Pallas kernels for 16% -> 16%
where the time goes in v8:
time: 658 us; the launch traced here: 656 us
  waiting for transfers between devices  322 us (49%)
  Pallas kernels  190 us (29%)
  starting transfers between devices  101 us (15%)
  local copies, waits for them, and re-layouts  41.7 us (6%)
    ppermute x78, waiting for transfers between devices, swap(): lax.ppermute(value, axis, perm=[(i, i ^ distance) for i in range(size)])  322 us
    ppermute x78, starting transfers between devices, swap(): lax.ppermute(value, axis, perm=[(i, i ^ distance) for i in range(size)])  101 us
    pallas_call x14, Pallas kernels, local_call(): pl.pallas_call(kernel, out_shape=out_shape, in_specs=[pl.BlockSpec(memory...  42.3 us
    pallas_call x1, Pallas kernels, next_apply(): pl.pallas_call(lambda *refs: next_apply_kernel(jitter, sends, *refs), out...  35.1 us
    pallas_call x2, Pallas kernels, half_gram(): pl.pallas_call(lambda *refs: half_gram_kernel(flip, *refs), out_shape=[ja...  28.2 us
    pallas_call x1, Pallas kernels, first_apply(): pl.pallas_call(lambda *refs: first_apply_kernel(jitter, send, col_count,...  25.4 us
    unnamed x132, local copies, waits for them, and re-layouts  22 us
    pallas_call x2, Pallas kernels, pack_pair(): pl.pallas_call(lambda *refs: pack_pair_kernel(col_count, *refs), out_shap...  17.8 us
  transfers between devices with their start and end apart: 78, of which 37 were waited for; matrix products, arithmetic and copies ran while one was open for 2% of the time, Pallas kernels for 16%

profile of v8, /device:TPU:0, one launch (start us, length us, event | category | flops | bytes accessed | tf_op | source)
XLA Modules:
  0.0 656.1 jit_solution(7227501818803131026)
XLA Ops:
  47.9 12.3 %collective-permute-done.7.refs_3_ = bf16[224,2048]{1,0:T(8,128)(2,1)} collective-permute-done((bf16[224,2048]{1,0:T(8,128)(2,1)S(1)}, bf16[224,2048]{1,0:T(8,128)(2,1)}, u32[]{:S(2)}, u32[]{:S(2)}) %collective-permute-start.7) | collective-permute-done | bytes 917536 | tf_op jit(solution)/shard_map/ppermute | solution.py:186
  85.7 28.4 %collective-permute-done.10.refs_3_ = bf16[1008,256]{1,0:T(8,128)(2,1)S(1)} collective-permute-done((bf16[1008,256]{1,0:T(8,128)(2,1)}, bf16[1008,256]{1,0:T(8,128)(2,1)S(1)}, u32[]{:S(2)}, u32[]{:S(2)}) %collective-permute-start.10) | collective-permute-done | bytes 516128 | tf_op jit(solution)/shard_map/ppermute | solution.py:186
  114.1 12.3 %collective-permute-done.12.refs_2_ = bf16[1008,256]{1,0:T(8,128)(2,1)S(1)} collective-permute-done((bf16[1008,256]{1,0:T(8,128)(2,1)}, bf16[1008,256]{1,0:T(8,128)(2,1)S(1)}, u32[]{:S(2)}, u32[]{:S(2)}) %collective-permute-start.12) | collective-permute-done | bytes 516128 | tf_op jit(solution)/shard_map/ppermute | solution.py:186
  128.7 8.9 %shard_map.50 = (bf16[2240,256]{1,0:T(8,128)(2,1)}, bf16[2240,256]{1,0:T(8,128)(2,1)}) custom-call(s32[10]{0:T(128)} %pad_add_fusion.1.refs_0_.meta_ref.refs_2_, bf16[224,18432]{1,0:T(8,128)(2,1)} %refs_1_.8, bf16[224,2048]{1,0:T(8,128)(2,1)} %copy-done.9, bf16[224,2048]{1,0:T(8,128)(2,1)} %copy-done.10, bf16[224,2048]{1,0:T(8,128)(2,1)} %copy-done.12), custom_call_target="tpu_custom_call" | custom-call | flops 2055208960 | bytes 29818880 | tf_op jit(solution)/shard_map/pallas_call | solution.py:281
  160.2 9.3 %collective-permute-done.17.refs_2_ = bf16[1008,256]{1,0:T(8,128)(2,1)S(1)} collective-permute-done((bf16[1008,256]{1,0:T(8,128)(2,1)}, bf16[1008,256]{1,0:T(8,128)(2,1)S(1)}, u32[]{:S(2)}, u32[]{:S(2)}) %collective-permute-start.17) | collective-permute-done | bytes 516128 | tf_op jit(solution)/shard_map/ppermute | solution.py:186
  169.5 15.2 %collective-permute-done.18.refs_3_ = bf16[1008,256]{1,0:T(8,128)(2,1)S(1)} collective-permute-done((bf16[1008,256]{1,0:T(8,128)(2,1)}, bf16[1008,256]{1,0:T(8,128)(2,1)S(1)}, u32[]{:S(2)}, u32[]{:S(2)}) %collective-permute-start.18) | collective-permute-done | bytes 516128 | tf_op jit(solution)/shard_map/ppermute | solution.py:186
  194.2 14.1 %shard_map.56 = (bf16[3584,512]{1,0:T(8,128)(2,1)}, bf16[3584,512]{1,0:T(8,128)(2,1)}) custom-call(s32[28]{0:T(128)} %constant.61.clone.refs_0_, s32[28]{0:T(128)} %constant.62.clone.refs_1_, s32[10]{0:T(128)} %pad_add_fusion.1.refs_0_.meta_ref.refs_2_, bf16[3584,640]{1,0:T(8,128)(2,1)} %shard_map.54.refs_3_), custom_call_target="tpu_custom_call" | custom-call | flops 4697620480 | bytes 11927552 | tf_op jit(solution)/shard_map/pallas_call | solution.py:549
  208.8 14.1 %shard_map.55 = (bf16[3584,512]{1,0:T(8,128)(2,1)}, bf16[3584,512]{1,0:T(8,128)(2,1)}) custom-call(s32[28]{0:T(128)} %constant.61.clone.refs_0_, s32[28]{0:T(128)} %constant.62.clone.refs_1_, s32[10]{0:T(128)} %pad_add_fusion.1.refs_0_.meta_ref.refs_2_, bf16[3584,640]{1,0:T(8,128)(2,1)} %shard_map.54.refs_3_), custom_call_target="tpu_custom_call" | custom-call | flops 4697620480 | bytes 11927552 | tf_op jit(solution)/shard_map/pallas_call | solution.py:549
  243.1 11.6 %collective-permute-done.26.refs_2_ = bf16[3584,128]{1,0:T(8,128)(2,1)S(1)} collective-permute-done((bf16[3584,128]{1,0:T(8,128)(2,1)}, bf16[3584,128]{1,0:T(8,128)(2,1)S(1)}, u32[]{:S(2)}, u32[]{:S(2)}) %collective-permute-start.26) | collective-permute-done | bytes 917536 | tf_op jit(solution)/shard_map/ppermute | solution.py:186
  254.7 19.0 %collective-permute-done.27.refs_3_ = bf16[3584,128]{1,0:T(8,128)(2,1)S(1)} collective-permute-done((bf16[3584,128]{1,0:T(8,128)(2,1)}, bf16[3584,128]{1,0:T(8,128)(2,1)S(1)}, u32[]{:S(2)}, u32[]{:S(2)}) %collective-permute-start.27) | collective-permute-done | bytes 917536 | tf_op jit(solution)/shard_map/ppermute | solution.py:186
  278.3 11.5 %collective-permute-start.29 = (bf16[896,128]{1,0:T(8,128)(2,1)}, bf16[896,128]{1,0:T(8,128)(2,1)S(1)}, u32[]{:S(2)}, u32[]{:S(2)}) collective-permute-start(bf16[896,128]{1,0:T(8,128)(2,1)} %get-tuple-element.206), channel_id=1, source_target_pairs={{0,16},{4,20},{8,24},{12,28},{16,0},{20,4},{24,8},{28,12},{1,17},{... | collective-permute-start | bytes 688136 | tf_op jit(solution)/shard_map/ppermute | solution.py:186
  294.8 10.8 %collective-permute-done.29.refs_1_ = bf16[896,128]{1,0:T(8,128)(2,1)S(1)} collective-permute-done((bf16[896,128]{1,0:T(8,128)(2,1)}, bf16[896,128]{1,0:T(8,128)(2,1)S(1)}, u32[]{:S(2)}, u32[]{:S(2)}) %collective-permute-start.29) | collective-permute-done | bytes 229408 | tf_op jit(solution)/shard_map/ppermute | solution.py:186
  317.0 12.5 %collective-permute-done.35.refs_2_ = bf16[896,128]{1,0:T(8,128)(2,1)S(1)} collective-permute-done((bf16[896,128]{1,0:T(8,128)(2,1)}, bf16[896,128]{1,0:T(8,128)(2,1)S(1)}, u32[]{:S(2)}, u32[]{:S(2)}) %collective-permute-start.35) | collective-permute-done | bytes 229408 | tf_op jit(solution)/shard_map/ppermute | solution.py:186
  350.5 9.8 %collective-permute-done.38.refs_1_ = bf16[896,128]{1,0:T(8,128)(2,1)S(1)} collective-permute-done((bf16[896,128]{1,0:T(8,128)(2,1)}, bf16[896,128]{1,0:T(8,128)(2,1)S(1)}, u32[]{:S(2)}, u32[]{:S(2)}) %collective-permute-start.38) | collective-permute-done | bytes 229408 | tf_op jit(solution)/shard_map/ppermute | solution.py:186
  368.6 11.3 %collective-permute-done.41.refs_2_ = bf16[896,128]{1,0:T(8,128)(2,1)S(1)} collective-permute-done((bf16[896,128]{1,0:T(8,128)(2,1)}, bf16[896,128]{1,0:T(8,128)(2,1)S(1)}, u32[]{:S(2)}, u32[]{:S(2)}) %collective-permute-start.41) | collective-permute-done | bytes 229408 | tf_op jit(solution)/shard_map/ppermute | solution.py:186
  404.4 19.5 %collective-permute-done.47.refs_8_ = bf16[3584,128]{1,0:T(8,128)(2,1)S(1)} collective-permute-done((bf16[3584,128]{1,0:T(8,128)(2,1)}, bf16[3584,128]{1,0:T(8,128)(2,1)S(1)}, u32[]{:S(2)}, u32[]{:S(2)}) %collective-permute-start.47) | collective-permute-done | bytes 917536 | tf_op jit(solution)/shard_map/ppermute | solution.py:186
  423.9 16.4 %collective-permute-done.48.refs_9_ = bf16[3584,128]{1,0:T(8,128)(2,1)S(1)} collective-permute-done((bf16[3584,128]{1,0:T(8,128)(2,1)}, bf16[3584,128]{1,0:T(8,128)(2,1)S(1)}, u32[]{:S(2)}, u32[]{:S(2)}) %collective-permute-start.48) | collective-permute-done | bytes 917536 | tf_op jit(solution)/shard_map/ppermute | solution.py:186
  447.9 25.4 %shard_map.65 = (bf16[1008,256]{1,0:T(8,128)(2,1)}, bf16[1008,256]{1,0:T(8,128)(2,1)}, bf16[1008,256]{1,0:T(8,128)(2,1)}, bf16[1008,256]{1,0:T(8,128)(2,1)}, bf16[7,512,3584]{2,1,0:T(8,128)(2,1)}) custom-call(s32[28]{0:T(128)} %constant.61.clone.refs_0_, s32[28]{0:T(128)} %constant.62.clone.refs_1_, s32[10]{0:T(128)} %pad_add_fusion.1.refs_0_.meta_ref.refs_2_, ...), custom_call_target="tpu_custom_call" | custom-call | flops 13153337344 | bytes 55050240 | tf_op jit(solution)/shard_map/pallas_call | solution.py:742
  477.2 35.1 %shard_map.66 = (bf16[1008,256]{1,0:T(8,128)(2,1)}, bf16[1008,256]{1,0:T(8,128)(2,1)}, bf16[1008,256]{1,0:T(8,128)(2,1)}, bf16[1008,256]{1,0:T(8,128)(2,1)}, bf1...) custom-call(s32[10]{0:T(128)} %pad_add_fusion.1.refs_0_.meta_ref.refs_2_,, ...), custom_call_target="tpu_custom_call" | custom-call | flops 39460012032 | bytes 56885248 | tf_op jit(solution)/shard_map/pallas_call | solution.py:797
  516.1 9.5 %collective-permute-start.61 = (bf16[1008,256]{1,0:T(8,128)(2,1)}, bf16[1008,256]{1,0:T(8,128)(2,1)S(1)}, u32[]{:S(2)}, u32[]{:S(2)}) collective-permute-start(bf16[1008,256]{1,0:T(8,128)(2,1)} %get-tuple-element.250), channel_id=1, source_target_pairs={{0,16},{4,20},{8,24},{12,28},{16,0},{20,4},{24,8},{28,12},{1,17},{... | collective-permute-start | bytes 1548296 | tf_op jit(solution)/shard_map/ppermute | solution.py:186
  526.6 9.0 %shard_map.68 = (bf16[224,2048]{1,0:T(8,128)(2,1)}, bf16[224,2048]{1,0:T(8,128)(2,1)}, bf16[224,2048]{1,0:T(8,128)(2,1)}, bf16[224,2048]{1,0:T(8,128)(2,1)}) custom-call(s32[10]{0:T(128)} %pad_add_fusion.1.refs_0_.meta_ref.refs_2_, bf16[1008,256]{1,0:T(8,128)(2,1)} %get-tuple-element.262.refs_1_, bf16[1008,256]{1,0:T(8,128)(2,1)} %copy-done.26, ...), custom_call_target="tpu_custom_call" | custom-call | flops 2055208960 | bytes 29818880 | tf_op jit(solution)/shard_map/pallas_call | solution.py:405
  541.8 18.7 %collective-permute-done.61.refs_3_ = bf16[1008,256]{1,0:T(8,128)(2,1)S(1)} collective-permute-done((bf16[1008,256]{1,0:T(8,128)(2,1)}, bf16[1008,256]{1,0:T(8,128)(2,1)S(1)}, u32[]{:S(2)}, u32[]{:S(2)}) %collective-permute-start.61) | collective-permute-done | bytes 516128 | tf_op jit(solution)/shard_map/ppermute | solution.py:186
  560.5 13.4 %collective-permute-done.63.refs_2_ = bf16[1008,256]{1,0:T(8,128)(2,1)S(1)} collective-permute-done((bf16[1008,256]{1,0:T(8,128)(2,1)S(1)}, bf16[1008,256]{1,0:T(8,128)(2,1)S(1)}, u32[]{:S(2)}, u32[]{:S(2)}) %collective-permute-start.63) | collective-permute-done | bytes 516128 | tf_op jit(solution)/shard_map/ppermute | solution.py:186
  624.2 19.4 %collective-permute-done.73 = bf16[224,2048]{1,0:T(8,128)(2,1)} collective-permute-done((bf16[224,2048]{1,0:T(8,128)(2,1)}, bf16[224,2048]{1,0:T(8,128)(2,1)}, u32[]{:S(2)}, u32[]{:S(2)}) %collective-permute-start.73) | collective-permute-done | bytes 917536 | tf_op jit(solution)/shard_map/ppermute | solution.py:186
  (314 shorter events, 288.0 us)
Async XLA Ops:
  19.5 40.7 %collective-permute-start.7 = (bf16[224,2048]{1,0:T(8,128)(2,1)S(1)}, bf16[224,2048]{1,0:T(8,128)(2,1)}, u32[]{:S(2)}, u32[]{:S(2)}) collective-permute-start(bf16[224,2048]{1,0:T(8,128)(2,1)S(1)} %get-tuple-element.299), channel_id=1, source_target_pairs={{0,2},{1,3},{2,0},{3,1},{4,6},{5,7},{6,4},{7,5},{8,10},{9,11},{10,... | collective-permute-start | bytes 2752520 | tf_op jit(solution)/shard_map/ppermute | solution.py:186
  20.4 39.8 %collective-permute-start.8 = (bf16[224,2048]{1,0:T(8,128)(2,1)S(1)}, bf16[224,2048]{1,0:T(8,128)(2,1)}, u32[]{:S(2)}, u32[]{:S(2)}) collective-permute-start(bf16[224,2048]{1,0:T(8,128)(2,1)S(1)} %get-tuple-element.298), channel_id=1, source_target_pairs={{0,3},{1,2},{2,1},{3,0},{4,7},{5,6},{6,5},{7,4},{8,11},{9,10},{10,... | collective-permute-start | bytes 2752520 | tf_op jit(solution)/shard_map/ppermute | solution.py:186
  80.8 45.6 %collective-permute-start.13 = (bf16[224,2048]{1,0:T(8,128)(2,1)S(1)}, bf16[224,2048]{1,0:T(8,128)(2,1)S(1)}, u32[]{:S(2)}, u32[]{:S(2)}) collective-permute-start(bf16[224,2048]{1,0:T(8,128)(2,1)S(1)} %get-tuple-element.297), channel_id=1, source_target_pairs={{0,1},{1,0},{2,3},{3,2},{4,5},{5,4},{6,7},{7,6},{8,9},{9,8},{10,11... | collective-permute-start | bytes 2752520 | tf_op jit(solution)/shard_map/ppermute | solution.py:186
  81.5 45.0 %collective-permute-start.14 = (bf16[224,2048]{1,0:T(8,128)(2,1)S(1)}, bf16[224,2048]{1,0:T(8,128)(2,1)S(1)}, u32[]{:S(2)}, u32[]{:S(2)}) collective-permute-start(bf16[224,2048]{1,0:T(8,128)(2,1)S(1)} %get-tuple-element.296), channel_id=1, source_target_pairs={{0,2},{1,3},{2,0},{3,1},{4,6},{5,7},{6,4},{7,5},{8,10},{9,11},{10,... | collective-permute-start | bytes 2752520 | tf_op jit(solution)/shard_map/ppermute | solution.py:186
  82.6 43.9 %collective-permute-start.15 = (bf16[224,2048]{1,0:T(8,128)(2,1)S(1)}, bf16[224,2048]{1,0:T(8,128)(2,1)S(1)}, u32[]{:S(2)}, u32[]{:S(2)}) collective-permute-start(bf16[224,2048]{1,0:T(8,128)(2,1)S(1)} %get-tuple-element.295), channel_id=1, source_target_pairs={{0,3},{1,2},{2,1},{3,0},{4,7},{5,6},{6,5},{7,4},{8,11},{9,10},{10,... | collective-permute-start | bytes 2752520 | tf_op jit(solution)/shard_map/ppermute | solution.py:186
  231.9 41.9 %collective-permute-start.27 = (bf16[3584,128]{1,0:T(8,128)(2,1)}, bf16[3584,128]{1,0:T(8,128)(2,1)S(1)}, u32[]{:S(2)}, u32[]{:S(2)}) collective-permute-start(bf16[3584,128]{1,0:T(8,128)(2,1)} %get-tuple-element.200), channel_id=1, source_target_pairs={{0,2},{1,3},{2,0},{3,1},{4,6},{5,7},{6,4},{7,5},{8,10},{9,11},{10,... | collective-permute-start | bytes 2752520 | tf_op jit(solution)/shard_map/ppermute | solution.py:186
  233.1 40.7 %collective-permute-start.28 = (bf16[3584,128]{1,0:T(8,128)(2,1)}, bf16[3584,128]{1,0:T(8,128)(2,1)S(1)}, u32[]{:S(2)}, u32[]{:S(2)}) collective-permute-start(bf16[3584,128]{1,0:T(8,128)(2,1)} %get-tuple-element.201), channel_id=1, source_target_pairs={{0,3},{1,2},{2,1},{3,0},{4,7},{5,6},{6,5},{7,4},{8,11},{9,10},{10,... | collective-permute-start | bytes 2752520 | tf_op jit(solution)/shard_map/ppermute | solution.py:186
  289.9 47.2 %collective-permute-start.32 = (bf16[3584,128]{1,0:T(8,128)(2,1)}, bf16[3584,128]{1,0:T(8,128)(2,1)S(1)}, u32[]{:S(2)}, u32[]{:S(2)}) collective-permute-start(bf16[3584,128]{1,0:T(8,128)(2,1)} %get-tuple-element.209), channel_id=1, source_target_pairs={{0,1},{1,0},{2,3},{3,2},{4,5},{5,4},{6,7},{7,6},{8,9},{9,8},{10,11... | collective-permute-start | bytes 2752520 | tf_op jit(solution)/shard_map/ppermute | solution.py:186
  291.3 45.8 %collective-permute-start.33 = (bf16[3584,128]{1,0:T(8,128)(2,1)}, bf16[3584,128]{1,0:T(8,128)(2,1)S(1)}, u32[]{:S(2)}, u32[]{:S(2)}) collective-permute-start(bf16[3584,128]{1,0:T(8,128)(2,1)} %get-tuple-element.210), channel_id=1, source_target_pairs={{0,2},{1,3},{2,0},{3,1},{4,6},{5,7},{6,4},{7,5},{8,10},{9,11},{10,... | collective-permute-start | bytes 2752520 | tf_op jit(solution)/shard_map/ppermute | solution.py:186
  291.9 45.3 %collective-permute-start.34 = (bf16[3584,128]{1,0:T(8,128)(2,1)}, bf16[3584,128]{1,0:T(8,128)(2,1)S(1)}, u32[]{:S(2)}, u32[]{:S(2)}) collective-permute-start(bf16[3584,128]{1,0:T(8,128)(2,1)} %get-tuple-element.211), channel_id=1, source_target_pairs={{0,3},{1,2},{2,1},{3,0},{4,7},{5,6},{6,5},{7,4},{8,11},{9,10},{10,... | collective-permute-start | bytes 2752520 | tf_op jit(solution)/shard_map/ppermute | solution.py:186
  348.5 48.6 %collective-permute-start.44 = (bf16[3584,128]{1,0:T(8,128)(2,1)}, bf16[3584,128]{1,0:T(8,128)(2,1)S(1)}, u32[]{:S(2)}, u32[]{:S(2)}) collective-permute-start(bf16[3584,128]{1,0:T(8,128)(2,1)} %shard_map.61.refs_3_), channel_id=1, source_target_pairs={{0,1},{1,0},{2,3},{3,2},{4,5},{5,4},{6,7},{7,6},{8,9},{9,8},{10,11... | collective-permute-start | bytes 2752520 | tf_op jit(solution)/shard_map/ppermute | solution.py:186
  349.7 47.4 %collective-permute-start.45 = (bf16[3584,128]{1,0:T(8,128)(2,1)}, bf16[3584,128]{1,0:T(8,128)(2,1)S(1)}, u32[]{:S(2)}, u32[]{:S(2)}) collective-permute-start(bf16[3584,128]{1,0:T(8,128)(2,1)} %shard_map.61.refs_3_), channel_id=1, source_target_pairs={{0,2},{1,3},{2,0},{3,1},{4,6},{5,7},{6,4},{7,5},{8,10},{9,11},{10,... | collective-permute-start | bytes 2752520 | tf_op jit(solution)/shard_map/ppermute | solution.py:186
  361.9 42.0 %collective-permute-start.50 = (bf16[3584,128]{1,0:T(8,128)(2,1)}, bf16[3584,128]{1,0:T(8,128)(2,1)S(1)}, u32[]{:S(2)}, u32[]{:S(2)}) collective-permute-start(bf16[3584,128]{1,0:T(8,128)(2,1)} %shard_map.61.refs_3_), channel_id=1, source_target_pairs={{0,4},{4,0},{8,12},{12,8},{16,20},{20,16},{24,28},{28,24},{1,5},{5... | collective-permute-start | bytes 2752520 | tf_op jit(solution)/shard_map/ppermute | solution.py:186
  401.6 38.7 %collective-permute-start.48 = (bf16[3584,128]{1,0:T(8,128)(2,1)}, bf16[3584,128]{1,0:T(8,128)(2,1)S(1)}, u32[]{:S(2)}, u32[]{:S(2)}) collective-permute-start(bf16[3584,128]{1,0:T(8,128)(2,1)} %shard_map.64.refs_7_), channel_id=1, source_target_pairs={{0,2},{1,3},{2,0},{3,1},{4,6},{5,7},{6,4},{7,5},{8,10},{9,11},{10,... | collective-permute-start | bytes 2752520 | tf_op jit(solution)/shard_map/ppermute | solution.py:186
  402.4 39.3 %collective-permute-start.49 = (bf16[3584,128]{1,0:T(8,128)(2,1)}, bf16[3584,128]{1,0:T(8,128)(2,1)S(1)}, u32[]{:S(2)}, u32[]{:S(2)}) collective-permute-start(bf16[3584,128]{1,0:T(8,128)(2,1)} %shard_map.64.refs_7_), channel_id=1, source_target_pairs={{0,3},{1,2},{2,1},{3,0},{4,7},{5,6},{6,5},{7,4},{8,11},{9,10},{10,... | collective-permute-start | bytes 2752520 | tf_op jit(solution)/shard_map/ppermute | solution.py:186
  403.9 38.4 %collective-permute-start.51 = (bf16[3584,128]{1,0:T(8,128)(2,1)S(1)}, bf16[3584,128]{1,0:T(8,128)(2,1)S(1)}, u32[]{:S(2)}, u32[]{:S(2)}) collective-permute-start(bf16[3584,128]{1,0:T(8,128)(2,1)S(1)} %collective-permute-done.44.refs_4_), channel_id=1, source_target_pairs={{0,4},{4,0},{8,12},{12,8},{16,20},{20,16},{24,28},{28,24},{1,5},{5... | collective-permute-start | bytes 2752520 | tf_op jit(solution)/shard_map/ppermute | solution.py:186
  473.3 39.0 %collective-permute-start.58 = (bf16[1008,256]{1,0:T(8,128)(2,1)}, bf16[1008,256]{1,0:T(8,128)(2,1)S(1)}, u32[]{:S(2)}, u32[]{:S(2)}) collective-permute-start(bf16[1008,256]{1,0:T(8,128)(2,1)} %get-tuple-element.229), channel_id=1, source_target_pairs={{0,16},{4,20},{8,24},{12,28},{16,0},{20,4},{24,8},{28,12},{1,17},{... | collective-permute-start | bytes 1548296 | tf_op jit(solution)/shard_map/ppermute | solution.py:186
  516.1 44.4 %collective-permute-start.61 = (bf16[1008,256]{1,0:T(8,128)(2,1)}, bf16[1008,256]{1,0:T(8,128)(2,1)S(1)}, u32[]{:S(2)}, u32[]{:S(2)}) collective-permute-start(bf16[1008,256]{1,0:T(8,128)(2,1)} %get-tuple-element.250), channel_id=1, source_target_pairs={{0,16},{4,20},{8,24},{12,28},{16,0},{20,4},{24,8},{28,12},{1,17},{... | collective-permute-start | bytes 1548296 | tf_op jit(solution)/shard_map/ppermute | solution.py:186
  535.5 38.4 %collective-permute-start.65 = (bf16[224,2048]{1,0:T(8,128)(2,1)}, bf16[224,2048]{1,0:T(8,128)(2,1)}, u32[]{:S(2)}, u32[]{:S(2)}) collective-permute-start(bf16[224,2048]{1,0:T(8,128)(2,1)} %get-tuple-element.267), channel_id=1, source_target_pairs={{0,1},{1,0},{2,3},{3,2},{4,5},{5,4},{6,7},{7,6},{8,9},{9,8},{10,11... | collective-permute-start | bytes 2752520 | tf_op jit(solution)/shard_map/ppermute | solution.py:186
  537.7 42.2 %collective-permute-start.66 = (bf16[224,2048]{1,0:T(8,128)(2,1)}, bf16[224,2048]{1,0:T(8,128)(2,1)}, u32[]{:S(2)}, u32[]{:S(2)}) collective-permute-start(bf16[224,2048]{1,0:T(8,128)(2,1)} %get-tuple-element.268), channel_id=1, source_target_pairs={{0,2},{1,3},{2,0},{3,1},{4,6},{5,7},{6,4},{7,5},{8,10},{9,11},{10,... | collective-permute-start | bytes 2752520 | tf_op jit(solution)/shard_map/ppermute | solution.py:186
  539.1 40.7 %collective-permute-start.67 = (bf16[224,2048]{1,0:T(8,128)(2,1)}, bf16[224,2048]{1,0:T(8,128)(2,1)}, u32[]{:S(2)}, u32[]{:S(2)}) collective-permute-start(bf16[224,2048]{1,0:T(8,128)(2,1)} %get-tuple-element.269), channel_id=1, source_target_pairs={{0,3},{1,2},{2,1},{3,0},{4,7},{5,6},{6,5},{7,4},{8,11},{9,10},{10,... | collective-permute-start | bytes 2752520 | tf_op jit(solution)/shard_map/ppermute | solution.py:186
  600.3 43.3 %collective-permute-start.73 = (bf16[224,2048]{1,0:T(8,128)(2,1)}, bf16[224,2048]{1,0:T(8,128)(2,1)}, u32[]{:S(2)}, u32[]{:S(2)}) collective-permute-start(bf16[224,2048]{1,0:T(8,128)(2,1)} %get-tuple-element.285), channel_id=1, source_target_pairs={{0,2},{1,3},{2,0},{3,1},{4,6},{5,7},{6,4},{7,5},{8,10},{9,11},{10,... | collective-permute-start | bytes 2752520 | tf_op jit(solution)/shard_map/ppermute | solution.py:186
  602.6 42.3 %collective-permute-start.74 = (bf16[224,2048]{1,0:T(8,128)(2,1)}, bf16[224,2048]{1,0:T(8,128)(2,1)}, u32[]{:S(2)}, u32[]{:S(2)}) collective-permute-start(bf16[224,2048]{1,0:T(8,128)(2,1)} %get-tuple-element.286), channel_id=1, source_target_pairs={{0,3},{1,2},{2,1},{3,0},{4,7},{5,6},{6,5},{7,4},{8,11},{9,10},{10,... | collective-permute-start | bytes 2752520 | tf_op jit(solution)/shard_map/ppermute | solution.py:186
  611.8 40.3 %collective-permute-start.76 = (bf16[224,512]{1,0:T(8,128)(2,1)}, bf16[224,512]{1,0:T(8,128)(2,1)S(1)}, u32[]{:S(2)}, u32[]{:S(2)}) collective-permute-start(bf16[224,512]{1,0:T(8,128)(2,1)} %get-tuple-element.293), channel_id=1, source_target_pairs={{0,2},{1,3},{2,0},{3,1},{4,6},{5,7},{6,4},{7,5},{8,10},{9,11},{10,... | collective-permute-start | bytes 688136 | tf_op jit(solution)/shard_map/ppermute | solution.py:186
  (120 other events, 1980.1 us)

commit v9 on v7

--- a/solution.py
+++ b/solution.py
@@ -187,17 +187,8 @@
 
 
 def pack_kernel(step, col_count, meta_ref, *refs):
-    pieces, outs, choose = refs[:col_count], refs[col_count:-1], refs[-1]
+    pieces, choose, outs = refs[:col_count], refs[col_count], refs[col_count + 1 :]
     turn = pl.program_id(0)
-    _, window, slots = choose.shape
-
-    @pl.when(turn == 0)
-    def _():
-        rows = lax.broadcasted_iota(jnp.int32, (window, slots), 0)
-        columns = lax.broadcasted_iota(jnp.int32, (window, slots), 1)
-        for k in range(col_count):
-            hit = (rows == columns + meta_ref[2 + k]) & (columns < meta_ref[2 + col_count + k])
-            choose[k] = jnp.where(hit, 1.0, 0.0).astype(jnp.bfloat16)
 
     total = jnp.dot(choose[0], pieces[0][...], preferred_element_type=jnp.float32)
     for k in range(1, col_count):
@@ -209,7 +200,7 @@
             out[...] = total.astype(jnp.bfloat16)
 
 
-def pack(meta, momentum, received, base, width, step, count, window):
+def pack(meta, choose, momentum, received, base, width, step, count, window):
     slots = momentum.shape[0]
     col_count = len(received) + 1
     first = base // width
@@ -226,9 +217,9 @@
                 )
             ]
             + [pl.BlockSpec((slots, width), lambda q, meta: (0, (meta[0] // step) ^ q))]
-            * (col_count - 1),
+            * (col_count - 1)
+            + [pl.BlockSpec(choose.shape, lambda q, meta: (0, 0, 0))],
             out_specs=[pl.BlockSpec((window, width), lambda q, meta: (0, 0))] * count,
-            scratch_shapes=[pltpu.VMEM((col_count, window, slots), jnp.bfloat16)],
         ),
         compiler_params=pltpu.CompilerParams(vmem_limit_bytes=VMEM_LIMIT),
         cost_estimate=pl.CostEstimate(
@@ -236,17 +227,12 @@
             bytes_accessed=2 * count * width * (slots * col_count + window),
             transcendentals=0,
         ),
-    )(meta, momentum, *received)
+    )(meta, momentum, *received, choose)
 
 
 def pack_pair_kernel(col_count, meta_ref, *refs):
-    pieces, keep, give, choose = refs[:col_count], refs[col_count], refs[col_count + 1], refs[-1]
+    pieces, choose, keep, give = refs[:col_count], refs[-3], refs[-2], refs[-1]
     other = pl.program_id(0) == 0
-    _, window, slots = choose.shape
-
-    @pl.when(other & (pl.program_id(1) == 0))
-    def _():
-        fill_choose(meta_ref, choose, 0)
 
     total = jnp.dot(choose[0], pieces[0][...], preferred_element_type=jnp.float32)
     for k in range(1, col_count):
@@ -261,17 +247,15 @@
         keep[...] = total.astype(jnp.bfloat16)
 
 
-def fill_choose(meta_ref, choose, slot_axis):
-    col_count = choose.shape[0]
-    shape = choose.shape[1:]
-    rows = lax.broadcasted_iota(jnp.int32, shape, slot_axis)
-    slots = lax.broadcasted_iota(jnp.int32, shape, 1 - slot_axis)
-    for k in range(col_count):
-        hit = (rows == slots + meta_ref[2 + k]) & (slots < meta_ref[2 + col_count + k])
-        choose[k] = jnp.where(hit, 1.0, 0.0).astype(jnp.bfloat16)
-
-
-def pack_pair(meta, momentum, received, base, width, row_count, window):
+def selections(meta, col_count, slots, window):
+    begin, length = meta[2 : 2 + col_count], meta[2 + col_count :]
+    row = jnp.arange(window, dtype=jnp.int32)[None, :, None]
+    slot = jnp.arange(slots, dtype=jnp.int32)[None, None, :]
+    hit = (row == slot + begin[:, None, None]) & (slot < length[:, None, None])
+    return hit.astype(jnp.bfloat16)
+
+
+def pack_pair(meta, choose, momentum, received, base, width, row_count, window):
     slots = momentum.shape[0]
     col_count = len(received) + 1
     pairs = row_count // 2
@@ -291,14 +275,14 @@
                 )
             ]
             + [pl.BlockSpec((slots, width), lambda e, q, meta: (0, block(e, q, meta)))]
-            * (col_count - 1),
+            * (col_count - 1)
+            + [pl.BlockSpec(choose.shape, lambda e, q, meta: (0, 0, 0))],
             out_specs=[
                 pl.BlockSpec((window, width), lambda e, q, meta: (jnp.where(e == 0, 0, q), 0)),
                 pl.BlockSpec(
                     (window, width), lambda e, q, meta: (jnp.where(e == 0, q, pairs - 1), 0)
                 ),
             ],
-            scratch_shapes=[pltpu.VMEM((col_count, window, slots), jnp.bfloat16)],
         ),
         compiler_params=pltpu.CompilerParams(vmem_limit_bytes=VMEM_LIMIT),
         cost_estimate=pl.CostEstimate(
@@ -306,7 +290,7 @@
             bytes_accessed=2 * row_count * width * (slots * col_count + window),
             transcendentals=0,
         ),
-    )(meta, momentum, *received)
+    )(meta, momentum, *received, choose)
 
 
 def join_kernel(even, window, meta_ref, keep, got, *outs):
@@ -372,13 +356,9 @@
 
 
 def unpack_pair_kernel(col_count, even, window, meta_ref, *refs):
-    got, outs, choose = refs[-2 - col_count], refs[-1 - col_count : -1], refs[-1]
-    pieces = refs[: -2 - col_count]
+    pieces, outs = refs[: -2 - col_count], refs[-col_count:]
+    got, choose = refs[-2 - col_count], refs[-1 - col_count]
     turn = pl.program_id(0)
-
-    @pl.when(turn == 0)
-    def _():
-        fill_choose(meta_ref, choose, 1)
 
     def place(block):
         for k in range(col_count):
@@ -399,7 +379,7 @@
         place(got[part, :])
 
 
-def unpack_pair(meta, pieces, got, col_count, slots, even, window):
+def unpack_pair(meta, choose, pieces, got, col_count, slots, even, window):
     width = got.shape[1]
     count = 2 * len(pieces)
     return pl.pallas_call(
@@ -408,10 +388,10 @@
         grid_spec=pltpu.PrefetchScalarGridSpec(
             num_scalar_prefetch=1,
             grid=(count,),
-            in_specs=[pl.BlockSpec(x.shape, lambda q, meta: (0, 0)) for x in (*pieces, got)],
+            in_specs=[pl.BlockSpec(x.shape, lambda q, meta: (0, 0)) for x in (*pieces, got)]
+            + [pl.BlockSpec(choose.shape, lambda q, meta: (0, 0, 0))],
             out_specs=[pl.BlockSpec((slots, width), lambda q, meta: (0, meta[0] ^ q))]
             * col_count,
-            scratch_shapes=[pltpu.VMEM((col_count, slots, window), jnp.bfloat16)],
         ),
         compiler_params=pltpu.CompilerParams(vmem_limit_bytes=VMEM_LIMIT),
         cost_estimate=pl.CostEstimate(
@@ -419,21 +399,12 @@
             bytes_accessed=2 * count * width * (slots * col_count + window),
             transcendentals=0,
         ),
-    )(meta, *pieces, got)
+    )(meta, *pieces, got, choose)
 
 
 def unpack_kernel(col_count, meta_ref, *refs):
-    pieces, outs, choose = refs[: -1 - col_count], refs[-1 - col_count : -1], refs[-1]
+    pieces, choose, outs = refs[: -1 - col_count], refs[-1 - col_count], refs[-col_count:]
     turn = pl.program_id(0)
-    _, slots, window = choose.shape
-
-    @pl.when(turn == 0)
-    def _():
-        rows = lax.broadcasted_iota(jnp.int32, (slots, window), 1)
-        columns = lax.broadcasted_iota(jnp.int32, (slots, window), 0)
-        for k in range(col_count):
-            hit = (rows == columns + meta_ref[2 + k]) & (columns < meta_ref[2 + col_count + k])
-            choose[k] = jnp.where(hit, 1.0, 0.0).astype(jnp.bfloat16)
 
     for q, piece in enumerate(pieces):
 
@@ -445,7 +416,7 @@
                 ).astype(jnp.bfloat16)
 
 
-def unpack(meta, pieces, col_count, slots, step):
+def unpack(meta, choose, pieces, col_count, slots, step):
     window, width = pieces[0].shape
     count = len(pieces)
     return pl.pallas_call(
@@ -454,10 +425,10 @@
         grid_spec=pltpu.PrefetchScalarGridSpec(
             num_scalar_prefetch=1,
             grid=(count,),
-            in_specs=[pl.BlockSpec((window, width), lambda q, meta: (0, 0))] * count,
+            in_specs=[pl.BlockSpec((window, width), lambda q, meta: (0, 0))] * count
+            + [pl.BlockSpec(choose.shape, lambda q, meta: (0, 0, 0))],
             out_specs=[pl.BlockSpec((slots, width), lambda q, meta: (0, (meta[0] // step) ^ q))]
             * col_count,
-            scratch_shapes=[pltpu.VMEM((col_count, slots, window), jnp.bfloat16)],
         ),
         compiler_params=pltpu.CompilerParams(vmem_limit_bytes=VMEM_LIMIT),
         cost_estimate=pl.CostEstimate(
@@ -465,7 +436,7 @@
             bytes_accessed=2 * count * width * (slots * col_count + window),
             transcendentals=0,
         ),
-    )(meta, *pieces)
+    )(meta, *pieces, choose)
 
 
 def merge_kernel(unit, share, distances, meta_ref, *refs):
@@ -525,9 +496,9 @@
 PART = HALF // PIECES
 
 
-def half_gram_kernel(flip, rows_ref, cols_ref, meta_ref, joined, *outs):
+def half_gram_kernel(flip, first, rows_ref, cols_ref, meta_ref, joined, *outs):
     turn = pl.program_id(0)
-    pair = (meta_ref[0] % 2 ^ flip) * HALF + turn
+    pair = (meta_ref[0] % 2 ^ flip) * HALF + first * PART + turn
     here = pl.ds(pl.multiple_of(rows_ref[pair] * TILE, TILE), TILE)
     there = pl.ds(pl.multiple_of(cols_ref[pair] * TILE, TILE), TILE)
     tile = lax.dot_general(
@@ -543,22 +514,23 @@
             out[...] = tile
 
 
-def half_gram(meta, joined, flip):
+def half_gram(meta, joined, flip, first, pieces):
+    count = pieces * PART
     width = joined.shape[1]
     place = lambda n: lambda p, rows, cols, meta: (jnp.clip(p - n * PART, 0, PART - 1), 0)
     return pl.pallas_call(
-        lambda *refs: half_gram_kernel(flip, *refs),
-        out_shape=[jax.ShapeDtypeStruct((PART * TILE, TILE), jnp.bfloat16)] * PIECES,
+        lambda *refs: half_gram_kernel(flip, first, *refs),
+        out_shape=[jax.ShapeDtypeStruct((PART * TILE, TILE), jnp.bfloat16)] * pieces,
         grid_spec=pltpu.PrefetchScalarGridSpec(
             num_scalar_prefetch=3,
-            grid=(HALF,),
+            grid=(count,),
             in_specs=[pl.BlockSpec((M, width), lambda p, rows, cols, meta: (0, 0))],
-            out_specs=[pl.BlockSpec((TILE, TILE), place(n)) for n in range(PIECES)],
+            out_specs=[pl.BlockSpec((TILE, TILE), place(n)) for n in range(pieces)],
         ),
         compiler_params=pltpu.CompilerParams(vmem_limit_bytes=VMEM_LIMIT),
         cost_estimate=pl.CostEstimate(
-            flops=2 * HALF * TILE * TILE * width,
-            bytes_accessed=2 * HALF * TILE * TILE + 2 * M * width,
+            flops=2 * count * TILE * TILE * width,
+            bytes_accessed=2 * count * TILE * TILE + 2 * M * width,
             transcendentals=0,
         ),
     )(jnp.asarray(PAIR_ROWS), jnp.asarray(PAIR_COLS), meta, joined)
@@ -830,13 +802,14 @@
     def over_pairs(blocks):
         return [swap(blocks[q], "row", row_count, 2 * q) for q in range(1, pair_count)]
 
-    give = half_gram(meta, joined, 1)
+    give = half_gram(meta, joined, 1, 0, PIECES)
     got = [swap(piece, "row", row_count, 1) for piece in give]
-    keep = half_gram(meta, joined, 0)
-
+    keep = half_gram(meta, joined, 0, 0, 1)
     early = add_halves(meta, keep[0], got[0], col_count)
+    early, joined = tie((early, joined))
     early_in = over_cols(early)
-    late = add_halves(meta, keep[1], got[1], col_count)
+    keep = half_gram(meta, joined, 0, 1, 1)
+    late = add_halves(meta, keep[0], got[1], col_count)
     late, early_in = tie((late, early_in))
     late_in = over_cols(late)
     early_parts = add_quarters(meta, [early[0]] + early_in, pair_count)
@@ -878,6 +851,9 @@
         [row[None], col[None], begins - (row * even - jitter), shard_ends[members] - begins]
     )
 
+    choose = selections(meta, col_count, slots, window)
+    spread = jnp.swapaxes(choose, 1, 2)
+
     wide = row_count * col_count * CHUNK
     number = (N // (row_count * col_count)) // CHUNK
     distances = list(range(pair_count))
@@ -908,14 +884,14 @@
 
     def gather_chunk(c, received):
         keep, give = pack_pair(
-            meta, momentum_shards, received, c * wide, CHUNK, row_count, window
+            meta, choose, momentum_shards, received, c * wide, CHUNK, row_count, window
         )
         return join(meta, keep, swap(give, "row", row_count, 1), even, window, pair_count)
 
     last, _ = fetch(number * wide, pair_count * LAST, shard_starts)
     received, last = fetch(0, row_count * CHUNK, last)
     pieces = pack(
-        meta, momentum_shards, last, number * wide, LAST, 2, pair_count, window
+        meta, choose, momentum_shards, last, number * wide, LAST, 2, pair_count, window
     )
     crossed_last, received = tie(across(pieces), received)
     joined = gather_chunk(0, received)
@@ -958,10 +934,10 @@
         if c < number:
             got = swap(cut(meta, crossed[c], even, window), "row", row_count, 1)
             parts = list(
-                unpack_pair(meta, crossed[c], got, col_count, slots, even, window)
+                unpack_pair(meta, spread, crossed[c], got, col_count, slots, even, window)
             )
         else:
-            parts = unpack(meta, crossed[c], col_count, slots, 2)
+            parts = unpack(meta, spread, crossed[c], col_count, slots, 2)
         if c + 1 == number:
             crossed[c + 1], parts[0] = tie(crossed[c + 1], parts[0])
         back = [parts[0]] + [swap(parts[k], "col", col_count, k) for k in range(1, col_count)]

time: 656 us -> 653 us (level)
  waiting for transfers between devices: 314 us -> 302 us
    ppermute x78, waiting for transfers between devices: 314 us -> 302 us  [swap(): lax.ppermute(value, axis, perm=[(i, i ^ distance) for i in range(size)])]
    pallas_call x2 -> x3, Pallas kernels: 28.2 us -> 31.7 us  [half_gram(): pl.pallas_call(lambda *refs: half_gram_kernel(flip, first, *refs), out_sh...]
    unnamed x132 -> x138, local copies, waits for them, and re-layouts: 22.1 us -> 23.3 us
  transfers between devices with their start and end apart: 78 -> 78, of which waited for: 38 -> 38; matrix products, arithmetic and copies ran while one was open for 3% -> 3% of each run, Pallas kernels for 16% -> 17%
where the time goes in v9:
time: 653 us; the launch traced here: 651 us
  waiting for transfers between devices  302 us (46%)
  Pallas kernels  195 us (30%)
  starting transfers between devices  107 us (16%)
  local copies, waits for them, and re-layouts  43.1 us (7%)
    ppermute x78, waiting for transfers between devices, swap(): lax.ppermute(value, axis, perm=[(i, i ^ distance) for i in range(size)])  302 us
    ppermute x78, starting transfers between devices, swap(): lax.ppermute(value, axis, perm=[(i, i ^ distance) for i in range(size)])  107 us
    pallas_call x14, Pallas kernels, local_call(): pl.pallas_call(kernel, out_shape=out_shape, in_specs=[pl.BlockSpec(memory...  42.4 us
    pallas_call x1, Pallas kernels, next_apply(): pl.pallas_call(lambda *refs: next_apply_kernel(jitter, sends, *refs), out...  35.1 us
    pallas_call x3, Pallas kernels, half_gram(): pl.pallas_call(lambda *refs: half_gram_kernel(flip, first, *refs), out_sh...  31.7 us
    pallas_call x1, Pallas kernels, first_apply(): pl.pallas_call(lambda *refs: first_apply_kernel(jitter, send, col_count,...  25.4 us
    unnamed x138, local copies, waits for them, and re-layouts  23.3 us
    pallas_call x2, Pallas kernels, pack_pair(): pl.pallas_call(lambda *refs: pack_pair_kernel(col_count, *refs), out_shap...  18.5 us
  transfers between devices with their start and end apart: 78, of which 38 were waited for; matrix products, arithmetic and copies ran while one was open for 3% of the time, Pallas kernels for 17%

profile of v9, /device:TPU:0, one launch (start us, length us, event | category | flops | bytes accessed | tf_op | source)
XLA Modules:
  0.0 651.0 jit_solution(677785152300606687)
XLA Ops:
  47.1 13.1 %collective-permute-done.7.refs_3_ = bf16[224,2048]{1,0:T(8,128)(2,1)S(1)} collective-permute-done((bf16[224,2048]{1,0:T(8,128)(2,1)S(1)}, bf16[224,2048]{1,0:T(8,128)(2,1)S(1)}, u32[]{:S(2)}, u32[]{:S(2)}) %collective-permute-start.7) | collective-permute-done | bytes 917536 | tf_op jit(solution)/shard_map/ppermute | solution.py:186
  61.5 9.2 %shard_map.47 = (bf16[2240,256]{1,0:T(8,128)(2,1)}, bf16[2240,256]{1,0:T(8,128)(2,1)}) custom-call(s32[10]{0:T(128)} %pad_add_fusion.1.refs_0_.meta_ref.refs_2_, bf16[224,18432]{1,0:T(8,128)(2,1)} %refs_1_.9, bf16[224,2048]{1,0:T(8,128)(2,1)} %copy-done.5, bf16[224,2048]{1,0:T(8,128)(2,1)} %copy-done.6, bf16[224,2048]{1,0:T(8,128)(2,1)} %copy-done.7, ...), custom_call_target="tpu_custom_call" | custom-call | flops 2055208960 | bytes 5963776 | tf_op jit(solution)/shard_map/pallas_call | solution.py:265
  87.4 28.4 %collective-permute-done.10.refs_3_ = bf16[1008,256]{1,0:T(8,128)(2,1)S(1)} collective-permute-done((bf16[1008,256]{1,0:T(8,128)(2,1)}, bf16[1008,256]{1,0:T(8,128)(2,1)S(1)}, u32[]{:S(2)}, u32[]{:S(2)}) %collective-permute-start.10) | collective-permute-done | bytes 516128 | tf_op jit(solution)/shard_map/ppermute | solution.py:186
  115.8 12.3 %collective-permute-done.12.refs_2_ = bf16[1008,256]{1,0:T(8,128)(2,1)S(1)} collective-permute-done((bf16[1008,256]{1,0:T(8,128)(2,1)}, bf16[1008,256]{1,0:T(8,128)(2,1)S(1)}, u32[]{:S(2)}, u32[]{:S(2)}) %collective-permute-start.12) | collective-permute-done | bytes 516128 | tf_op jit(solution)/shard_map/ppermute | solution.py:186
  130.4 9.2 %shard_map.50 = (bf16[2240,256]{1,0:T(8,128)(2,1)}, bf16[2240,256]{1,0:T(8,128)(2,1)}) custom-call(s32[10]{0:T(128)} %pad_add_fusion.1.refs_0_.meta_ref.refs_2_, bf16[224,18432]{1,0:T(8,128)(2,1)} %refs_1_.9, bf16[224,2048]{1,0:T(8,128)(2,1)} %copy-done.8, bf16[224,2048]{1,0:T(8,128)(2,1)} %copy-done.9, bf16[224,2048]{1,0:T(8,128)(2,1)} %copy-done.10, ...), custom_call_target="tpu_custom_call" | custom-call | flops 2055208960 | bytes 5963776 | tf_op jit(solution)/shard_map/pallas_call | solution.py:265
  162.1 9.3 %collective-permute-done.17.refs_2_ = bf16[1008,256]{1,0:T(8,128)(2,1)S(1)} collective-permute-done((bf16[1008,256]{1,0:T(8,128)(2,1)}, bf16[1008,256]{1,0:T(8,128)(2,1)S(1)}, u32[]{:S(2)}, u32[]{:S(2)}) %collective-permute-start.17) | collective-permute-done | bytes 516128 | tf_op jit(solution)/shard_map/ppermute | solution.py:186
  171.4 15.2 %collective-permute-done.18.refs_3_ = bf16[1008,256]{1,0:T(8,128)(2,1)S(1)} collective-permute-done((bf16[1008,256]{1,0:T(8,128)(2,1)}, bf16[1008,256]{1,0:T(8,128)(2,1)S(1)}, u32[]{:S(2)}, u32[]{:S(2)}) %collective-permute-start.18) | collective-permute-done | bytes 516128 | tf_op jit(solution)/shard_map/ppermute | solution.py:186
  196.2 14.1 %shard_map.56 = (bf16[3584,512]{1,0:T(8,128)(2,1)}, bf16[3584,512]{1,0:T(8,128)(2,1)}) custom-call(s32[28]{0:T(128)} %constant.61.clone.refs_0_, s32[28]{0:T(128)} %constant.62.clone.refs_1_, s32[10]{0:T(128)} %pad_add_fusion.1.refs_0_.meta_ref.refs_2_, bf16[3584,640]{1,0:T(8,128)(2,1)} %shard_map.54.refs_3_), custom_call_target="tpu_custom_call" | custom-call | flops 4697620480 | bytes 11927552 | tf_op jit(solution)/shard_map/pallas_call | solution.py:521
  231.5 8.8 %shard_map.58.refs_0_.refs_1_.refs_2_.refs_3_ = bf16[3584,512]{1,0:T(8,128)(2,1)} custom-call(s32[28]{0:T(128)} %constant.61.clone.refs_0_, s32[28]{0:T(128)} %constant.62.clone.refs_1_, s32[10]{0:T(128)} %pad_add_fusion.1.refs_0_.meta_ref.refs_2_, bf16[3584,640]{1,0:T(8,128)(2,1)} %shard_map.54.refs_3_), custom_call_target="tpu_custom_call" | custom-call | flops 2348810240 | bytes 8257536 | tf_op jit(solution)/shard_map/pallas_call | solution.py:521
  251.5 19.0 %collective-permute-done.27.refs_3_ = bf16[3584,128]{1,0:T(8,128)(2,1)S(1)} collective-permute-done((bf16[3584,128]{1,0:T(8,128)(2,1)}, bf16[3584,128]{1,0:T(8,128)(2,1)S(1)}, u32[]{:S(2)}, u32[]{:S(2)}) %collective-permute-start.27) | collective-permute-done | bytes 917536 | tf_op jit(solution)/shard_map/ppermute | solution.py:186
  275.1 10.6 %collective-permute-start.29 = (bf16[896,128]{1,0:T(8,128)(2,1)}, bf16[896,128]{1,0:T(8,128)(2,1)S(1)}, u32[]{:S(2)}, u32[]{:S(2)}) collective-permute-start(bf16[896,128]{1,0:T(8,128)(2,1)} %get-tuple-element.212), channel_id=1, source_target_pairs={{0,8},{4,12},{8,0},{12,4},{16,24},{20,28},{24,16},{28,20},{1,9},{5... | collective-permute-start | bytes 688136 | tf_op jit(solution)/shard_map/ppermute | solution.py:186
  294.3 12.5 %collective-permute-done.30.refs_2_ = bf16[896,128]{1,0:T(8,128)(2,1)S(1)} collective-permute-done((bf16[896,128]{1,0:T(8,128)(2,1)}, bf16[896,128]{1,0:T(8,128)(2,1)S(1)}, u32[]{:S(2)}, u32[]{:S(2)}) %collective-permute-start.30) | collective-permute-done | bytes 229408 | tf_op jit(solution)/shard_map/ppermute | solution.py:186
  350.3 10.0 %collective-permute-done.39.refs_2_ = bf16[896,128]{1,0:T(8,128)(2,1)S(1)} collective-permute-done((bf16[896,128]{1,0:T(8,128)(2,1)}, bf16[896,128]{1,0:T(8,128)(2,1)S(1)}, u32[]{:S(2)}, u32[]{:S(2)}) %collective-permute-start.39) | collective-permute-done | bytes 229408 | tf_op jit(solution)/shard_map/ppermute | solution.py:186
  373.3 9.3 %collective-permute-done.42.refs_2_ = bf16[896,128]{1,0:T(8,128)(2,1)S(1)} collective-permute-done((bf16[896,128]{1,0:T(8,128)(2,1)}, bf16[896,128]{1,0:T(8,128)(2,1)S(1)}, u32[]{:S(2)}, u32[]{:S(2)}) %collective-permute-start.42) | collective-permute-done | bytes 229408 | tf_op jit(solution)/shard_map/ppermute | solution.py:186
  398.8 19.5 %collective-permute-done.47.refs_8_ = bf16[3584,128]{1,0:T(8,128)(2,1)S(1)} collective-permute-done((bf16[3584,128]{1,0:T(8,128)(2,1)}, bf16[3584,128]{1,0:T(8,128)(2,1)S(1)}, u32[]{:S(2)}, u32[]{:S(2)}) %collective-permute-start.47) | collective-permute-done | bytes 917536 | tf_op jit(solution)/shard_map/ppermute | solution.py:186
  418.2 16.3 %collective-permute-done.48.refs_9_ = bf16[3584,128]{1,0:T(8,128)(2,1)S(1)} collective-permute-done((bf16[3584,128]{1,0:T(8,128)(2,1)}, bf16[3584,128]{1,0:T(8,128)(2,1)S(1)}, u32[]{:S(2)}, u32[]{:S(2)}) %collective-permute-start.48) | collective-permute-done | bytes 917536 | tf_op jit(solution)/shard_map/ppermute | solution.py:186
  442.1 25.4 %shard_map.66 = (bf16[1008,256]{1,0:T(8,128)(2,1)}, bf16[1008,256]{1,0:T(8,128)(2,1)}, bf16[1008,256]{1,0:T(8,128)(2,1)}, bf16[1008,256]{1,0:T(8,128)(2,1)}, bf16[7,512,3584]{2,1,0:T(8,128)(2,1)}) custom-call(s32[28]{0:T(128)} %constant.61.clone.refs_0_, s32[28]{0:T(128)} %constant.62.clone.refs_1_, s32[10]{0:T(128)} %pad_add_fusion.1.refs_0_.meta_ref.refs_2_, ...), custom_call_target="tpu_custom_call" | custom-call | flops 13153337344 | bytes 55050240 | tf_op jit(solution)/shard_map/pallas_call | solution.py:714
  473.4 35.1 %shard_map.67 = (bf16[1008,256]{1,0:T(8,128)(2,1)}, bf16[1008,256]{1,0:T(8,128)(2,1)}, bf16[1008,256]{1,0:T(8,128)(2,1)}, bf16[1008,256]{1,0:T(8,128)(2,1)}, bf1...) custom-call(s32[10]{0:T(128)} %pad_add_fusion.1.refs_0_.meta_ref.refs_2_,, ...), custom_call_target="tpu_custom_call" | custom-call | flops 19730006016 | bytes 56885248 | tf_op jit(solution)/shard_map/pallas_call | solution.py:769
  513.8 9.2 %collective-permute-start.61 = (bf16[1008,256]{1,0:T(8,128)(2,1)}, bf16[1008,256]{1,0:T(8,128)(2,1)S(1)}, u32[]{:S(2)}, u32[]{:S(2)}) collective-permute-start(bf16[1008,256]{1,0:T(8,128)(2,1)} %get-tuple-element.256), channel_id=1, source_target_pairs={{0,16},{4,20},{8,24},{12,28},{16,0},{20,4},{24,8},{28,12},{1,17},{... | collective-permute-start | bytes 1548296 | tf_op jit(solution)/shard_map/ppermute | solution.py:186
  524.0 9.2 %shard_map.69 = (bf16[224,2048]{1,0:T(8,128)(2,1)}, bf16[224,2048]{1,0:T(8,128)(2,1)}, bf16[224,2048]{1,0:T(8,128)(2,1)}, bf16[224,2048]{1,0:T(8,128)(2,1)}) custom-call(s32[10]{0:T(128)} %pad_add_fusion.1.refs_0_.meta_ref.refs_2_, bf16[1008,256]{1,0:T(8,128)(2,1)} %get-tuple-element.268.refs_1_, bf16[1008,256]{1,0:T(8,128)(2,1)} %copy-done.29, ...), custom_call_target="tpu_custom_call" | custom-call | flops 2055208960 | bytes 5963776 | tf_op jit(solution)/shard_map/pallas_call | solution.py:385
  538.0 19.9 %collective-permute-done.61.refs_3_ = bf16[1008,256]{1,0:T(8,128)(2,1)S(1)} collective-permute-done((bf16[1008,256]{1,0:T(8,128)(2,1)}, bf16[1008,256]{1,0:T(8,128)(2,1)S(1)}, u32[]{:S(2)}, u32[]{:S(2)}) %collective-permute-start.61) | collective-permute-done | bytes 516128 | tf_op jit(solution)/shard_map/ppermute | solution.py:186
  558.0 13.4 %collective-permute-done.63.refs_2_ = bf16[1008,256]{1,0:T(8,128)(2,1)S(1)} collective-permute-done((bf16[1008,256]{1,0:T(8,128)(2,1)S(1)}, bf16[1008,256]{1,0:T(8,128)(2,1)S(1)}, u32[]{:S(2)}, u32[]{:S(2)}) %collective-permute-start.63) | collective-permute-done | bytes 516128 | tf_op jit(solution)/shard_map/ppermute | solution.py:186
  584.8 9.0 %shard_map.71 = (bf16[224,2048]{1,0:T(8,128)(2,1)}, bf16[224,2048]{1,0:T(8,128)(2,1)}, bf16[224,2048]{1,0:T(8,128)(2,1)}, bf16[224,2048]{1,0:T(8,128)(2,1)}) custom-call(s32[10]{0:T(128)} %pad_add_fusion.1.refs_0_.meta_ref.refs_2_, bf16[1008,256]{1,0:T(8,128)(2,1)} %get-tuple-element.284.refs_1_, bf16[1008,256]{1,0:T(8,128)(2,1)} %copy-done.26, ...), custom_call_target="tpu_custom_call" | custom-call | flops 2055208960 | bytes 5963776 | tf_op jit(solution)/shard_map/pallas_call | solution.py:385
  620.2 18.7 %collective-permute-done.73 = bf16[224,2048]{1,0:T(8,128)(2,1)} collective-permute-done((bf16[224,2048]{1,0:T(8,128)(2,1)}, bf16[224,2048]{1,0:T(8,128)(2,1)}, u32[]{:S(2)}, u32[]{:S(2)}) %collective-permute-start.73) | collective-permute-done | bytes 917536 | tf_op jit(solution)/shard_map/ppermute | solution.py:186
  (325 shorter events, 293.5 us)
Async XLA Ops:
  19.7 40.6 %collective-permute-start.7 = (bf16[224,2048]{1,0:T(8,128)(2,1)S(1)}, bf16[224,2048]{1,0:T(8,128)(2,1)S(1)}, u32[]{:S(2)}, u32[]{:S(2)}) collective-permute-start(bf16[224,2048]{1,0:T(8,128)(2,1)S(1)} %get-tuple-element.305), channel_id=1, source_target_pairs={{0,2},{1,3},{2,0},{3,1},{4,6},{5,7},{6,4},{7,5},{8,10},{9,11},{10,... | collective-permute-start | bytes 2752520 | tf_op jit(solution)/shard_map/ppermute | solution.py:186
  20.6 39.7 %collective-permute-start.8 = (bf16[224,2048]{1,0:T(8,128)(2,1)S(1)}, bf16[224,2048]{1,0:T(8,128)(2,1)S(1)}, u32[]{:S(2)}, u32[]{:S(2)}) collective-permute-start(bf16[224,2048]{1,0:T(8,128)(2,1)S(1)} %get-tuple-element.304), channel_id=1, source_target_pairs={{0,3},{1,2},{2,1},{3,0},{4,7},{5,6},{6,5},{7,4},{8,11},{9,10},{10,... | collective-permute-start | bytes 2752520 | tf_op jit(solution)/shard_map/ppermute | solution.py:186
  82.5 45.7 %collective-permute-start.13 = (bf16[224,2048]{1,0:T(8,128)(2,1)S(1)}, bf16[224,2048]{1,0:T(8,128)(2,1)S(1)}, u32[]{:S(2)}, u32[]{:S(2)}) collective-permute-start(bf16[224,2048]{1,0:T(8,128)(2,1)S(1)} %get-tuple-element.303), channel_id=1, source_target_pairs={{0,1},{1,0},{2,3},{3,2},{4,5},{5,4},{6,7},{7,6},{8,9},{9,8},{10,11... | collective-permute-start | bytes 2752520 | tf_op jit(solution)/shard_map/ppermute | solution.py:186
  83.1 45.0 %collective-permute-start.14 = (bf16[224,2048]{1,0:T(8,128)(2,1)S(1)}, bf16[224,2048]{1,0:T(8,128)(2,1)S(1)}, u32[]{:S(2)}, u32[]{:S(2)}) collective-permute-start(bf16[224,2048]{1,0:T(8,128)(2,1)S(1)} %get-tuple-element.302), channel_id=1, source_target_pairs={{0,2},{1,3},{2,0},{3,1},{4,6},{5,7},{6,4},{7,5},{8,10},{9,11},{10,... | collective-permute-start | bytes 2752520 | tf_op jit(solution)/shard_map/ppermute | solution.py:186
  83.9 44.2 %collective-permute-start.15 = (bf16[224,2048]{1,0:T(8,128)(2,1)S(1)}, bf16[224,2048]{1,0:T(8,128)(2,1)S(1)}, u32[]{:S(2)}, u32[]{:S(2)}) collective-permute-start(bf16[224,2048]{1,0:T(8,128)(2,1)S(1)} %get-tuple-element.301), channel_id=1, source_target_pairs={{0,3},{1,2},{2,1},{3,0},{4,7},{5,6},{6,5},{7,4},{8,11},{9,10},{10,... | collective-permute-start | bytes 2752520 | tf_op jit(solution)/shard_map/ppermute | solution.py:186
  148.4 38.2 %collective-permute-start.18 = (bf16[1008,256]{1,0:T(8,128)(2,1)}, bf16[1008,256]{1,0:T(8,128)(2,1)S(1)}, u32[]{:S(2)}, u32[]{:S(2)}) collective-permute-start(bf16[1008,256]{1,0:T(8,128)(2,1)} %get-tuple-element.187), channel_id=1, source_target_pairs={{0,16},{4,20},{8,24},{12,28},{16,0},{20,4},{24,8},{28,12},{1,17},{... | collective-permute-start | bytes 1548296 | tf_op jit(solution)/shard_map/ppermute | solution.py:186
  228.6 41.9 %collective-permute-start.27 = (bf16[3584,128]{1,0:T(8,128)(2,1)}, bf16[3584,128]{1,0:T(8,128)(2,1)S(1)}, u32[]{:S(2)}, u32[]{:S(2)}) collective-permute-start(bf16[3584,128]{1,0:T(8,128)(2,1)} %get-tuple-element.206), channel_id=1, source_target_pairs={{0,2},{1,3},{2,0},{3,1},{4,6},{5,7},{6,4},{7,5},{8,10},{9,11},{10,... | collective-permute-start | bytes 2752520 | tf_op jit(solution)/shard_map/ppermute | solution.py:186
  229.5 41.0 %collective-permute-start.28 = (bf16[3584,128]{1,0:T(8,128)(2,1)}, bf16[3584,128]{1,0:T(8,128)(2,1)S(1)}, u32[]{:S(2)}, u32[]{:S(2)}) collective-permute-start(bf16[3584,128]{1,0:T(8,128)(2,1)} %get-tuple-element.207), channel_id=1, source_target_pairs={{0,3},{1,2},{2,1},{3,0},{4,7},{5,6},{6,5},{7,4},{8,11},{9,10},{10,... | collective-permute-start | bytes 2752520 | tf_op jit(solution)/shard_map/ppermute | solution.py:186
  285.7 46.0 %collective-permute-start.32 = (bf16[3584,128]{1,0:T(8,128)(2,1)}, bf16[3584,128]{1,0:T(8,128)(2,1)S(1)}, u32[]{:S(2)}, u32[]{:S(2)}) collective-permute-start(bf16[3584,128]{1,0:T(8,128)(2,1)} %get-tuple-element.215), channel_id=1, source_target_pairs={{0,1},{1,0},{2,3},{3,2},{4,5},{5,4},{6,7},{7,6},{8,9},{9,8},{10,11... | collective-permute-start | bytes 2752520 | tf_op jit(solution)/shard_map/ppermute | solution.py:186
  287.2 44.6 %collective-permute-start.33 = (bf16[3584,128]{1,0:T(8,128)(2,1)}, bf16[3584,128]{1,0:T(8,128)(2,1)S(1)}, u32[]{:S(2)}, u32[]{:S(2)}) collective-permute-start(bf16[3584,128]{1,0:T(8,128)(2,1)} %get-tuple-element.216), channel_id=1, source_target_pairs={{0,2},{1,3},{2,0},{3,1},{4,6},{5,7},{6,4},{7,5},{8,10},{9,11},{10,... | collective-permute-start | bytes 2752520 | tf_op jit(solution)/shard_map/ppermute | solution.py:186
  287.7 44.1 %collective-permute-start.34 = (bf16[3584,128]{1,0:T(8,128)(2,1)}, bf16[3584,128]{1,0:T(8,128)(2,1)S(1)}, u32[]{:S(2)}, u32[]{:S(2)}) collective-permute-start(bf16[3584,128]{1,0:T(8,128)(2,1)} %get-tuple-element.217), channel_id=1, source_target_pairs={{0,3},{1,2},{2,1},{3,0},{4,7},{5,6},{6,5},{7,4},{8,11},{9,10},{10,... | collective-permute-start | bytes 2752520 | tf_op jit(solution)/shard_map/ppermute | solution.py:186
  345.8 45.6 %collective-permute-start.44 = (bf16[3584,128]{1,0:T(8,128)(2,1)}, bf16[3584,128]{1,0:T(8,128)(2,1)S(1)}, u32[]{:S(2)}, u32[]{:S(2)}) collective-permute-start(bf16[3584,128]{1,0:T(8,128)(2,1)} %shard_map.62.refs_3_), channel_id=1, source_target_pairs={{0,1},{1,0},{2,3},{3,2},{4,5},{5,4},{6,7},{7,6},{8,9},{9,8},{10,11... | collective-permute-start | bytes 2752520 | tf_op jit(solution)/shard_map/ppermute | solution.py:186
  346.1 45.3 %collective-permute-start.45 = (bf16[3584,128]{1,0:T(8,128)(2,1)}, bf16[3584,128]{1,0:T(8,128)(2,1)S(1)}, u32[]{:S(2)}, u32[]{:S(2)}) collective-permute-start(bf16[3584,128]{1,0:T(8,128)(2,1)} %shard_map.62.refs_3_), channel_id=1, source_target_pairs={{0,2},{1,3},{2,0},{3,1},{4,6},{5,7},{6,4},{7,5},{8,10},{9,11},{10,... | collective-permute-start | bytes 2752520 | tf_op jit(solution)/shard_map/ppermute | solution.py:186
  348.8 42.7 %collective-permute-start.46 = (bf16[3584,128]{1,0:T(8,128)(2,1)}, bf16[3584,128]{1,0:T(8,128)(2,1)S(1)}, u32[]{:S(2)}, u32[]{:S(2)}) collective-permute-start(bf16[3584,128]{1,0:T(8,128)(2,1)} %shard_map.62.refs_3_), channel_id=1, source_target_pairs={{0,3},{1,2},{2,1},{3,0},{4,7},{5,6},{6,5},{7,4},{8,11},{9,10},{10,... | collective-permute-start | bytes 2752520 | tf_op jit(solution)/shard_map/ppermute | solution.py:186
  395.0 39.6 %collective-permute-start.48 = (bf16[3584,128]{1,0:T(8,128)(2,1)}, bf16[3584,128]{1,0:T(8,128)(2,1)S(1)}, u32[]{:S(2)}, u32[]{:S(2)}) collective-permute-start(bf16[3584,128]{1,0:T(8,128)(2,1)} %shard_map.65.refs_7_), channel_id=1, source_target_pairs={{0,2},{1,3},{2,0},{3,1},{4,6},{5,7},{6,4},{7,5},{8,10},{9,11},{10,... | collective-permute-start | bytes 2752520 | tf_op jit(solution)/shard_map/ppermute | solution.py:186
  396.8 39.2 %collective-permute-start.49 = (bf16[3584,128]{1,0:T(8,128)(2,1)}, bf16[3584,128]{1,0:T(8,128)(2,1)S(1)}, u32[]{:S(2)}, u32[]{:S(2)}) collective-permute-start(bf16[3584,128]{1,0:T(8,128)(2,1)} %shard_map.65.refs_7_), channel_id=1, source_target_pairs={{0,3},{1,2},{2,1},{3,0},{4,7},{5,6},{6,5},{7,4},{8,11},{9,10},{10,... | collective-permute-start | bytes 2752520 | tf_op jit(solution)/shard_map/ppermute | solution.py:186
  398.2 38.3 %collective-permute-start.51 = (bf16[3584,128]{1,0:T(8,128)(2,1)S(1)}, bf16[3584,128]{1,0:T(8,128)(2,1)S(1)}, u32[]{:S(2)}, u32[]{:S(2)}) collective-permute-start(bf16[3584,128]{1,0:T(8,128)(2,1)S(1)} %collective-permute-done.44.refs_4_), channel_id=1, source_target_pairs={{0,4},{4,0},{8,12},{12,8},{16,20},{20,16},{24,28},{28,24},{1,5},{5... | collective-permute-start | bytes 2752520 | tf_op jit(solution)/shard_map/ppermute | solution.py:186
  467.6 41.0 %collective-permute-start.58 = (bf16[1008,256]{1,0:T(8,128)(2,1)}, bf16[1008,256]{1,0:T(8,128)(2,1)S(1)}, u32[]{:S(2)}, u32[]{:S(2)}) collective-permute-start(bf16[1008,256]{1,0:T(8,128)(2,1)} %get-tuple-element.235), channel_id=1, source_target_pairs={{0,16},{4,20},{8,24},{12,28},{16,0},{20,4},{24,8},{28,12},{1,17},{... | collective-permute-start | bytes 1548296 | tf_op jit(solution)/shard_map/ppermute | solution.py:186
  513.8 44.2 %collective-permute-start.61 = (bf16[1008,256]{1,0:T(8,128)(2,1)}, bf16[1008,256]{1,0:T(8,128)(2,1)S(1)}, u32[]{:S(2)}, u32[]{:S(2)}) collective-permute-start(bf16[1008,256]{1,0:T(8,128)(2,1)} %get-tuple-element.256), channel_id=1, source_target_pairs={{0,16},{4,20},{8,24},{12,28},{16,0},{20,4},{24,8},{28,12},{1,17},{... | collective-permute-start | bytes 1548296 | tf_op jit(solution)/shard_map/ppermute | solution.py:186
  535.4 42.2 %collective-permute-start.66 = (bf16[224,2048]{1,0:T(8,128)(2,1)}, bf16[224,2048]{1,0:T(8,128)(2,1)}, u32[]{:S(2)}, u32[]{:S(2)}) collective-permute-start(bf16[224,2048]{1,0:T(8,128)(2,1)} %get-tuple-element.274), channel_id=1, source_target_pairs={{0,2},{1,3},{2,0},{3,1},{4,6},{5,7},{6,4},{7,5},{8,10},{9,11},{10,... | collective-permute-start | bytes 2752520 | tf_op jit(solution)/shard_map/ppermute | solution.py:186
  536.2 41.3 %collective-permute-start.67 = (bf16[224,2048]{1,0:T(8,128)(2,1)}, bf16[224,2048]{1,0:T(8,128)(2,1)}, u32[]{:S(2)}, u32[]{:S(2)}) collective-permute-start(bf16[224,2048]{1,0:T(8,128)(2,1)} %get-tuple-element.275), channel_id=1, source_target_pairs={{0,3},{1,2},{2,1},{3,0},{4,7},{5,6},{6,5},{7,4},{8,11},{9,10},{10,... | collective-permute-start | bytes 2752520 | tf_op jit(solution)/shard_map/ppermute | solution.py:186
  595.6 43.3 %collective-permute-start.73 = (bf16[224,2048]{1,0:T(8,128)(2,1)}, bf16[224,2048]{1,0:T(8,128)(2,1)}, u32[]{:S(2)}, u32[]{:S(2)}) collective-permute-start(bf16[224,2048]{1,0:T(8,128)(2,1)} %get-tuple-element.291), channel_id=1, source_target_pairs={{0,2},{1,3},{2,0},{3,1},{4,6},{5,7},{6,4},{7,5},{8,10},{9,11},{10,... | collective-permute-start | bytes 2752520 | tf_op jit(solution)/shard_map/ppermute | solution.py:186
  598.5 41.7 %collective-permute-start.74 = (bf16[224,2048]{1,0:T(8,128)(2,1)}, bf16[224,2048]{1,0:T(8,128)(2,1)}, u32[]{:S(2)}, u32[]{:S(2)}) collective-permute-start(bf16[224,2048]{1,0:T(8,128)(2,1)} %get-tuple-element.292), channel_id=1, source_target_pairs={{0,3},{1,2},{2,1},{3,0},{4,7},{5,6},{6,5},{7,4},{8,11},{9,10},{10,... | collective-permute-start | bytes 2752520 | tf_op jit(solution)/shard_map/ppermute | solution.py:186
  607.1 39.9 %collective-permute-start.76 = (bf16[224,512]{1,0:T(8,128)(2,1)}, bf16[224,512]{1,0:T(8,128)(2,1)S(1)}, u32[]{:S(2)}, u32[]{:S(2)}) collective-permute-start(bf16[224,512]{1,0:T(8,128)(2,1)} %get-tuple-element.299), channel_id=1, source_target_pairs={{0,2},{1,3},{2,0},{3,1},{4,6},{5,7},{6,4},{7,5},{8,10},{9,11},{10,... | collective-permute-start | bytes 688136 | tf_op jit(solution)/shard_map/ppermute | solution.py:186
  (123 other events, 2022.1 us)

commit v10 on v9

--- a/solution.py
+++ b/solution.py
@@ -232,19 +232,17 @@
 
 def pack_pair_kernel(col_count, meta_ref, *refs):
     pieces, choose, keep, give = refs[:col_count], refs[-3], refs[-2], refs[-1]
-    other = pl.program_id(0) == 0
-
+    width = keep.shape[1]
     total = jnp.dot(choose[0], pieces[0][...], preferred_element_type=jnp.float32)
     for k in range(1, col_count):
         total += jnp.dot(choose[k], pieces[k][...], preferred_element_type=jnp.float32)
-
-    @pl.when(other)
-    def _():
-        give[...] = total.astype(jnp.bfloat16)
-
-    @pl.when(jnp.logical_not(other))
-    def _():
-        keep[...] = total.astype(jnp.bfloat16)
+    block = total.astype(jnp.bfloat16)
+    for core, (low, high) in enumerate(((keep, give), (give, keep))):
+
+        @pl.when(meta_ref[0] % 2 == core)
+        def _():
+            low[...] = block[:, :width]
+            high[...] = block[:, width:]
 
 
 def selections(meta, col_count, slots, window):
@@ -259,30 +257,25 @@
     slots = momentum.shape[0]
     col_count = len(received) + 1
     pairs = row_count // 2
-    first = base // width
-    block = lambda e, q, meta: meta[0] ^ (2 * q + 1 - e)
+    first = base // (2 * width)
+    block = lambda q, meta: (meta[0] // 2) ^ q
     shape = jax.ShapeDtypeStruct((pairs * window, width), jnp.bfloat16)
     return pl.pallas_call(
         lambda *refs: pack_pair_kernel(col_count, *refs),
         out_shape=[shape, shape],
         grid_spec=pltpu.PrefetchScalarGridSpec(
             num_scalar_prefetch=1,
-            grid=(2, pairs),
+            grid=(pairs,),
             in_specs=[
                 pl.BlockSpec(
-                    (slots, width),
-                    lambda e, q, meta: (0, first + meta[1] * row_count + block(e, q, meta)),
+                    (slots, 2 * width),
+                    lambda q, meta: (0, first + meta[1] * pairs + block(q, meta)),
                 )
             ]
-            + [pl.BlockSpec((slots, width), lambda e, q, meta: (0, block(e, q, meta)))]
+            + [pl.BlockSpec((slots, 2 * width), lambda q, meta: (0, block(q, meta)))]
             * (col_count - 1)
-            + [pl.BlockSpec(choose.shape, lambda e, q, meta: (0, 0, 0))],
-            out_specs=[
-                pl.BlockSpec((window, width), lambda e, q, meta: (jnp.where(e == 0, 0, q), 0)),
-                pl.BlockSpec(
-                    (window, width), lambda e, q, meta: (jnp.where(e == 0, q, pairs - 1), 0)
-                ),
-            ],
+            + [pl.BlockSpec(choose.shape, lambda q, meta: (0, 0, 0))],
+            out_specs=[pl.BlockSpec((window, width), lambda q, meta: (q, 0))] * 2,
         ),
         compiler_params=pltpu.CompilerParams(vmem_limit_bytes=VMEM_LIMIT),
         cost_estimate=pl.CostEstimate(

time: 653 us -> 649 us (level)
  transfers between devices with their start and end apart: 78 -> 78, of which waited for: 38 -> 36; matrix products, arithmetic and copies ran while one was open for 3% -> 3% of each run, Pallas kernels for 17% -> 17%
where the time goes in v10:
time: 649 us; the launch traced here: 647 us
  waiting for transfers between devices  301 us (46%)
  Pallas kernels  191 us (29%)
  starting transfers between devices  108 us (17%)
  local copies, waits for them, and re-layouts  43.1 us (7%)
    ppermute x78, waiting for transfers between devices, swap(): lax.ppermute(value, axis, perm=[(i, i ^ distance) for i in range(size)])  301 us
    ppermute x78, starting transfers between devices, swap(): lax.ppermute(value, axis, perm=[(i, i ^ distance) for i in range(size)])  108 us
    pallas_call x14, Pallas kernels, local_call(): pl.pallas_call(kernel, out_shape=out_shape, in_specs=[pl.BlockSpec(memory...  42.4 us
    pallas_call x1, Pallas kernels, next_apply(): pl.pallas_call(lambda *refs: next_apply_kernel(jitter, sends, *refs), out...  35.1 us
    pallas_call x3, Pallas kernels, half_gram(): pl.pallas_call(lambda *refs: half_gram_kernel(flip, first, *refs), out_sh...  31.7 us
    pallas_call x1, Pallas kernels, first_apply(): pl.pallas_call(lambda *refs: first_apply_kernel(jitter, send, col_count,...  25.4 us
    unnamed x138, local copies, waits for them, and re-layouts  23.3 us
    pallas_call x2, Pallas kernels, unpack_pair(): pl.pallas_call(lambda *refs: unpack_pair_kernel(col_count, even, window,...  18.1 us
  transfers between devices with their start and end apart: 78, of which 36 were waited for; matrix products, arithmetic and copies ran while one was open for 3% of the time, Pallas kernels for 17%

profile of v10, /device:TPU:0, one launch (start us, length us, event | category | flops | bytes accessed | tf_op | source)
XLA Modules:
  0.0 647.1 jit_solution(17773912192585314090)
XLA Ops:
  33.5 8.3 %collective-permute-done.3.refs_3_ = bf16[560,128]{1,0:T(8,128)(2,1)S(1)} collective-permute-done((bf16[560,128]{1,0:T(8,128)(2,1)}, bf16[560,128]{1,0:T(8,128)(2,1)S(1)}, u32[]{:S(2)}, u32[]{:S(2)}) %collective-permute-start.3) | collective-permute-done | bytes 143392 | tf_op jit(solution)/shard_map/ppermute | solution.py:186
  47.1 13.1 %collective-permute-done.7.refs_3_ = bf16[224,2048]{1,0:T(8,128)(2,1)S(1)} collective-permute-done((bf16[224,2048]{1,0:T(8,128)(2,1)S(1)}, bf16[224,2048]{1,0:T(8,128)(2,1)S(1)}, u32[]{:S(2)}, u32[]{:S(2)}) %collective-permute-start.7) | collective-permute-done | bytes 917536 | tf_op jit(solution)/shard_map/ppermute | solution.py:186
  85.5 28.4 %collective-permute-done.10.refs_3_ = bf16[1008,256]{1,0:T(8,128)(2,1)S(1)} collective-permute-done((bf16[1008,256]{1,0:T(8,128)(2,1)}, bf16[1008,256]{1,0:T(8,128)(2,1)S(1)}, u32[]{:S(2)}, u32[]{:S(2)}) %collective-permute-start.10) | collective-permute-done | bytes 516128 | tf_op jit(solution)/shard_map/ppermute | solution.py:186
  113.9 12.3 %collective-permute-done.12.refs_2_ = bf16[1008,256]{1,0:T(8,128)(2,1)S(1)} collective-permute-done((bf16[1008,256]{1,0:T(8,128)(2,1)}, bf16[1008,256]{1,0:T(8,128)(2,1)S(1)}, u32[]{:S(2)}, u32[]{:S(2)}) %collective-permute-start.12) | collective-permute-done | bytes 516128 | tf_op jit(solution)/shard_map/ppermute | solution.py:186
  158.3 9.3 %collective-permute-done.17.refs_2_ = bf16[1008,256]{1,0:T(8,128)(2,1)S(1)} collective-permute-done((bf16[1008,256]{1,0:T(8,128)(2,1)}, bf16[1008,256]{1,0:T(8,128)(2,1)S(1)}, u32[]{:S(2)}, u32[]{:S(2)}) %collective-permute-start.17) | collective-permute-done | bytes 516128 | tf_op jit(solution)/shard_map/ppermute | solution.py:186
  167.6 15.2 %collective-permute-done.18.refs_3_ = bf16[1008,256]{1,0:T(8,128)(2,1)S(1)} collective-permute-done((bf16[1008,256]{1,0:T(8,128)(2,1)}, bf16[1008,256]{1,0:T(8,128)(2,1)S(1)}, u32[]{:S(2)}, u32[]{:S(2)}) %collective-permute-start.18) | collective-permute-done | bytes 516128 | tf_op jit(solution)/shard_map/ppermute | solution.py:186
  192.4 14.1 %shard_map.56 = (bf16[3584,512]{1,0:T(8,128)(2,1)}, bf16[3584,512]{1,0:T(8,128)(2,1)}) custom-call(s32[28]{0:T(128)} %constant.61.clone.refs_0_, s32[28]{0:T(128)} %constant.62.clone.refs_1_, s32[10]{0:T(128)} %pad_add_fusion.1.refs_0_.meta_ref.refs_2_, bf16[3584,640]{1,0:T(8,128)(2,1)} %shard_map.54.refs_3_), custom_call_target="tpu_custom_call" | custom-call | flops 4697620480 | bytes 11927552 | tf_op jit(solution)/shard_map/pallas_call | solution.py:514
  207.0 8.8 %shard_map.55.refs_0_.refs_1_.refs_2_.refs_3_ = bf16[3584,512]{1,0:T(8,128)(2,1)} custom-call(s32[28]{0:T(128)} %constant.61.clone.refs_0_, s32[28]{0:T(128)} %constant.62.clone.refs_1_, s32[10]{0:T(128)} %pad_add_fusion.1.refs_0_.meta_ref.refs_2_, bf16[3584,640]{1,0:T(8,128)(2,1)} %shard_map.54.refs_3_), custom_call_target="tpu_custom_call" | custom-call | flops 2348810240 | bytes 8257536 | tf_op jit(solution)/shard_map/pallas_call | solution.py:514
  227.7 8.8 %shard_map.58.refs_0_.refs_1_.refs_2_.refs_3_ = bf16[3584,512]{1,0:T(8,128)(2,1)} custom-call(s32[28]{0:T(128)} %constant.61.clone.refs_0_, s32[28]{0:T(128)} %constant.62.clone.refs_1_, s32[10]{0:T(128)} %pad_add_fusion.1.refs_0_.meta_ref.refs_2_, bf16[3584,640]{1,0:T(8,128)(2,1)} %shard_map.54.refs_3_), custom_call_target="tpu_custom_call" | custom-call | flops 2348810240 | bytes 8257536 | tf_op jit(solution)/shard_map/pallas_call | solution.py:514
  247.7 19.0 %collective-permute-done.27.refs_3_ = bf16[3584,128]{1,0:T(8,128)(2,1)S(1)} collective-permute-done((bf16[3584,128]{1,0:T(8,128)(2,1)}, bf16[3584,128]{1,0:T(8,128)(2,1)S(1)}, u32[]{:S(2)}, u32[]{:S(2)}) %collective-permute-start.27) | collective-permute-done | bytes 917536 | tf_op jit(solution)/shard_map/ppermute | solution.py:186
  271.3 10.6 %collective-permute-start.29 = (bf16[896,128]{1,0:T(8,128)(2,1)}, bf16[896,128]{1,0:T(8,128)(2,1)S(1)}, u32[]{:S(2)}, u32[]{:S(2)}) collective-permute-start(bf16[896,128]{1,0:T(8,128)(2,1)} %get-tuple-element.212), channel_id=1, source_target_pairs={{0,8},{4,12},{8,0},{12,4},{16,24},{20,28},{24,16},{28,20},{1,9},{5... | collective-permute-start | bytes 688136 | tf_op jit(solution)/shard_map/ppermute | solution.py:186
  290.4 12.5 %collective-permute-done.30.refs_2_ = bf16[896,128]{1,0:T(8,128)(2,1)S(1)} collective-permute-done((bf16[896,128]{1,0:T(8,128)(2,1)}, bf16[896,128]{1,0:T(8,128)(2,1)S(1)}, u32[]{:S(2)}, u32[]{:S(2)}) %collective-permute-start.30) | collective-permute-done | bytes 229408 | tf_op jit(solution)/shard_map/ppermute | solution.py:186
  346.5 10.0 %collective-permute-done.39.refs_2_ = bf16[896,128]{1,0:T(8,128)(2,1)S(1)} collective-permute-done((bf16[896,128]{1,0:T(8,128)(2,1)}, bf16[896,128]{1,0:T(8,128)(2,1)S(1)}, u32[]{:S(2)}, u32[]{:S(2)}) %collective-permute-start.39) | collective-permute-done | bytes 229408 | tf_op jit(solution)/shard_map/ppermute | solution.py:186
  369.5 9.3 %collective-permute-done.42.refs_2_ = bf16[896,128]{1,0:T(8,128)(2,1)S(1)} collective-permute-done((bf16[896,128]{1,0:T(8,128)(2,1)}, bf16[896,128]{1,0:T(8,128)(2,1)S(1)}, u32[]{:S(2)}, u32[]{:S(2)}) %collective-permute-start.42) | collective-permute-done | bytes 229408 | tf_op jit(solution)/shard_map/ppermute | solution.py:186
  394.9 19.5 %collective-permute-done.47.refs_8_ = bf16[3584,128]{1,0:T(8,128)(2,1)S(1)} collective-permute-done((bf16[3584,128]{1,0:T(8,128)(2,1)}, bf16[3584,128]{1,0:T(8,128)(2,1)S(1)}, u32[]{:S(2)}, u32[]{:S(2)}) %collective-permute-start.47) | collective-permute-done | bytes 917536 | tf_op jit(solution)/shard_map/ppermute | solution.py:186
  414.9 17.2 %collective-permute-done.49.refs_10_ = bf16[3584,128]{1,0:T(8,128)(2,1)S(1)} collective-permute-done((bf16[3584,128]{1,0:T(8,128)(2,1)}, bf16[3584,128]{1,0:T(8,128)(2,1)S(1)}, u32[]{:S(2)}, u32[]{:S(2)}) %collective-permute-start.49) | collective-permute-done | bytes 917536 | tf_op jit(solution)/shard_map/ppermute | solution.py:186
  438.3 25.4 %shard_map.66 = (bf16[1008,256]{1,0:T(8,128)(2,1)}, bf16[1008,256]{1,0:T(8,128)(2,1)}, bf16[1008,256]{1,0:T(8,128)(2,1)}, bf16[1008,256]{1,0:T(8,128)(2,1)}, bf16[7,512,3584]{2,1,0:T(8,128)(2,1)}) custom-call(s32[28]{0:T(128)} %constant.61.clone.refs_0_, s32[28]{0:T(128)} %constant.62.clone.refs_1_, s32[10]{0:T(128)} %pad_add_fusion.1.refs_0_.meta_ref.refs_2_, ...), custom_call_target="tpu_custom_call" | custom-call | flops 13153337344 | bytes 55050240 | tf_op jit(solution)/shard_map/pallas_call | solution.py:707
  469.6 35.1 %shard_map.67 = (bf16[1008,256]{1,0:T(8,128)(2,1)}, bf16[1008,256]{1,0:T(8,128)(2,1)}, bf16[1008,256]{1,0:T(8,128)(2,1)}, bf16[1008,256]{1,0:T(8,128)(2,1)}, bf1...) custom-call(s32[10]{0:T(128)} %pad_add_fusion.1.refs_0_.meta_ref.refs_2_,, ...), custom_call_target="tpu_custom_call" | custom-call | flops 19730006016 | bytes 56885248 | tf_op jit(solution)/shard_map/pallas_call | solution.py:762
  509.9 9.2 %collective-permute-start.61 = (bf16[1008,256]{1,0:T(8,128)(2,1)}, bf16[1008,256]{1,0:T(8,128)(2,1)S(1)}, u32[]{:S(2)}, u32[]{:S(2)}) collective-permute-start(bf16[1008,256]{1,0:T(8,128)(2,1)} %get-tuple-element.256), channel_id=1, source_target_pairs={{0,16},{4,20},{8,24},{12,28},{16,0},{20,4},{24,8},{28,12},{1,17},{... | collective-permute-start | bytes 1548296 | tf_op jit(solution)/shard_map/ppermute | solution.py:186
  520.2 9.1 %shard_map.69 = (bf16[224,2048]{1,0:T(8,128)(2,1)}, bf16[224,2048]{1,0:T(8,128)(2,1)}, bf16[224,2048]{1,0:T(8,128)(2,1)}, bf16[224,2048]{1,0:T(8,128)(2,1)}) custom-call(s32[10]{0:T(128)} %pad_add_fusion.1.refs_0_.meta_ref.refs_2_, bf16[1008,256]{1,0:T(8,128)(2,1)} %get-tuple-element.268.refs_1_, bf16[1008,256]{1,0:T(8,128)(2,1)} %copy-done.29, ...), custom_call_target="tpu_custom_call" | custom-call | flops 2055208960 | bytes 5963776 | tf_op jit(solution)/shard_map/pallas_call | solution.py:378
  534.2 19.9 %collective-permute-done.61.refs_3_ = bf16[1008,256]{1,0:T(8,128)(2,1)S(1)} collective-permute-done((bf16[1008,256]{1,0:T(8,128)(2,1)}, bf16[1008,256]{1,0:T(8,128)(2,1)S(1)}, u32[]{:S(2)}, u32[]{:S(2)}) %collective-permute-start.61) | collective-permute-done | bytes 516128 | tf_op jit(solution)/shard_map/ppermute | solution.py:186
  554.1 13.4 %collective-permute-done.63.refs_2_ = bf16[1008,256]{1,0:T(8,128)(2,1)S(1)} collective-permute-done((bf16[1008,256]{1,0:T(8,128)(2,1)S(1)}, bf16[1008,256]{1,0:T(8,128)(2,1)S(1)}, u32[]{:S(2)}, u32[]{:S(2)}) %collective-permute-start.63) | collective-permute-done | bytes 516128 | tf_op jit(solution)/shard_map/ppermute | solution.py:186
  580.9 9.0 %shard_map.71 = (bf16[224,2048]{1,0:T(8,128)(2,1)}, bf16[224,2048]{1,0:T(8,128)(2,1)}, bf16[224,2048]{1,0:T(8,128)(2,1)}, bf16[224,2048]{1,0:T(8,128)(2,1)}) custom-call(s32[10]{0:T(128)} %pad_add_fusion.1.refs_0_.meta_ref.refs_2_, bf16[1008,256]{1,0:T(8,128)(2,1)} %get-tuple-element.284.refs_1_, bf16[1008,256]{1,0:T(8,128)(2,1)} %copy-done.26, ...), custom_call_target="tpu_custom_call" | custom-call | flops 2055208960 | bytes 5963776 | tf_op jit(solution)/shard_map/pallas_call | solution.py:378
  616.3 18.6 %collective-permute-done.73 = bf16[224,2048]{1,0:T(8,128)(2,1)} collective-permute-done((bf16[224,2048]{1,0:T(8,128)(2,1)}, bf16[224,2048]{1,0:T(8,128)(2,1)}, u32[]{:S(2)}, u32[]{:S(2)}) %collective-permute-start.73) | collective-permute-done | bytes 917536 | tf_op jit(solution)/shard_map/ppermute | solution.py:186
  (325 shorter events, 290.1 us)
Async XLA Ops:
  19.7 40.6 %collective-permute-start.7 = (bf16[224,2048]{1,0:T(8,128)(2,1)S(1)}, bf16[224,2048]{1,0:T(8,128)(2,1)S(1)}, u32[]{:S(2)}, u32[]{:S(2)}) collective-permute-start(bf16[224,2048]{1,0:T(8,128)(2,1)S(1)} %get-tuple-element.305), channel_id=1, source_target_pairs={{0,2},{1,3},{2,0},{3,1},{4,6},{5,7},{6,4},{7,5},{8,10},{9,11},{10,... | collective-permute-start | bytes 2752520 | tf_op jit(solution)/shard_map/ppermute | solution.py:186
  20.6 39.7 %collective-permute-start.8 = (bf16[224,2048]{1,0:T(8,128)(2,1)S(1)}, bf16[224,2048]{1,0:T(8,128)(2,1)S(1)}, u32[]{:S(2)}, u32[]{:S(2)}) collective-permute-start(bf16[224,2048]{1,0:T(8,128)(2,1)S(1)} %get-tuple-element.304), channel_id=1, source_target_pairs={{0,3},{1,2},{2,1},{3,0},{4,7},{5,6},{6,5},{7,4},{8,11},{9,10},{10,... | collective-permute-start | bytes 2752520 | tf_op jit(solution)/shard_map/ppermute | solution.py:186
  80.6 45.7 %collective-permute-start.13 = (bf16[224,2048]{1,0:T(8,128)(2,1)S(1)}, bf16[224,2048]{1,0:T(8,128)(2,1)S(1)}, u32[]{:S(2)}, u32[]{:S(2)}) collective-permute-start(bf16[224,2048]{1,0:T(8,128)(2,1)S(1)} %get-tuple-element.303), channel_id=1, source_target_pairs={{0,1},{1,0},{2,3},{3,2},{4,5},{5,4},{6,7},{7,6},{8,9},{9,8},{10,11... | collective-permute-start | bytes 2752520 | tf_op jit(solution)/shard_map/ppermute | solution.py:186
  81.2 45.0 %collective-permute-start.14 = (bf16[224,2048]{1,0:T(8,128)(2,1)S(1)}, bf16[224,2048]{1,0:T(8,128)(2,1)S(1)}, u32[]{:S(2)}, u32[]{:S(2)}) collective-permute-start(bf16[224,2048]{1,0:T(8,128)(2,1)S(1)} %get-tuple-element.302), channel_id=1, source_target_pairs={{0,2},{1,3},{2,0},{3,1},{4,6},{5,7},{6,4},{7,5},{8,10},{9,11},{10,... | collective-permute-start | bytes 2752520 | tf_op jit(solution)/shard_map/ppermute | solution.py:186
  82.0 44.2 %collective-permute-start.15 = (bf16[224,2048]{1,0:T(8,128)(2,1)S(1)}, bf16[224,2048]{1,0:T(8,128)(2,1)S(1)}, u32[]{:S(2)}, u32[]{:S(2)}) collective-permute-start(bf16[224,2048]{1,0:T(8,128)(2,1)S(1)} %get-tuple-element.301), channel_id=1, source_target_pairs={{0,3},{1,2},{2,1},{3,0},{4,7},{5,6},{6,5},{7,4},{8,11},{9,10},{10,... | collective-permute-start | bytes 2752520 | tf_op jit(solution)/shard_map/ppermute | solution.py:186
  144.6 38.2 %collective-permute-start.18 = (bf16[1008,256]{1,0:T(8,128)(2,1)}, bf16[1008,256]{1,0:T(8,128)(2,1)S(1)}, u32[]{:S(2)}, u32[]{:S(2)}) collective-permute-start(bf16[1008,256]{1,0:T(8,128)(2,1)} %get-tuple-element.187), channel_id=1, source_target_pairs={{0,16},{4,20},{8,24},{12,28},{16,0},{20,4},{24,8},{28,12},{1,17},{... | collective-permute-start | bytes 1548296 | tf_op jit(solution)/shard_map/ppermute | solution.py:186
  224.8 41.9 %collective-permute-start.27 = (bf16[3584,128]{1,0:T(8,128)(2,1)}, bf16[3584,128]{1,0:T(8,128)(2,1)S(1)}, u32[]{:S(2)}, u32[]{:S(2)}) collective-permute-start(bf16[3584,128]{1,0:T(8,128)(2,1)} %get-tuple-element.206), channel_id=1, source_target_pairs={{0,2},{1,3},{2,0},{3,1},{4,6},{5,7},{6,4},{7,5},{8,10},{9,11},{10,... | collective-permute-start | bytes 2752520 | tf_op jit(solution)/shard_map/ppermute | solution.py:186
  225.6 41.0 %collective-permute-start.28 = (bf16[3584,128]{1,0:T(8,128)(2,1)}, bf16[3584,128]{1,0:T(8,128)(2,1)S(1)}, u32[]{:S(2)}, u32[]{:S(2)}) collective-permute-start(bf16[3584,128]{1,0:T(8,128)(2,1)} %get-tuple-element.207), channel_id=1, source_target_pairs={{0,3},{1,2},{2,1},{3,0},{4,7},{5,6},{6,5},{7,4},{8,11},{9,10},{10,... | collective-permute-start | bytes 2752520 | tf_op jit(solution)/shard_map/ppermute | solution.py:186
  281.9 46.0 %collective-permute-start.32 = (bf16[3584,128]{1,0:T(8,128)(2,1)}, bf16[3584,128]{1,0:T(8,128)(2,1)S(1)}, u32[]{:S(2)}, u32[]{:S(2)}) collective-permute-start(bf16[3584,128]{1,0:T(8,128)(2,1)} %get-tuple-element.215), channel_id=1, source_target_pairs={{0,1},{1,0},{2,3},{3,2},{4,5},{5,4},{6,7},{7,6},{8,9},{9,8},{10,11... | collective-permute-start | bytes 2752520 | tf_op jit(solution)/shard_map/ppermute | solution.py:186
  283.3 44.6 %collective-permute-start.33 = (bf16[3584,128]{1,0:T(8,128)(2,1)}, bf16[3584,128]{1,0:T(8,128)(2,1)S(1)}, u32[]{:S(2)}, u32[]{:S(2)}) collective-permute-start(bf16[3584,128]{1,0:T(8,128)(2,1)} %get-tuple-element.216), channel_id=1, source_target_pairs={{0,2},{1,3},{2,0},{3,1},{4,6},{5,7},{6,4},{7,5},{8,10},{9,11},{10,... | collective-permute-start | bytes 2752520 | tf_op jit(solution)/shard_map/ppermute | solution.py:186
  283.9 44.1 %collective-permute-start.34 = (bf16[3584,128]{1,0:T(8,128)(2,1)}, bf16[3584,128]{1,0:T(8,128)(2,1)S(1)}, u32[]{:S(2)}, u32[]{:S(2)}) collective-permute-start(bf16[3584,128]{1,0:T(8,128)(2,1)} %get-tuple-element.217), channel_id=1, source_target_pairs={{0,3},{1,2},{2,1},{3,0},{4,7},{5,6},{6,5},{7,4},{8,11},{9,10},{10,... | collective-permute-start | bytes 2752520 | tf_op jit(solution)/shard_map/ppermute | solution.py:186
  342.0 45.6 %collective-permute-start.44 = (bf16[3584,128]{1,0:T(8,128)(2,1)}, bf16[3584,128]{1,0:T(8,128)(2,1)S(1)}, u32[]{:S(2)}, u32[]{:S(2)}) collective-permute-start(bf16[3584,128]{1,0:T(8,128)(2,1)} %shard_map.62.refs_3_), channel_id=1, source_target_pairs={{0,1},{1,0},{2,3},{3,2},{4,5},{5,4},{6,7},{7,6},{8,9},{9,8},{10,11... | collective-permute-start | bytes 2752520 | tf_op jit(solution)/shard_map/ppermute | solution.py:186
  342.3 45.3 %collective-permute-start.45 = (bf16[3584,128]{1,0:T(8,128)(2,1)}, bf16[3584,128]{1,0:T(8,128)(2,1)S(1)}, u32[]{:S(2)}, u32[]{:S(2)}) collective-permute-start(bf16[3584,128]{1,0:T(8,128)(2,1)} %shard_map.62.refs_3_), channel_id=1, source_target_pairs={{0,2},{1,3},{2,0},{3,1},{4,6},{5,7},{6,4},{7,5},{8,10},{9,11},{10,... | collective-permute-start | bytes 2752520 | tf_op jit(solution)/shard_map/ppermute | solution.py:186
  345.0 42.7 %collective-permute-start.46 = (bf16[3584,128]{1,0:T(8,128)(2,1)}, bf16[3584,128]{1,0:T(8,128)(2,1)S(1)}, u32[]{:S(2)}, u32[]{:S(2)}) collective-permute-start(bf16[3584,128]{1,0:T(8,128)(2,1)} %shard_map.62.refs_3_), channel_id=1, source_target_pairs={{0,3},{1,2},{2,1},{3,0},{4,7},{5,6},{6,5},{7,4},{8,11},{9,10},{10,... | collective-permute-start | bytes 2752520 | tf_op jit(solution)/shard_map/ppermute | solution.py:186
  392.9 39.2 %collective-permute-start.49 = (bf16[3584,128]{1,0:T(8,128)(2,1)}, bf16[3584,128]{1,0:T(8,128)(2,1)S(1)}, u32[]{:S(2)}, u32[]{:S(2)}) collective-permute-start(bf16[3584,128]{1,0:T(8,128)(2,1)} %shard_map.65.refs_7_), channel_id=1, source_target_pairs={{0,3},{1,2},{2,1},{3,0},{4,7},{5,6},{6,5},{7,4},{8,11},{9,10},{10,... | collective-permute-start | bytes 2752520 | tf_op jit(solution)/shard_map/ppermute | solution.py:186
  394.4 38.3 %collective-permute-start.51 = (bf16[3584,128]{1,0:T(8,128)(2,1)S(1)}, bf16[3584,128]{1,0:T(8,128)(2,1)S(1)}, u32[]{:S(2)}, u32[]{:S(2)}) collective-permute-start(bf16[3584,128]{1,0:T(8,128)(2,1)S(1)} %collective-permute-done.44.refs_4_), channel_id=1, source_target_pairs={{0,4},{4,0},{8,12},{12,8},{16,20},{20,16},{24,28},{28,24},{1,5},{5... | collective-permute-start | bytes 2752520 | tf_op jit(solution)/shard_map/ppermute | solution.py:186
  463.7 41.0 %collective-permute-start.58 = (bf16[1008,256]{1,0:T(8,128)(2,1)}, bf16[1008,256]{1,0:T(8,128)(2,1)S(1)}, u32[]{:S(2)}, u32[]{:S(2)}) collective-permute-start(bf16[1008,256]{1,0:T(8,128)(2,1)} %get-tuple-element.235), channel_id=1, source_target_pairs={{0,16},{4,20},{8,24},{12,28},{16,0},{20,4},{24,8},{28,12},{1,17},{... | collective-permute-start | bytes 1548296 | tf_op jit(solution)/shard_map/ppermute | solution.py:186
  509.9 44.2 %collective-permute-start.61 = (bf16[1008,256]{1,0:T(8,128)(2,1)}, bf16[1008,256]{1,0:T(8,128)(2,1)S(1)}, u32[]{:S(2)}, u32[]{:S(2)}) collective-permute-start(bf16[1008,256]{1,0:T(8,128)(2,1)} %get-tuple-element.256), channel_id=1, source_target_pairs={{0,16},{4,20},{8,24},{12,28},{16,0},{20,4},{24,8},{28,12},{1,17},{... | collective-permute-start | bytes 1548296 | tf_op jit(solution)/shard_map/ppermute | solution.py:186
  529.3 38.2 %collective-permute-start.65 = (bf16[224,2048]{1,0:T(8,128)(2,1)}, bf16[224,2048]{1,0:T(8,128)(2,1)}, u32[]{:S(2)}, u32[]{:S(2)}) collective-permute-start(bf16[224,2048]{1,0:T(8,128)(2,1)} %get-tuple-element.273), channel_id=1, source_target_pairs={{0,1},{1,0},{2,3},{3,2},{4,5},{5,4},{6,7},{7,6},{8,9},{9,8},{10,11... | collective-permute-start | bytes 2752520 | tf_op jit(solution)/shard_map/ppermute | solution.py:186
  531.6 42.2 %collective-permute-start.66 = (bf16[224,2048]{1,0:T(8,128)(2,1)}, bf16[224,2048]{1,0:T(8,128)(2,1)}, u32[]{:S(2)}, u32[]{:S(2)}) collective-permute-start(bf16[224,2048]{1,0:T(8,128)(2,1)} %get-tuple-element.274), channel_id=1, source_target_pairs={{0,2},{1,3},{2,0},{3,1},{4,6},{5,7},{6,4},{7,5},{8,10},{9,11},{10,... | collective-permute-start | bytes 2752520 | tf_op jit(solution)/shard_map/ppermute | solution.py:186
  532.3 41.4 %collective-permute-start.67 = (bf16[224,2048]{1,0:T(8,128)(2,1)}, bf16[224,2048]{1,0:T(8,128)(2,1)}, u32[]{:S(2)}, u32[]{:S(2)}) collective-permute-start(bf16[224,2048]{1,0:T(8,128)(2,1)} %get-tuple-element.275), channel_id=1, source_target_pairs={{0,3},{1,2},{2,1},{3,0},{4,7},{5,6},{6,5},{7,4},{8,11},{9,10},{10,... | collective-permute-start | bytes 2752520 | tf_op jit(solution)/shard_map/ppermute | solution.py:186
  591.7 43.3 %collective-permute-start.73 = (bf16[224,2048]{1,0:T(8,128)(2,1)}, bf16[224,2048]{1,0:T(8,128)(2,1)}, u32[]{:S(2)}, u32[]{:S(2)}) collective-permute-start(bf16[224,2048]{1,0:T(8,128)(2,1)} %get-tuple-element.291), channel_id=1, source_target_pairs={{0,2},{1,3},{2,0},{3,1},{4,6},{5,7},{6,4},{7,5},{8,10},{9,11},{10,... | collective-permute-start | bytes 2752520 | tf_op jit(solution)/shard_map/ppermute | solution.py:186
  594.7 41.6 %collective-permute-start.74 = (bf16[224,2048]{1,0:T(8,128)(2,1)}, bf16[224,2048]{1,0:T(8,128)(2,1)}, u32[]{:S(2)}, u32[]{:S(2)}) collective-permute-start(bf16[224,2048]{1,0:T(8,128)(2,1)} %get-tuple-element.292), channel_id=1, source_target_pairs={{0,3},{1,2},{2,1},{3,0},{4,7},{5,6},{6,5},{7,4},{8,11},{9,10},{10,... | collective-permute-start | bytes 2752520 | tf_op jit(solution)/shard_map/ppermute | solution.py:186
  603.2 39.9 %collective-permute-start.76 = (bf16[224,512]{1,0:T(8,128)(2,1)}, bf16[224,512]{1,0:T(8,128)(2,1)S(1)}, u32[]{:S(2)}, u32[]{:S(2)}) collective-permute-start(bf16[224,512]{1,0:T(8,128)(2,1)} %get-tuple-element.299), channel_id=1, source_target_pairs={{0,2},{1,3},{2,0},{3,1},{4,6},{5,7},{6,4},{7,5},{8,10},{9,11},{10,... | collective-permute-start | bytes 688136 | tf_op jit(solution)/shard_map/ppermute | solution.py:186
  (123 other events, 2020.3 us)
